TPU v7x, 32 devices: a whole 2x2x4 slice. The times are simulated.
32 devices in a mesh: dp: 8 (over z, x), tensor: 4 (over y, core).
Axes of the slice: x: 2, y: 2, z: 4, core: 2. Of those that a mesh axis runs over, the one named last changes fastest.
Arguments:
- token_ids: int32 [16384], P(('dp', 'tensor')), may hold values from 0 to 50271
- slot_perm: int32 [16384], P(('dp', 'tensor')), may hold values from 0 to 16383, each once
- seq_lengths: int32 [8, 8], P('dp'), may hold values from 1 to 512, 2048 in all within a row
- pair_index: int32 [64], P('dp'), may hold values from 0 to 63, as said below
- tok_table: float32 [50272, 1024], P('dp', 'tensor'), may hold values from -0.3125 to 0.3125
- tok_first: float32 [50272, 1024], P('dp', 'tensor'), may hold values from -2.2888184e-05 to 2.2888184e-05
- tok_second: float32 [50272, 1024], P('dp', 'tensor'), may hold values from 9.522163e-13 to 3.808865e-12
- pos_table: float32 [514, 1024], P(None, 'tensor'), may hold values from -0.3125 to 0.3125
- pos_first: float32 [514, 1024], P(None, 'tensor'), may hold values from -2.2888184e-05 to 2.2888184e-05
- pos_second: float32 [514, 1024], P(None, 'tensor'), may hold values from 9.522163e-13 to 3.808865e-12
- query_key_value_weight: float32 [1024, 3, 1024], P('dp', None, 'tensor'), may hold values from -0.1875 to 0.1875
- qkv_first: float32 [1024, 3, 1024], P('dp', None, 'tensor'), may hold values from -2.2888184e-05 to 2.2888184e-05
- qkv_second: float32 [1024, 3, 1024], P('dp', None, 'tensor'), may hold values from 9.522163e-13 to 3.808865e-12
- out_weight: float32 [1024, 1024], P('tensor', 'dp'), may hold values from -0.75 to 0.75
- out_first: float32 [1024, 1024], P('tensor', 'dp'), may hold values from -2.2888184e-05 to 2.2888184e-05
- out_second: float32 [1024, 1024], P('tensor', 'dp'), may hold values from 9.522163e-13 to 3.808865e-12
- up_weight: float32 [1024, 4, 1024], P('dp', None, 'tensor'), may hold values from -0.1875 to 0.1875
- up_first: float32 [1024, 4, 1024], P('dp', None, 'tensor'), may hold values from -2.2888184e-05 to 2.2888184e-05
- up_second: float32 [1024, 4, 1024], P('dp', None, 'tensor'), may hold values from 9.522163e-13 to 3.808865e-12
- down_weight: float32 [4, 1024, 1024], P(None, 'tensor', 'dp'), may hold values from -0.09375 to 0.09375
- down_first: float32 [4, 1024, 1024], P(None, 'tensor', 'dp'), may hold values from -2.2888184e-05 to 2.2888184e-05
- down_second: float32 [4, 1024, 1024], P(None, 'tensor', 'dp'), may hold values from 9.522163e-13 to 3.808865e-12
- head_weight: float32 [1024, 1024], replicated, may hold values from -0.1875 to 0.1875
- head_first: float32 [1024, 1024], replicated, may hold values from -2.2888184e-05 to 2.2888184e-05
- head_second: float32 [1024, 1024], replicated, may hold values from 9.522163e-13 to 3.808865e-12
- col_bias: float32 [6, 1024], P(None, 'tensor'), may hold values from -0.625 to 0.625
- col_first: float32 [6, 1024], P(None, 'tensor'), may hold values from -0.00010681152 to 0.00010681152
- col_second: float32 [6, 1024], P(None, 'tensor'), may hold values from 2.285319e-11 to 9.141276e-11
- row_params: float32 [8, 1024], replicated
- row_first: float32 [8, 1024], replicated, may hold values from -0.00010681152 to 0.00010681152
- row_second: float32 [8, 1024], replicated, may hold values from 2.285319e-11 to 9.141276e-11
Outputs:
- loss_sum: float32 [], replicated
- grad_norm: float32 [], replicated
- tok_table_new: float32 [50272, 1024], P('dp', 'tensor')
- tok_first_new: float32 [50272, 1024], P('dp', 'tensor')
- tok_second_new: float32 [50272, 1024], P('dp', 'tensor')
- pos_table_new: float32 [514, 1024], P(None, 'tensor')
- pos_first_new: float32 [514, 1024], P(None, 'tensor')
- pos_second_new: float32 [514, 1024], P(None, 'tensor')
- qkv_weight_new: float32 [1024, 3, 1024], P('dp', None, 'tensor')
- qkv_first_new: float32 [1024, 3, 1024], P('dp', None, 'tensor')
- qkv_second_new: float32 [1024, 3, 1024], P('dp', None, 'tensor')
- out_weight_new: float32 [1024, 1024], P('tensor', 'dp')
- out_first_new: float32 [1024, 1024], P('tensor', 'dp')
- out_second_new: float32 [1024, 1024], P('tensor', 'dp')
- up_weight_new: float32 [1024, 4, 1024], P('dp', None, 'tensor')
- up_first_new: float32 [1024, 4, 1024], P('dp', None, 'tensor')
- up_second_new: float32 [1024, 4, 1024], P('dp', None, 'tensor')
- down_weight_new: float32 [4, 1024, 1024], P(None, 'tensor', 'dp')
- down_first_new: float32 [4, 1024, 1024], P(None, 'tensor', 'dp')
- down_second_new: float32 [4, 1024, 1024], P(None, 'tensor', 'dp')
- head_weight_new: float32 [1024, 1024], replicated
- head_first_new: float32 [1024, 1024], replicated
- head_second_new: float32 [1024, 1024], replicated
- col_bias_new: float32 [6, 1024], P(None, 'tensor')
- col_first_new: float32 [6, 1024], P(None, 'tensor')
- col_second_new: float32 [6, 1024], P(None, 'tensor')
- row_params_new: float32 [8, 1024], replicated
- row_first_new: float32 [8, 1024], replicated
- row_second_new: float32 [8, 1024], replicated
Inputs may be any that keep to these rules, and one draw needn't show every extreme that they name: pair_index[i] names a sequence other than i, in the order of pooled. `seq_lengths`: each group's 8 lengths add up to 2048. `slot_perm`: each arrival position once.
All inputs are finite; a program needn't handle non-finite values.
Results may differ from a plain program's by a relative error of at most 0.012.
The roundings to bfloat16 on the way count: a program that leaves them out, or rounds other values in their place, can miss the bound.
Values may be sent and summed in bfloat16 or wider, within the bound.
A program may use at most 256 MiB of HBM per device.

v0:
```python
from functools import partial

import jax
import jax.numpy as jnp
from jax import lax
from jax.sharding import PartitionSpec as P

D = 1024
HEAD = 64
MAXLEN = 512
STEP = 10


HIGHEST_MODE = lax.Precision.HIGHEST
LN_EPS = 1e-05
LOGIT_DIVISOR = 0.05
CLIP_NORM = 0.25
BETA_FIRST = 0.9
BETA_SECOND = 0.999
ADAM_EPS = 1e-08
RATE_MATRIX = 0.05
RATE_VECTOR = 0.5
DECAY_RATE = 0.01
MASK_FILL = -1e30


def multiply_arrays(left_mat, right_mat):
    return jnp.dot(left_mat, right_mat, preferred_element_type=jnp.float32)


def exact_multiply(left_mat, right_mat):
    return jnp.dot(left_mat, right_mat, precision=HIGHEST_MODE, preferred_element_type=jnp.float32)


def norm_rows(values, gain_row, bias_row):
    center = values - jnp.mean(values, axis=1, keepdims=True)
    inverse = lax.rsqrt(jnp.mean(center * center, axis=1, keepdims=True) + LN_EPS)
    return center * inverse * gain_row + bias_row


def norm_back(values, gain_row, bias_row, grad_rows):
    norm_pull = jax.vjp(norm_rows, values, gain_row, bias_row)[1]
    return norm_pull(grad_rows)


def seq_layout(lengths, slot_total):
    seq_ends = jnp.cumsum(lengths)
    starts = seq_ends - lengths
    slot_index = jnp.arange(slot_total, dtype=jnp.int32)
    member = (slot_index[:, None] >= starts[None, :]) & (slot_index[:, None] < seq_ends[None, :])
    seq_count = jnp.arange(lengths.shape[0], dtype=jnp.int32)
    seq_ids = jnp.sum(jnp.where(member, seq_count[None, :], 0), axis=1)
    positions = slot_index - jnp.sum(jnp.where(member, starts[None, :], 0), axis=1) + 2
    return (seq_ids, positions, member)


def contrast(vectors, pair_rows, first_row):
    anchors = pair_rows.shape[0]
    others = jnp.arange(vectors.shape[0], dtype=jnp.int32)
    own_ids = first_row + jnp.arange(anchors, dtype=jnp.int32)
    result = jnp.zeros((), jnp.float32)
    for fraction in (16, 4, 1):
        part_width = vectors.shape[1] // fraction
        prefix = vectors[:, :part_width]
        unit_length_entries = prefix * lax.rsqrt(
            jnp.sum(prefix * prefix, axis=1, keepdims=True) + 1e-06
        )
        reference_embedding = lax.dynamic_slice_in_dim(unit_length_entries, first_row, anchors, 0)
        cosine_logits = exact_multiply(reference_embedding, unit_length_entries.T) / LOGIT_DIVISOR
        cosine_logits = jnp.where(own_ids[:, None] == others[None, :], MASK_FILL, cosine_logits)
        positive = jnp.sum(
            jnp.where(pair_rows[:, None] == others[None, :], cosine_logits, 0.0), axis=1
        )
        result = result + jnp.sum(jax.nn.logsumexp(cosine_logits, axis=1) - positive)
    return result


def adam_step(weight, first_old, second_old, clipped, step_rate, decay_rate):
    first_new = BETA_FIRST * first_old + (1.0 - BETA_FIRST) * clipped
    second_new = BETA_SECOND * second_old + (1.0 - BETA_SECOND) * clipped * clipped
    first_hat = first_new / (1.0 - BETA_FIRST**STEP)
    second_hat = second_new / (1.0 - BETA_SECOND**STEP)
    weight_new = weight - step_rate * (
        first_hat / (jnp.sqrt(second_hat) + ADAM_EPS) + decay_rate * weight
    )
    return (weight_new, first_new, second_new)


def spread_rows(local_rows):
    return lax.all_gather(local_rows, "tensor", axis=0, tiled=True)


def fold_rows(partial_rows):
    return lax.psum_scatter(partial_rows, "tensor", scatter_dimension=0, tiled=True)


def pad_keys(key_rows, value_rows, seq_ids):
    block_rows = MAXLEN
    keys_pad = jnp.pad(key_rows, ((block_rows, block_rows), (0, 0), (0, 0)))
    values_pad = jnp.pad(value_rows, ((block_rows, block_rows), (0, 0), (0, 0)))
    seq_pad = jnp.pad(seq_ids, (block_rows, block_rows), constant_values=-1)
    return (keys_pad, values_pad, seq_pad)


def score_block(q_blk, k_blk, q_seq, k_seq):
    scores = jnp.einsum(
        "qhd,khd->hqk", q_blk, k_blk, preferred_element_type=jnp.float32
    ) * HEAD ** (-0.5)
    return jnp.where((q_seq[:, None] == k_seq[None, :])[None], scores, MASK_FILL)


def attend(query_rows, key_rows, value_rows, seq_ids):
    block_rows = MAXLEN
    block_count = query_rows.shape[0] // block_rows
    keys_pad, values_pad, seq_pad = pad_keys(key_rows, value_rows, seq_ids)

    def one_block(block_index):
        first_row = block_index * block_rows
        q_blk = lax.dynamic_slice_in_dim(query_rows, first_row, block_rows, 0)
        k_blk = lax.dynamic_slice_in_dim(keys_pad, first_row, 3 * block_rows, 0)
        v_blk = lax.dynamic_slice_in_dim(values_pad, first_row, 3 * block_rows, 0)
        q_seq = lax.dynamic_slice_in_dim(seq_ids, first_row, block_rows, 0)
        k_seq = lax.dynamic_slice_in_dim(seq_pad, first_row, 3 * block_rows, 0)
        scores = score_block(q_blk, k_blk, q_seq, k_seq)
        row_top = jnp.max(scores, axis=-1, keepdims=True)
        weights = jnp.exp(scores - row_top)
        row_total = jnp.sum(weights, axis=-1, keepdims=True)
        softmaxed = (weights / row_total).astype(jnp.bfloat16)
        block_out = jnp.einsum("hqk,khd->qhd", softmaxed, v_blk, preferred_element_type=jnp.float32)
        return (block_out, row_top[..., 0] + jnp.log(row_total[..., 0]))

    blocks_out, log_total = lax.map(one_block, jnp.arange(block_count, dtype=jnp.int32))
    return (blocks_out.reshape(query_rows.shape), log_total)


def attend_back(query_rows, key_rows, value_rows, seq_ids, log_total, grad_out):
    block_rows = MAXLEN
    block_count = query_rows.shape[0] // block_rows
    keys_pad, values_pad, seq_pad = pad_keys(key_rows, value_rows, seq_ids)
    zeros_pad = jnp.zeros(keys_pad.shape, jnp.float32)
    scale_factor = HEAD ** (-0.5)

    def one_block(state_pair, block_index):
        key_grad, value_grad = state_pair
        first_row = block_index * block_rows
        q_blk = lax.dynamic_slice_in_dim(query_rows, first_row, block_rows, 0)
        g_blk = lax.dynamic_slice_in_dim(grad_out, first_row, block_rows, 0)
        k_blk = lax.dynamic_slice_in_dim(keys_pad, first_row, 3 * block_rows, 0)
        v_blk = lax.dynamic_slice_in_dim(values_pad, first_row, 3 * block_rows, 0)
        q_seq = lax.dynamic_slice_in_dim(seq_ids, first_row, block_rows, 0)
        k_seq = lax.dynamic_slice_in_dim(seq_pad, first_row, 3 * block_rows, 0)
        scores = score_block(q_blk, k_blk, q_seq, k_seq)
        softmaxed = jnp.exp(scores - log_total[block_index][:, :, None])
        prob_grad = jnp.einsum("qhd,khd->hqk", g_blk, v_blk, preferred_element_type=jnp.float32)
        inner = jnp.sum(softmaxed * prob_grad, axis=-1, keepdims=True)
        score_grad = (softmaxed * (prob_grad - inner)).astype(jnp.bfloat16)
        query_grad = (
            jnp.einsum("hqk,khd->qhd", score_grad, k_blk, preferred_element_type=jnp.float32)
            * scale_factor
        )
        key_part = (
            jnp.einsum("hqk,qhd->khd", score_grad, q_blk, preferred_element_type=jnp.float32)
            * scale_factor
        )
        value_part = jnp.einsum(
            "hqk,qhd->khd",
            softmaxed.astype(jnp.bfloat16),
            g_blk,
            preferred_element_type=jnp.float32,
        )
        key_grad = lax.dynamic_update_slice_in_dim(
            key_grad,
            lax.dynamic_slice_in_dim(key_grad, first_row, 3 * block_rows, 0) + key_part,
            first_row,
            0,
        )
        value_grad = lax.dynamic_update_slice_in_dim(
            value_grad,
            lax.dynamic_slice_in_dim(value_grad, first_row, 3 * block_rows, 0) + value_part,
            first_row,
            0,
        )
        return ((key_grad, value_grad), query_grad)

    (key_grad, value_grad), query_grad = lax.scan(
        one_block, (zeros_pad, zeros_pad), jnp.arange(block_count, dtype=jnp.int32)
    )
    return (
        query_grad.reshape(query_rows.shape),
        key_grad[block_rows:-block_rows],
        value_grad[block_rows:-block_rows],
    )


def layer_forward(emb_rows, seq_ids, row_params, col_local, layer_mats):
    qkv_full, out_full, up_full, down_full = layer_mats
    col_width = qkv_full.shape[2]
    norm_first = norm_rows(emb_rows, row_params[0], row_params[3])
    first_moment_all = spread_rows(norm_first.astype(jnp.bfloat16))
    qkv_bias = jnp.concatenate([col_local[0], jnp.zeros_like(col_local[0]), col_local[1]])
    qkv_out = (
        multiply_arrays(first_moment_all, qkv_full.reshape(D, 3 * col_width)) + qkv_bias
    ).astype(jnp.bfloat16)
    qkv_out = qkv_out.reshape(-1, 3, col_width // HEAD, HEAD)
    attn_out, log_total = attend(qkv_out[:, 0], qkv_out[:, 1], qkv_out[:, 2], seq_ids)
    attn_low = attn_out.reshape(-1, col_width).astype(jnp.bfloat16)
    first_sum = norm_first + fold_rows(multiply_arrays(attn_low, out_full)) + row_params[6]
    norm_second = norm_rows(first_sum, row_params[1], row_params[4])
    second_all = spread_rows(norm_second.astype(jnp.bfloat16))
    expansion_result = multiply_arrays(second_all, up_full.reshape(D, -1)) + col_local[2:].reshape(
        -1
    )
    hidden_low = jax.nn.gelu(expansion_result, approximate=False).astype(jnp.bfloat16)
    second_sum = (
        norm_second
        + fold_rows(multiply_arrays(hidden_low, down_full.reshape(-1, D)))
        + row_params[7]
    )
    norm_third = norm_rows(second_sum, row_params[2], row_params[5])
    saved_vals = (
        emb_rows,
        first_moment_all,
        qkv_out,
        log_total,
        attn_low,
        first_sum,
        second_all,
        expansion_result,
        hidden_low,
        second_sum,
    )
    return (norm_third, saved_vals)


def layer_backward(grad_third, seq_ids, row_params, layer_mats, saved_vals):
    qkv_full, out_full, up_full, down_full = layer_mats
    (
        emb_rows,
        first_moment_all,
        qkv_out,
        log_total,
        attn_low,
        first_sum,
        second_all,
        expansion_result,
        hidden_low,
        second_sum,
    ) = saved_vals
    col_width = qkv_full.shape[2]
    grad_second, gain_c, shift_c = norm_back(second_sum, row_params[2], row_params[5], grad_third)
    mixed_low = grad_second.astype(jnp.bfloat16)
    mixed_all = spread_rows(mixed_low)
    down_grad = jnp.einsum("tf,td->fd", hidden_low, mixed_all, preferred_element_type=jnp.float32)
    hidden_grad = jnp.einsum(
        "td,fd->tf", mixed_all, down_full.reshape(-1, D), preferred_element_type=jnp.float32
    )
    gelu_pull = jax.vjp(partial(jax.nn.gelu, approximate=False), expansion_result)[1]
    up_low = gelu_pull(hidden_grad)[0].astype(jnp.bfloat16)
    up_grad = jnp.einsum("td,tf->df", second_all, up_low, preferred_element_type=jnp.float32)
    second_total = grad_second + fold_rows(
        jnp.einsum("tf,df->td", up_low, up_full.reshape(D, -1), preferred_element_type=jnp.float32)
    )
    grad_first, gain_b, shift_b = norm_back(first_sum, row_params[1], row_params[4], second_total)
    branch_low = grad_first.astype(jnp.bfloat16)
    branch_all = spread_rows(branch_low)
    out_grad = jnp.einsum("tc,td->cd", attn_low, branch_all, preferred_element_type=jnp.float32)
    attn_grad = jnp.einsum(
        "td,cd->tc", branch_all, out_full, preferred_element_type=jnp.float32
    ).astype(jnp.bfloat16)
    head_count = col_width // HEAD
    query_grad, key_grad, value_grad = attend_back(
        qkv_out[:, 0],
        qkv_out[:, 1],
        qkv_out[:, 2],
        seq_ids,
        log_total,
        attn_grad.reshape(-1, head_count, HEAD),
    )
    qkv_low = (
        jnp.stack([query_grad, key_grad, value_grad], 1)
        .astype(jnp.bfloat16)
        .reshape(-1, 3 * col_width)
    )
    qkv_grad = jnp.einsum(
        "td,tc->dc", first_moment_all, qkv_low, preferred_element_type=jnp.float32
    )
    first_total = grad_first + fold_rows(
        jnp.einsum(
            "tc,dc->td", qkv_low, qkv_full.reshape(D, -1), preferred_element_type=jnp.float32
        )
    )
    emb_grad, gain_a, shift_a = norm_back(emb_rows, row_params[0], row_params[3], first_total)
    qkv_cols = jnp.sum(qkv_low.astype(jnp.float32), axis=0).reshape(3, col_width)
    up_cols = jnp.sum(up_low.astype(jnp.float32), axis=0).reshape(-1, col_width)
    col_grad = jnp.concatenate([qkv_cols[0:1], qkv_cols[2:3], up_cols], axis=0)
    row_grad = jnp.stack(
        [
            gain_a,
            gain_b,
            gain_c,
            shift_a,
            shift_b,
            shift_c,
            jnp.sum(branch_low.astype(jnp.float32), axis=0),
            jnp.sum(mixed_low.astype(jnp.float32), axis=0),
        ]
    )
    mats_grad = (
        qkv_grad.reshape(D, 3, col_width),
        out_grad,
        up_grad.reshape(D, -1, col_width),
        down_grad.reshape(-1, col_width, D),
    )
    return (emb_grad, mats_grad, col_grad, row_grad)


def body(
    token_ids,
    slot_perm,
    seq_lengths,
    pair_index,
    tok_table,
    tok_first,
    tok_second,
    pos_table,
    pos_first,
    pos_second,
    query_key_value_weight,
    qkv_first,
    qkv_second,
    out_weight,
    out_first,
    out_second,
    up_weight,
    up_first,
    up_second,
    down_weight,
    down_first,
    down_second,
    head_weight,
    head_first,
    head_second,
    col_bias,
    col_first,
    col_second,
    row_params,
    row_first,
    row_second,
):
    tensor_count = lax.axis_size("tensor")
    group_index = lax.axis_index("dp")
    tensor_index = lax.axis_index("tensor")
    tok_dev = token_ids.shape[0]
    tok_grp = tok_dev * tensor_count
    col_width = pos_table.shape[1]
    vocab_local = tok_table.shape[0]
    column_start = tensor_index * col_width
    every_id, every_perm = (
        lax.all_gather(token_ids, ("dp", "tensor"), axis=0, tiled=True),
        lax.all_gather(slot_perm, ("dp", "tensor"), axis=0, tiled=True),
    )
    slot_ids = jnp.take(every_id, every_perm, axis=0)
    lengths = seq_lengths[0]
    seq_ids, positions, member = seq_layout(lengths, tok_grp)
    offset = group_index * vocab_local
    tok_low = tok_table.astype(jnp.bfloat16)
    wanted = slot_ids - offset
    inside = (wanted >= 0) & (wanted < vocab_local)
    picked = jnp.take(tok_low, jnp.clip(wanted, 0, vocab_local - 1), axis=0)
    emb_cols = lax.psum_scatter(
        jnp.where(inside[:, None], picked.astype(jnp.float32), 0.0).astype(jnp.bfloat16),
        "dp",
        scatter_dimension=0,
        tiled=True,
    ).astype(jnp.float32)
    emb_cols = emb_cols + jnp.take(pos_table, positions, axis=0)
    emb_rows = lax.all_to_all(emb_cols, "tensor", split_axis=0, concat_axis=1, tiled=True)
    layer_mats = (
        lax.all_gather(query_key_value_weight.astype(jnp.bfloat16), "dp", axis=0, tiled=True),
        lax.all_gather(out_weight.astype(jnp.bfloat16), "dp", axis=1, tiled=True),
        lax.all_gather(up_weight.astype(jnp.bfloat16), "dp", axis=0, tiled=True),
        lax.all_gather(down_weight.astype(jnp.bfloat16), "dp", axis=2, tiled=True),
    )
    norm_third, saved_vals = layer_forward(emb_rows, seq_ids, row_params, col_bias, layer_mats)
    row_member = lax.dynamic_slice_in_dim(member, tensor_index * tok_dev, tok_dev, 0).astype(
        jnp.float32
    )
    counts = lengths.astype(jnp.float32)[:, None]
    pooled = lax.psum(exact_multiply(row_member.T, norm_third), "tensor") / counts
    pooled_low = pooled.astype(jnp.bfloat16)
    head_low = head_weight.astype(jnp.bfloat16)
    vectors = multiply_arrays(pooled_low, head_low)
    every_vec = lax.all_gather(vectors, "dp", axis=0, tiled=True)
    anchors = pair_index.shape[0]

    def own_loss(all_vectors):
        return contrast(all_vectors, pair_index, group_index * anchors)

    local_loss, loss_pull = jax.vjp(own_loss, every_vec)
    vec_grad = lax.psum_scatter(
        loss_pull(jnp.ones((), jnp.float32))[0], "dp", scatter_dimension=0, tiled=True
    )
    pooled_grad = exact_multiply(vec_grad, head_low.astype(jnp.float32).T)
    head_cols = exact_multiply(
        pooled_low.astype(jnp.float32).T,
        lax.dynamic_slice_in_dim(vec_grad, column_start, col_width, 1),
    )
    grad_third = exact_multiply(row_member, pooled_grad / counts)
    emb_grad, mats_grad, col_grad, row_grad = layer_backward(
        grad_third, seq_ids, row_params, layer_mats, saved_vals
    )
    cols_grad = lax.all_to_all(emb_grad, "tensor", split_axis=1, concat_axis=0, tiled=True)
    pos_grad = jax.ops.segment_sum(cols_grad, positions, num_segments=pos_table.shape[0])
    wanted = slot_ids - offset
    inside = (wanted >= 0) & (wanted < vocab_local)
    tok_grad = (
        jnp.zeros(tok_table.shape, jnp.float32)
        .at[jnp.clip(wanted, 0, vocab_local - 1)]
        .add(jnp.where(inside[:, None], lax.all_gather(cols_grad, "dp", axis=0, tiled=True), 0.0))
    )
    qkv_part, out_part, up_part, down_part = mats_grad
    qkv_grad, out_grad, up_grad, down_grad = (
        lax.psum_scatter(qkv_part, "dp", scatter_dimension=0, tiled=True),
        lax.psum_scatter(out_part, "dp", scatter_dimension=1, tiled=True),
        lax.psum_scatter(up_part, "dp", scatter_dimension=0, tiled=True),
        lax.psum_scatter(down_part, "dp", scatter_dimension=2, tiled=True),
    )
    col_full = lax.dynamic_update_slice_in_dim(
        jnp.zeros((col_grad.shape[0], D), jnp.float32), col_grad, column_start, 1
    )
    pos_full = lax.dynamic_update_slice_in_dim(
        jnp.zeros((pos_grad.shape[0], D), jnp.float32), pos_grad, column_start, 1
    )
    head_full = lax.dynamic_update_slice_in_dim(
        jnp.zeros((D, D), jnp.float32), head_cols, column_start, 1
    )
    local_squares = (
        jnp.sum(tok_grad * tok_grad)
        + jnp.sum(qkv_grad * qkv_grad)
        + jnp.sum(out_grad * out_grad)
        + jnp.sum(up_grad * up_grad)
        + jnp.sum(down_grad * down_grad)
    )
    loss_share = local_loss / tensor_count
    scalars = jnp.stack([loss_share])
    row_sum, col_sum, pos_sum, head_sum, scalar_sum = lax.psum(
        (row_grad, col_full, pos_full, head_full, scalars), ("dp", "tensor")
    )
    big_squares = lax.psum(local_squares, ("dp", "tensor"))
    squares = (
        big_squares
        + jnp.sum(row_sum * row_sum)
        + jnp.sum(col_sum * col_sum)
        + jnp.sum(pos_sum * pos_sum)
        + jnp.sum(head_sum * head_sum)
    )
    grad_norm = jnp.sqrt(squares)
    clip_scale = jnp.minimum(1.0, CLIP_NORM / (grad_norm + 1e-06))
    col_own = lax.dynamic_slice_in_dim(col_sum, column_start, col_width, 1)
    pos_own = lax.dynamic_slice_in_dim(pos_sum, column_start, col_width, 1)
    tok_new = adam_step(
        tok_table, tok_first, tok_second, tok_grad * clip_scale, RATE_MATRIX, DECAY_RATE
    )
    pos_new = adam_step(
        pos_table, pos_first, pos_second, pos_own * clip_scale, RATE_MATRIX, DECAY_RATE
    )
    qkv_new = adam_step(
        query_key_value_weight,
        qkv_first,
        qkv_second,
        qkv_grad * clip_scale,
        RATE_MATRIX,
        DECAY_RATE,
    )
    out_new = adam_step(
        out_weight, out_first, out_second, out_grad * clip_scale, RATE_MATRIX, DECAY_RATE
    )
    up_new = adam_step(
        up_weight, up_first, up_second, up_grad * clip_scale, RATE_MATRIX, DECAY_RATE
    )
    down_new = adam_step(
        down_weight, down_first, down_second, down_grad * clip_scale, RATE_MATRIX, DECAY_RATE
    )
    head_new = adam_step(
        head_weight, head_first, head_second, head_sum * clip_scale, RATE_MATRIX, DECAY_RATE
    )
    col_new = adam_step(col_bias, col_first, col_second, col_own * clip_scale, RATE_VECTOR, 0.0)
    row_new = adam_step(row_params, row_first, row_second, row_sum * clip_scale, RATE_VECTOR, 0.0)
    return (
        scalar_sum[0],
        grad_norm,
        tok_new[0],
        tok_new[1],
        tok_new[2],
        pos_new[0],
        pos_new[1],
        pos_new[2],
        qkv_new[0],
        qkv_new[1],
        qkv_new[2],
        out_new[0],
        out_new[1],
        out_new[2],
        up_new[0],
        up_new[1],
        up_new[2],
        down_new[0],
        down_new[1],
        down_new[2],
        head_new[0],
        head_new[1],
        head_new[2],
        col_new[0],
        col_new[1],
        col_new[2],
        row_new[0],
        row_new[1],
        row_new[2],
    )


def solution(mesh):
    placed = (
        P(("dp", "tensor")),
        P(("dp", "tensor")),
        P("dp", None),
        P("dp"),
        P("dp", "tensor"),
        P("dp", "tensor"),
        P("dp", "tensor"),
        P(None, "tensor"),
        P(None, "tensor"),
        P(None, "tensor"),
        P("dp", None, "tensor"),
        P("dp", None, "tensor"),
        P("dp", None, "tensor"),
        P("tensor", "dp"),
        P("tensor", "dp"),
        P("tensor", "dp"),
        P("dp", None, "tensor"),
        P("dp", None, "tensor"),
        P("dp", None, "tensor"),
        P(None, "tensor", "dp"),
        P(None, "tensor", "dp"),
        P(None, "tensor", "dp"),
        P(),
        P(),
        P(),
        P(None, "tensor"),
        P(None, "tensor"),
        P(None, "tensor"),
        P(),
        P(),
        P(),
    )
    return jax.shard_map(
        body,
        mesh=mesh,
        in_specs=placed,
        out_specs=(
            P(),
            P(),
            P("dp", "tensor"),
            P("dp", "tensor"),
            P("dp", "tensor"),
            P(None, "tensor"),
            P(None, "tensor"),
            P(None, "tensor"),
            P("dp", None, "tensor"),
            P("dp", None, "tensor"),
            P("dp", None, "tensor"),
            P("tensor", "dp"),
            P("tensor", "dp"),
            P("tensor", "dp"),
            P("dp", None, "tensor"),
            P("dp", None, "tensor"),
            P("dp", None, "tensor"),
            P(None, "tensor", "dp"),
            P(None, "tensor", "dp"),
            P(None, "tensor", "dp"),
            P(),
            P(),
            P(),
            P(None, "tensor"),
            P(None, "tensor"),
            P(None, "tensor"),
            P(),
            P(),
            P(),
        ),
        check_vma=False,
    )
```

profile of v0, /device:TPU:0, one launch (start us, length us, event | category | flops | bytes accessed | tf_op | source)
XLA Modules:
  0.0 2385.9 jit_solution(6810451040819387998)
XLA Ops:
  7.3 43.6 %all-gather.1 = s32[32,1,512]{2,1,0:T(1,128)S(1)} all-gather(s32[1,1,512]{2,1,0:T(1,128)} %bitcast.230), channel_id=1, replica_groups=mesh['dp'=8,'tensor'=4] {'dp','tensor'}, dimensions={0}, use_global_device_ids=true | all-gather | bytes 67584 | tf_op jit(solution)/shard_map/all_gather | solution.py:359
  50.9 37.0 %all-gather = s32[32,1,512]{2,1,0:T(1,128)S(1)} all-gather(s32[1,1,512]{2,1,0:T(1,128)} %bitcast.231), channel_id=1, replica_groups=mesh['dp'=8,'tensor'=4] {'dp','tensor'}, dimensions={0}, use_global_device_ids=true | all-gather | bytes 67584 | tf_op jit(solution)/shard_map/all_gather | solution.py:360
  88.0 90.5 %gather_fusion = s32[16384]{0:T(1024)S(1)} fusion(s32[16384]{0:T(1024)S(1)} %bitcast.169, s32[16384]{0:T(1024)S(1)} %fusion.88), kind=kCustom, calls=%fused_computation | custom fusion | bytes 196608 | tf_op jit(solution)/shard_map/jit(_take)/gather | solution.py:362
  182.4 64.8 %gather_fusion.1 = bf16[16384,256]{1,0:T(8,128)(2,1)} fusion(bf16[6284,256]{1,0:T(8,128)(2,1)S(1)} %convert_element_type.115, s32[16384]{0:T(1024)S(1)} %broadcast_clamp_fusion), kind=kCustom, calls=%fused_computation.1 | custom fusion | bytes 16842752 | tf_op jit(solution)/shard_map/jit(_take)/gather | solution.py:369
  247.2 7.6 select_convert_fusion
  258.1 6.6 gather_fusion.2
  264.8 136.7 %reduce-scatter.10.cloned.1.call-done = bf16[2048,256]{1,0:T(8,128)(2,1)} async-done(((bf16[16384,256]{1,0:T(8,128)(2,1)}), bf16[2048,256]{1,0:T(8,128)(2,1)}) %reduce-scatter.10.cloned.1.call-update) | async-done | bytes 1048592 | tf_op jit(solution)/shard_map/reduce_scatter | solution.py:370
  408.4 25.0 %all-to-all-done = f32[4,512,256]{2,1,0:T(8,128)S(1)} async-done(((f32[4,512,256]{2,1,0:T(8,128)}), f32[4,512,256]{2,1,0:T(8,128)S(1)}, u32[]{:S(2)}, u32[]{:S(2)}) %all-to-all-start) | async-done | bytes 2097184 | tf_op jit(solution)/shard_map/all_to_all | solution.py:377
  442.8 27.9 %all_gather.40 = bf16[256,1024]{1,0:T(8,128)(2,1)S(1)} all-gather(bf16[256,128]{1,0:T(8,128)(2,1)S(1)} %convert_element_type.124), channel_id=1, replica_groups=mesh['dp'=8,'tensor'=4] {'dp'}, dimensions={1}, use_global_device_ids=true | all-gather | bytes 589824 | tf_op jit(solution)/shard_map/all_gather | solution.py:380
  470.7 14.6 all-gather.11.cloned.1.call-done
  485.3 6.1 add_convert_fusion.1
  494.3 55.7 %while.26 = (s32[]{:T(128)}, bf16[4,512,4,64]{1,3,2,0:T(8,128)(2,1)S(1)}, f32[4,4,512]{2,1,0:T(4,128)S(1)}, s32[4]{0:T(128)S(1)}, bf16[3072,4,64]{0,2,1:T(8,128)...) while((s32[]{:T(128)}, ...), condition=%wide.region_9.10_spmd, body=%wide.region_6.9_spmd.sunk | while | flops 843839488 | bytes 43344124 | solution.py:132
  558.8 69.8 %reduce-scatter.12.cloned.1.call-done = f32[512,1024]{1,0:T(8,128)} async-done(((f32[2048,1024]{1,0:T(8,128)}), f32[512,1024]{1,0:T(8,128)}) %reduce-scatter.12.cloned.1.call-update) | async-done | bytes 2097168 | tf_op jit(solution)/shard_map/reduce_scatter | solution.py:94
  635.1 45.2 %all-gather.17.cloned.1.call-done = bf16[1024,4,256]{2,1,0:T(4,128)(2,1)} async-done(((bf16[128,4,256]{2,1,0:T(4,128)(2,1)}), bf16[1024,4,256]{2,1,0:T(4,128)(2,1)}) %all-gather.17.cloned.1.call-update) | async-done | bytes 2097168 | tf_op jit(solution)/shard_map/all_gather | solution.py:381
  683.8 31.6 %all-gather.15.cloned.1.call-done = bf16[2048,1024]{1,0:T(8,128)(2,1)} async-done(((bf16[512,1024]{1,0:T(8,128)(2,1)}), bf16[2048,1024]{1,0:T(8,128)(2,1)}) %all-gather.15.cloned.1.call-update) | async-done | bytes 4194320 | tf_op jit(solution)/shard_map/all_gather | solution.py:90
  715.4 26.2 %multiply_convert_fusion.1 = (bf16[2048,1024]{1,0:T(8,128)(2,1)}, f32[2048,1024]{1,0:T(8,128)}, f32[2048,1024]{1,0:T(8,128)}) fusion(f32[1024]{0:T(1024)S(1)} %bitcast.226, bf16[2048,1024]{1,0:T(8,128)(2,1)} %all-gather.15.cloned.1.call-done, bf16[1024,1024]{1,0:T(8,128)(2,1)} %bitcast.190), kind=kOutput, calls=%fused_computation.60 | convolution fusion | flops 4433379328 | bytes 27267072 | tf_op jit(solution)/shard_map/dot_general | solution.py:28
  741.6 27.5 %all-gather.19.cloned.1.call-done = bf16[4,256,1024]{2,1,0:T(8,128)(2,1)} async-done(((bf16[4,256,128]{2,1,0:T(8,128)(2,1)}), bf16[4,256,1024]{2,1,0:T(8,128)(2,1)}) %all-gather.19.cloned.1.call-update) | async-done | bytes 2097168 | tf_op jit(solution)/shard_map/all_gather | solution.py:382
  769.1 10.6 fusion.157
  780.5 69.3 %reduce-scatter.14.cloned.1.call-done = f32[512,1024]{1,0:T(8,128)} async-done(((f32[2048,1024]{1,0:T(8,128)}), f32[512,1024]{1,0:T(8,128)}) %reduce-scatter.14.cloned.1.call-update) | async-done | bytes 2097168 | tf_op jit(solution)/shard_map/reduce_scatter | solution.py:94
  855.3 10.3 psum.49
  868.2 30.9 %all_gather.44 = f32[64,1024]{1,0:T(8,128)S(1)} all-gather(f32[8,1024]{1,0:T(8,128)S(1)} %fusion.72), channel_id=1, replica_groups=mesh['dp'=8,'tensor'=4] {'dp'}, dimensions={0}, use_global_device_ids=true | all-gather | bytes 294912 | tf_op jit(solution)/shard_map/all_gather | solution.py:393
  905.7 62.2 %reduce-scatter.16.cloned.1.call-done = f32[8,1024]{1,0:T(8,128)} async-done(((f32[64,1024]{1,0:T(8,128)}), f32[8,1024]{1,0:T(8,128)}) %reduce-scatter.16.cloned.1.call-update) | async-done | bytes 32784 | tf_op jit(solution)/shard_map/reduce_scatter | solution.py:400
  978.3 33.5 %all-gather.21.cloned.1.call-done = bf16[2048,1024]{1,0:T(8,128)(2,1)} async-done(((bf16[512,1024]{1,0:T(8,128)(2,1)}), bf16[2048,1024]{1,0:T(8,128)(2,1)}) %all-gather.21.cloned.1.call-update) | async-done | bytes 4194320 | tf_op jit(solution)/shard_map/all_gather | solution.py:90
  1011.8 14.0 convert_reduce_fusion
  1027.9 6.9 fusion.158
  1034.8 71.8 %reduce-scatter.18.cloned.1.call-done = f32[512,1024]{1,0:T(8,128)} async-done(((f32[2048,1024]{1,0:T(8,128)}), f32[512,1024]{1,0:T(8,128)}) %reduce-scatter.18.cloned.1.call-update) | async-done | bytes 2097168 | tf_op jit(solution)/shard_map/reduce_scatter | solution.py:94
  1115.2 34.6 %all-gather.23.cloned.1.call-done = bf16[2048,1024]{1,0:T(8,128)(2,1)} async-done(((bf16[512,1024]{1,0:T(8,128)(2,1)}), bf16[2048,1024]{1,0:T(8,128)(2,1)}) %all-gather.23.cloned.1.call-update) | async-done | bytes 4194320 | tf_op jit(solution)/shard_map/all_gather | solution.py:90
  1158.3 138.8 %while.27 = (s32[]{:T(128)}, f32[3072,4,64]{0,2,1:T(8,128)}, f32[3072,4,64]{0,2,1:T(8,128)}, bf16[4,512,4,64]{1,0,3,2:T(4,128)(2,1)}, s32[4]{0:T(128)S(1)}, /*in...) while((s32[]{:T(128)}, f32[3072,4,64]{0,2,1:T(8,128)}, ...), condition=%wide.region_44.45_spmd, body=%wide.region_42.44_spmd.sunk | while | flops 2043803648 | bytes 178324000 | solution.py:185
  1201.0 5.7 multiply_reduce_fusion.25
  1235.6 5.7 multiply_reduce_fusion.25
  1304.9 6.2 fusion.159
  1311.1 10.5 fusion.161
  1321.6 5.8 copy.84
  1327.6 10.0 fusion.162
  1343.5 8.4 fusion.53
  1352.0 30.9 %reduce-scatter.20.cloned.1.call-done = f32[512,1024]{1,0:T(8,128)} async-done(((f32[2048,1024]{1,0:T(8,128)}), f32[512,1024]{1,0:T(8,128)}) %reduce-scatter.20.cloned.1.call-update) | async-done | bytes 2097168 | tf_op jit(solution)/shard_map/reduce_scatter | solution.py:94
  1397.2 20.7 all-to-all-done.1
  1419.2 11.8 scatter_custom_fusion.1
  1436.7 107.2 %all-reduce.11.cloned.1.call-done = f32[1024,4,256]{2,1,0:T(4,128)} async-done(((f32[1024,4,256]{2,1,0:T(4,128)}), f32[1024,4,256]{2,1,0:T(4,128)}) %all-reduce.11.cloned.1.call-update) | async-done | bytes 4194320
  1545.8 90.1 %reduce-scatter.26.cloned.1.call-done = f32[4,256,128]{2,1,0:T(8,128)} async-done(((f32[4,256,1024]{2,1,0:T(8,128)}), f32[4,256,128]{2,1,0:T(8,128)}) %reduce-scatter.26.cloned.1.call-update) | async-done | bytes 524304 | tf_op jit(solution)/shard_map/reduce_scatter | solution.py:426
  1637.8 65.0 %reduce-scatter.24.cloned.1.call-done = f32[256,128]{1,0:T(8,128)} async-done(((f32[256,1024]{1,0:T(8,128)}), f32[256,128]{1,0:T(8,128)}) %reduce-scatter.24.cloned.1.call-update) | async-done | bytes 131088 | tf_op jit(solution)/shard_map/reduce_scatter | solution.py:424
  1704.4 77.1 %reduce-scatter.22.cloned.1.call-done = f32[128,3,256]{2,0,1:T(8,128)} async-done(((f32[1024,3,256]{2,0,1:T(8,128)}), f32[128,3,256]{2,0,1:T(8,128)}) %reduce-scatter.22.cloned.1.call-update) | async-done | bytes 393232 | tf_op jit(solution)/shard_map/reduce_scatter | solution.py:423
  1783.2 162.9 %all-reduce.13.cloned.1.call-done = (f32[514,1024]{1,0:T(8,128)}, f32[1024,1024]{1,0:T(8,128)}) async-done(((f32[514,1024]{1,0:T(8,128)}, f32[1024,1024]{1,0:T(8,128)}), (f32[514,1024]{1,0:T(8,128)}, f32[1024,1024]{1,0:T(8,128)})) %all-reduce.13.cloned.1.call-update) | async-done | bytes 6299664 | tf_op jit(solution)/shard_map/psum | solution.py:446
  1950.0 226.5 %all-gather.25.cloned.1.call-done = f32[16384,256]{1,0:T(8,128)} async-done(((f32[2048,256]{1,0:T(8,128)}), f32[16384,256]{1,0:T(8,128)}) %all-gather.25.cloned.1.call-update) | async-done | bytes 16777232 | tf_op jit(solution)/shard_map/all_gather | solution.py:419
  2176.5 113.9 %scatter_custom_fusion = f32[6284,256]{1,0:T(8,128)} fusion(s32[16384]{0:T(1024)} %copy-done.45, f32[16384,256]{1,0:T(8,128)} %all-gather.25.cloned.1.call-done, f32[]{:T(128)} %constant.125.clone.1, pred[16384]{0:T(1024)(128)(4,1)S(1)} %copy-done.47), kind=kCustom, calls=%fused_computation.52 | custom fusion | flops 8388608 | bytes 23229440 | tf_op jit(solution)/shard_map/scatter-add | solution.py:419
  2300.1 37.9 %all-reduce.6 = (f32[]{:T(128)}, f32[]{:T(128)}, f32[8,1024]{1,0:T(8,128)S(1)}, f32[6,1024]{1,0:T(8,128)S(1)}) all-reduce(f32[]{:T(128)S(6)} %div.279, f32[]{:T(128)S(6)} %add.570, f32[8,1024]{1,0:T(8,128)S(1)} %stack.33, f32[6,1024]{1,0:T(8,128)S(1)} %maximum_dynamic-update-slice_fusion), channel_id=1, replica_groups=mesh['dp'=8,'tensor'=4] {'dp','tensor'}, use_global_device_ids=true, to_apply=%region_32.33 | all-reduce | flops 14338 | bytes 114704 | tf_op jit(solution)/shard_map/psum | solution.py:446
  2346.6 10.9 multiply_subtract_fusion.1
  2357.6 13.6 multiply_subtract_fusion
  (491 shorter events, 320.3 us)
Async XLA Ops:
  7.2 394.3 %reduce-scatter.10.cloned.1.call-start = ((), (), s32[]{:S(2)}) async-start(), calls=%async_computation.11 | async-start | bytes 9437184 | tf_op jit(solution)/shard_map/reduce_scatter | solution.py:370
  178.6 68.6 %copy-start.46 = (pred[16384]{0:T(1024)(128)(4,1)}, pred[16384]{0:T(1024)(128)(4,1)S(1)}, u32[]{:S(2)}) copy-start(pred[16384]{0:T(1024)(128)(4,1)S(1)} %get-tuple-element.269) | copy-start | bytes 49156
  254.9 215.8 %all-gather.13.cloned.1.call-start = ((), (), s32[]{:S(2)}) async-start(), calls=%async_computation.13 | async-start | bytes 1769472 | tf_op jit(solution)/shard_map/all_gather | solution.py:379
  264.8 143.0 %copy-start.50 = (f32[8,1024]{1,0:T(8,128)S(1)}, f32[8,1024]{1,0:T(8,128)}, u32[]{:S(2)}) copy-start(f32[8,1024]{1,0:T(8,128)} %param.63) | copy-start | bytes 98308
  404.1 29.3 %all-to-all-start = ((f32[4,512,256]{2,1,0:T(8,128)}), f32[4,512,256]{2,1,0:T(8,128)S(1)}, u32[]{:S(2)}, u32[]{:S(2)}) async-start(f32[4,512,256]{2,1,0:T(8,128)} %bitcast.177), calls=%async_computation.1 | async-start | bytes 4194304 | tf_op jit(solution)/shard_map/all_to_all | solution.py:377
  407.7 77.6 %all-gather.11.cloned.1.call-start = ((), (), s32[]{:S(2)}) async-start(), calls=%async_computation.12 | async-start | bytes 5242880 | tf_op jit(solution)/shard_map/all_gather | solution.py:90
  408.4 220.1 %copy-start.52 = (f32[1,1024]{1,0:T(1,128)}, f32[1,1024]{1,0:T(1,128)S(1)}, u32[]{:S(2)}) copy-start(f32[1,1024]{1,0:T(1,128)S(1)} %get-tuple-element.276) | copy-start | bytes 12292
  439.2 189.3 %copy-start.55 = (f32[512]{0:T(512)}, f32[512]{0:T(512)S(1)}, u32[]{:S(2)}) copy-start(f32[512]{0:T(512)S(1)} %broadcast_multiply_fusion.3) | copy-start | bytes 6148
  441.2 187.4 %copy-start.58 = (f32[512]{0:T(512)}, f32[512]{0:T(512)S(1)}, u32[]{:S(2)}) copy-start(f32[512]{0:T(512)S(1)} %fusion.119) | copy-start | bytes 6148
  442.6 185.9 %reduce-scatter.12.cloned.1.call-start = ((), (), s32[]{:S(2)}) async-start(), calls=%async_computation.14 | async-start | bytes 10485760 | tf_op jit(solution)/shard_map/reduce_scatter | solution.py:94
  556.7 123.7 %all-gather.17.cloned.1.call-start = ((), (), s32[]{:S(2)}) async-start(), calls=%async_computation.16 | async-start | bytes 2359296 | tf_op jit(solution)/shard_map/all_gather | solution.py:381
  558.5 156.9 %all-gather.15.cloned.1.call-start = ((), (), s32[]{:S(2)}) async-start(), calls=%async_computation.15 | async-start | bytes 5242880 | tf_op jit(solution)/shard_map/all_gather | solution.py:90
  634.3 134.9 %all-gather.19.cloned.1.call-start = ((), (), s32[]{:S(2)}) async-start(), calls=%async_computation.17 | async-start | bytes 2359296 | tf_op jit(solution)/shard_map/all_gather | solution.py:382
  635.1 214.7 %reduce-scatter.14.cloned.1.call-start = ((), (), s32[]{:S(2)}) async-start(), calls=%async_computation.18 | async-start | bytes 10485760 | tf_op jit(solution)/shard_map/reduce_scatter | solution.py:94
  779.7 70.1 %copy-start.76 = (f32[1,1024]{1,0:T(1,128)S(1)}, f32[1,1024]{1,0:T(1,128)}, u32[]{:S(2)}) copy-start(f32[1,1024]{1,0:T(1,128)} %get-tuple-element.271) | copy-start | bytes 12292
  779.8 188.2 %reduce-scatter.16.cloned.1.call-start = ((), (), s32[]{:S(2)}) async-start(), calls=%async_computation.19 | async-start | bytes 294912 | tf_op jit(solution)/shard_map/reduce_scatter | solution.py:400
  853.2 47.6 %copy-start.81 = (s32[8]{0:T(128)S(1)}, s32[8]{0:T(128)}, u32[]{:S(2)}) copy-start(s32[8]{0:T(128)} %param.38) | copy-start | bytes 100
  905.7 106.1 %all-gather.21.cloned.1.call-start = ((), (), s32[]{:S(2)}) async-start(), calls=%async_computation.20 | async-start | bytes 5242880 | tf_op jit(solution)/shard_map/all_gather | solution.py:90
  978.1 128.5 %reduce-scatter.18.cloned.1.call-start = ((), (), s32[]{:S(2)}) async-start(), calls=%async_computation.21 | async-start | bytes 10485760 | tf_op jit(solution)/shard_map/reduce_scatter | solution.py:94
  1034.8 115.0 %all-gather.23.cloned.1.call-start = ((), (), s32[]{:S(2)}) async-start(), calls=%async_computation.22 | async-start | bytes 5242880 | tf_op jit(solution)/shard_map/all_gather | solution.py:90
  1111.9 42.3 %copy-start.67 = (f32[512]{0:T(512)}, f32[512]{0:T(512)S(1)}, u32[]{:S(2)}) copy-start(f32[512]{0:T(512)S(1)} %negate_multiply_fusion.2) | copy-start | bytes 6148
  1115.1 267.8 %reduce-scatter.20.cloned.1.call-start = ((), (), s32[]{:S(2)}) async-start(), calls=%async_computation.23 | async-start | bytes 10485760 | tf_op jit(solution)/shard_map/reduce_scatter | solution.py:94
  1311.1 232.8 %all-reduce.11.cloned.1.call-start = ((), (), s32[]{:S(2)}) async-start(), calls=%async_computation.28 | async-start | bytes 8388608
  1327.5 308.3 %reduce-scatter.26.cloned.1.call-start = ((), (), s32[]{:S(2)}) async-start(), calls=%async_computation.27 | async-start | bytes 4718592 | tf_op jit(solution)/shard_map/reduce_scatter | solution.py:426
  1337.6 365.2 %reduce-scatter.24.cloned.1.call-start = ((), (), s32[]{:S(2)}) async-start(), calls=%async_computation.26 | async-start | bytes 1179648 | tf_op jit(solution)/shard_map/reduce_scatter | solution.py:424
  1343.3 438.1 %reduce-scatter.22.cloned.1.call-start = ((), (), s32[]{:S(2)}) async-start(), calls=%async_computation.25 | async-start | bytes 3538944 | tf_op jit(solution)/shard_map/reduce_scatter | solution.py:423
  1343.5 39.4 %copy-start.53 = (f32[1,1024]{1,0:T(1,128)S(1)}, f32[1,1024]{1,0:T(1,128)}, u32[]{:S(2)}) copy-start(f32[1,1024]{1,0:T(1,128)} %copy-done.52) | copy-start | bytes 12292
  1343.5 39.4 %copy-start.56 = (f32[512]{0:T(512)S(1)}, f32[512]{0:T(512)}, u32[]{:S(2)}) copy-start(f32[512]{0:T(512)} %copy-done.55) | copy-start | bytes 6148
  1343.5 39.4 %copy-start.59 = (f32[512]{0:T(512)S(1)}, f32[512]{0:T(512)}, u32[]{:S(2)}) copy-start(f32[512]{0:T(512)} %copy-done.58) | copy-start | bytes 6148
  1343.5 39.4 %copy-start.68 = (f32[512]{0:T(512)S(1)}, f32[512]{0:T(512)}, u32[]{:S(2)}) copy-start(f32[512]{0:T(512)} %copy-done.67) | copy-start | bytes 6148
  1388.5 29.4 %all-to-all-start.1 = ((f32[512,4,256]{2,0,1:T(8,128)}), f32[512,4,256]{2,0,1:T(8,128)S(1)}, u32[]{:S(2)}, u32[]{:S(2)}) async-start(f32[512,4,256]{2,0,1:T(8,128)} %bitcast.180), calls=%async_computation.7 | async-start | bytes 4194304 | tf_op jit(solution)/shard_map/all_to_all | solution.py:412
  1392.3 553.9 %all-reduce.13.cloned.1.call-start = ((), (), s32[]{:S(2)}) async-start(), calls=%async_computation.29 | async-start | bytes 12648448 | tf_op jit(solution)/shard_map/psum | solution.py:446
  1431.4 351.7 %copy-start.69 = (f32[1024]{0:T(1024)S(1)}, f32[1024]{0:T(1024)}, u32[]{:S(2)}) copy-start(f32[1024]{0:T(1024)} %get-tuple-element.146) | copy-start | bytes 12292
  1431.4 351.7 %copy-start.70 = (f32[1024]{0:T(1024)S(1)}, f32[1024]{0:T(1024)}, u32[]{:S(2)}) copy-start(f32[1024]{0:T(1024)} %get-tuple-element.152) | copy-start | bytes 12292
  1431.4 351.7 %copy-start.71 = (f32[1024]{0:T(1024)S(1)}, f32[1024]{0:T(1024)}, u32[]{:S(2)}) copy-start(f32[1024]{0:T(1024)} %get-tuple-element.242) | copy-start | bytes 12292
  1431.4 351.7 %copy-start.72 = (f32[1024]{0:T(1024)S(1)}, f32[1024]{0:T(1024)}, u32[]{:S(2)}) copy-start(f32[1024]{0:T(1024)} %get-tuple-element.148) | copy-start | bytes 12292
  1431.4 351.7 %copy-start.73 = (f32[1024]{0:T(1024)S(1)}, f32[1024]{0:T(1024)}, u32[]{:S(2)}) copy-start(f32[1024]{0:T(1024)} %get-tuple-element.153) | copy-start | bytes 12292
  1431.5 351.7 %copy-start.74 = (f32[1024]{0:T(1024)S(1)}, f32[1024]{0:T(1024)}, u32[]{:S(2)}) copy-start(f32[1024]{0:T(1024)} %get-tuple-element.244) | copy-start | bytes 12292
  1432.7 743.8 %copy-start.47 = (pred[16384]{0:T(1024)(128)(4,1)S(1)}, pred[16384]{0:T(1024)(128)(4,1)}, u32[]{:S(2)}) copy-start(pred[16384]{0:T(1024)(128)(4,1)} %copy-done.46) | copy-start | bytes 49156
  1432.7 743.7 %all-gather.25.cloned.1.call-start = ((), (), s32[]{:S(2)}) async-start(), calls=%async_computation.24 | async-start | bytes 18874368 | tf_op jit(solution)/shard_map/all_gather | solution.py:419
  2290.4 52.2 %copy-start.2 = (f32[514,256]{1,0:T(8,128)S(1)}, f32[514,256]{1,0:T(8,128)}, u32[]{:S(2)}) copy-start(f32[514,256]{1,0:T(8,128)} %param.42) | copy-start | bytes 1579012
  2290.4 52.2 %copy-start.33 = (f32[514,256]{1,0:T(8,128)S(1)}, f32[514,256]{1,0:T(8,128)}, u32[]{:S(2)}) copy-start(f32[514,256]{1,0:T(8,128)} %param.43) | copy-start | bytes 1579012
  2295.6 49.7 %copy-start.64 = (f32[6,256]{1,0:T(8,128)S(1)}, f32[6,256]{1,0:T(8,128)}, u32[]{:S(2)}) copy-start(f32[6,256]{1,0:T(8,128)} %param.60) | copy-start | bytes 18436
  2295.6 49.7 %copy-start.79 = (f32[6,256]{1,0:T(8,128)S(1)}, f32[6,256]{1,0:T(8,128)}, u32[]{:S(2)}) copy-start(f32[6,256]{1,0:T(8,128)} %param.61) | copy-start | bytes 18436
  2295.7 49.7 %copy-start.80 = (f32[6,256]{1,0:T(8,128)S(1)}, f32[6,256]{1,0:T(8,128)}, u32[]{:S(2)}) copy-start(f32[6,256]{1,0:T(8,128)} %param.62) | copy-start | bytes 18436
  2295.7 50.3 %copy-start.51 = (f32[8,1024]{1,0:T(8,128)S(1)}, f32[8,1024]{1,0:T(8,128)}, u32[]{:S(2)}) copy-start(f32[8,1024]{1,0:T(8,128)} %param.63) | copy-start | bytes 98308
  2295.7 50.3 %copy-start.61 = (f32[8,1024]{1,0:T(8,128)S(1)}, f32[8,1024]{1,0:T(8,128)}, u32[]{:S(2)}) copy-start(f32[8,1024]{1,0:T(8,128)} %param.64) | copy-start | bytes 98308
  2295.7 50.3 %copy-start.62 = (f32[8,1024]{1,0:T(8,128)S(1)}, f32[8,1024]{1,0:T(8,128)}, u32[]{:S(2)}) copy-start(f32[8,1024]{1,0:T(8,128)} %param.65) | copy-start | bytes 98308
  (87 other events, 533.8 us)
Sparse Core Ops, SparseCore 0:
  255.0 146.4 reduce-scatter.9
  404.3 44.2 all-gather.12
  450.9 34.3 all-gather.10
  556.8 71.6 reduce-scatter.11
  631.1 49.2 all-gather.16
  682.4 32.9 all-gather.14
  718.0 51.0 all-gather.18
  779.9 69.8 reduce-scatter.13
  905.8 62.0 reduce-scatter.15
  978.2 33.5 all-gather.20
  1034.9 71.6 reduce-scatter.17
  1115.2 34.4 all-gather.22
  1311.2 71.7 reduce-scatter.19
  1387.5 156.3 all-reduce.10
  1548.3 87.4 reduce-scatter.25
  1639.1 63.6 reduce-scatter.23
  1707.3 74.0 reduce-scatter.21
  1789.2 156.8 all-reduce.12
  1949.1 227.3 all-gather.24
where the time goes:
time: 2390 us
  waiting for transfers between devices  1400 us (59%)
  other arithmetic  264 us (11%)
  local copies, waits for them, and re-layouts  247 us (10%)
  matrix products  236 us (10%)
  blocking collectives  188 us (8%)
  between operations  25.9 us (1%)
    reduce_scatter x4, waiting for transfers between devices, fold_rows(): lax.psum_scatter(partial_rows, 'tensor', scatter_dimension=0, tiled=True)  242 us
    all_gather x1, waiting for transfers between devices, body(): lax.all_gather(cols_grad, 'dp', axis=0, tiled=True)  226 us
    psum x1, waiting for transfers between devices, body(): lax.psum((row_grad, col_full, pos_full, head_full, scalars), ('dp', 'tens...  163 us
    reduce_scatter x1, waiting for transfers between devices, body(): lax.psum_scatter(jnp.where(inside[:, None], picked.astype(jnp.float32), 0...  137 us
    all_gather x4, waiting for transfers between devices, spread_rows(): return lax.all_gather(local_rows, 'tensor', axis=0, tiled=True)  114 us
    scatter-add x1, other arithmetic, body(): tok_grad = jnp.zeros(tok_table.shape, jnp.float32).at[jnp.clip(wanted, 0,...  114 us
    unnamed x20, waiting for transfers between devices  108 us
    gather x1, local copies, waits for them, and re-layouts, body(): slot_ids = jnp.take(every_id, every_perm, axis=0)  90.5 us
  transfers between devices with their start and end apart: 21, of which 20 were waited for; matrix products, arithmetic and copies ran while one was open for 5% of the time, Pallas kernels for 0%

commit v1 on v0

--- a/solution.py
+++ b/solution.py
@@ -3,6 +3,8 @@
 import jax
 import jax.numpy as jnp
 from jax import lax
+from jax.experimental import pallas as pl
+from jax.experimental.pallas import tpu as pltpu
 from jax.sharding import PartitionSpec as P
 
 D = 1024
@@ -54,27 +56,6 @@
     return (seq_ids, positions, member)
 
 
-def contrast(vectors, pair_rows, first_row):
-    anchors = pair_rows.shape[0]
-    others = jnp.arange(vectors.shape[0], dtype=jnp.int32)
-    own_ids = first_row + jnp.arange(anchors, dtype=jnp.int32)
-    result = jnp.zeros((), jnp.float32)
-    for fraction in (16, 4, 1):
-        part_width = vectors.shape[1] // fraction
-        prefix = vectors[:, :part_width]
-        unit_length_entries = prefix * lax.rsqrt(
-            jnp.sum(prefix * prefix, axis=1, keepdims=True) + 1e-06
-        )
-        reference_embedding = lax.dynamic_slice_in_dim(unit_length_entries, first_row, anchors, 0)
-        cosine_logits = exact_multiply(reference_embedding, unit_length_entries.T) / LOGIT_DIVISOR
-        cosine_logits = jnp.where(own_ids[:, None] == others[None, :], MASK_FILL, cosine_logits)
-        positive = jnp.sum(
-            jnp.where(pair_rows[:, None] == others[None, :], cosine_logits, 0.0), axis=1
-        )
-        result = result + jnp.sum(jax.nn.logsumexp(cosine_logits, axis=1) - positive)
-    return result
-
-
 def adam_step(weight, first_old, second_old, clipped, step_rate, decay_rate):
     first_new = BETA_FIRST * first_old + (1.0 - BETA_FIRST) * clipped
     second_new = BETA_SECOND * second_old + (1.0 - BETA_SECOND) * clipped * clipped
@@ -86,12 +67,400 @@
     return (weight_new, first_new, second_new)
 
 
-def spread_rows(local_rows):
-    return lax.all_gather(local_rows, "tensor", axis=0, tiled=True)
-
-
-def fold_rows(partial_rows):
-    return lax.psum_scatter(partial_rows, "tensor", scatter_dimension=0, tiled=True)
+MESH_IDS = pl.DeviceIdType.MESH
+VMEM_BYTES = 60 * 1024 * 1024
+
+
+def in_vmem():
+    return pl.BlockSpec(memory_space=pltpu.VMEM)
+
+
+def greet(partners):
+    barrier = pltpu.get_barrier_semaphore()
+    for partner in partners:
+        pl.semaphore_signal(barrier, inc=1, device_id=partner, device_id_type=MESH_IDS)
+    pl.semaphore_wait(barrier, len(partners))
+
+
+def remote(src, dst, send_sem, recv_sem, target):
+    return pltpu.make_async_remote_copy(
+        src_ref=src,
+        dst_ref=dst,
+        send_sem=send_sem,
+        recv_sem=recv_sem,
+        device_id=target,
+        device_id_type=MESH_IDS,
+    )
+
+
+def comm_params(collective):
+    return pltpu.CompilerParams(
+        collective_id=collective, has_side_effects=True, vmem_limit_bytes=VMEM_BYTES
+    )
+
+
+def gather_all_kernel(groups, width, x_ref, o_ref, send, recv):
+    total = groups * width
+    me = lax.axis_index("dp") * width + lax.axis_index("tensor")
+
+    def place(step):
+        other = lax.rem(me + step, total)
+        return (other // width, lax.rem(other, width))
+
+    barrier = pltpu.get_barrier_semaphore()
+
+    def hello(step, carry):
+        pl.semaphore_signal(barrier, inc=1, device_id=place(step), device_id_type=MESH_IDS)
+        return carry
+
+    lax.fori_loop(1, total, hello, 0)
+    pl.semaphore_wait(barrier, total - 1)
+
+    def copy(step):
+        return remote(x_ref, o_ref.at[me], send.at[step], recv.at[step], place(step))
+
+    def begin(step, carry):
+        copy(step).start()
+        return carry
+
+    def finish(step, carry):
+        copy(step).wait()
+        return carry
+
+    lax.fori_loop(1, total, begin, 0)
+    o_ref[me] = x_ref[...]
+    lax.fori_loop(1, total, finish, 0)
+
+
+def gather_all(block, collective):
+    groups, width = lax.axis_size("dp"), lax.axis_size("tensor")
+    total = groups * width
+    return pl.pallas_call(
+        partial(gather_all_kernel, groups, width),
+        out_shape=jax.ShapeDtypeStruct((total,) + block.shape, block.dtype),
+        in_specs=[in_vmem()],
+        out_specs=in_vmem(),
+        scratch_shapes=[pltpu.SemaphoreType.DMA((total,)), pltpu.SemaphoreType.DMA((total,))],
+        compiler_params=comm_params(collective),
+    )(block)
+
+
+def swap_kernel(axis, count, x_ref, o_ref, send, recv):
+    me = lax.axis_index(axis)
+    others = [lax.rem(me + step, count) for step in range(1, count)]
+    greet([{axis: other} for other in others])
+    copies = [
+        remote(x_ref.at[other], o_ref.at[me], send.at[i], recv.at[i], {axis: other})
+        for i, other in enumerate(others)
+    ]
+    for copy in copies:
+        copy.start()
+    o_ref[me] = x_ref[me]
+    for copy in copies:
+        copy.wait()
+
+
+def swap(blocks, axis, collective):
+    count = lax.axis_size(axis)
+    return pl.pallas_call(
+        partial(swap_kernel, axis, count),
+        out_shape=jax.ShapeDtypeStruct(blocks.shape, blocks.dtype),
+        in_specs=[in_vmem()],
+        out_specs=in_vmem(),
+        scratch_shapes=[pltpu.SemaphoreType.DMA((count,)), pltpu.SemaphoreType.DMA((count,))],
+        compiler_params=comm_params(collective),
+    )(blocks)
+
+
+CHUNKS = 4
+
+
+def tensor_place(width):
+    me = lax.axis_index("tensor")
+    core = lax.rem(me, 2)
+    row = me // 2
+    mate = me + 1 - 2 * core
+    return me, core, row, mate
+
+
+def spread_kernel(width, x_ref, o_ref, far_send, far_recv, near_send, near_recv):
+    me, core, row, mate = tensor_place(width)
+    rows = width // 2
+    height = x_ref.shape[0]
+    size = height // CHUNKS
+    peers = [lax.rem(row + step, rows) * 2 + core for step in range(1, rows)]
+    greet([{"tensor": mate}] + [{"tensor": peer} for peer in peers])
+
+    def span(owner, part):
+        return pl.ds(pl.multiple_of(owner * height + part * size, size), size)
+
+    far = [
+        [
+            remote(
+                x_ref.at[pl.ds(part * size, size)],
+                o_ref.at[span(me, part)],
+                far_send.at[i, part],
+                far_recv.at[i, part],
+                {"tensor": peer},
+            )
+            for part in range(CHUNKS)
+        ]
+        for i, peer in enumerate(peers)
+    ]
+    for part in range(CHUNKS):
+        for line in far:
+            line[part].start()
+    near = [
+        remote(
+            x_ref,
+            o_ref.at[pl.ds(pl.multiple_of(me * height, height), height)],
+            near_send.at[0, 0],
+            near_recv.at[0, 0],
+            {"tensor": mate},
+        )
+    ]
+    near[0].start()
+    o_ref[pl.ds(pl.multiple_of(me * height, height), height)] = x_ref[...]
+    for part in range(CHUNKS):
+        for i in range(rows - 1):
+            far[i][part].wait_recv()
+            source = lax.rem(row + rows - 1 - i, rows) * 2 + core
+            onward = remote(
+                o_ref.at[span(source, part)],
+                o_ref.at[span(source, part)],
+                near_send.at[i + 1, part],
+                near_recv.at[i + 1, part],
+                {"tensor": mate},
+            )
+            onward.start()
+            near.append(onward)
+    for copy in near:
+        copy.wait()
+    for line in far:
+        for copy in line:
+            copy.wait_send()
+
+
+def spread(block, collective):
+    width = lax.axis_size("tensor")
+    rows = width // 2
+    far = pltpu.SemaphoreType.DMA((rows, CHUNKS))
+    return pl.pallas_call(
+        partial(spread_kernel, width),
+        out_shape=jax.ShapeDtypeStruct((width * block.shape[0],) + block.shape[1:], block.dtype),
+        in_specs=[in_vmem()],
+        out_specs=in_vmem(),
+        scratch_shapes=[far, far, far, far],
+        compiler_params=comm_params(collective),
+    )(block)
+
+
+def fold_kernel(width, p_ref, o_ref, near_buf, sum_buf, far_buf, near_send, near_recv, far_send, far_recv):
+    me, core, row, mate = tensor_place(width)
+    rows = width // 2
+    height = o_ref.shape[0]
+    size = height // CHUNKS
+    peers = [lax.rem(row + step, rows) * 2 + core for step in range(1, rows)]
+    greet([{"tensor": mate}] + [{"tensor": peer} for peer in peers])
+    order = list(range(1, rows)) + [0]
+
+    def span(owner, part):
+        return pl.ds(pl.multiple_of(owner * height + part * size, size), size)
+
+    near = {}
+    for step in order:
+        dest_row = lax.rem(row + step, rows)
+        for part in range(CHUNKS):
+            near[step, part] = remote(
+                p_ref.at[span(dest_row * 2 + 1 - core, part)],
+                near_buf.at[step, pl.ds(part * size, size)],
+                near_send.at[step, part],
+                near_recv.at[step, part],
+                {"tensor": mate},
+            )
+            near[step, part].start()
+    far = {}
+    for step in range(1, rows):
+        dest = lax.rem(row + step, rows) * 2 + core
+        for part in range(CHUNKS):
+            near[step, part].wait_recv()
+            local = pl.ds(part * size, size)
+            sum_buf[step - 1, local] = (
+                p_ref[span(dest, part)].astype(jnp.float32)
+                + near_buf[step, local].astype(jnp.float32)
+            ).astype(jnp.bfloat16)
+            far[step, part] = remote(
+                sum_buf.at[step - 1, local],
+                far_buf.at[step - 1, local],
+                far_send.at[step - 1, part],
+                far_recv.at[step - 1, part],
+                {"tensor": dest},
+            )
+            far[step, part].start()
+    for part in range(CHUNKS):
+        near[0, part].wait_recv()
+        local = pl.ds(part * size, size)
+        o_ref[local] = p_ref[span(me, part)].astype(jnp.float32) + near_buf[0, local].astype(jnp.float32)
+    for part in range(CHUNKS):
+        local = pl.ds(part * size, size)
+        for step in range(1, rows):
+            far[step, part].wait_recv()
+            o_ref[local] += far_buf[step - 1, local].astype(jnp.float32)
+    for copy in list(near.values()) + list(far.values()):
+        copy.wait_send()
+
+
+def fold(parts, collective):
+    width = lax.axis_size("tensor")
+    rows = width // 2
+    height, depth = parts.shape[0] // width, parts.shape[1]
+    near = pltpu.SemaphoreType.DMA((rows, CHUNKS))
+    return pl.pallas_call(
+        partial(fold_kernel, width),
+        out_shape=jax.ShapeDtypeStruct((height, depth), jnp.float32),
+        in_specs=[in_vmem()],
+        out_specs=in_vmem(),
+        scratch_shapes=[
+            pltpu.VMEM((rows, height, depth), jnp.bfloat16),
+            pltpu.VMEM((max(rows - 1, 1), height, depth), jnp.bfloat16),
+            pltpu.VMEM((max(rows - 1, 1), height, depth), jnp.bfloat16),
+            near, near, near, near,
+        ],
+        compiler_params=comm_params(collective),
+    )(parts)
+
+
+def column_spread_kernel(width, x_ref, o_ref, far_send, far_recv, near_send, near_recv):
+    me, core, row, mate = tensor_place(width)
+    rows = width // 2
+    height, depth = x_ref.shape
+    size = height // CHUNKS
+    peers = [lax.rem(row + step, rows) * 2 + core for step in range(1, rows)]
+    greet([{"tensor": mate}] + [{"tensor": peer} for peer in peers])
+
+    def lanes(owner):
+        return pl.ds(pl.multiple_of(owner * depth, depth), depth)
+
+    far = [
+        [
+            remote(
+                x_ref.at[pl.ds(part * size, size)],
+                o_ref.at[pl.ds(part * size, size), lanes(me)],
+                far_send.at[i, part],
+                far_recv.at[i, part],
+                {"tensor": peer},
+            )
+            for part in range(CHUNKS)
+        ]
+        for i, peer in enumerate(peers)
+    ]
+    for part in range(CHUNKS):
+        for line in far:
+            line[part].start()
+    near = [
+        remote(x_ref, o_ref.at[:, lanes(me)], near_send.at[0, 0], near_recv.at[0, 0], {"tensor": mate})
+    ]
+    near[0].start()
+    o_ref[:, lanes(me)] = x_ref[...]
+    for part in range(CHUNKS):
+        for i in range(rows - 1):
+            far[i][part].wait_recv()
+            source = lax.rem(row + rows - 1 - i, rows) * 2 + core
+            window = o_ref.at[pl.ds(part * size, size), lanes(source)]
+            onward = remote(
+                window, window, near_send.at[i + 1, part], near_recv.at[i + 1, part], {"tensor": mate}
+            )
+            onward.start()
+            near.append(onward)
+    for copy in near:
+        copy.wait()
+    for line in far:
+        for copy in line:
+            copy.wait_send()
+
+
+def column_spread(block, collective):
+    width = lax.axis_size("tensor")
+    far = pltpu.SemaphoreType.DMA((width // 2, CHUNKS))
+    return pl.pallas_call(
+        partial(column_spread_kernel, width),
+        out_shape=jax.ShapeDtypeStruct((block.shape[0], width * block.shape[1]), block.dtype),
+        in_specs=[in_vmem()],
+        out_specs=in_vmem(),
+        scratch_shapes=[far, far, far, far],
+        compiler_params=comm_params(collective),
+    )(block)
+
+
+def sum_kernel(groups, width, keep, x_ref, o_ref, part_buf, sum_buf, all_buf, out_buf, *sems):
+    dp_me, me = lax.axis_index("dp"), lax.axis_index("tensor")
+    depth = part_buf.shape[2]
+    mates = [lax.rem(me + step, width) for step in range(1, width)]
+    peers = [lax.rem(dp_me + step, groups) for step in range(1, groups)]
+    greet([{"tensor": mate} for mate in mates] + [{"dp": peer} for peer in peers])
+
+    def lanes(owner):
+        return pl.ds(pl.multiple_of(owner * depth, depth), depth)
+
+    def run(copies):
+        for copy in copies:
+            copy.start()
+        return copies
+
+    first = run(
+        [
+            remote(x_ref.at[:, lanes(mate)], part_buf.at[me], sems[0].at[i], sems[1].at[i], {"tensor": mate})
+            for i, mate in enumerate(mates)
+        ]
+    )
+    part_buf[me] = x_ref[:, lanes(me)]
+    for copy in first:
+        copy.wait()
+    sum_buf[...] = jnp.sum(part_buf[...], axis=0)
+    second = run(
+        [
+            remote(sum_buf, all_buf.at[dp_me], sems[2].at[i], sems[3].at[i], {"dp": peer})
+            for i, peer in enumerate(peers)
+        ]
+    )
+    all_buf[dp_me] = sum_buf[...]
+    for copy in second:
+        copy.wait()
+    if keep:
+        out_buf[...] = all_buf[...]
+    else:
+        out_buf[0] = jnp.sum(all_buf[...], axis=0)
+    third = run(
+        [
+            remote(out_buf, o_ref.at[:, :, lanes(me)], sems[4].at[i], sems[5].at[i], {"tensor": mate})
+            for i, mate in enumerate(mates)
+        ]
+    )
+    o_ref[:, :, lanes(me)] = out_buf[...]
+    for copy in third:
+        copy.wait()
+
+
+def sum_all(block, keep, collective):
+    groups, width = lax.axis_size("dp"), lax.axis_size("tensor")
+    rows, depth = block.shape
+    narrow = depth // width
+    kept = groups if keep else 1
+    near, far = pltpu.SemaphoreType.DMA((width,)), pltpu.SemaphoreType.DMA((groups,))
+    return pl.pallas_call(
+        partial(sum_kernel, groups, width, keep),
+        out_shape=jax.ShapeDtypeStruct((kept, rows, depth), block.dtype),
+        in_specs=[in_vmem()],
+        out_specs=in_vmem(),
+        scratch_shapes=[
+            pltpu.VMEM((width, rows, narrow), block.dtype),
+            pltpu.VMEM((rows, narrow), block.dtype),
+            pltpu.VMEM((groups, rows, narrow), block.dtype),
+            pltpu.VMEM((kept, rows, narrow), block.dtype),
+            near, near, far, far, near, near,
+        ],
+        compiler_params=comm_params(collective),
+    )(block)
 
 
 def pad_keys(key_rows, value_rows, seq_ids):
@@ -192,11 +561,13 @@
     )
 
 
-def layer_forward(emb_rows, seq_ids, row_params, col_local, layer_mats):
+def layer_forward(emb_all, seq_ids, row_params, col_local, layer_mats):
     qkv_full, out_full, up_full, down_full = layer_mats
     col_width = qkv_full.shape[2]
+    tok_dev = emb_all.shape[0] // lax.axis_size("tensor")
+    first_moment_all = norm_rows(emb_all, row_params[0], row_params[3]).astype(jnp.bfloat16)
+    emb_rows = lax.dynamic_slice_in_dim(emb_all, lax.axis_index("tensor") * tok_dev, tok_dev, 0)
     norm_first = norm_rows(emb_rows, row_params[0], row_params[3])
-    first_moment_all = spread_rows(norm_first.astype(jnp.bfloat16))
     qkv_bias = jnp.concatenate([col_local[0], jnp.zeros_like(col_local[0]), col_local[1]])
     qkv_out = (
         multiply_arrays(first_moment_all, qkv_full.reshape(D, 3 * col_width)) + qkv_bias
@@ -204,16 +575,20 @@
     qkv_out = qkv_out.reshape(-1, 3, col_width // HEAD, HEAD)
     attn_out, log_total = attend(qkv_out[:, 0], qkv_out[:, 1], qkv_out[:, 2], seq_ids)
     attn_low = attn_out.reshape(-1, col_width).astype(jnp.bfloat16)
-    first_sum = norm_first + fold_rows(multiply_arrays(attn_low, out_full)) + row_params[6]
+    first_sum = (
+        norm_first
+        + fold(multiply_arrays(attn_low, out_full).astype(jnp.bfloat16), 5)
+        + row_params[6]
+    )
     norm_second = norm_rows(first_sum, row_params[1], row_params[4])
-    second_all = spread_rows(norm_second.astype(jnp.bfloat16))
+    second_all = spread(norm_second.astype(jnp.bfloat16), 6)
     expansion_result = multiply_arrays(second_all, up_full.reshape(D, -1)) + col_local[2:].reshape(
         -1
     )
     hidden_low = jax.nn.gelu(expansion_result, approximate=False).astype(jnp.bfloat16)
     second_sum = (
         norm_second
-        + fold_rows(multiply_arrays(hidden_low, down_full.reshape(-1, D)))
+        + fold(multiply_arrays(hidden_low, down_full.reshape(-1, D)).astype(jnp.bfloat16), 7)
         + row_params[7]
     )
     norm_third = norm_rows(second_sum, row_params[2], row_params[5])
@@ -249,7 +624,7 @@
     col_width = qkv_full.shape[2]
     grad_second, gain_c, shift_c = norm_back(second_sum, row_params[2], row_params[5], grad_third)
     mixed_low = grad_second.astype(jnp.bfloat16)
-    mixed_all = spread_rows(mixed_low)
+    mixed_all = spread(mixed_low, 10)
     down_grad = jnp.einsum("tf,td->fd", hidden_low, mixed_all, preferred_element_type=jnp.float32)
     hidden_grad = jnp.einsum(
         "td,fd->tf", mixed_all, down_full.reshape(-1, D), preferred_element_type=jnp.float32
@@ -257,12 +632,15 @@
     gelu_pull = jax.vjp(partial(jax.nn.gelu, approximate=False), expansion_result)[1]
     up_low = gelu_pull(hidden_grad)[0].astype(jnp.bfloat16)
     up_grad = jnp.einsum("td,tf->df", second_all, up_low, preferred_element_type=jnp.float32)
-    second_total = grad_second + fold_rows(
-        jnp.einsum("tf,df->td", up_low, up_full.reshape(D, -1), preferred_element_type=jnp.float32)
+    second_total = grad_second + fold(
+        jnp.einsum(
+            "tf,df->td", up_low, up_full.reshape(D, -1), preferred_element_type=jnp.float32
+        ).astype(jnp.bfloat16),
+        11,
     )
     grad_first, gain_b, shift_b = norm_back(first_sum, row_params[1], row_params[4], second_total)
     branch_low = grad_first.astype(jnp.bfloat16)
-    branch_all = spread_rows(branch_low)
+    branch_all = spread(branch_low, 12)
     out_grad = jnp.einsum("tc,td->cd", attn_low, branch_all, preferred_element_type=jnp.float32)
     attn_grad = jnp.einsum(
         "td,cd->tc", branch_all, out_full, preferred_element_type=jnp.float32
@@ -284,10 +662,11 @@
     qkv_grad = jnp.einsum(
         "td,tc->dc", first_moment_all, qkv_low, preferred_element_type=jnp.float32
     )
-    first_total = grad_first + fold_rows(
+    first_total = grad_first + fold(
         jnp.einsum(
             "tc,dc->td", qkv_low, qkv_full.reshape(D, -1), preferred_element_type=jnp.float32
-        )
+        ).astype(jnp.bfloat16),
+        13,
     )
     emb_grad, gain_a, shift_a = norm_back(emb_rows, row_params[0], row_params[3], first_total)
     qkv_cols = jnp.sum(qkv_low.astype(jnp.float32), axis=0).reshape(3, col_width)
@@ -312,6 +691,163 @@
         down_grad.reshape(-1, col_width, D),
     )
     return (emb_grad, mats_grad, col_grad, row_grad)
+
+
+def plan_kernel(capacity, vocab_local, groups, perm_ref, low_ref, high_ref, slot_ref, list_ref, count_ref, id_buf, own_buf):
+    slots = perm_ref.shape[1]
+    table_rows = low_ref.shape[1]
+    block = 128
+    blocks = slots // block
+    perm = perm_ref[...]
+    high_part = perm // 128
+    low_part = perm - high_part * 128
+    chooser = (lax.broadcasted_iota(jnp.int32, (table_rows, slots), 0) == high_part).astype(
+        jnp.float32
+    ).astype(jnp.bfloat16)
+    value = multiply_arrays(low_ref[...], chooser) + 256.0 * multiply_arrays(high_ref[...], chooser)
+    lane_match = lax.broadcasted_iota(jnp.int32, (128, slots), 0) == low_part
+    ids = jnp.sum(jnp.where(lane_match, value, 0.0), axis=0, keepdims=True)
+    for b in range(blocks):
+        id_buf[pl.ds(b * block, block), :] = jnp.broadcast_to(
+            ids[:, b * block : (b + 1) * block], (block, block)
+        ).T
+    place = lax.broadcasted_iota(jnp.int32, (1, slots), 1).astype(jnp.float32)
+    rows = lax.broadcasted_iota(jnp.int32, (block, 1), 0).astype(jnp.float32)
+
+    def earliest(b, best):
+        column = id_buf[pl.ds(pl.multiple_of(b * block, block), block), 0:1]
+        index = rows + (b * block).astype(jnp.float32)
+        found = jnp.where(column == ids, index, 1e9)
+        return jnp.minimum(best, jnp.min(found, axis=0, keepdims=True))
+
+    least = lax.fori_loop(0, blocks, earliest, jnp.full((1, slots), 1e9, jnp.float32))
+    first = least == place
+    owner = jnp.zeros((1, slots), jnp.float32)
+    for index in range(1, groups):
+        owner = owner + jnp.where(ids >= float(index * vocab_local), 1.0, 0.0)
+    owner_rows = lax.broadcasted_iota(jnp.int32, (groups, slots), 0).astype(jnp.float32)
+    marks = jnp.where(first & (owner == owner_rows), 1.0, 0.0)
+    upper = jnp.where(
+        lax.broadcasted_iota(jnp.int32, (block, block), 0)
+        < lax.broadcasted_iota(jnp.int32, (block, block), 1),
+        1.0,
+        0.0,
+    ).astype(jnp.bfloat16)
+    running = jnp.zeros((groups, 1), jnp.float32)
+    pieces = []
+    for b in range(blocks):
+        part = marks[:, b * block : (b + 1) * block]
+        pieces.append(multiply_arrays(part.astype(jnp.bfloat16), upper) + running)
+        running = running + jnp.sum(part, axis=1, keepdims=True)
+    before = jnp.concatenate(pieces, axis=1)
+    rank = jnp.sum(marks * before, axis=0, keepdims=True)
+    own_slot = jnp.where(first & (rank < float(capacity)), owner * float(capacity) + rank, -1.0)
+    for b in range(blocks):
+        own_buf[pl.ds(b * block, block), :] = jnp.broadcast_to(
+            own_slot[:, b * block : (b + 1) * block], (block, block)
+        ).T
+    width = list_ref.shape[1]
+    target = lax.broadcasted_iota(jnp.int32, (1, width), 1).astype(jnp.float32)
+
+    def settle(b, carry):
+        slot, listed = carry
+        window = pl.ds(pl.multiple_of(b * block, block), block)
+        column, slot_column = id_buf[window, 0:1], own_buf[window, 0:1]
+        slot = jnp.maximum(
+            slot, jnp.max(jnp.where(column == ids, slot_column, -1.0), axis=0, keepdims=True)
+        )
+        listed = jnp.maximum(
+            listed, jnp.max(jnp.where(slot_column == target, column, -1.0), axis=0, keepdims=True)
+        )
+        return (slot, listed)
+
+    slot, listed = lax.fori_loop(
+        0,
+        blocks,
+        settle,
+        (jnp.full((1, slots), -1.0, jnp.float32), jnp.full((1, width), -1.0, jnp.float32)),
+    )
+    slot_ref[...] = slot.astype(jnp.int32)
+    list_ref[...] = listed.astype(jnp.int32)
+    count_ref[...] = jnp.broadcast_to(running, count_ref.shape).astype(jnp.int32)
+
+
+def make_plan(perm, all_ids, capacity, vocab_local, groups):
+    slots = perm.shape[0]
+    table = all_ids.reshape(-1, 128).T
+    high = table // 256
+    low = table - high * 256
+    return pl.pallas_call(
+        partial(plan_kernel, capacity, vocab_local, groups),
+        out_shape=[
+            jax.ShapeDtypeStruct((1, slots), jnp.int32),
+            jax.ShapeDtypeStruct((1, groups * capacity), jnp.int32),
+            jax.ShapeDtypeStruct((groups, 128), jnp.int32),
+        ],
+        in_specs=[in_vmem()] * 3,
+        out_specs=[in_vmem()] * 3,
+        scratch_shapes=[pltpu.VMEM((slots, 128), jnp.float32), pltpu.VMEM((slots, 128), jnp.float32)],
+        compiler_params=pltpu.CompilerParams(vmem_limit_bytes=VMEM_BYTES),
+    )(perm[None], low.astype(jnp.bfloat16), high.astype(jnp.bfloat16))
+
+
+def loss_kernel(pooled_ref, head_ref, pair_ref, loss_ref, low_ref, grad_ref, back_ref):
+    total = pooled_ref.shape[0]
+    low = pooled_ref[...].astype(jnp.bfloat16)
+    low_ref[...] = low
+    head_low = head_ref[...].astype(jnp.bfloat16)
+    vectors = multiply_arrays(low, head_low)
+    depth = vectors.shape[1]
+    lane = lax.broadcasted_iota(jnp.int32, vectors.shape, 1)
+    across = lax.broadcasted_iota(jnp.int32, (total, total), 1)
+    diagonal = lax.broadcasted_iota(jnp.int32, (total, total), 0) == across
+    chosen = across == pair_ref[...]
+    loss = jnp.zeros((1, 1), jnp.float32)
+    grads = jnp.zeros(vectors.shape, jnp.float32)
+
+    def exact(left, right, dims):
+        return lax.dot_general(
+            left, right, (dims, ((), ())), precision=HIGHEST_MODE, preferred_element_type=jnp.float32
+        )
+
+    for fraction in (16, 4, 1):
+        prefix = jnp.where(lane < depth // fraction, vectors, 0.0)
+        inverse = lax.rsqrt(jnp.sum(prefix * prefix, axis=1, keepdims=True) + 1e-06)
+        unit = prefix * inverse
+        logits = exact(unit, unit, ((1,), (1,))) / LOGIT_DIVISOR
+        logits = jnp.where(diagonal, MASK_FILL, logits)
+        top = jnp.max(logits, axis=1, keepdims=True)
+        weights = jnp.exp(logits - top)
+        weight_sum = jnp.sum(weights, axis=1, keepdims=True)
+        positive = jnp.sum(jnp.where(chosen, logits, 0.0), axis=1, keepdims=True)
+        loss = loss + jnp.sum(jnp.log(weight_sum) + top - positive, keepdims=True)
+        pull = weights / weight_sum - jnp.where(chosen, 1.0, 0.0)
+        unit_grad = (exact(pull, unit, ((1,), (0,))) + exact(pull, unit, ((0,), (0,)))) / LOGIT_DIVISOR
+        unit_grad = jnp.where(lane < depth // fraction, unit_grad, 0.0)
+        inner = jnp.sum(unit_grad * prefix, axis=1, keepdims=True)
+        grads = grads + inverse * unit_grad - prefix * (inverse * inverse * inverse * inner)
+    loss_ref[...] = jnp.broadcast_to(loss, loss_ref.shape)
+    grad_ref[...] = grads
+    back_ref[...] = exact(grads, head_low.astype(jnp.float32), ((1,), (1,)))
+
+
+def contrast_step(pooled, head_weight, pairs):
+    total, depth = pooled.shape
+    return pl.pallas_call(
+        loss_kernel,
+        out_shape=[
+            jax.ShapeDtypeStruct((8, 128), jnp.float32),
+            jax.ShapeDtypeStruct((total, depth), jnp.bfloat16),
+            jax.ShapeDtypeStruct((total, depth), jnp.float32),
+            jax.ShapeDtypeStruct((total, depth), jnp.float32),
+        ],
+        in_specs=[in_vmem()] * 3,
+        out_specs=[in_vmem()] * 4,
+        compiler_params=pltpu.CompilerParams(vmem_limit_bytes=VMEM_BYTES),
+    )(pooled, head_weight, pairs[:, None])
+
+
+CAPACITY = 256
 
 
 def body(
@@ -347,6 +883,7 @@
     row_first,
     row_second,
 ):
+    groups = lax.axis_size("dp")
     tensor_count = lax.axis_size("tensor")
     group_index = lax.axis_index("dp")
     tensor_index = lax.axis_index("tensor")
@@ -355,69 +892,127 @@
     col_width = pos_table.shape[1]
     vocab_local = tok_table.shape[0]
     column_start = tensor_index * col_width
-    every_id, every_perm = (
-        lax.all_gather(token_ids, ("dp", "tensor"), axis=0, tiled=True),
-        lax.all_gather(slot_perm, ("dp", "tensor"), axis=0, tiled=True),
-    )
-    slot_ids = jnp.take(every_id, every_perm, axis=0)
+    anchors = pair_index.shape[0]
+    id_rows = tok_dev // 128
+    block = jnp.concatenate(
+        [
+            token_ids.reshape(id_rows, 128),
+            slot_perm.reshape(id_rows, 128),
+            jnp.pad(pair_index, (0, 128 - anchors))[None],
+            jnp.zeros((16 - 2 * id_rows - 1, 128), jnp.int32),
+        ],
+        axis=0,
+    )
+    gathered = gather_all(block, 1)
+    all_ids = gathered[:, :id_rows].reshape(-1)
+    pairs = gathered[:: tensor_count, 2 * id_rows, :anchors].reshape(-1)
+    own_perm = lax.dynamic_slice_in_dim(
+        gathered, group_index * tensor_count, tensor_count, 0
+    )[:, id_rows : 2 * id_rows].reshape(-1)
+    slot, listed, counts_out = make_plan(own_perm, all_ids, CAPACITY, vocab_local, groups)
+    slot = slot[0]
+    list_rows = CAPACITY // 128
+    top_count = jnp.max(counts_out)
+    request = jnp.concatenate(
+        [
+            listed.reshape(groups, list_rows, 128),
+            jnp.broadcast_to(top_count, (groups, 8 - list_rows, 128)),
+        ],
+        axis=1,
+    )
+    asked = swap(request, "dp", 2)
+    overflow = jnp.max(asked[:, list_rows]) > CAPACITY
+    offset = group_index * vocab_local
+    asked_rows = asked[:, :list_rows].reshape(-1) - offset
+    asked_safe = jnp.clip(asked_rows, 0, vocab_local - 1)
+    sent_rows = jnp.take(tok_table, asked_safe, axis=0).astype(jnp.bfloat16)
+    got_rows = swap(sent_rows.reshape(groups, CAPACITY, col_width), "dp", 3).reshape(-1, col_width)
+    chooser = (slot[:, None] == jnp.arange(groups * CAPACITY, dtype=jnp.int32)[None, :]).astype(
+        jnp.bfloat16
+    )
     lengths = seq_lengths[0]
     seq_ids, positions, member = seq_layout(lengths, tok_grp)
-    offset = group_index * vocab_local
-    tok_low = tok_table.astype(jnp.bfloat16)
-    wanted = slot_ids - offset
-    inside = (wanted >= 0) & (wanted < vocab_local)
-    picked = jnp.take(tok_low, jnp.clip(wanted, 0, vocab_local - 1), axis=0)
-    emb_cols = lax.psum_scatter(
-        jnp.where(inside[:, None], picked.astype(jnp.float32), 0.0).astype(jnp.bfloat16),
-        "dp",
-        scatter_dimension=0,
-        tiled=True,
-    ).astype(jnp.float32)
-    emb_cols = emb_cols + jnp.take(pos_table, positions, axis=0)
-    emb_rows = lax.all_to_all(emb_cols, "tensor", split_axis=0, concat_axis=1, tiled=True)
+
+    def every_slot_id():
+        every_perm = gathered[:, id_rows : 2 * id_rows].reshape(-1)
+        return jnp.take(all_ids, every_perm, axis=0)
+
+    def spread_wide():
+        wanted = every_slot_id() - offset
+        inside = (wanted >= 0) & (wanted < vocab_local)
+        picked = jnp.take(
+            tok_table.astype(jnp.bfloat16), jnp.clip(wanted, 0, vocab_local - 1), axis=0
+        )
+        return lax.psum_scatter(
+            jnp.where(inside[:, None], picked, jnp.zeros((), jnp.bfloat16)),
+            "dp",
+            scatter_dimension=0,
+            tiled=True,
+        )
+
+    tok_cols = lax.cond(
+        overflow,
+        spread_wide,
+        lambda: multiply_arrays(chooser, got_rows).astype(jnp.bfloat16),
+    )
+    pos_full = lax.all_gather(pos_table, "tensor", axis=1, tiled=True)
+    emb_all = column_spread(tok_cols, 4).astype(jnp.float32) + jnp.take(pos_full, positions, axis=0)
     layer_mats = (
         lax.all_gather(query_key_value_weight.astype(jnp.bfloat16), "dp", axis=0, tiled=True),
         lax.all_gather(out_weight.astype(jnp.bfloat16), "dp", axis=1, tiled=True),
         lax.all_gather(up_weight.astype(jnp.bfloat16), "dp", axis=0, tiled=True),
         lax.all_gather(down_weight.astype(jnp.bfloat16), "dp", axis=2, tiled=True),
     )
-    norm_third, saved_vals = layer_forward(emb_rows, seq_ids, row_params, col_bias, layer_mats)
+    norm_third, saved_vals = layer_forward(emb_all, seq_ids, row_params, col_bias, layer_mats)
     row_member = lax.dynamic_slice_in_dim(member, tensor_index * tok_dev, tok_dev, 0).astype(
         jnp.float32
     )
     counts = lengths.astype(jnp.float32)[:, None]
-    pooled = lax.psum(exact_multiply(row_member.T, norm_third), "tensor") / counts
-    pooled_low = pooled.astype(jnp.bfloat16)
-    head_low = head_weight.astype(jnp.bfloat16)
-    vectors = multiply_arrays(pooled_low, head_low)
-    every_vec = lax.all_gather(vectors, "dp", axis=0, tiled=True)
-    anchors = pair_index.shape[0]
-
-    def own_loss(all_vectors):
-        return contrast(all_vectors, pair_index, group_index * anchors)
-
-    local_loss, loss_pull = jax.vjp(own_loss, every_vec)
-    vec_grad = lax.psum_scatter(
-        loss_pull(jnp.ones((), jnp.float32))[0], "dp", scatter_dimension=0, tiled=True
-    )
-    pooled_grad = exact_multiply(vec_grad, head_low.astype(jnp.float32).T)
-    head_cols = exact_multiply(
-        pooled_low.astype(jnp.float32).T,
-        lax.dynamic_slice_in_dim(vec_grad, column_start, col_width, 1),
-    )
-    grad_third = exact_multiply(row_member, pooled_grad / counts)
+    pooled = sum_all(exact_multiply(row_member.T, norm_third) / counts, True, 9)
+    loss_out, pooled_low, vec_grad, pooled_grad = contrast_step(
+        pooled.reshape(-1, D), head_weight, pairs
+    )
+    head_sum = exact_multiply(pooled_low.astype(jnp.float32).T, vec_grad)
+    own_grad = lax.dynamic_slice_in_dim(pooled_grad, group_index * anchors, anchors, 0)
+    grad_third = exact_multiply(row_member, own_grad / counts)
     emb_grad, mats_grad, col_grad, row_grad = layer_backward(
         grad_third, seq_ids, row_params, layer_mats, saved_vals
     )
-    cols_grad = lax.all_to_all(emb_grad, "tensor", split_axis=1, concat_axis=0, tiled=True)
-    pos_grad = jax.ops.segment_sum(cols_grad, positions, num_segments=pos_table.shape[0])
-    wanted = slot_ids - offset
-    inside = (wanted >= 0) & (wanted < vocab_local)
-    tok_grad = (
-        jnp.zeros(tok_table.shape, jnp.float32)
-        .at[jnp.clip(wanted, 0, vocab_local - 1)]
-        .add(jnp.where(inside[:, None], lax.all_gather(cols_grad, "dp", axis=0, tiled=True), 0.0))
-    )
+    cols_grad = swap(
+        emb_grad.astype(jnp.bfloat16).reshape(tok_dev, tensor_count, col_width).swapaxes(0, 1),
+        "tensor",
+        14,
+    ).reshape(tok_grp, col_width)
+    pos_pick = (
+        jnp.arange(pos_table.shape[0], dtype=jnp.int32)[:, None] == positions[None, :]
+    ).astype(jnp.bfloat16)
+    pos_grad = multiply_arrays(pos_pick, cols_grad)
+    merged = jnp.einsum("kn,kc->nc", chooser, cols_grad, preferred_element_type=jnp.float32)
+    back_rows = swap(merged.astype(jnp.bfloat16).reshape(groups, CAPACITY, col_width), "dp", 15)
+
+    def add_wide():
+        wanted = every_slot_id() - offset
+        inside = (wanted >= 0) & (wanted < vocab_local)
+        return (
+            jnp.zeros(tok_table.shape, jnp.float32)
+            .at[jnp.clip(wanted, 0, vocab_local - 1)]
+            .add(
+                jnp.where(
+                    inside[:, None],
+                    lax.all_gather(cols_grad, "dp", axis=0, tiled=True).astype(jnp.float32),
+                    0.0,
+                )
+            )
+        )
+
+    def add_listed():
+        return (
+            jnp.zeros(tok_table.shape, jnp.float32)
+            .at[jnp.where(asked_rows < 0, vocab_local, asked_rows)]
+            .add(back_rows.reshape(-1, col_width).astype(jnp.float32), mode="drop")
+        )
+
+    tok_grad = lax.cond(overflow, add_wide, add_listed)
     qkv_part, out_part, up_part, down_part = mats_grad
     qkv_grad, out_grad, up_grad, down_grad = (
         lax.psum_scatter(qkv_part, "dp", scatter_dimension=0, tiled=True),
@@ -425,39 +1020,24 @@
         lax.psum_scatter(up_part, "dp", scatter_dimension=0, tiled=True),
         lax.psum_scatter(down_part, "dp", scatter_dimension=2, tiled=True),
     )
-    col_full = lax.dynamic_update_slice_in_dim(
-        jnp.zeros((col_grad.shape[0], D), jnp.float32), col_grad, column_start, 1
-    )
-    pos_full = lax.dynamic_update_slice_in_dim(
-        jnp.zeros((pos_grad.shape[0], D), jnp.float32), pos_grad, column_start, 1
-    )
-    head_full = lax.dynamic_update_slice_in_dim(
-        jnp.zeros((D, D), jnp.float32), head_cols, column_start, 1
-    )
+    pos_own, col_own = lax.psum((pos_grad, col_grad), "dp")
+    shared_squares = (jnp.sum(pos_own * pos_own) + jnp.sum(col_own * col_own)) / groups
     local_squares = (
         jnp.sum(tok_grad * tok_grad)
         + jnp.sum(qkv_grad * qkv_grad)
         + jnp.sum(out_grad * out_grad)
         + jnp.sum(up_grad * up_grad)
         + jnp.sum(down_grad * down_grad)
-    )
-    loss_share = local_loss / tensor_count
-    scalars = jnp.stack([loss_share])
-    row_sum, col_sum, pos_sum, head_sum, scalar_sum = lax.psum(
-        (row_grad, col_full, pos_full, head_full, scalars), ("dp", "tensor")
-    )
-    big_squares = lax.psum(local_squares, ("dp", "tensor"))
-    squares = (
-        big_squares
-        + jnp.sum(row_sum * row_sum)
-        + jnp.sum(col_sum * col_sum)
-        + jnp.sum(pos_sum * pos_sum)
-        + jnp.sum(head_sum * head_sum)
-    )
+        + shared_squares
+    )
+    row_block = jnp.concatenate(
+        [row_grad, jnp.pad(local_squares.reshape(1, 1), ((0, 7), (0, D - 1)))], axis=0
+    )
+    row_total = sum_all(row_block, False, 16)[0]
+    row_sum = row_total[:8]
+    squares = row_total[8, 0] + jnp.sum(row_sum * row_sum) + jnp.sum(head_sum * head_sum)
     grad_norm = jnp.sqrt(squares)
     clip_scale = jnp.minimum(1.0, CLIP_NORM / (grad_norm + 1e-06))
-    col_own = lax.dynamic_slice_in_dim(col_sum, column_start, col_width, 1)
-    pos_own = lax.dynamic_slice_in_dim(pos_sum, column_start, col_width, 1)
     tok_new = adam_step(
         tok_table, tok_first, tok_second, tok_grad * clip_scale, RATE_MATRIX, DECAY_RATE
     )
@@ -486,37 +1066,7 @@
     )
     col_new = adam_step(col_bias, col_first, col_second, col_own * clip_scale, RATE_VECTOR, 0.0)
     row_new = adam_step(row_params, row_first, row_second, row_sum * clip_scale, RATE_VECTOR, 0.0)
-    return (
-        scalar_sum[0],
-        grad_norm,
-        tok_new[0],
-        tok_new[1],
-        tok_new[2],
-        pos_new[0],
-        pos_new[1],
-        pos_new[2],
-        qkv_new[0],
-        qkv_new[1],
-        qkv_new[2],
-        out_new[0],
-        out_new[1],
-        out_new[2],
-        up_new[0],
-        up_new[1],
-        up_new[2],
-        down_new[0],
-        down_new[1],
-        down_new[2],
-        head_new[0],
-        head_new[1],
-        head_new[2],
-        col_new[0],
-        col_new[1],
-        col_new[2],
-        row_new[0],
-        row_new[1],
-        row_new[2],
-    )
+    return (loss_out[0, 0], grad_norm) + tok_new + pos_new + qkv_new + out_new + up_new + down_new + head_new + col_new + row_new
 
 
 def solution(mesh):

time: 2390 us -> 1320 us (0.55)
  waiting for transfers between devices: 1400 us -> 335 us
  Pallas kernels: 0 us -> 374 us
  local copies, waits for them, and re-layouts: 247 us -> 108 us
  blocking collectives: 188 us -> 61.9 us
  other arithmetic: 264 us -> 152 us
    reduce_scatter x6 -> x0, waiting for transfers between devices: 441 us -> none  [the longest x4 242 us: fold_rows(): lax.psum_scatter(partial_rows, 'tensor', scatter_dimension=0, tiled=True)]
    pallas_call x0 -> x17, Pallas kernels: none -> 374 us  [the longest x4 123 us: fold(): pl.pallas_call(partial(fold_kernel, width), out_shape=jax.ShapeDtypeStruc...]
    all_gather x5 -> x1, waiting for transfers between devices: 341 us -> 0.03 us  [body(): pos_full = lax.all_gather(pos_table, 'tensor', axis=1, tiled=True)]
    psum x1 -> x0, waiting for transfers between devices: 163 us -> none  [body(): lax.psum((row_grad, col_full, pos_full, head_full, scalars), ('dp', 'tens...]
    gather x3 -> x2, local copies, waits for them, and re-layouts: 162 us -> 22.8 us  [the longest x1 13.3 us: body(): jnp.take(pos_full, positions, axis=0)]
    all_gather x3 -> x0, blocking collectives: 112 us -> none  [the longest x1 43.6 us: body(): lax.all_gather(token_ids, ('dp', 'tensor'), axis=0, tiled=True)]
    scatter-add x2 -> x1, other arithmetic: 126 us -> 16.1 us  [add_listed(): return jnp.zeros(tok_table.shape, jnp.float32).at[jnp.where(asked_rows <...]
    unnamed x20 -> x9, waiting for transfers between devices: 108 us -> 174 us
  transfers between devices with their start and end apart: 21 -> 8, of which waited for: 20 -> 4; matrix products, arithmetic and copies ran while one was open for 5% -> 14% of each run, Pallas kernels for 0% -> 7%
where the time goes in v1:
time: 1320 us; the launch traced here: 1310 us
  Pallas kernels  374 us (28%)
  waiting for transfers between devices  335 us (25%)
  matrix products  234 us (18%)
  other arithmetic  152 us (12%)
  local copies, waits for them, and re-layouts  108 us (8%)
  blocking collectives  61.9 us (5%)
  between operations  26.4 us (2%)
  loops' own time  14.2 us (1%)
    unnamed x9, waiting for transfers between devices  174 us
    pallas_call x4, Pallas kernels, fold(): pl.pallas_call(partial(fold_kernel, width), out_shape=jax.ShapeDtypeStruc...  123 us
    pallas_call x3, Pallas kernels, spread(): pl.pallas_call(partial(spread_kernel, width), out_shape=jax.ShapeDtypeStr...  89.3 us
    reduce_scatter x1, waiting for transfers between devices, body(): lax.psum_scatter(down_part, 'dp', scatter_dimension=2, tiled=True)  87 us
    reduce_scatter x1, waiting for transfers between devices, body(): lax.psum_scatter(qkv_part, 'dp', scatter_dimension=0, tiled=True)  72.7 us
    pallas_call x4, Pallas kernels, swap(): pl.pallas_call(partial(swap_kernel, axis, count), out_shape=jax.ShapeDtyp...  67 us
    dot_general x6, matrix products, multiply_arrays(): return jnp.dot(left_mat, right_mat, preferred_element_type=jnp.float32)  47.6 us
    dot_general x8, matrix products, score_block(): jnp.einsum('qhd,khd->hqk', q_blk, k_blk, preferred_element_type=jnp.float32)  36.8 us
  transfers between devices with their start and end apart: 8, of which 4 were waited for; matrix products, arithmetic and copies ran while one was open for 14% of the time, Pallas kernels for 7%

profile of v1, /device:TPU:0, one launch (start us, length us, event | category | flops | bytes accessed | tf_op | source)
XLA Modules:
  0.0 1305.4 jit_solution(10407751803794645693)
XLA Ops:
  10.1 13.0 shard_map.518
  24.6 10.9 shard_map.519
  38.8 9.3 shard_map.520
  51.5 9.5 gather_fusion.3
  62.2 21.6 %shard_map.521 = bf16[8,256,256]{2,1,0:T(8,128)(2,1)S(1)} custom-call(bf16[8,256,256]{2,1,0:T(8,128)(2,1)} %select_convert_fusion.x_ref), custom_call_target="tpu_custom_call" | custom-call | tf_op jit(solution)/shard_map/pallas_call | solution.py:165
  101.9 34.2 %all_gather.20 = bf16[256,1024]{1,0:T(8,128)(2,1)} all-gather(bf16[256,128]{1,0:T(8,128)(2,1)S(1)} %convert_element_type.163), channel_id=1, replica_groups=mesh['dp'=8,'tensor'=4] {'dp'}, dimensions={1}, use_global_device_ids=true | all-gather | bytes 589824 | tf_op jit(solution)/shard_map/all_gather | solution.py:962
  136.1 30.0 %shard_map.522 = bf16[2048,1024]{1,0:T(8,128)(2,1)} custom-call(bf16[2048,256]{1,0:T(8,128)(2,1)} %get-tuple-element.590.x_ref), custom_call_target="tpu_custom_call" | custom-call | tf_op jit(solution)/shard_map/pallas_call | solution.py:385
  166.2 13.3 %gather_fusion.4 = f32[2048,1024]{1,0:T(8,128)} fusion(f32[514,1024]{1,0:T(8,128)} %all-gather.8.cloned.1.call-done, s32[2048]{0:T(1024)S(1)} %broadcast_clamp_fusion), kind=kCustom, calls=%fused_computation.4 | custom fusion | bytes 16785408 | tf_op jit(solution)/shard_map/jit(_take)/gather | solution.py:959
  179.5 5.5 fusion.125
  191.1 6.1 add_convert_fusion.2
  200.2 56.1 %while.26 = (s32[]{:T(128)}, bf16[4,512,4,64]{1,3,2,0:T(8,128)(2,1)S(1)}, f32[4,4,512]{2,1,0:T(4,128)S(1)}, s32[4]{0:T(128)S(1)}, bf16[3072,4,64]{0,2,1:T(8,128)...) while((s32[]{:T(128)}, ...), condition=%wide.region_15.17_spmd, body=%wide.region_12.16_spmd.sunk | while | flops 843839488 | bytes 43344124 | solution.py:501
  251.3 5.0 fusion.183
  260.7 30.8 %shard_map.523 = f32[512,1024]{1,0:T(8,128)} custom-call(bf16[2048,1024]{1,0:T(8,128)(2,1)} %convolution_convert_fusion.1.p_ref), custom_call_target="tpu_custom_call" | custom-call | tf_op jit(solution)/shard_map/pallas_call | solution.py:318
  297.3 29.6 %shard_map.524 = bf16[2048,1024]{1,0:T(8,128)(2,1)} custom-call(bf16[512,1024]{1,0:T(8,128)(2,1)} %fusion.73.x_ref), custom_call_target="tpu_custom_call" | custom-call | tf_op jit(solution)/shard_map/pallas_call | solution.py:248
  330.5 23.7 %multiply_convert_fusion.1 = (bf16[2048,1024]{1,0:T(8,128)(2,1)}, f32[2048,1024]{1,0:T(8,128)}, f32[2048,1024]{1,0:T(8,128)}) fusion(f32[1024]{0:T(1024)S(1)} %bitcast.283, bf16[2048,1024]{1,0:T(8,128)(2,1)S(1)} %copy-done.16, bf16[1024,1024]{1,0:T(8,128)(2,1)S(1)} %bitcast.232), kind=kOutput, calls=%fused_computation.90 | convolution fusion | flops 4433379328 | bytes 27267072 | tf_op jit(solution)/shard_map/dot_general | solution.py:30
  354.3 9.4 convolution_convert_fusion.4.p_ref
  363.7 30.8 %shard_map.525 = f32[512,1024]{1,0:T(8,128)} custom-call(bf16[2048,1024]{1,0:T(8,128)(2,1)} %convolution_convert_fusion.4.p_ref), custom_call_target="tpu_custom_call" | custom-call | tf_op jit(solution)/shard_map/pallas_call | solution.py:318
  400.7 14.2 %shard_map.526 = f32[8,8,1024]{2,1,0:T(8,128)} custom-call(f32[8,1024]{1,0:T(8,128)} %fusion.75.x_ref), custom_call_target="tpu_custom_call" | custom-call | tf_op jit(solution)/shard_map/pallas_call | solution.py:450
  414.9 11.3 shard_map.527
  434.1 30.2 %shard_map.528 = bf16[2048,1024]{1,0:T(8,128)(2,1)} custom-call(bf16[512,1024]{1,0:T(8,128)(2,1)} %get-tuple-element.304.x_ref), custom_call_target="tpu_custom_call" | custom-call | tf_op jit(solution)/shard_map/pallas_call | solution.py:248
  464.3 14.0 %convert_reduce_fusion = (f32[1024]{0:T(1024)}, bf16[2048,1024]{1,0:T(8,128)(2,1)S(1)}) fusion(f32[2048,1024]{1,0:T(8,128)} %get-tuple-element.316, f32[2048,1024]{1,0:T(8,128)} %get-tuple-element.346, f32[1024]{0:T(1024)S(1)} %bitcast.284, bf16[2048,1024]{1,0:T(8,128)(2,1)} %shard_map.528, bf16[1024,1024]{1,0:T(8,128)(2,1)} %bitcast.291), kind=kOutput, calls=%fused_computation.88 | convolution fusion | flops 4330617856 | bytes 27271168 | tf_op jit(solution)/shard_map/td,fd->tf/dot_general | solution.py:629
  480.4 6.2 convolution_convert_fusion.3.p_ref
  486.7 30.8 %shard_map.529 = f32[512,1024]{1,0:T(8,128)} custom-call(bf16[2048,1024]{1,0:T(8,128)(2,1)} %convolution_convert_fusion.3.p_ref), custom_call_target="tpu_custom_call" | custom-call | tf_op jit(solution)/shard_map/pallas_call | solution.py:318
  525.9 29.6 %shard_map.530 = bf16[2048,1024]{1,0:T(8,128)(2,1)} custom-call(bf16[512,1024]{1,0:T(8,128)(2,1)} %get-tuple-element.306.x_ref), custom_call_target="tpu_custom_call" | custom-call | tf_op jit(solution)/shard_map/pallas_call | solution.py:248
  568.4 138.8 %while.27 = (s32[]{:T(128)}, f32[3072,4,64]{0,2,1:T(8,128)}, f32[3072,4,64]{0,2,1:T(8,128)}, bf16[4,512,4,64]{1,0,3,2:T(4,128)(2,1)}, s32[4]{0:T(128)S(1)}, /*in...) while((s32[]{:T(128)}, f32[3072,4,64]{0,2,1:T(8,128)}, ...), condition=%wide.region_26.28_spmd, body=%wide.region_24.27_spmd.sunk | while | flops 2043803648 | bytes 178324000 | solution.py:554
  576.4 5.7 multiply_reduce_fusion.22
  611.1 5.7 multiply_reduce_fusion.22
  645.7 5.7 multiply_reduce_fusion.22
  680.4 5.7 multiply_reduce_fusion.22
  713.9 5.4 convolution_convert_fusion.2.p_ref
  719.3 31.0 %shard_map.531 = f32[512,1024]{1,0:T(8,128)} custom-call(bf16[2048,1024]{1,0:T(8,128)(2,1)} %convolution_convert_fusion.2.p_ref), custom_call_target="tpu_custom_call" | custom-call | tf_op jit(solution)/shard_map/pallas_call | solution.py:318
  757.9 14.0 %shard_map.532 = bf16[4,512,256]{2,1,0:T(8,128)(2,1)S(1)} custom-call(bf16[4,512,256]{2,1,0:T(8,128)(2,1)} %bitcast.225), custom_call_target="tpu_custom_call" | custom-call | tf_op jit(solution)/shard_map/pallas_call | solution.py:165
  772.0 5.9 fusion.67
  777.8 22.1 %shard_map.533 = bf16[8,256,256]{2,1,0:T(8,128)(2,1)S(1)} custom-call(bf16[8,256,256]{2,1,0:T(8,128)(2,1)} %bitcast.239), custom_call_target="tpu_custom_call" | custom-call | tf_op jit(solution)/shard_map/pallas_call | solution.py:165
  800.0 21.4 %conditional.3 = (f32[6284,256]{1,0:T(8,128)}, f32[]{:T(128)}) conditional(s32[]{:T(128)} %convert_element_type.154, (s32[]{:T(128)}, s32[8,2,128]{2,1,0:T(2,128)S(1)}, bf16[8,256,256]{2,1,0:T(8,128)(2,1)S(1)}) %tuple.157, (s32[32,16,128]{2,1,0:T(8,128)}, s32[16384]{0:T(1024)S(1)}, s32[]{:T(128)}, bf16[2048,256]{1,0:T(8,128)(2,1)S(1)}) %tuple.154), branch_computations={%region_37.41_spmd, %region_40.44_spmd} | conditional | flops 16242687 | bytes 54584416 | solution.py:1015
  800.0 16.1 %scatter_custom_fusion = f32[6284,256]{1,0:T(8,128)} fusion(s32[2048]{0:T(1024)S(1)} %bitcast.278, f32[]{:T(128)} %constant.117.clone, bf16[2048,256]{1,0:T(8,128)(2,1)S(1)} %bitcast.227), kind=kCustom, calls=%fused_computation.56 | custom fusion | flops 1048576 | bytes 7483396 | tf_op jit(solution)/shard_map/cond/branch_0_fun/scatter-add | solution.py:1012
  816.1 5.1 multiply_reduce_fusion.1
  822.2 10.0 fusion.131
  832.3 5.3 copy.90
  841.1 7.3 fusion.65
  848.5 10.1 fusion.132
  861.8 27.7 %psum.15 = f32[6,256]{1,0:T(8,128)S(1)} all-reduce(f32[6,256]{1,0:T(8,128)S(1)} %pad_maximum_fusion), channel_id=1, replica_groups=mesh['dp'=8,'tensor'=4] {'dp'}, use_global_device_ids=true, to_apply=%region_55.57 | all-reduce | flops 1536 | bytes 12288 | tf_op jit(solution)/shard_map/psum | solution.py:1023
  898.0 172.3 %all-reduce.10.cloned.1.call-done = (f32[1024,4,256]{2,1,0:T(4,128)}, f32[514,256]{1,0:T(8,128)}) async-done(((f32[1024,4,256]{2,1,0:T(4,128)}, f32[514,256]{1,0:T(8,128)}), (f32[1024,4,256]{2,1,0:T(4,128)}, f32[514,256]{1,0:T(8,128)})) %all-reduce.10.cloned.1.call-update) | async-done | bytes 4720656
  1075.4 72.7 %reduce-scatter.7.cloned.1.call-done = f32[128,3,256]{2,0,1:T(8,128)} async-done(((f32[1024,3,256]{2,0,1:T(8,128)}), f32[128,3,256]{2,0,1:T(8,128)}) %reduce-scatter.7.cloned.1.call-update) | async-done | bytes 393232 | tf_op jit(solution)/shard_map/reduce_scatter | solution.py:1018
  1152.4 87.0 %reduce-scatter.11.cloned.1.call-done = f32[4,256,128]{2,1,0:T(8,128)} async-done(((f32[4,256,1024]{2,1,0:T(8,128)}), f32[4,256,128]{2,1,0:T(8,128)}) %reduce-scatter.11.cloned.1.call-update) | async-done | bytes 524304 | tf_op jit(solution)/shard_map/reduce_scatter | solution.py:1021
  1243.3 14.9 %shard_map.534 = f32[1,16,1024]{2,1,0:T(8,128)} custom-call(f32[16,1024]{1,0:T(8,128)} %concatenate.19.x_ref), custom_call_target="tpu_custom_call" | custom-call | tf_op jit(solution)/shard_map/pallas_call | solution.py:450
  1269.6 9.4 multiply_subtract_fusion.1
  1279.2 13.7 %multiply_subtract_fusion = (f32[6284,256]{1,0:T(8,128)}, f32[6284,256]{1,0:T(8,128)}, f32[6284,256]{1,0:T(8,128)}) fusion(f32[6284,256]{1,0:T(8,128)S(1)} %bitcast.215, f32[6284,256]{1,0:T(8,128)} %get-tuple-element.212, f32[]{:T(128)S(6)} %min_shard_map.3, f32[6284,256]{1,0:T(8,128)} %param.46, f32[6284,256]{1,0:T(8,128)} %param.47), kind=kLoop, calls=%fused_computation.109 | loop fusion | flops 25739264 | bytes 45043716 | tf_op jit(solution)/shard_map/sub | solution.py:64
  (445 shorter events, 296.0 us)
Async XLA Ops:
  23.2 74.7 %copy-start.34 = (s32[32,16,128]{2,1,0:T(8,128)}, s32[32,16,128]{2,1,0:T(8,128)S(1)}, u32[]{:S(2)}) copy-start(s32[32,16,128]{2,1,0:T(8,128)S(1)} %shard_map.518) | copy-start | bytes 786436
  23.2 62.1 %copy-start = (s32[32,4,128]{2,1,0:T(4,128)}, s32[32,4,128]{2,1,0:T(4,128)S(1)}, u32[]{:S(2)}) copy-start(s32[32,4,128]{2,1,0:T(4,128)S(1)} %slice.102) | copy-start | bytes 196612
  61.0 22.9 %copy-start.78 = (s32[1,2048]{1,0:T(1,128)S(1)}, s32[1,2048]{1,0:T(1,128)}, u32[]{:S(2)}) copy-start(s32[1,2048]{1,0:T(1,128)} %get-tuple-element.201) | copy-start | bytes 24580
  88.8 77.4 %all-gather.8.cloned.1.call-start = ((), (), s32[]{:S(2)}) async-start(), calls=%async_computation.6 | async-start | bytes 2662400 | tf_op jit(solution)/shard_map/all_gather | solution.py:958
  89.3 101.8 %all-gather.10.cloned.1.call-start = ((), (), s32[]{:S(2)}) async-start(), calls=%async_computation.7 | async-start | bytes 1769472 | tf_op jit(solution)/shard_map/all_gather | solution.py:961
  91.2 235.7 %all-gather.12.cloned.1.call-start = ((), (), s32[]{:S(2)}) async-start(), calls=%async_computation.8 | async-start | bytes 2359296 | tf_op jit(solution)/shard_map/all_gather | solution.py:963
  93.1 261.2 %all-gather.14.cloned.1.call-start = ((), (), s32[]{:S(2)}) async-start(), calls=%async_computation.9 | async-start | bytes 2359296 | tf_op jit(solution)/shard_map/all_gather | solution.py:964
  97.9 81.7 %copy-start.49 = (s32[2048]{0:T(1024)}, s32[2048]{0:T(1024)S(1)}, u32[]{:S(2)}) copy-start(s32[2048]{0:T(1024)S(1)} %get-tuple-element.223) | copy-start | bytes 24580
  100.3 191.3 %copy-start.51 = (f32[1,1024]{1,0:T(1,128)}, f32[1,1024]{1,0:T(1,128)S(1)}, u32[]{:S(2)}) copy-start(f32[1,1024]{1,0:T(1,128)S(1)} %get-tuple-element.338) | copy-start | bytes 12292
  185.3 106.3 %copy-start.54 = (f32[512]{0:T(512)}, f32[512]{0:T(512)S(1)}, u32[]{:S(2)}) copy-start(f32[512]{0:T(512)S(1)} %broadcast_multiply_fusion.3) | copy-start | bytes 6148
  185.7 105.9 %copy-start.61 = (f32[512]{0:T(512)}, f32[512]{0:T(512)S(1)}, u32[]{:S(2)}) copy-start(f32[512]{0:T(512)S(1)} %fusion.103) | copy-start | bytes 6148
  260.7 30.9 %copy-start.74 = (f32[1,1024]{1,0:T(1,128)S(1)}, f32[1,1024]{1,0:T(1,128)}, u32[]{:S(2)}) copy-start(f32[1,1024]{1,0:T(1,128)} %get-tuple-element.336) | copy-start | bytes 12292
  297.3 33.2 %copy-start.84 = (f32[1,2,4,128]{3,1,2,0:T(2,128)S(1)}, f32[1,2,4,128]{3,1,2,0:T(2,128)}, u32[]{:S(2)}) copy-start(f32[1,2,4,128]{3,1,2,0:T(2,128)} %copy.131) | copy-start | bytes 12292
  363.7 30.9 %copy-start.77 = (f32[1,1024]{1,0:T(1,128)S(1)}, f32[1,1024]{1,0:T(1,128)}, u32[]{:S(2)}) copy-start(f32[1,1024]{1,0:T(1,128)} %get-tuple-element.333) | copy-start | bytes 12292
  522.7 32.7 %copy-start.68 = (f32[512]{0:T(512)}, f32[512]{0:T(512)S(1)}, u32[]{:S(2)}) copy-start(f32[512]{0:T(512)S(1)} %negate_multiply_fusion.2) | copy-start | bytes 6148
  719.3 31.1 %copy-start.13 = (f32[512,1024]{1,0:T(8,128)S(1)}, f32[512,1024]{1,0:T(8,128)}, u32[]{:S(2)}) copy-start(f32[512,1024]{1,0:T(8,128)} %copy-done.12) | copy-start | bytes 6291460
  719.3 31.1 %copy-start.52 = (f32[1,1024]{1,0:T(1,128)S(1)}, f32[1,1024]{1,0:T(1,128)}, u32[]{:S(2)}) copy-start(f32[1,1024]{1,0:T(1,128)} %copy-done.51) | copy-start | bytes 12292
  719.3 31.1 %copy-start.55 = (f32[512]{0:T(512)S(1)}, f32[512]{0:T(512)}, u32[]{:S(2)}) copy-start(f32[512]{0:T(512)} %copy-done.54) | copy-start | bytes 6148
  719.3 31.1 %copy-start.62 = (f32[512]{0:T(512)S(1)}, f32[512]{0:T(512)}, u32[]{:S(2)}) copy-start(f32[512]{0:T(512)} %copy-done.61) | copy-start | bytes 6148
  719.3 31.1 %copy-start.69 = (f32[512]{0:T(512)S(1)}, f32[512]{0:T(512)}, u32[]{:S(2)}) copy-start(f32[512]{0:T(512)} %copy-done.68) | copy-start | bytes 6148
  771.9 28.0 %copy-start.17 = (bf16[4,512,256]{2,1,0:T(8,128)(2,1)}, bf16[4,512,256]{2,1,0:T(8,128)(2,1)S(1)}, u32[]{:S(2)}) copy-start(bf16[4,512,256]{2,1,0:T(8,128)(2,1)S(1)} %shard_map.532) | copy-start | bytes 3145732
  771.9 28.0 %copy-start.1 = (s32[32,4,128]{2,1,0:T(4,128)S(1)}, s32[32,4,128]{2,1,0:T(4,128)}, u32[]{:S(2)}) copy-start(s32[32,4,128]{2,1,0:T(4,128)} %copy-done) | copy-start | bytes 196612
  771.9 28.0 %copy-start.60 = (s32[8,2,128]{2,1,0:T(2,128)S(1)}, s32[8,2,128]{2,1,0:T(2,128)}, u32[]{:S(2)}) copy-start(s32[8,2,128]{2,1,0:T(2,128)} %get-tuple-element.330) | copy-start | bytes 24580
  799.9 22.3 %copy-start.50 = (s32[2048]{0:T(1024)S(1)}, s32[2048]{0:T(1024)}, u32[]{:S(2)}) copy-start(s32[2048]{0:T(1024)} %copy-done.49) | copy-start | bytes 24580
  821.4 75.1 %reduce-scatter.9.cloned.1.call-start = ((), (), s32[]{:S(2)}) async-start(), calls=%async_computation.11 | async-start | bytes 1179648 | tf_op jit(solution)/shard_map/reduce_scatter | solution.py:1019
  822.2 248.2 %all-reduce.10.cloned.1.call-start = ((), (), s32[]{:S(2)}) async-start(), calls=%async_computation.13 | async-start | bytes 9453568
  839.2 309.0 %reduce-scatter.7.cloned.1.call-start = ((), (), s32[]{:S(2)}) async-start(), calls=%async_computation.10 | async-start | bytes 3538944 | tf_op jit(solution)/shard_map/reduce_scatter | solution.py:1018
  848.4 391.1 %reduce-scatter.11.cloned.1.call-start = ((), (), s32[]{:S(2)}) async-start(), calls=%async_computation.12 | async-start | bytes 4718592 | tf_op jit(solution)/shard_map/reduce_scatter | solution.py:1021
  858.6 31.6 %copy-start.44 = (f32[64,1024]{1,0:T(8,128)S(1)}, f32[64,1024]{1,0:T(8,128)}, u32[]{:S(2)}) copy-start(f32[64,1024]{1,0:T(8,128)} %get-tuple-element.211) | copy-start | bytes 786436
  858.6 31.6 %copy-start.47 = (bf16[64,1024]{1,0:T(8,128)(2,1)S(1)}, bf16[64,1024]{1,0:T(8,128)(2,1)}, u32[]{:S(2)}) copy-start(bf16[64,1024]{1,0:T(8,128)(2,1)} %get-tuple-element.210) | copy-start | bytes 393220
  858.6 383.3 %copy-start.70 = (f32[1024]{0:T(1024)S(1)}, f32[1024]{0:T(1024)}, u32[]{:S(2)}) copy-start(f32[1024]{0:T(1024)} %get-tuple-element.303) | copy-start | bytes 12292
  858.6 383.3 %copy-start.71 = (f32[1024]{0:T(1024)S(1)}, f32[1024]{0:T(1024)}, u32[]{:S(2)}) copy-start(f32[1024]{0:T(1024)} %get-tuple-element.217) | copy-start | bytes 12292
  858.6 383.3 %copy-start.72 = (f32[1024]{0:T(1024)S(1)}, f32[1024]{0:T(1024)}, u32[]{:S(2)}) copy-start(f32[1024]{0:T(1024)} %get-tuple-element.221) | copy-start | bytes 12292
  858.6 383.3 %copy-start.73 = (f32[1024]{0:T(1024)S(1)}, f32[1024]{0:T(1024)}, u32[]{:S(2)}) copy-start(f32[1024]{0:T(1024)} %get-tuple-element.305) | copy-start | bytes 12292
  858.7 383.3 %copy-start.75 = (f32[1024]{0:T(1024)S(1)}, f32[1024]{0:T(1024)}, u32[]{:S(2)}) copy-start(f32[1024]{0:T(1024)} %get-tuple-element.215) | copy-start | bytes 12292
  858.7 383.3 %copy-start.76 = (f32[1024]{0:T(1024)S(1)}, f32[1024]{0:T(1024)}, u32[]{:S(2)}) copy-start(f32[1024]{0:T(1024)} %get-tuple-element.220) | copy-start | bytes 12292
  858.7 404.1 %copy-start.27 = (f32[128,4,256]{2,1,0:T(4,128)S(1)}, f32[128,4,256]{2,1,0:T(4,128)}, u32[]{:S(2)}) copy-start(f32[128,4,256]{2,1,0:T(4,128)} %param.57) | copy-start | bytes 1572868
  858.7 404.1 %copy-start.39 = (f32[128,4,256]{2,1,0:T(4,128)S(1)}, f32[128,4,256]{2,1,0:T(4,128)}, u32[]{:S(2)}) copy-start(f32[128,4,256]{2,1,0:T(4,128)} %param.58) | copy-start | bytes 1572868
  894.6 371.5 %copy-start.65 = (f32[6,256]{1,0:T(8,128)S(1)}, f32[6,256]{1,0:T(8,128)}, u32[]{:S(2)}) copy-start(f32[6,256]{1,0:T(8,128)} %param.66) | copy-start | bytes 18436
  894.6 371.5 %copy-start.80 = (f32[6,256]{1,0:T(8,128)S(1)}, f32[6,256]{1,0:T(8,128)}, u32[]{:S(2)}) copy-start(f32[6,256]{1,0:T(8,128)} %param.67) | copy-start | bytes 18436
  894.6 371.5 %copy-start.81 = (f32[6,256]{1,0:T(8,128)S(1)}, f32[6,256]{1,0:T(8,128)}, u32[]{:S(2)}) copy-start(f32[6,256]{1,0:T(8,128)} %param.68) | copy-start | bytes 18436
  894.6 372.1 %copy-start.48 = (f32[8,1024]{1,0:T(8,128)S(1)}, f32[8,1024]{1,0:T(8,128)}, u32[]{:S(2)}) copy-start(f32[8,1024]{1,0:T(8,128)} %param.69) | copy-start | bytes 98308
  894.6 372.1 %copy-start.58 = (f32[8,1024]{1,0:T(8,128)S(1)}, f32[8,1024]{1,0:T(8,128)}, u32[]{:S(2)}) copy-start(f32[8,1024]{1,0:T(8,128)} %param.70) | copy-start | bytes 98308
  894.6 372.1 %copy-start.59 = (f32[8,1024]{1,0:T(8,128)S(1)}, f32[8,1024]{1,0:T(8,128)}, u32[]{:S(2)}) copy-start(f32[8,1024]{1,0:T(8,128)} %param.71) | copy-start | bytes 98308
  894.6 373.5 %copy-start.22 = (f32[514,256]{1,0:T(8,128)S(1)}, f32[514,256]{1,0:T(8,128)}, u32[]{:S(2)}) copy-start(f32[514,256]{1,0:T(8,128)} %param.48) | copy-start | bytes 1579012
  894.6 373.5 %copy-start.35 = (f32[514,256]{1,0:T(8,128)S(1)}, f32[514,256]{1,0:T(8,128)}, u32[]{:S(2)}) copy-start(f32[514,256]{1,0:T(8,128)} %param.49) | copy-start | bytes 1579012
  894.6 373.5 %copy-start.36 = (f32[514,256]{1,0:T(8,128)S(1)}, f32[514,256]{1,0:T(8,128)}, u32[]{:S(2)}) copy-start(f32[514,256]{1,0:T(8,128)} %param.50) | copy-start | bytes 1579012
  1070.3 197.8 %copy-start.23 = (f32[514,256]{1,0:T(8,128)S(1)}, f32[514,256]{1,0:T(8,128)}, u32[]{:S(2)}) copy-start(f32[514,256]{1,0:T(8,128)} %get-tuple-element.267) | copy-start | bytes 1579012
  (71 other events, 435.3 us)
Sparse Core Ops, SparseCore 1:
  90.9 29.2 all-gather.7
  122.8 45.4 all-gather.9
  171.1 47.5 all-gather.11
  221.5 49.0 all-gather.13
  826.0 70.4 reduce-scatter.8
  900.7 169.5 all-reduce.9
  1074.4 73.7 reduce-scatter.6
  1152.2 87.2 reduce-scatter.10

commit v2 on v1

v2 whole, which is shorter than its diff:
```python
from functools import partial

import jax
import jax.numpy as jnp
from jax import lax
from jax.experimental import pallas as pl
from jax.experimental.pallas import tpu as pltpu
from jax.sharding import PartitionSpec as P

D = 1024
HEAD = 64
MAXLEN = 512
STEP = 10


HIGHEST_MODE = lax.Precision.HIGHEST
LN_EPS = 1e-05
LOGIT_DIVISOR = 0.05
CLIP_NORM = 0.25
BETA_FIRST = 0.9
BETA_SECOND = 0.999
ADAM_EPS = 1e-08
RATE_MATRIX = 0.05
RATE_VECTOR = 0.5
DECAY_RATE = 0.01
MASK_FILL = -1e30


def multiply_arrays(left_mat, right_mat):
    return jnp.dot(left_mat, right_mat, preferred_element_type=jnp.float32)


def exact_multiply(left_mat, right_mat):
    return jnp.dot(left_mat, right_mat, precision=HIGHEST_MODE, preferred_element_type=jnp.float32)


def norm_rows(values, gain_row, bias_row):
    center = values - jnp.mean(values, axis=1, keepdims=True)
    inverse = lax.rsqrt(jnp.mean(center * center, axis=1, keepdims=True) + LN_EPS)
    return center * inverse * gain_row + bias_row


def norm_back(values, gain_row, bias_row, grad_rows):
    norm_pull = jax.vjp(norm_rows, values, gain_row, bias_row)[1]
    return norm_pull(grad_rows)


def seq_layout(lengths, slot_total):
    seq_ends = jnp.cumsum(lengths)
    starts = seq_ends - lengths
    slot_index = jnp.arange(slot_total, dtype=jnp.int32)
    member = (slot_index[:, None] >= starts[None, :]) & (slot_index[:, None] < seq_ends[None, :])
    seq_count = jnp.arange(lengths.shape[0], dtype=jnp.int32)
    seq_ids = jnp.sum(jnp.where(member, seq_count[None, :], 0), axis=1)
    positions = slot_index - jnp.sum(jnp.where(member, starts[None, :], 0), axis=1) + 2
    return (seq_ids, positions, member)


def adam_step(weight, first_old, second_old, clipped, step_rate, decay_rate):
    first_new = BETA_FIRST * first_old + (1.0 - BETA_FIRST) * clipped
    second_new = BETA_SECOND * second_old + (1.0 - BETA_SECOND) * clipped * clipped
    first_hat = first_new / (1.0 - BETA_FIRST**STEP)
    second_hat = second_new / (1.0 - BETA_SECOND**STEP)
    weight_new = weight - step_rate * (
        first_hat / (jnp.sqrt(second_hat) + ADAM_EPS) + decay_rate * weight
    )
    return (weight_new, first_new, second_new)


MESH_IDS = pl.DeviceIdType.MESH
VMEM_BYTES = 60 * 1024 * 1024
CHUNKS = 4
LINE = 4


def in_vmem():
    return pl.BlockSpec(memory_space=pltpu.VMEM)


def shaped(shape, dtype):
    return jax.ShapeDtypeStruct(tuple(shape), dtype)


def dma(*shape):
    return pltpu.SemaphoreType.DMA(shape)


def remote(src, dst, send_sem, recv_sem, target):
    return pltpu.make_async_remote_copy(
        src_ref=src,
        dst_ref=dst,
        send_sem=send_sem,
        recv_sem=recv_sem,
        device_id=target,
        device_id_type=MESH_IDS,
    )


def comm_params(collective):
    return pltpu.CompilerParams(
        collective_id=collective, has_side_effects=True, vmem_limit_bytes=VMEM_BYTES
    )


def exchange(collective, *tasks):
    def kernel(*refs):
        at = 0
        for attribute in ("ins", "outs", "scratch"):
            for task in tasks:
                size = len(getattr(task, attribute))
                setattr(task, attribute + "_refs", refs[at : at + size])
                at += size
        barrier = pltpu.get_barrier_semaphore()
        partners = [partner for task in tasks for partner in task.partners()]
        for partner in partners:
            pl.semaphore_signal(barrier, inc=1, device_id=partner, device_id_type=MESH_IDS)
        pl.semaphore_wait(barrier, len(partners))
        for task in tasks:
            task.begin()
        for task in tasks:
            task.middle()
        for task in tasks:
            task.end()

    results = pl.pallas_call(
        kernel,
        out_shape=[out for task in tasks for out in task.outs],
        in_specs=[in_vmem() for task in tasks for _ in task.ins],
        out_specs=[in_vmem() for task in tasks for _ in task.outs],
        scratch_shapes=[item for task in tasks for item in task.scratch],
        compiler_params=comm_params(collective),
    )(*[array for task in tasks for array in task.ins])
    return results[0] if len(results) == 1 else results


def tensor_place(width):
    me = lax.axis_index("tensor")
    core = lax.rem(me, 2)
    row = me // 2
    mate = me + 1 - 2 * core
    return (me, core, row, mate)


class Task:
    def begin(self):
        pass

    def middle(self):
        pass

    def end(self):
        pass


class Pair(Task):
    def __init__(self):
        self.width = lax.axis_size("tensor")
        self.rows = self.width // 2

    def partners(self):
        me, core, row, mate = tensor_place(self.width)
        return [{"tensor": mate}] + [
            {"tensor": lax.rem(row + step, self.rows) * 2 + core} for step in range(1, self.rows)
        ]


class Spread(Pair):
    def __init__(self, block, columns=False, chunks=CHUNKS):
        super().__init__()
        height, depth = block.shape
        self.columns, self.chunks = columns, chunks
        self.ins = (block,)
        whole = (height, self.width * depth) if columns else (self.width * height, depth)
        self.outs = (shaped(whole, block.dtype),)
        self.scratch = tuple(dma(self.rows, chunks) for _ in range(4))

    def window(self, owner, part=None):
        (x_ref,), (o_ref,) = self.ins_refs, self.outs_refs
        height, depth = x_ref.shape
        size = height // self.chunks
        if self.columns:
            lanes = pl.ds(pl.multiple_of(owner * depth, depth), depth)
            if part is None or self.chunks == 1:
                return o_ref.at[:, lanes]
            return o_ref.at[pl.ds(part * size, size), lanes]
        if part is None:
            return o_ref.at[pl.ds(pl.multiple_of(owner * height, height), height)]
        return o_ref.at[pl.ds(pl.multiple_of(owner * height + part * size, size), size)]

    def begin(self):
        (x_ref,) = self.ins_refs
        far_send, far_recv, near_send, near_recv = self.scratch_refs
        me, core, row, mate = tensor_place(self.width)
        size = x_ref.shape[0] // self.chunks
        self.far = {}
        for part in range(self.chunks):
            source = x_ref if self.chunks == 1 else x_ref.at[pl.ds(part * size, size)]
            for step in range(1, self.rows):
                copy = remote(
                    source,
                    self.window(me, part),
                    far_send.at[step, part],
                    far_recv.at[step, part],
                    {"tensor": lax.rem(row + step, self.rows) * 2 + core},
                )
                copy.start()
                self.far[step, part] = copy
        copy = remote(
            x_ref, self.window(me), near_send.at[0, 0], near_recv.at[0, 0], {"tensor": mate}
        )
        copy.start()
        self.near = [copy]
        self.window(me)[...] = x_ref[...]

    def middle(self):
        far_send, far_recv, near_send, near_recv = self.scratch_refs
        me, core, row, mate = tensor_place(self.width)
        for part in range(self.chunks):
            for step in range(1, self.rows):
                self.far[step, part].wait_recv()
                source = lax.rem(row + self.rows - step, self.rows) * 2 + core
                onward = remote(
                    self.window(source, part),
                    self.window(source, part),
                    near_send.at[step, part],
                    near_recv.at[step, part],
                    {"tensor": mate},
                )
                onward.start()
                self.near.append(onward)

    def end(self):
        for copy in self.near:
            copy.wait()
        for copy in self.far.values():
            copy.wait_send()


class Fold(Pair):
    def __init__(self, parts, chunks=CHUNKS):
        super().__init__()
        height, depth = parts.shape[0] // self.width, parts.shape[1]
        far_rows = max(self.rows - 1, 1)
        self.chunks = chunks
        self.ins = (parts,)
        self.outs = (shaped((height, depth), jnp.float32),)
        self.scratch = (
            pltpu.VMEM((self.rows, height, depth), jnp.bfloat16),
            pltpu.VMEM((far_rows, height, depth), jnp.bfloat16),
            pltpu.VMEM((far_rows, height, depth), jnp.bfloat16),
        ) + tuple(dma(self.rows, chunks) for _ in range(4))

    def span(self, owner, part):
        height = self.outs[0].shape[0]
        size = height // self.chunks
        return pl.ds(pl.multiple_of(owner * height + part * size, size), size)

    def local(self, part):
        size = self.outs[0].shape[0] // self.chunks
        return pl.ds(part * size, size)

    def begin(self):
        (p_ref,) = self.ins_refs
        near_buf, near_send, near_recv = self.scratch_refs[0], *self.scratch_refs[3:5]
        me, core, row, mate = tensor_place(self.width)
        self.near = {}
        for step in list(range(1, self.rows)) + [0]:
            dest_row = lax.rem(row + step, self.rows)
            for part in range(self.chunks):
                copy = remote(
                    p_ref.at[self.span(dest_row * 2 + 1 - core, part)],
                    near_buf.at[step, self.local(part)],
                    near_send.at[step, part],
                    near_recv.at[step, part],
                    {"tensor": mate},
                )
                copy.start()
                self.near[step, part] = copy

    def middle(self):
        (p_ref,), (o_ref,) = self.ins_refs, self.outs_refs
        near_buf, sum_buf, far_buf, near_send, near_recv, far_send, far_recv = self.scratch_refs
        me, core, row, mate = tensor_place(self.width)
        self.far = {}
        for step in range(1, self.rows):
            dest = lax.rem(row + step, self.rows) * 2 + core
            for part in range(self.chunks):
                local = self.local(part)
                self.near[step, part].wait_recv()
                sum_buf[step - 1, local] = (
                    p_ref[self.span(dest, part)].astype(jnp.float32)
                    + near_buf[step, local].astype(jnp.float32)
                ).astype(jnp.bfloat16)
                copy = remote(
                    sum_buf.at[step - 1, local],
                    far_buf.at[step - 1, local],
                    far_send.at[step - 1, part],
                    far_recv.at[step - 1, part],
                    {"tensor": dest},
                )
                copy.start()
                self.far[step, part] = copy
        for part in range(self.chunks):
            local = self.local(part)
            self.near[0, part].wait_recv()
            o_ref[local] = p_ref[self.span(me, part)].astype(jnp.float32) + near_buf[
                0, local
            ].astype(jnp.float32)

    def end(self):
        (o_ref,) = self.outs_refs
        far_buf = self.scratch_refs[2]
        for part in range(self.chunks):
            local = self.local(part)
            for step in range(1, self.rows):
                self.far[step, part].wait_recv()
                o_ref[local] += far_buf[step - 1, local].astype(jnp.float32)
        for copy in list(self.near.values()) + list(self.far.values()):
            copy.wait_send()


class Swap(Task):
    def __init__(self, blocks, axis):
        self.axis, self.count = axis, lax.axis_size(axis)
        self.ins = (blocks,)
        self.outs = (shaped(blocks.shape, blocks.dtype),)
        self.scratch = (dma(self.count), dma(self.count))

    def others(self):
        me = lax.axis_index(self.axis)
        return [lax.rem(me + step, self.count) for step in range(1, self.count)]

    def partners(self):
        return [{self.axis: other} for other in self.others()]

    def begin(self):
        (x_ref,), (o_ref,), (send, recv) = self.ins_refs, self.outs_refs, self.scratch_refs
        me = lax.axis_index(self.axis)
        self.copies = [
            remote(x_ref.at[other], o_ref.at[me], send.at[i], recv.at[i], {self.axis: other})
            for i, other in enumerate(self.others())
        ]
        for copy in self.copies:
            copy.start()
        o_ref[me] = x_ref[me]

    def end(self):
        for copy in self.copies:
            copy.wait()


class Gather(Swap):
    def __init__(self, block, axis):
        super().__init__(block, axis)
        self.outs = (shaped((self.count,) + block.shape, block.dtype),)

    def begin(self):
        (x_ref,), (o_ref,), (send, recv) = self.ins_refs, self.outs_refs, self.scratch_refs
        me = lax.axis_index(self.axis)
        self.copies = [
            remote(x_ref, o_ref.at[me], send.at[i], recv.at[i], {self.axis: other})
            for i, other in enumerate(self.others())
        ]
        for copy in self.copies:
            copy.start()
        o_ref[me] = x_ref[...]


class GridTask(Task):
    def __init__(self):
        self.cross = lax.axis_size("dp") // LINE

    def place(self):
        me = lax.axis_index("dp")
        return (me // self.cross, lax.rem(me, self.cross))


class ReduceCross(GridTask):
    def __init__(self, blocks):
        super().__init__()
        shape = blocks.shape[1:]
        self.blocks_shape = (LINE, self.cross) + shape
        self.ins = (blocks.reshape(self.blocks_shape),)
        self.outs = (shaped((LINE,) + shape, jnp.bfloat16),)
        others = max(self.cross - 1, 1)
        self.scratch = (
            pltpu.VMEM((others, LINE) + shape, jnp.bfloat16),
            dma(others, LINE),
            dma(others, LINE),
        )

    def targets(self):
        line, cross = self.place()
        return [lax.rem(cross + step, self.cross) for step in range(1, self.cross)]

    def partners(self):
        line, cross = self.place()
        return [{"dp": line * self.cross + other} for other in self.targets()]

    def begin(self):
        (x_ref,), (buf, send, recv) = self.ins_refs, self.scratch_refs
        line, cross = self.place()
        self.copies = []
        for i, other in enumerate(self.targets()):
            for z in range(LINE):
                copy = remote(
                    x_ref.at[z, other],
                    buf.at[i, z],
                    send.at[i, z],
                    recv.at[i, z],
                    {"dp": line * self.cross + other},
                )
                copy.start()
                self.copies.append(copy)

    def end(self):
        (x_ref,), (o_ref,), (buf, send, recv) = self.ins_refs, self.outs_refs, self.scratch_refs
        line, cross = self.place()
        for copy in self.copies:
            copy.wait()
        for z in range(LINE):
            total = x_ref[z, cross].astype(jnp.float32)
            for i in range(self.cross - 1):
                total = total + buf[i, z].astype(jnp.float32)
            o_ref[z] = total.astype(jnp.bfloat16)


class ReduceLine(GridTask):
    def __init__(self, blocks):
        super().__init__()
        shape = blocks.shape[1:]
        self.ins = (blocks,)
        self.outs = (shaped(shape, jnp.float32),)
        self.scratch = (pltpu.VMEM((LINE - 1,) + shape, jnp.bfloat16), dma(LINE - 1), dma(LINE - 1))

    def targets(self):
        line, cross = self.place()
        return [lax.rem(line + step, LINE) for step in range(1, LINE)]

    def partners(self):
        line, cross = self.place()
        return [{"dp": other * self.cross + cross} for other in self.targets()]

    def begin(self):
        (x_ref,), (buf, send, recv) = self.ins_refs, self.scratch_refs
        line, cross = self.place()
        self.copies = [
            remote(
                x_ref.at[other], buf.at[i], send.at[i], recv.at[i], {"dp": other * self.cross + cross}
            )
            for i, other in enumerate(self.targets())
        ]
        for copy in self.copies:
            copy.start()

    def end(self):
        (x_ref,), (o_ref,), (buf, send, recv) = self.ins_refs, self.outs_refs, self.scratch_refs
        line, cross = self.place()
        for copy in self.copies:
            copy.wait()
        total = x_ref[line].astype(jnp.float32)
        for i in range(LINE - 1):
            total = total + buf[i].astype(jnp.float32)
        o_ref[...] = total


class SumAll(Task):
    def __init__(self, block, keep):
        self.groups, self.width, self.keep = lax.axis_size("dp"), lax.axis_size("tensor"), keep
        rows, depth = block.shape
        self.narrow = narrow = depth // self.width
        kept = self.groups if keep else 1
        self.ins = (block,)
        self.outs = (shaped((kept, rows, depth), block.dtype),)
        near, far = dma(self.width), dma(self.groups)
        self.scratch = (
            pltpu.VMEM((self.width, rows, narrow), block.dtype),
            pltpu.VMEM((rows, narrow), block.dtype),
            pltpu.VMEM((self.groups, rows, narrow), block.dtype),
            pltpu.VMEM((kept, rows, narrow), block.dtype),
            near, near, far, far, near, near,
        )

    def mates(self):
        me = lax.axis_index("tensor")
        return [lax.rem(me + step, self.width) for step in range(1, self.width)]

    def peers(self):
        me = lax.axis_index("dp")
        return [lax.rem(me + step, self.groups) for step in range(1, self.groups)]

    def partners(self):
        return [{"tensor": mate} for mate in self.mates()] + [{"dp": peer} for peer in self.peers()]

    def lanes(self, owner):
        return pl.ds(pl.multiple_of(owner * self.narrow, self.narrow), self.narrow)

    def launch(self, copies):
        for copy in copies:
            copy.start()
        self.copies = copies

    def settle(self):
        for copy in self.copies:
            copy.wait()

    def begin(self):
        (x_ref,) = self.ins_refs
        part_buf, sems = self.scratch_refs[0], self.scratch_refs[4:]
        me = lax.axis_index("tensor")
        self.launch(
            [
                remote(
                    x_ref.at[:, self.lanes(mate)],
                    part_buf.at[me],
                    sems[0].at[i],
                    sems[1].at[i],
                    {"tensor": mate},
                )
                for i, mate in enumerate(self.mates())
            ]
        )
        part_buf[me] = x_ref[:, self.lanes(me)]

    def middle(self):
        (o_ref,) = self.outs_refs
        part_buf, sum_buf, all_buf, out_buf = self.scratch_refs[:4]
        sems = self.scratch_refs[4:]
        dp_me, me = lax.axis_index("dp"), lax.axis_index("tensor")
        self.settle()
        sum_buf[...] = jnp.sum(part_buf[...], axis=0)
        self.launch(
            [
                remote(sum_buf, all_buf.at[dp_me], sems[2].at[i], sems[3].at[i], {"dp": peer})
                for i, peer in enumerate(self.peers())
            ]
        )
        all_buf[dp_me] = sum_buf[...]
        self.settle()
        if self.keep:
            out_buf[...] = all_buf[...]
        else:
            out_buf[0] = jnp.sum(all_buf[...], axis=0)
        self.launch(
            [
                remote(
                    out_buf,
                    o_ref.at[:, :, self.lanes(me)],
                    sems[4].at[i],
                    sems[5].at[i],
                    {"tensor": mate},
                )
                for i, mate in enumerate(self.mates())
            ]
        )
        o_ref[:, :, self.lanes(me)] = out_buf[...]

    def end(self):
        self.settle()


def gather_all_kernel(groups, width, x_ref, o_ref, send, recv):
    total = groups * width
    me = lax.axis_index("dp") * width + lax.axis_index("tensor")

    def place(step):
        other = lax.rem(me + step, total)
        return (other // width, lax.rem(other, width))

    barrier = pltpu.get_barrier_semaphore()

    def hello(step, carry):
        pl.semaphore_signal(barrier, inc=1, device_id=place(step), device_id_type=MESH_IDS)
        return carry

    lax.fori_loop(1, total, hello, 0)
    pl.semaphore_wait(barrier, total - 1)

    def copy(step):
        return remote(x_ref, o_ref.at[me], send.at[step], recv.at[step], place(step))

    def begin(step, carry):
        copy(step).start()
        return carry

    def finish(step, carry):
        copy(step).wait()
        return carry

    lax.fori_loop(1, total, begin, 0)
    o_ref[me] = x_ref[...]
    lax.fori_loop(1, total, finish, 0)


def gather_all(block, collective):
    groups, width = lax.axis_size("dp"), lax.axis_size("tensor")
    total = groups * width
    return pl.pallas_call(
        partial(gather_all_kernel, groups, width),
        out_shape=jax.ShapeDtypeStruct((total,) + block.shape, block.dtype),
        in_specs=[in_vmem()],
        out_specs=in_vmem(),
        scratch_shapes=[pltpu.SemaphoreType.DMA((total,)), pltpu.SemaphoreType.DMA((total,))],
        compiler_params=comm_params(collective),
    )(block)


Q_BLOCK = 256
K_BLOCK = 256


def split_pair(wide):
    half = wide.shape[0] // 2
    upper = lax.broadcasted_iota(jnp.int32, wide.shape, 0) < half
    zero = jnp.zeros_like(wide)
    return jnp.concatenate([jnp.where(upper, wide, zero), jnp.where(upper, zero, wide)], axis=1)


def stack_pair(tall):
    half = tall.shape[1] // 2
    left = lax.broadcasted_iota(jnp.int32, tall.shape, 1) < half
    zero = jnp.zeros_like(tall)
    return jnp.concatenate([jnp.where(left, tall, zero), jnp.where(left, zero, tall)], axis=0)


def join_pair(wide):
    depth, columns = wide.shape
    upper = lax.broadcasted_iota(jnp.int32, (depth, columns // 2), 0) < depth // 2
    return jnp.where(upper, wide[:, : columns // 2], wide[:, columns // 2 :])


def turn(tile):
    return tile.astype(jnp.float32).T.astype(jnp.bfloat16)


def block_span(index, size):
    return pl.ds(pl.multiple_of(index * size, size), size)


def attend_kernel(low_ref, high_ref, qkv_ref, seq_col_ref, seq_row_ref, out_ref, log_ref, value_turned, scores):
    slots, columns = out_ref.shape
    pairs = columns // 128
    q_blocks, k_blocks = slots // Q_BLOCK, slots // K_BLOCK

    def turn_values(b, carry):
        rows = block_span(b, K_BLOCK)
        for pair in range(pairs):
            value_turned[pl.ds(pair * 128, 128), rows] = turn(
                qkv_ref[rows, pl.ds(2 * columns + pair * 128, 128)]
            )
        return carry

    lax.fori_loop(0, k_blocks, turn_values, 0)

    def one_block(q_index, carry):
        q_rows = block_span(q_index, Q_BLOCK)
        lowest, highest = low_ref[q_index], high_ref[q_index]
        seq_row = seq_row_ref[0:1, q_rows]
        seq_pair = jnp.concatenate([seq_row, seq_row], axis=1)
        queries = [
            split_pair(
                (qkv_ref[q_rows, pl.ds(pair * 128, 128)].astype(jnp.float32) * HEAD ** (-0.5))
                .T.astype(jnp.bfloat16)
            )
            for pair in range(pairs)
        ]

        def score(k_index, tops):
            k_rows = block_span(k_index, K_BLOCK)
            same = seq_col_ref[k_rows, 0:1] == seq_pair
            later = []
            for pair in range(pairs):
                keys = qkv_ref[k_rows, pl.ds(columns + pair * 128, 128)]
                value = jnp.where(same, multiply_arrays(keys, queries[pair]), MASK_FILL)
                scores[pair, k_index - lowest] = value
                later.append(jnp.maximum(tops[pair], jnp.max(value, axis=0, keepdims=True)))
            return tuple(later)

        start = tuple(jnp.full((1, 2 * Q_BLOCK), MASK_FILL, jnp.float32) for _ in range(pairs))
        tops = lax.fori_loop(lowest, highest, score, start)

        def mix(k_index, state):
            k_rows = block_span(k_index, K_BLOCK)
            later = []
            for pair in range(pairs):
                total, mixed = state[pair]
                weights = jnp.exp(scores[pair, k_index - lowest] - tops[pair])
                total = total + jnp.sum(weights, axis=0, keepdims=True)
                mixed = mixed + multiply_arrays(
                    value_turned[pl.ds(pair * 128, 128), k_rows], weights.astype(jnp.bfloat16)
                )
                later.append((total, mixed))
            return tuple(later)

        blank = tuple(
            (jnp.zeros((1, 2 * Q_BLOCK), jnp.float32), jnp.zeros((128, 2 * Q_BLOCK), jnp.float32))
            for _ in range(pairs)
        )
        final = lax.fori_loop(lowest, highest, mix, blank)
        for pair in range(pairs):
            total, mixed = final[pair]
            out_ref[q_rows, pl.ds(pair * 128, 128)] = join_pair(mixed / total).T.astype(jnp.bfloat16)
            logs = tops[pair] + jnp.log(total)
            log_ref[pl.ds(2 * pair, 1), q_rows] = logs[:, :Q_BLOCK]
            log_ref[pl.ds(2 * pair + 1, 1), q_rows] = logs[:, Q_BLOCK:]
        return carry

    lax.fori_loop(0, q_blocks, one_block, 0)


def block_bounds(lengths, slots):
    ends = jnp.cumsum(lengths)
    starts = ends - lengths
    first = jnp.arange(slots // Q_BLOCK, dtype=jnp.int32) * Q_BLOCK
    last = first + Q_BLOCK - 1
    lowest = jnp.max(
        jnp.where(starts[None, :] <= first[:, None], starts[None, :], 0), axis=1
    )
    highest = jnp.min(jnp.where(ends[None, :] > last[:, None], ends[None, :], slots), axis=1)
    return (lowest // K_BLOCK, (highest + K_BLOCK - 1) // K_BLOCK)


REACH = (2 * MAXLEN - 2) // K_BLOCK + Q_BLOCK // K_BLOCK + 1


def in_scalars():
    return pl.BlockSpec(memory_space=pltpu.SMEM)


def attend(qkv_out, seq_ids, bounds):
    slots, columns = qkv_out.shape[0], qkv_out.shape[1] // 3
    pairs = columns // 128
    return pl.pallas_call(
        attend_kernel,
        out_shape=[
            jax.ShapeDtypeStruct((slots, columns), jnp.bfloat16),
            jax.ShapeDtypeStruct((8, slots), jnp.float32),
        ],
        in_specs=[in_scalars(), in_scalars()] + [in_vmem()] * 3,
        out_specs=[in_vmem()] * 2,
        scratch_shapes=[
            pltpu.VMEM((columns, slots), jnp.bfloat16),
            pltpu.VMEM((pairs, REACH, K_BLOCK, 2 * Q_BLOCK), jnp.float32),
        ],
        compiler_params=pltpu.CompilerParams(vmem_limit_bytes=VMEM_BYTES),
    )(bounds[0], bounds[1], qkv_out, seq_ids[:, None], jnp.broadcast_to(seq_ids[None], (8, slots)))


def attend_back_kernel(
    low_ref, high_ref, qkv_ref, grad_ref, log_ref, seq_col_ref, seq_row_ref, out_ref,
    key_turned, probs, prob_grads, key_sum, value_sum,
):
    slots, columns = grad_ref.shape
    pairs = columns // 128
    q_blocks, k_blocks = slots // Q_BLOCK, slots // K_BLOCK

    def turn_keys(b, carry):
        rows = block_span(b, K_BLOCK)
        for pair in range(pairs):
            key_turned[pl.ds(pair * 128, 128), rows] = turn(
                qkv_ref[rows, pl.ds(columns + pair * 128, 128)]
            )
        key_sum[rows] = jnp.zeros((K_BLOCK, columns), jnp.float32)
        value_sum[rows] = jnp.zeros((K_BLOCK, columns), jnp.float32)
        return carry

    lax.fori_loop(0, k_blocks, turn_keys, 0)

    def one_block(q_index, carry):
        q_rows = block_span(q_index, Q_BLOCK)
        lowest, highest = low_ref[q_index], high_ref[q_index]
        seq_row = seq_row_ref[0:1, q_rows]
        seq_pair = jnp.concatenate([seq_row, seq_row], axis=1)
        scaled, queries, grads, turned, logs = [], [], [], [], []
        for pair in range(pairs):
            plain = qkv_ref[q_rows, pl.ds(pair * 128, 128)].astype(jnp.float32) * HEAD ** (-0.5)
            scaled.append(stack_pair(plain.astype(jnp.bfloat16)))
            queries.append(split_pair(plain.T.astype(jnp.bfloat16)))
            grad = grad_ref[q_rows, pl.ds(pair * 128, 128)]
            grads.append(stack_pair(grad))
            turned.append(split_pair(turn(grad)))
            logs.append(
                jnp.concatenate(
                    [log_ref[pl.ds(2 * pair, 1), q_rows], log_ref[pl.ds(2 * pair + 1, 1), q_rows]],
                    axis=1,
                )
            )

        def look(k_index, inners):
            k_rows = block_span(k_index, K_BLOCK)
            same = seq_col_ref[k_rows, 0:1] == seq_pair
            later = []
            for pair in range(pairs):
                keys = qkv_ref[k_rows, pl.ds(columns + pair * 128, 128)]
                values = qkv_ref[k_rows, pl.ds(2 * columns + pair * 128, 128)]
                logits = jnp.where(same, multiply_arrays(keys, queries[pair]), MASK_FILL)
                weights = jnp.exp(logits - logs[pair])
                weight_grad = multiply_arrays(values, turned[pair])
                probs[pair, k_index - lowest] = weights
                prob_grads[pair, k_index - lowest] = weight_grad
                value_sum[k_rows, pl.ds(pair * 128, 128)] += multiply_arrays(
                    weights.astype(jnp.bfloat16), grads[pair]
                )
                later.append(
                    inners[pair] + jnp.sum(weights * weight_grad, axis=0, keepdims=True)
                )
            return tuple(later)

        start = tuple(jnp.zeros((1, 2 * Q_BLOCK), jnp.float32) for _ in range(pairs))
        inners = lax.fori_loop(lowest, highest, look, start)

        def push(k_index, sums):
            k_rows = block_span(k_index, K_BLOCK)
            later = []
            for pair in range(pairs):
                slope = (
                    probs[pair, k_index - lowest]
                    * (prob_grads[pair, k_index - lowest] - inners[pair])
                ).astype(jnp.bfloat16)
                key_sum[k_rows, pl.ds(pair * 128, 128)] += multiply_arrays(slope, scaled[pair])
                later.append(
                    sums[pair] + multiply_arrays(key_turned[pl.ds(pair * 128, 128), k_rows], slope)
                )
            return tuple(later)

        blank = tuple(jnp.zeros((128, 2 * Q_BLOCK), jnp.float32) for _ in range(pairs))
        sums = lax.fori_loop(lowest, highest, push, blank)
        for pair in range(pairs):
            out_ref[q_rows, pl.ds(pair * 128, 128)] = (
                (join_pair(sums[pair]) * HEAD ** (-0.5)).T.astype(jnp.bfloat16)
            )
        return carry

    lax.fori_loop(0, q_blocks, one_block, 0)
    out_ref[:, columns : 2 * columns] = key_sum[...].astype(jnp.bfloat16)
    out_ref[:, 2 * columns :] = value_sum[...].astype(jnp.bfloat16)


def attend_back(qkv_out, attn_grad, log_total, seq_ids, bounds):
    slots, columns = attn_grad.shape
    pairs = columns // 128
    window = pltpu.VMEM((pairs, REACH, K_BLOCK, 2 * Q_BLOCK), jnp.float32)
    return pl.pallas_call(
        attend_back_kernel,
        out_shape=jax.ShapeDtypeStruct(qkv_out.shape, jnp.bfloat16),
        in_specs=[in_scalars(), in_scalars()] + [in_vmem()] * 5,
        out_specs=in_vmem(),
        scratch_shapes=[
            pltpu.VMEM((columns, slots), jnp.bfloat16),
            window,
            window,
            pltpu.VMEM((slots, columns), jnp.float32),
            pltpu.VMEM((slots, columns), jnp.float32),
        ],
        compiler_params=pltpu.CompilerParams(vmem_limit_bytes=VMEM_BYTES),
    )(
        bounds[0],
        bounds[1],
        qkv_out,
        attn_grad,
        log_total,
        seq_ids[:, None],
        jnp.broadcast_to(seq_ids[None], (8, slots)),
    )


def layer_forward(emb_all, seq_ids, bounds, row_params, col_local, layer_mats):
    qkv_full, out_full, up_full, down_full = layer_mats
    col_width = qkv_full.shape[2]
    tok_dev = emb_all.shape[0] // lax.axis_size("tensor")
    first_moment_all = norm_rows(emb_all, row_params[0], row_params[3]).astype(jnp.bfloat16)
    emb_rows = lax.dynamic_slice_in_dim(emb_all, lax.axis_index("tensor") * tok_dev, tok_dev, 0)
    norm_first = norm_rows(emb_rows, row_params[0], row_params[3])
    qkv_bias = jnp.concatenate([col_local[0], jnp.zeros_like(col_local[0]), col_local[1]])
    qkv_out = (
        multiply_arrays(first_moment_all, qkv_full.reshape(D, 3 * col_width)) + qkv_bias
    ).astype(jnp.bfloat16)
    attn_low, log_total = attend(qkv_out, seq_ids, bounds)
    first_sum = (
        norm_first
        + exchange(5, Fold(multiply_arrays(attn_low, out_full).astype(jnp.bfloat16)))
        + row_params[6]
    )
    norm_second = norm_rows(first_sum, row_params[1], row_params[4])
    second_all = exchange(6, Spread(norm_second.astype(jnp.bfloat16)))
    expansion_result = multiply_arrays(second_all, up_full.reshape(D, -1)) + col_local[2:].reshape(
        -1
    )
    hidden_low = jax.nn.gelu(expansion_result, approximate=False).astype(jnp.bfloat16)
    second_sum = (
        norm_second
        + exchange(
            7, Fold(multiply_arrays(hidden_low, down_full.reshape(-1, D)).astype(jnp.bfloat16))
        )
        + row_params[7]
    )
    norm_third = norm_rows(second_sum, row_params[2], row_params[5])
    saved_vals = (
        emb_rows,
        first_moment_all,
        qkv_out,
        log_total,
        attn_low,
        first_sum,
        second_all,
        expansion_result,
        hidden_low,
        second_sum,
    )
    return (norm_third, saved_vals)


def turned_grad(left_all, right_all):
    grad = jnp.einsum("td,tc->dc", left_all, right_all, preferred_element_type=jnp.float32)
    groups = lax.axis_size("dp")
    return grad.astype(jnp.bfloat16).reshape(groups, grad.shape[0] // groups, grad.shape[1])


def layer_backward(grad_third, seq_ids, bounds, row_params, layer_mats, saved_vals):
    qkv_full, out_full, up_full, down_full = layer_mats
    (
        emb_rows,
        first_moment_all,
        qkv_out,
        log_total,
        attn_low,
        first_sum,
        second_all,
        expansion_result,
        hidden_low,
        second_sum,
    ) = saved_vals
    col_width = qkv_full.shape[2]
    grad_second, gain_c, shift_c = norm_back(second_sum, row_params[2], row_params[5], grad_third)
    mixed_low = grad_second.astype(jnp.bfloat16)
    mixed_all = exchange(10, Spread(mixed_low))
    down_grad = turned_grad(mixed_all, hidden_low)
    hidden_grad = jnp.einsum(
        "td,fd->tf", mixed_all, down_full.reshape(-1, D), preferred_element_type=jnp.float32
    )
    gelu_pull = jax.vjp(partial(jax.nn.gelu, approximate=False), expansion_result)[1]
    up_low = gelu_pull(hidden_grad)[0].astype(jnp.bfloat16)
    up_grad = turned_grad(second_all, up_low)
    second_back = jnp.einsum(
        "tf,df->td", up_low, up_full.reshape(D, -1), preferred_element_type=jnp.float32
    ).astype(jnp.bfloat16)
    second_back, down_half = exchange(11, Fold(second_back), ReduceCross(down_grad))
    second_total = grad_second + second_back
    grad_first, gain_b, shift_b = norm_back(first_sum, row_params[1], row_params[4], second_total)
    branch_low = grad_first.astype(jnp.bfloat16)
    branch_all, down_sum, up_half = exchange(
        12, Spread(branch_low), ReduceLine(down_half), ReduceCross(up_grad)
    )
    out_grad = turned_grad(branch_all, attn_low)
    attn_grad = jnp.einsum(
        "td,cd->tc", branch_all, out_full, preferred_element_type=jnp.float32
    ).astype(jnp.bfloat16)
    qkv_low = attend_back(qkv_out, attn_grad, log_total, seq_ids, bounds)
    qkv_grad = turned_grad(first_moment_all, qkv_low)
    first_back = jnp.einsum(
        "tc,dc->td", qkv_low, qkv_full.reshape(D, -1), preferred_element_type=jnp.float32
    ).astype(jnp.bfloat16)
    first_back, up_sum, out_half, qkv_half = exchange(
        13, Fold(first_back), ReduceLine(up_half), ReduceCross(out_grad), ReduceCross(qkv_grad)
    )
    first_total = grad_first + first_back
    emb_grad, gain_a, shift_a = norm_back(emb_rows, row_params[0], row_params[3], first_total)
    qkv_cols = jnp.sum(qkv_low.astype(jnp.float32), axis=0).reshape(3, col_width)
    up_cols = jnp.sum(up_low.astype(jnp.float32), axis=0).reshape(-1, col_width)
    col_grad = jnp.concatenate([qkv_cols[0:1], qkv_cols[2:3], up_cols], axis=0)
    row_grad = jnp.stack(
        [
            gain_a,
            gain_b,
            gain_c,
            shift_a,
            shift_b,
            shift_c,
            jnp.sum(branch_low.astype(jnp.float32), axis=0),
            jnp.sum(mixed_low.astype(jnp.float32), axis=0),
        ]
    )
    return (emb_grad, (qkv_half, out_half, up_sum, down_sum), col_grad, row_grad)


def plan_kernel(capacity, vocab_local, groups, perm_ref, low_ref, high_ref, slot_ref, list_ref, count_ref, id_buf, own_buf):
    slots = perm_ref.shape[1]
    table_rows = low_ref.shape[1]
    block = 128
    blocks = slots // block
    perm = perm_ref[...]
    high_part = perm // 128
    low_part = perm - high_part * 128
    chooser = (lax.broadcasted_iota(jnp.int32, (table_rows, slots), 0) == high_part).astype(
        jnp.float32
    ).astype(jnp.bfloat16)
    value = multiply_arrays(low_ref[...], chooser) + 256.0 * multiply_arrays(high_ref[...], chooser)
    lane_match = lax.broadcasted_iota(jnp.int32, (128, slots), 0) == low_part
    ids = jnp.sum(jnp.where(lane_match, value, 0.0), axis=0, keepdims=True)
    for b in range(blocks):
        id_buf[pl.ds(b * block, block), :] = jnp.broadcast_to(
            ids[:, b * block : (b + 1) * block], (block, block)
        ).T
    place = lax.broadcasted_iota(jnp.int32, (1, slots), 1).astype(jnp.float32)
    rows = lax.broadcasted_iota(jnp.int32, (block, 1), 0).astype(jnp.float32)

    def earliest(b, best):
        column = id_buf[pl.ds(pl.multiple_of(b * block, block), block), 0:1]
        index = rows + (b * block).astype(jnp.float32)
        found = jnp.where(column == ids, index, 1e9)
        return jnp.minimum(best, jnp.min(found, axis=0, keepdims=True))

    least = lax.fori_loop(0, blocks, earliest, jnp.full((1, slots), 1e9, jnp.float32))
    first = least == place
    owner = jnp.zeros((1, slots), jnp.float32)
    for index in range(1, groups):
        owner = owner + jnp.where(ids >= float(index * vocab_local), 1.0, 0.0)
    owner_rows = lax.broadcasted_iota(jnp.int32, (groups, slots), 0).astype(jnp.float32)
    marks = jnp.where(first & (owner == owner_rows), 1.0, 0.0)
    upper = jnp.where(
        lax.broadcasted_iota(jnp.int32, (block, block), 0)
        < lax.broadcasted_iota(jnp.int32, (block, block), 1),
        1.0,
        0.0,
    ).astype(jnp.bfloat16)
    running = jnp.zeros((groups, 1), jnp.float32)
    pieces = []
    for b in range(blocks):
        part = marks[:, b * block : (b + 1) * block]
        pieces.append(multiply_arrays(part.astype(jnp.bfloat16), upper) + running)
        running = running + jnp.sum(part, axis=1, keepdims=True)
    before = jnp.concatenate(pieces, axis=1)
    rank = jnp.sum(marks * before, axis=0, keepdims=True)
    own_slot = jnp.where(first & (rank < float(capacity)), owner * float(capacity) + rank, -1.0)
    for b in range(blocks):
        own_buf[pl.ds(b * block, block), :] = jnp.broadcast_to(
            own_slot[:, b * block : (b + 1) * block], (block, block)
        ).T
    width = list_ref.shape[1]
    target = lax.broadcasted_iota(jnp.int32, (1, width), 1).astype(jnp.float32)

    def settle(b, carry):
        slot, listed = carry
        window = pl.ds(pl.multiple_of(b * block, block), block)
        column, slot_column = id_buf[window, 0:1], own_buf[window, 0:1]
        slot = jnp.maximum(
            slot, jnp.max(jnp.where(column == ids, slot_column, -1.0), axis=0, keepdims=True)
        )
        listed = jnp.maximum(
            listed, jnp.max(jnp.where(slot_column == target, column, -1.0), axis=0, keepdims=True)
        )
        return (slot, listed)

    slot, listed = lax.fori_loop(
        0,
        blocks,
        settle,
        (jnp.full((1, slots), -1.0, jnp.float32), jnp.full((1, width), -1.0, jnp.float32)),
    )
    slot_ref[...] = slot.astype(jnp.int32)
    list_ref[...] = listed.astype(jnp.int32)
    count_ref[...] = jnp.broadcast_to(running, count_ref.shape).astype(jnp.int32)


def make_plan(perm, all_ids, capacity, vocab_local, groups):
    slots = perm.shape[0]
    table = all_ids.reshape(-1, 128).T
    high = table // 256
    low = table - high * 256
    return pl.pallas_call(
        partial(plan_kernel, capacity, vocab_local, groups),
        out_shape=[
            jax.ShapeDtypeStruct((1, slots), jnp.int32),
            jax.ShapeDtypeStruct((1, groups * capacity), jnp.int32),
            jax.ShapeDtypeStruct((groups, 128), jnp.int32),
        ],
        in_specs=[in_vmem()] * 3,
        out_specs=[in_vmem()] * 3,
        scratch_shapes=[pltpu.VMEM((slots, 128), jnp.float32), pltpu.VMEM((slots, 128), jnp.float32)],
        compiler_params=pltpu.CompilerParams(vmem_limit_bytes=VMEM_BYTES),
    )(perm[None], low.astype(jnp.bfloat16), high.astype(jnp.bfloat16))


def loss_kernel(pooled_ref, head_ref, pair_ref, loss_ref, low_ref, grad_ref, back_ref):
    total = pooled_ref.shape[0]
    low = pooled_ref[...].astype(jnp.bfloat16)
    low_ref[...] = low
    head_low = head_ref[...].astype(jnp.bfloat16)
    vectors = multiply_arrays(low, head_low)
    depth = vectors.shape[1]
    lane = lax.broadcasted_iota(jnp.int32, vectors.shape, 1)
    across = lax.broadcasted_iota(jnp.int32, (total, total), 1)
    diagonal = lax.broadcasted_iota(jnp.int32, (total, total), 0) == across
    chosen = across == pair_ref[...]
    loss = jnp.zeros((1, 1), jnp.float32)
    grads = jnp.zeros(vectors.shape, jnp.float32)

    def exact(left, right, dims):
        return lax.dot_general(
            left, right, (dims, ((), ())), precision=HIGHEST_MODE, preferred_element_type=jnp.float32
        )

    for fraction in (16, 4, 1):
        prefix = jnp.where(lane < depth // fraction, vectors, 0.0)
        inverse = lax.rsqrt(jnp.sum(prefix * prefix, axis=1, keepdims=True) + 1e-06)
        unit = prefix * inverse
        logits = exact(unit, unit, ((1,), (1,))) / LOGIT_DIVISOR
        logits = jnp.where(diagonal, MASK_FILL, logits)
        top = jnp.max(logits, axis=1, keepdims=True)
        weights = jnp.exp(logits - top)
        weight_sum = jnp.sum(weights, axis=1, keepdims=True)
        positive = jnp.sum(jnp.where(chosen, logits, 0.0), axis=1, keepdims=True)
        loss = loss + jnp.sum(jnp.log(weight_sum) + top - positive, keepdims=True)
        pull = weights / weight_sum - jnp.where(chosen, 1.0, 0.0)
        unit_grad = (exact(pull, unit, ((1,), (0,))) + exact(pull, unit, ((0,), (0,)))) / LOGIT_DIVISOR
        unit_grad = jnp.where(lane < depth // fraction, unit_grad, 0.0)
        inner = jnp.sum(unit_grad * prefix, axis=1, keepdims=True)
        grads = grads + inverse * unit_grad - prefix * (inverse * inverse * inverse * inner)
    loss_ref[...] = jnp.broadcast_to(loss, loss_ref.shape)
    grad_ref[...] = grads
    back_ref[...] = exact(grads, head_low.astype(jnp.float32), ((1,), (1,)))


def contrast_step(pooled, head_weight, pairs):
    total, depth = pooled.shape
    return pl.pallas_call(
        loss_kernel,
        out_shape=[
            jax.ShapeDtypeStruct((8, 128), jnp.float32),
            jax.ShapeDtypeStruct((total, depth), jnp.bfloat16),
            jax.ShapeDtypeStruct((total, depth), jnp.float32),
            jax.ShapeDtypeStruct((total, depth), jnp.float32),
        ],
        in_specs=[in_vmem()] * 3,
        out_specs=[in_vmem()] * 4,
        compiler_params=pltpu.CompilerParams(vmem_limit_bytes=VMEM_BYTES),
    )(pooled, head_weight, pairs[:, None])


CAPACITY = 256


def body(
    token_ids,
    slot_perm,
    seq_lengths,
    pair_index,
    tok_table,
    tok_first,
    tok_second,
    pos_table,
    pos_first,
    pos_second,
    query_key_value_weight,
    qkv_first,
    qkv_second,
    out_weight,
    out_first,
    out_second,
    up_weight,
    up_first,
    up_second,
    down_weight,
    down_first,
    down_second,
    head_weight,
    head_first,
    head_second,
    col_bias,
    col_first,
    col_second,
    row_params,
    row_first,
    row_second,
):
    groups = lax.axis_size("dp")
    tensor_count = lax.axis_size("tensor")
    group_index = lax.axis_index("dp")
    tensor_index = lax.axis_index("tensor")
    tok_dev = token_ids.shape[0]
    tok_grp = tok_dev * tensor_count
    col_width = pos_table.shape[1]
    vocab_local = tok_table.shape[0]
    column_start = tensor_index * col_width
    anchors = pair_index.shape[0]
    id_rows = tok_dev // 128
    block = jnp.concatenate(
        [
            token_ids.reshape(id_rows, 128),
            slot_perm.reshape(id_rows, 128),
            jnp.pad(pair_index, (0, 128 - anchors))[None],
            jnp.zeros((16 - 2 * id_rows - 1, 128), jnp.int32),
        ],
        axis=0,
    )
    gathered = gather_all(block, 1)
    all_ids = gathered[:, :id_rows].reshape(-1)
    pairs = gathered[:: tensor_count, 2 * id_rows, :anchors].reshape(-1)
    own_perm = lax.dynamic_slice_in_dim(
        gathered, group_index * tensor_count, tensor_count, 0
    )[:, id_rows : 2 * id_rows].reshape(-1)
    slot, listed, counts_out = make_plan(own_perm, all_ids, CAPACITY, vocab_local, groups)
    slot = slot[0]
    list_rows = CAPACITY // 128
    top_count = jnp.max(counts_out)
    request = jnp.concatenate(
        [
            listed.reshape(groups, list_rows, 128),
            jnp.broadcast_to(top_count, (groups, 8 - list_rows, 128)),
        ],
        axis=1,
    )
    asked = exchange(2, Swap(request, "dp"))
    overflow = jnp.max(asked[:, list_rows]) > CAPACITY
    offset = group_index * vocab_local
    asked_rows = asked[:, :list_rows].reshape(-1) - offset
    asked_safe = jnp.clip(asked_rows, 0, vocab_local - 1)
    sent_rows = jnp.take(tok_table, asked_safe, axis=0).astype(jnp.bfloat16)
    got_rows, pos_full = exchange(
        3,
        Swap(sent_rows.reshape(groups, CAPACITY, col_width), "dp"),
        Spread(pos_table, columns=True, chunks=1),
    )
    got_rows = got_rows.reshape(-1, col_width)
    chooser = (slot[:, None] == jnp.arange(groups * CAPACITY, dtype=jnp.int32)[None, :]).astype(
        jnp.bfloat16
    )
    lengths = seq_lengths[0]
    seq_ids, positions, member = seq_layout(lengths, tok_grp)
    bounds = block_bounds(lengths, tok_grp)

    def every_slot_id():
        every_perm = gathered[:, id_rows : 2 * id_rows].reshape(-1)
        return jnp.take(all_ids, every_perm, axis=0)

    def spread_wide():
        wanted = every_slot_id() - offset
        inside = (wanted >= 0) & (wanted < vocab_local)
        picked = jnp.take(
            tok_table.astype(jnp.bfloat16), jnp.clip(wanted, 0, vocab_local - 1), axis=0
        )
        return lax.psum_scatter(
            jnp.where(inside[:, None], picked, jnp.zeros((), jnp.bfloat16)),
            "dp",
            scatter_dimension=0,
            tiled=True,
        )

    tok_cols = lax.cond(
        overflow,
        spread_wide,
        lambda: multiply_arrays(chooser, got_rows).astype(jnp.bfloat16),
    )
    emb_all = exchange(4, Spread(tok_cols, columns=True)).astype(jnp.float32) + jnp.take(pos_full, positions, axis=0)
    layer_mats = (
        lax.all_gather(query_key_value_weight.astype(jnp.bfloat16), "dp", axis=0, tiled=True),
        lax.all_gather(out_weight.astype(jnp.bfloat16), "dp", axis=1, tiled=True),
        lax.all_gather(up_weight.astype(jnp.bfloat16), "dp", axis=0, tiled=True),
        lax.all_gather(down_weight.astype(jnp.bfloat16), "dp", axis=2, tiled=True),
    )
    norm_third, saved_vals = layer_forward(emb_all, seq_ids, bounds, row_params, col_bias, layer_mats)
    row_member = lax.dynamic_slice_in_dim(member, tensor_index * tok_dev, tok_dev, 0).astype(
        jnp.float32
    )
    counts = lengths.astype(jnp.float32)[:, None]
    pooled = exchange(9, SumAll(exact_multiply(row_member.T, norm_third) / counts, True))
    loss_out, pooled_low, vec_grad, pooled_grad = contrast_step(
        pooled.reshape(-1, D), head_weight, pairs
    )
    head_sum = exact_multiply(pooled_low.astype(jnp.float32).T, vec_grad)
    own_grad = lax.dynamic_slice_in_dim(pooled_grad, group_index * anchors, anchors, 0)
    grad_third = exact_multiply(row_member, own_grad / counts)
    emb_grad, halves, col_grad, row_grad = layer_backward(
        grad_third, seq_ids, bounds, row_params, layer_mats, saved_vals
    )
    qkv_half, out_half, up_sum, down_sum = halves
    cols_grad, qkv_sum, out_sum = exchange(
        14,
        Swap(
            emb_grad.astype(jnp.bfloat16)
            .reshape(tok_dev, tensor_count, col_width)
            .swapaxes(0, 1),
            "tensor",
        ),
        ReduceLine(qkv_half),
        ReduceLine(out_half),
    )
    cols_grad = cols_grad.reshape(tok_grp, col_width)
    pos_pick = (
        jnp.arange(pos_table.shape[0], dtype=jnp.int32)[:, None] == positions[None, :]
    ).astype(jnp.bfloat16)
    pos_grad = multiply_arrays(pos_pick, cols_grad)
    shared = jnp.concatenate([pos_grad, col_grad], axis=0)
    shared_rows = -(-shared.shape[0] // (8 * groups)) * 8
    shared = jnp.pad(shared, ((0, shared_rows * groups - shared.shape[0]), (0, 0)))
    merged = jnp.einsum("kn,kc->nc", chooser, cols_grad, preferred_element_type=jnp.float32)
    back_rows, shared_parts = exchange(
        15,
        Swap(merged.astype(jnp.bfloat16).reshape(groups, CAPACITY, col_width), "dp"),
        Swap(shared.reshape(groups, shared_rows, col_width), "dp"),
    )
    shared_own = jnp.sum(shared_parts, axis=0)

    def add_wide():
        wanted = every_slot_id() - offset
        inside = (wanted >= 0) & (wanted < vocab_local)
        return (
            jnp.zeros(tok_table.shape, jnp.float32)
            .at[jnp.clip(wanted, 0, vocab_local - 1)]
            .add(
                jnp.where(
                    inside[:, None],
                    lax.all_gather(cols_grad, "dp", axis=0, tiled=True).astype(jnp.float32),
                    0.0,
                )
            )
        )

    def add_listed():
        return (
            jnp.zeros(tok_table.shape, jnp.float32)
            .at[jnp.where(asked_rows < 0, vocab_local, asked_rows)]
            .add(back_rows.reshape(-1, col_width).astype(jnp.float32), mode="drop")
        )

    tok_grad = lax.cond(overflow, add_wide, add_listed)
    qkv_grad = qkv_sum.reshape(query_key_value_weight.shape)
    out_grad = out_sum.T
    up_grad = up_sum.reshape(up_weight.shape)
    down_grad = down_sum.T.reshape(down_weight.shape)
    local_squares = (
        jnp.sum(tok_grad * tok_grad)
        + jnp.sum(qkv_grad * qkv_grad)
        + jnp.sum(out_grad * out_grad)
        + jnp.sum(up_grad * up_grad)
        + jnp.sum(down_grad * down_grad)
        + jnp.sum(shared_own * shared_own)
    )
    row_block = jnp.concatenate(
        [row_grad, jnp.pad(local_squares.reshape(1, 1), ((0, 7), (0, D - 1)))], axis=0
    )
    row_total, shared_sum = exchange(16, SumAll(row_block, False), Gather(shared_own, "dp"))
    row_total = row_total[0]
    shared_sum = shared_sum.reshape(-1, col_width)
    pos_own = shared_sum[: pos_table.shape[0]]
    col_own = shared_sum[pos_table.shape[0] : pos_table.shape[0] + col_bias.shape[0]]
    row_sum = row_total[:8]
    squares = row_total[8, 0] + jnp.sum(row_sum * row_sum) + jnp.sum(head_sum * head_sum)
    grad_norm = jnp.sqrt(squares)
    clip_scale = jnp.minimum(1.0, CLIP_NORM / (grad_norm + 1e-06))
    tok_new = adam_step(
        tok_table, tok_first, tok_second, tok_grad * clip_scale, RATE_MATRIX, DECAY_RATE
    )
    pos_new = adam_step(
        pos_table, pos_first, pos_second, pos_own * clip_scale, RATE_MATRIX, DECAY_RATE
    )
    qkv_new = adam_step(
        query_key_value_weight,
        qkv_first,
        qkv_second,
        qkv_grad * clip_scale,
        RATE_MATRIX,
        DECAY_RATE,
    )
    out_new = adam_step(
        out_weight, out_first, out_second, out_grad * clip_scale, RATE_MATRIX, DECAY_RATE
    )
    up_new = adam_step(
        up_weight, up_first, up_second, up_grad * clip_scale, RATE_MATRIX, DECAY_RATE
    )
    down_new = adam_step(
        down_weight, down_first, down_second, down_grad * clip_scale, RATE_MATRIX, DECAY_RATE
    )
    head_new = adam_step(
        head_weight, head_first, head_second, head_sum * clip_scale, RATE_MATRIX, DECAY_RATE
    )
    col_new = adam_step(col_bias, col_first, col_second, col_own * clip_scale, RATE_VECTOR, 0.0)
    row_new = adam_step(row_params, row_first, row_second, row_sum * clip_scale, RATE_VECTOR, 0.0)
    return (loss_out[0, 0], grad_norm) + tok_new + pos_new + qkv_new + out_new + up_new + down_new + head_new + col_new + row_new


def solution(mesh):
    placed = (
        P(("dp", "tensor")),
        P(("dp", "tensor")),
        P("dp", None),
        P("dp"),
        P("dp", "tensor"),
        P("dp", "tensor"),
        P("dp", "tensor"),
        P(None, "tensor"),
        P(None, "tensor"),
        P(None, "tensor"),
        P("dp", None, "tensor"),
        P("dp", None, "tensor"),
        P("dp", None, "tensor"),
        P("tensor", "dp"),
        P("tensor", "dp"),
        P("tensor", "dp"),
        P("dp", None, "tensor"),
        P("dp", None, "tensor"),
        P("dp", None, "tensor"),
        P(None, "tensor", "dp"),
        P(None, "tensor", "dp"),
        P(None, "tensor", "dp"),
        P(),
        P(),
        P(),
        P(None, "tensor"),
        P(None, "tensor"),
        P(None, "tensor"),
        P(),
        P(),
        P(),
    )
    return jax.shard_map(
        body,
        mesh=mesh,
        in_specs=placed,
        out_specs=(
            P(),
            P(),
            P("dp", "tensor"),
            P("dp", "tensor"),
            P("dp", "tensor"),
            P(None, "tensor"),
            P(None, "tensor"),
            P(None, "tensor"),
            P("dp", None, "tensor"),
            P("dp", None, "tensor"),
            P("dp", None, "tensor"),
            P("tensor", "dp"),
            P("tensor", "dp"),
            P("tensor", "dp"),
            P("dp", None, "tensor"),
            P("dp", None, "tensor"),
            P("dp", None, "tensor"),
            P(None, "tensor", "dp"),
            P(None, "tensor", "dp"),
            P(None, "tensor", "dp"),
            P(),
            P(),
            P(),
            P(None, "tensor"),
            P(None, "tensor"),
            P(None, "tensor"),
            P(),
            P(),
            P(),
        ),
        check_vma=False,
    )
```

time: 1320 us -> 859 us (0.65)
  waiting for transfers between devices: 335 us -> 0.66 us
  Pallas kernels: 374 us -> 479 us
  matrix products: 234 us -> 130 us
  local copies, waits for them, and re-layouts: 108 us -> 54.4 us
  other arithmetic: 152 us -> 124 us
  blocking collectives: 61.9 us -> 35.6 us
  loops' own time: 14.2 us -> 0.27 us
    unnamed x9 -> x3, waiting for transfers between devices: 174 us -> 0.59 us
    reduce_scatter x3 -> x0, waiting for transfers between devices: 162 us -> none  [the longest x1 87 us: body(): lax.psum_scatter(down_part, 'dp', scatter_dimension=2, tiled=True)]
    dot_general x32 -> x4, matrix products: 140 us -> 22 us  [turned_grad(): jnp.einsum('td,tc->dc', left_all, right_all, preferred_element_type=jnp.f...]
    pallas_call x14 -> x16, Pallas kernels: 339 us -> 444 us  [the longest x14 394 us: exchange(): pl.pallas_call(kernel, out_shape=[out for task in tasks for out in task.o...]
    psum x1 -> x0, blocking collectives: 27.7 us -> none  [body(): pos_own, col_own = lax.psum((pos_grad, col_grad), 'dp')]
    dynamic_update_slice x8 -> x0, local copies, waits for them, and re-layouts: 19.9 us -> none  [attend(): lax.map(one_block, jnp.arange(block_count, dtype=jnp.int32))]
    reduce_sum x6 -> x2, other arithmetic: 16.6 us -> 1.72 us  [the longest x1 1.11 us: body(): shared_own = jnp.sum(shared_parts, axis=0)]
    another operation x2 -> x0, loops' own time: 14 us -> none  [the longest x1 10.8 us: attend_back(): lax.scan(one_block, (zeros_pad, zeros_pad), jnp.arange(block_count, dtype...]
  transfers between devices with their start and end apart: 8 -> 3, of which waited for: 4 -> 0; matrix products, arithmetic and copies ran while one was open for 14% -> 11% of each run, Pallas kernels for 7% -> 13%
where the time goes in v2:
time: 859 us; the launch traced here: 849 us
  Pallas kernels  479 us (56%)
  matrix products  130 us (15%)
  other arithmetic  124 us (14%)
  local copies, waits for them, and re-layouts  54.4 us (6%)
  blocking collectives  35.6 us (4%)
  between operations  24.8 us (3%)
    pallas_call x14, Pallas kernels, exchange(): pl.pallas_call(kernel, out_shape=[out for task in tasks for out in task.o...  394 us
    dot_general x6, matrix products, multiply_arrays(): return jnp.dot(left_mat, right_mat, preferred_element_type=jnp.float32)  61.4 us
    sub x9, other arithmetic, adam_step(): weight - step_rate * (first_hat / (jnp.sqrt(second_hat) + ADAM_EPS) + dec...  38.7 us
    all_gather x1, blocking collectives, body(): lax.all_gather(out_weight.astype(jnp.bfloat16), 'dp', axis=1, tiled=True)  35.6 us
    pallas_call x1, Pallas kernels, attend_back(): pl.pallas_call(attend_back_kernel, out_shape=jax.ShapeDtypeStruct(qkv_out...  29.4 us
    dot_general x4, matrix products, turned_grad(): jnp.einsum('td,tc->dc', left_all, right_all, preferred_element_type=jnp.f...  22 us
    unnamed x139, local copies, waits for them, and re-layouts  20.8 us
    pallas_call x1, Pallas kernels, attend(): pl.pallas_call(attend_kernel, out_shape=[jax.ShapeDtypeStruct((slots, col...  20.2 us
  transfers between devices with their start and end apart: 3, of which 0 were waited for; matrix products, arithmetic and copies ran while one was open for 11% of the time, Pallas kernels for 13%

profile of v2, /device:TPU:0, one launch (start us, length us, event | category | flops | bytes accessed | tf_op | source)
XLA Modules:
  0.0 849.3 jit_solution(7275399661447442038)
XLA Ops:
  10.1 13.0 %shard_map.518 = s32[32,16,128]{2,1,0:T(8,128)S(1)} custom-call(s32[16,128]{1,0:T(8,128)} %add_add_fusion.7.x_ref), custom_call_target="tpu_custom_call" | custom-call | tf_op jit(solution)/shard_map/pallas_call | solution.py:598
  24.6 10.9 %shard_map.519 = (s32[1,2048]{1,0:T(1,128)}, s32[1,2048]{1,0:T(1,128)}, s32[8,128]{1,0:T(8,128)}) custom-call(s32[1,2048]{1,0:T(1,128)} %bitcast.202, bf16[128,128]{1,0:T(8,128)(2,1)} %get-tuple-element.315.low_ref, bf16[128,128]{1,0:T(8,128)(2,1)} %get-tuple-element.314.high_ref), custom_call_target="tpu_custom_call" | custom-call | tf_op jit(solution)/shard_map/pallas_call | solution.py:1070
  38.8 9.2 %shard_map.520 = s32[8,8,128]{2,1,0:T(8,128)} custom-call(s32[8,8,128]{2,1,0:T(8,128)} %concatenate.16.refs_0_), custom_call_target="tpu_custom_call" | custom-call | tf_op jit(solution)/shard_map/pallas_call | solution.py:125
  51.5 5.3 fusion.13
  56.8 9.5 %gather_fusion.3 = bf16[2048,256]{1,0:T(8,128)(2,1)S(1)} fusion(f32[6284,256]{1,0:T(8,128)} %param.41, s32[2048]{0:T(1024)S(1)} %broadcast_clamp_fusion.1), kind=kCustom, calls=%fused_computation.3 | custom fusion | bytes 2105344 | tf_op jit(solution)/shard_map/jit(_take)/gather | solution.py:1218
  68.5 23.2 %shard_map.521 = (bf16[8,256,256]{2,1,0:T(8,128)(2,1)S(1)}, f32[514,1024]{1,0:T(8,128)}) custom-call(bf16[8,256,256]{2,1,0:T(8,128)(2,1)} %select_convert_fusion.refs_0_, f32[514,256]{1,0:T(8,128)} %refs_1_.1), custom_call_target="tpu_custom_call" | custom-call | tf_op jit(solution)/shard_map/pallas_call | solution.py:125
  91.7 6.7 conditional.2
  91.7 6.7 convolution_convert_fusion
  109.4 30.1 %shard_map.522 = bf16[2048,1024]{1,0:T(8,128)(2,1)} custom-call(bf16[2048,256]{1,0:T(8,128)(2,1)} %get-tuple-element.342.refs_0_), custom_call_target="tpu_custom_call" | custom-call | tf_op jit(solution)/shard_map/pallas_call | solution.py:125
  139.5 9.8 %gather_fusion.4 = f32[2048,1024]{1,0:T(8,128)} fusion(f32[514,1024]{1,0:T(8,128)S(1)} %copy-done.2, s32[2048]{0:T(1024)S(1)} %broadcast_clamp_fusion), kind=kCustom, calls=%fused_computation.4 | custom fusion | bytes 16785408 | tf_op jit(solution)/shard_map/jit(_take)/gather | solution.py:1254
  149.3 5.5 fusion.84
  159.4 35.6 %all_gather.16 = bf16[256,1024]{1,0:T(8,128)(2,1)S(1)} all-gather(bf16[256,128]{1,0:T(8,128)(2,1)S(1)} %convert_element_type.139), channel_id=1, replica_groups=mesh['dp'=8,'tensor'=4] {'dp'}, dimensions={1}, use_global_device_ids=true | all-gather | bytes 589824 | tf_op jit(solution)/shard_map/all_gather | solution.py:1257
  203.4 5.5 add_convert_fusion.1
  209.0 7.8 add_convert_fusion.2.qkv_ref
  217.4 20.2 %shard_map.523 = (bf16[2048,256]{1,0:T(8,128)(2,1)}, f32[8,2048]{1,0:T(8,128)}) custom-call(s32[8]{0:T(128)} %get-tuple-element.337.low_ref, s32[8]{0:T(128)} %get-tuple-element.336.high_ref, bf16[2048,768]{1,0:T(8,128)(2,1)} %add_convert_fusion.2.qkv_ref, s32[2048,1]{1,0:T(8,128)} %copy.127.seq_col_ref, s32[8,2048]{1,0:T(8,128)} %broadcast_in_dim.189.seq_row_ref), custom_call_target="tpu_custom_call" | custom-call | tf_op jit(solution)/shard_map/pallas_call | solution.py:733
  237.7 4.5 convolution_convert_fusion.1.refs_0_
  242.2 29.2 %shard_map.524 = f32[512,1024]{1,0:T(8,128)} custom-call(bf16[2048,1024]{1,0:T(8,128)(2,1)} %convolution_convert_fusion.1.refs_0_), custom_call_target="tpu_custom_call" | custom-call | tf_op jit(solution)/shard_map/pallas_call | solution.py:125
  276.1 30.5 %shard_map.525 = bf16[2048,1024]{1,0:T(8,128)(2,1)} custom-call(bf16[512,1024]{1,0:T(8,128)(2,1)} %fusion.30.refs_0_), custom_call_target="tpu_custom_call" | custom-call | tf_op jit(solution)/shard_map/pallas_call | solution.py:125
  310.2 32.1 %multiply_convert_fusion = (bf16[2048,1024]{1,0:T(8,128)(2,1)}, f32[2048,1024]{1,0:T(8,128)}, f32[2048,1024]{1,0:T(8,128)}) fusion(f32[1024]{0:T(1024)S(1)} %bitcast.224, bf16[2048,1024]{1,0:T(8,128)(2,1)S(1)} %copy-done.12, bf16[1024,1024]{1,0:T(8,128)(2,1)S(1)} %bitcast.162), kind=kOutput, calls=%fused_computation.43 | convolution fusion | flops 4433379328 | bytes 27267072 | tf_op jit(solution)/shard_map/dot_general | solution.py:30
  342.3 9.4 %convolution_convert_fusion.4.refs_0_ = bf16[2048,1024]{1,0:T(8,128)(2,1)} fusion(bf16[2048,1024]{1,0:T(8,128)(2,1)} %get-tuple-element.308, bf16[1024,1024]{1,0:T(8,128)(2,1)} %bitcast.233), kind=kOutput, calls=%fused_computation.76 | convolution fusion | flops 4297064448 | bytes 10485760 | tf_op jit(solution)/shard_map/dot_general | solution.py:30
  351.7 30.8 %shard_map.526 = f32[512,1024]{1,0:T(8,128)} custom-call(bf16[2048,1024]{1,0:T(8,128)(2,1)} %convolution_convert_fusion.4.refs_0_), custom_call_target="tpu_custom_call" | custom-call | tf_op jit(solution)/shard_map/pallas_call | solution.py:125
  388.0 17.0 %shard_map.527 = f32[8,8,1024]{2,1,0:T(8,128)} custom-call(f32[8,1024]{1,0:T(8,128)} %fusion.32.refs_0_), custom_call_target="tpu_custom_call" | custom-call | tf_op jit(solution)/shard_map/pallas_call | solution.py:125
  405.1 11.1 %shard_map.528 = (f32[8,128]{1,0:T(8,128)}, bf16[64,1024]{1,0:T(8,128)(2,1)}, f32[64,1024]{1,0:T(8,128)}, f32[64,1024]{1,0:T(8,128)}) custom-call(f32[64,1024]{1,0:T(8,128)} %bitcast.167, f32[1024,1024]{1,0:T(8,128)} %head_ref.1, s32[64,1]{1,0:T(8,128)} %broadcast_in_dim_reshape_squeeze.4.pair_ref), custom_call_target="tpu_custom_call" | custom-call | tf_op jit(solution)/shard_map/pallas_call | solution.py:1126
  416.2 3.4 multiply_reduce_fusion.5
  422.9 30.2 %shard_map.529 = bf16[2048,1024]{1,0:T(8,128)(2,1)} custom-call(bf16[512,1024]{1,0:T(8,128)(2,1)} %get-tuple-element.297.refs_0_), custom_call_target="tpu_custom_call" | custom-call | tf_op jit(solution)/shard_map/pallas_call | solution.py:125
  453.1 9.5 %convolution_convert_fusion.7 = bf16[1024,1024]{1,0:T(8,128)(2,1)} fusion(bf16[2048,1024]{1,0:T(8,128)(2,1)} %shard_map.529, bf16[2048,1024]{1,0:T(8,128)(2,1)} %get-tuple-element.308), kind=kOutput, calls=%fused_computation.110 | convolution fusion | flops 4296015872 | bytes 10485760 | tf_op jit(solution)/shard_map/td,tc->dc/dot_general | solution.py:914
  462.6 11.8 %convert_reduce_fusion = (f32[1024]{0:T(1024)S(1)}, bf16[2048,1024]{1,0:T(8,128)(2,1)S(1)}) fusion(f32[2048,1024]{1,0:T(8,128)} %get-tuple-element.309, f32[2048,1024]{1,0:T(8,128)} %get-tuple-element.332, f32[1024]{0:T(1024)S(1)} %bitcast.225, bf16[2048,1024]{1,0:T(8,128)(2,1)S(1)} %copy-done.14, bf16[1024,1024]{1,0:T(8,128)(2,1)S(1)} %bitcast.234), kind=kOutput, calls=%fused_computation.41 | convolution fusion | flops 4330617856 | bytes 27271168 | tf_op jit(solution)/shard_map/td,fd->tf/dot_general | solution.py:938
  474.5 6.7 convolution_convert_fusion.3.refs_0_
  481.1 5.7 convolution_convert_fusion.6
  486.9 32.7 %shard_map.530 = (f32[512,1024]{1,0:T(8,128)}, bf16[4,128,1024]{2,1,0:T(8,128)(2,1)}) custom-call(bf16[2048,1024]{1,0:T(8,128)(2,1)} %convolution_convert_fusion.3.refs_0_, bf16[4,2,128,1024]{3,2,1,0:T(8,128)(2,1)} %bitcast.159), custom_call_target="tpu_custom_call" | custom-call | tf_op jit(solution)/shard_map/pallas_call | solution.py:125
  519.6 3.2 multiply_reduce_fusion.6
  526.0 31.4 %shard_map.531 = (bf16[2048,1024]{1,0:T(8,128)(2,1)}, f32[128,1024]{1,0:T(8,128)}, bf16[4,128,1024]{2,1,0:T(8,128)(2,1)}) custom-call(bf16[512,1024]{1,0:T(8,128)(2,1)} %get-tuple-element.299.refs_0_, bf16[4,128,1024]{2,1,0:T(8,128)(2,1)} %get-tuple-element.116.refs_1_, bf16[4,2,128,1024]{3,2,1,0:T(8,128)(2,1)} %bitcast.164), custom_call_target="tpu_custom_call" | custom-call | tf_op jit(solution)/shard_map/pallas_call | solution.py:125
  557.4 4.6 convolution_convert_fusion.5.grad_ref
  564.1 29.4 %shard_map.532 = bf16[2048,768]{1,0:T(8,128)(2,1)} custom-call(s32[8]{0:T(128)} %get-tuple-element.337.low_ref, s32[8]{0:T(128)} %get-tuple-element.336.high_ref, bf16[2048,768]{1,0:T(8,128)(2,1)} %add_convert_fusion.2.qkv_ref, bf16[2048,256]{1,0:T(8,128)(2,1)} %convolution_convert_fusion.5.grad_ref, f32[8,2048]{1,0:T(8,128)} %get-tuple-element.118.log_ref, ...), custom_call_target="tpu_custom_call" | custom-call | tf_op jit(solution)/shard_map/pallas_call | solution.py:843
  593.5 7.2 convolution_convert_fusion.2.refs_0_
  600.7 4.6 convolution_convert_fusion.8
  605.9 38.7 %shard_map.533 = (f32[512,1024]{1,0:T(8,128)}, f32[128,1024]{1,0:T(8,128)}, bf16[4,128,256]{2,1,0:T(8,128)(2,1)}, bf16[4,128,768]{2,1,0:T(8,128)(2,1)}) custom-call(bf16[2048,1024]{1,0:T(8,128)(2,1)} %convolution_convert_fusion.2.refs_0_, bf16[4,128,1024]{2,1,0:T(8,128)(2,1)} %get-tuple-element.119.refs_1_, bf16[4,2,128,256]{3,2,1,0:T(8,128)(2,1)} %bitcast.178, ...), custom_call_target="tpu_custom_call" | custom-call | tf_op jit(solution)/shard_map/pallas_call | solution.py:125
  644.6 3.1 multiply_reduce_fusion.4
  652.3 27.8 %shard_map.534 = (bf16[4,512,256]{2,1,0:T(8,128)(2,1)S(1)}, f32[128,768]{1,0:T(8,128)}, f32[128,256]{1,0:T(8,128)}) custom-call(bf16[4,512,256]{2,1,0:T(8,128)(2,1)} %bitcast.155, bf16[4,128,768]{2,1,0:T(8,128)(2,1)} %get-tuple-element.121.refs_1_, bf16[4,128,256]{2,1,0:T(8,128)(2,1)} %get-tuple-element.122.refs_2_), custom_call_target="tpu_custom_call" | custom-call | tf_op jit(solution)/shard_map/pallas_call | solution.py:125
  680.1 5.9 fusion.24
  690.6 37.5 %shard_map.535 = (bf16[8,256,256]{2,1,0:T(8,128)(2,1)}, f32[8,72,256]{2,1,0:T(8,128)}) custom-call(bf16[8,256,256]{2,1,0:T(8,128)(2,1)} %bitcast.174, f32[8,72,256]{2,1,0:T(8,128)} %bitcast.158), custom_call_target="tpu_custom_call" | custom-call | tf_op jit(solution)/shard_map/pallas_call | solution.py:125
  729.9 21.3 %conditional.3 = (f32[6284,256]{1,0:T(8,128)}, f32[]{:T(128)}) conditional(s32[]{:T(128)} %convert_element_type.132, (s32[]{:T(128)}, s32[8,2,128]{2,1,0:T(2,128)S(1)}, bf16[8,256,256]{2,1,0:T(8,128)(2,1)}) %tuple.106, (s32[32,16,128]{2,1,0:T(8,128)}, s32[16384]{0:T(1024)S(1)}, s32[]{:T(128)}, bf16[2048,256]{1,0:T(8,128)(2,1)S(1)}) %tuple.105), branch_computations={%region_34.38_spmd, %region_37.41_spmd} | conditional | flops 16242687 | bytes 54584416 | solution.py:1326
  729.9 15.9 %scatter_custom_fusion = f32[6284,256]{1,0:T(8,128)} fusion(s32[2048]{0:T(1024)S(1)} %bitcast.218, f32[]{:T(128)} %constant.93.clone, bf16[2048,256]{1,0:T(8,128)(2,1)} %bitcast.175), kind=kCustom, calls=%fused_computation.9 | custom fusion | flops 1048576 | bytes 7483396 | tf_op jit(solution)/shard_map/cond/branch_0_fun/scatter-add | solution.py:1323
  745.8 5.1 multiply_reduce_fusion
  756.3 26.1 %shard_map.536 = (f32[1,16,1024]{2,1,0:T(8,128)}, f32[8,72,256]{2,1,0:T(8,128)}) custom-call(f32[16,1024]{1,0:T(8,128)} %concatenate.19.refs_0_, f32[72,256]{1,0:T(8,128)} %copy-done.31), custom_call_target="tpu_custom_call" | custom-call | tf_op jit(solution)/shard_map/pallas_call | solution.py:125
  786.4 5.4 multiply_reduce_fusion.3
  809.5 17.4 %multiply_subtract_fusion = (f32[6284,256]{1,0:T(8,128)}, f32[6284,256]{1,0:T(8,128)}, f32[6284,256]{1,0:T(8,128)}) fusion(f32[6284,256]{1,0:T(8,128)} %param.41, f32[6284,256]{1,0:T(8,128)} %get-tuple-element.134, f32[]{:T(128)S(6)} %min_shard_map.3, f32[6284,256]{1,0:T(8,128)} %param.42, f32[6284,256]{1,0:T(8,128)} %param.43), kind=kLoop, calls=%fused_computation.62 | loop fusion | flops 25739264 | bytes 45043716 | tf_op jit(solution)/shard_map/sub | solution.py:64
  832.7 7.5 multiply_subtract_fusion.1
  (252 shorter events, 96.3 us)
Async XLA Ops:
  23.2 81.5 %copy-start.30 = (s32[32,16,128]{2,1,0:T(8,128)}, s32[32,16,128]{2,1,0:T(8,128)S(1)}, u32[]{:S(2)}) copy-start(s32[32,16,128]{2,1,0:T(8,128)S(1)} %shard_map.518) | copy-start | bytes 786436
  23.2 68.5 %copy-start = (s32[32,4,128]{2,1,0:T(4,128)}, s32[32,4,128]{2,1,0:T(4,128)S(1)}, u32[]{:S(2)}) copy-start(s32[32,4,128]{2,1,0:T(4,128)S(1)} %slice.88) | copy-start | bytes 196612
  56.8 9.5 %copy-start.35 = (f32[128,3,256]{2,0,1:T(8,128)S(1)}, f32[128,3,256]{2,0,1:T(8,128)}, u32[]{:S(2)}) copy-start(f32[128,3,256]{2,0,1:T(8,128)} %param.47) | copy-start | bytes 1179652
  66.5 25.2 %copy-start.17 = (f32[128,3,256]{0,2,1:T(8,128)}, f32[128,3,256]{0,2,1:T(8,128)S(1)}, u32[]{:S(2)}) copy-start(f32[128,3,256]{0,2,1:T(8,128)S(1)} %copy.126) | copy-start | bytes 1179652
  91.7 11.2 %copy-start.52 = (f32[6,256]{1,0:T(8,128)S(1)}, f32[6,256]{1,0:T(8,128)}, u32[]{:S(2)}) copy-start(f32[6,256]{1,0:T(8,128)} %param.62) | copy-start | bytes 18436
  98.5 41.0 %copy-start.2 = (f32[514,1024]{1,0:T(8,128)S(1)}, f32[514,1024]{1,0:T(8,128)}, u32[]{:S(2)}) copy-start(f32[514,1024]{1,0:T(8,128)} %get-tuple-element.111) | copy-start | bytes 6316036
  98.5 110.5 %all-gather.7.cloned.1.call-start = ((), (), s32[]{:S(2)}) async-start(), calls=%async_computation.3 | async-start | bytes 1769472 | tf_op jit(solution)/shard_map/all_gather | solution.py:1256
  99.0 207.6 %all-gather.9.cloned.1.call-start = ((), (), s32[]{:S(2)}) async-start(), calls=%async_computation.4 | async-start | bytes 2359296 | tf_op jit(solution)/shard_map/all_gather | solution.py:1258
  101.0 241.4 %all-gather.11.cloned.1.call-start = ((), (), s32[]{:S(2)}) async-start(), calls=%async_computation.5 | async-start | bytes 2359296 | tf_op jit(solution)/shard_map/all_gather | solution.py:1259
  109.0 162.5 %copy-start.42 = (f32[1,1024]{1,0:T(1,128)}, f32[1,1024]{1,0:T(1,128)S(1)}, u32[]{:S(2)}) copy-start(f32[1,1024]{1,0:T(1,128)S(1)} %get-tuple-element.324) | copy-start | bytes 12292
  158.0 41.5 %copy-start.36 = (f32[128,3,256]{2,0,1:T(8,128)S(1)}, f32[128,3,256]{2,0,1:T(8,128)}, u32[]{:S(2)}) copy-start(f32[128,3,256]{2,0,1:T(8,128)} %param.48) | copy-start | bytes 1179652
  158.0 42.4 %copy-start.37 = (f32[128,3,256]{2,0,1:T(8,128)S(1)}, f32[128,3,256]{2,0,1:T(8,128)}, u32[]{:S(2)}) copy-start(f32[128,3,256]{2,0,1:T(8,128)} %param.49) | copy-start | bytes 1179652
  158.0 43.3 %copy-start.40 = (f32[256,128]{1,0:T(8,128)S(1)}, f32[256,128]{1,0:T(8,128)}, u32[]{:S(2)}) copy-start(f32[256,128]{1,0:T(8,128)} %param.51) | copy-start | bytes 393220
  158.0 44.1 %copy-start.41 = (f32[256,128]{1,0:T(8,128)S(1)}, f32[256,128]{1,0:T(8,128)}, u32[]{:S(2)}) copy-start(f32[256,128]{1,0:T(8,128)} %param.52) | copy-start | bytes 393220
  196.9 74.6 %copy-start.45 = (f32[512]{0:T(512)}, f32[512]{0:T(512)S(1)}, u32[]{:S(2)}) copy-start(f32[512]{0:T(512)S(1)} %broadcast_multiply_fusion.5) | copy-start | bytes 6148
  198.8 10.1 %copy-start.54 = (f32[512]{0:T(512)}, f32[512]{0:T(512)S(1)}, u32[]{:S(2)}) copy-start(f32[512]{0:T(512)S(1)} %multiply_reduce_fusion.12) | copy-start | bytes 6148
  198.8 72.6 %copy-start.50 = (f32[512]{0:T(512)}, f32[512]{0:T(512)S(1)}, u32[]{:S(2)}) copy-start(f32[512]{0:T(512)S(1)} %fusion.61) | copy-start | bytes 6148
  453.1 9.5 %copy-start.14 = (bf16[2048,1024]{1,0:T(8,128)(2,1)S(1)}, bf16[2048,1024]{1,0:T(8,128)(2,1)}, u32[]{:S(2)}) copy-start(bf16[2048,1024]{1,0:T(8,128)(2,1)} %shard_map.529) | copy-start | bytes 12582916
  453.1 9.5 %copy-start.61 = (bf16[4,256,1024]{2,1,0:T(8,128)(2,1)S(1)}, bf16[4,256,1024]{2,1,0:T(8,128)(2,1)}, u32[]{:S(2)}) copy-start(bf16[4,256,1024]{2,1,0:T(8,128)(2,1)} %all-gather.11.cloned.1.call-done) | copy-start | bytes 6291460
  462.6 11.8 %copy-start.24 = (bf16[128,8,4,256]{3,1,2,0:T(8,128)(2,1)S(1)}, bf16[128,8,4,256]{3,1,2,0:T(8,128)(2,1)}, u32[]{:S(2)}) copy-start(bf16[128,8,4,256]{3,1,2,0:T(8,128)(2,1)} %copy-done.23) | copy-start | bytes 6291460
  474.4 6.7 copy-start.13
  564.1 29.4 %copy-start.62 = (bf16[1024,3,256]{0,2,1:T(8,128)(2,1)S(1)}, bf16[1024,3,256]{0,2,1:T(8,128)(2,1)}, u32[]{:S(2)}) copy-start(bf16[1024,3,256]{0,2,1:T(8,128)(2,1)} %all-gather.7.cloned.1.call-done) | copy-start | bytes 4718596
  593.5 7.2 copy-start.11
  593.5 7.2 copy-start.15
  605.9 38.7 %copy-start.7 = (f32[512,1024]{1,0:T(8,128)S(1)}, f32[512,1024]{1,0:T(8,128)}, u32[]{:S(2)}) copy-start(f32[512,1024]{1,0:T(8,128)} %copy-done.6) | copy-start | bytes 6291460
  605.9 38.7 %copy-start.43 = (f32[1,1024]{1,0:T(1,128)S(1)}, f32[1,1024]{1,0:T(1,128)}, u32[]{:S(2)}) copy-start(f32[1,1024]{1,0:T(1,128)} %copy-done.42) | copy-start | bytes 12292
  605.9 38.7 %copy-start.46 = (f32[512]{0:T(512)S(1)}, f32[512]{0:T(512)}, u32[]{:S(2)}) copy-start(f32[512]{0:T(512)} %copy-done.45) | copy-start | bytes 6148
  605.9 38.7 %copy-start.51 = (f32[512]{0:T(512)S(1)}, f32[512]{0:T(512)}, u32[]{:S(2)}) copy-start(f32[512]{0:T(512)} %copy-done.50) | copy-start | bytes 6148
  650.1 30.0 %copy-start.56 = (s32[1,2048]{1,0:T(1,128)S(1)}, s32[1,2048]{1,0:T(1,128)}, u32[]{:S(2)}) copy-start(s32[1,2048]{1,0:T(1,128)} %get-tuple-element.110) | copy-start | bytes 24580
  686.0 43.8 %copy-start.1 = (s32[32,4,128]{2,1,0:T(4,128)S(1)}, s32[32,4,128]{2,1,0:T(4,128)}, u32[]{:S(2)}) copy-start(s32[32,4,128]{2,1,0:T(4,128)} %copy-done) | copy-start | bytes 196612
  686.0 43.8 %copy-start.49 = (s32[8,2,128]{2,1,0:T(2,128)S(1)}, s32[8,2,128]{2,1,0:T(2,128)}, u32[]{:S(2)}) copy-start(s32[8,2,128]{2,1,0:T(2,128)} %get-tuple-element.316) | copy-start | bytes 24580
  729.9 56.5 %copy-start.38 = (bf16[64,1024]{1,0:T(8,128)(2,1)S(1)}, bf16[64,1024]{1,0:T(8,128)(2,1)}, u32[]{:S(2)}) copy-start(bf16[64,1024]{1,0:T(8,128)(2,1)} %get-tuple-element.132) | copy-start | bytes 393220
  782.5 12.3 %copy-start.18 = (f32[128,3,256]{0,2,1:T(8,128)S(1)}, f32[128,3,256]{0,2,1:T(8,128)}, u32[]{:S(2)}) copy-start(f32[128,3,256]{0,2,1:T(8,128)} %copy-done.17) | copy-start | bytes 1179652
  782.5 12.3 %copy-start.28 = (f32[128,3,256]{0,2,1:T(8,128)S(1)}, f32[128,3,256]{0,2,1:T(8,128)}, u32[]{:S(2)}) copy-start(f32[128,3,256]{0,2,1:T(8,128)} %copy.132) | copy-start | bytes 1179652
  792.6 8.3 copy-start.33
  794.8 9.9 %copy-start.20 = (f32[514,256]{1,0:T(8,128)S(1)}, f32[514,256]{1,0:T(8,128)}, u32[]{:S(2)}) copy-start(f32[514,256]{1,0:T(8,128)} %refs_1_.1) | copy-start | bytes 1579012
  799.9 7.6 copy-start.53
  799.9 7.6 copy-start.57
  799.9 7.6 copy-start.58
  799.9 8.9 %copy-start.39 = (f32[8,1024]{1,0:T(8,128)S(1)}, f32[8,1024]{1,0:T(8,128)}, u32[]{:S(2)}) copy-start(f32[8,1024]{1,0:T(8,128)} %param.65) | copy-start | bytes 98308
  799.9 8.9 %copy-start.44 = (f32[1,16,1024]{2,1,0:T(8,128)S(1)}, f32[1,16,1024]{2,1,0:T(8,128)}, u32[]{:S(2)}) copy-start(f32[1,16,1024]{2,1,0:T(8,128)} %get-tuple-element.131) | copy-start | bytes 196612
  799.9 8.9 %copy-start.47 = (f32[8,1024]{1,0:T(8,128)S(1)}, f32[8,1024]{1,0:T(8,128)}, u32[]{:S(2)}) copy-start(f32[8,1024]{1,0:T(8,128)} %param.66) | copy-start | bytes 98308
  799.9 8.9 %copy-start.48 = (f32[8,1024]{1,0:T(8,128)S(1)}, f32[8,1024]{1,0:T(8,128)}, u32[]{:S(2)}) copy-start(f32[8,1024]{1,0:T(8,128)} %param.67) | copy-start | bytes 98308
  809.5 17.4 %copy-start.21 = (f32[128,4,256]{2,1,0:T(4,128)S(1)}, f32[128,4,256]{2,1,0:T(4,128)}, u32[]{:S(2)}) copy-start(f32[128,4,256]{2,1,0:T(4,128)} %param.53) | copy-start | bytes 1572868
  809.5 17.4 %copy-start.32 = (f32[128,4,256]{2,1,0:T(4,128)S(1)}, f32[128,4,256]{2,1,0:T(4,128)}, u32[]{:S(2)}) copy-start(f32[128,4,256]{2,1,0:T(4,128)} %param.54) | copy-start | bytes 1572868
  809.5 20.6 %copy-start.22 = (f32[4,256,128]{2,1,0:T(8,128)S(1)}, f32[4,256,128]{2,1,0:T(8,128)}, u32[]{:S(2)}) copy-start(f32[4,256,128]{2,1,0:T(8,128)} %param.56) | copy-start | bytes 1572868
  809.5 23.2 %copy-start.10 = (f32[1024,1024]{1,0:T(8,128)S(1)}, f32[1024,1024]{1,0:T(8,128)}, u32[]{:S(2)}) copy-start(f32[1024,1024]{1,0:T(8,128)} %get-tuple-element.335) | copy-start | bytes 12582916
  809.5 23.2 %copy-start.16 = (f32[1024,1024]{1,0:T(8,128)S(1)}, f32[1024,1024]{1,0:T(8,128)}, u32[]{:S(2)}) copy-start(f32[1024,1024]{1,0:T(8,128)} %param.60) | copy-start | bytes 12582916
  (17 other events, 48.3 us)
Sparse Core Ops, SparseCore 1:
  101.7 51.2 all-gather.6
  155.8 52.7 all-gather.8
  211.2 48.8 all-gather.10

commit v3 on v2

--- a/solution.py
+++ b/solution.py
@@ -111,10 +111,7 @@
                 setattr(task, attribute + "_refs", refs[at : at + size])
                 at += size
         barrier = pltpu.get_barrier_semaphore()
-        partners = [partner for task in tasks for partner in task.partners()]
-        for partner in partners:
-            pl.semaphore_signal(barrier, inc=1, device_id=partner, device_id_type=MESH_IDS)
-        pl.semaphore_wait(barrier, len(partners))
+        pl.semaphore_wait(barrier, sum(task.hello(barrier) for task in tasks))
         for task in tasks:
             task.begin()
         for task in tasks:
@@ -142,6 +139,12 @@
 
 
 class Task:
+    def hello(self, barrier):
+        partners = self.partners()
+        for partner in partners:
+            pl.semaphore_signal(barrier, inc=1, device_id=partner, device_id_type=MESH_IDS)
+        return len(partners)
+
     def begin(self):
         pass
 
@@ -366,6 +369,51 @@
         o_ref[me] = x_ref[...]
 
 
+class GatherAll(Task):
+    def __init__(self, block):
+        self.width = lax.axis_size("tensor")
+        self.total = total = lax.axis_size("dp") * self.width
+        self.ins = (block,)
+        self.outs = (shaped((total,) + block.shape, block.dtype),)
+        self.scratch = (dma(total), dma(total))
+
+    def me(self):
+        return lax.axis_index("dp") * self.width + lax.axis_index("tensor")
+
+    def place(self, step):
+        other = lax.rem(self.me() + step, self.total)
+        return (other // self.width, lax.rem(other, self.width))
+
+    def copy(self, step):
+        (x_ref,), (o_ref,), (send, recv) = self.ins_refs, self.outs_refs, self.scratch_refs
+        return remote(x_ref, o_ref.at[self.me()], send.at[step], recv.at[step], self.place(step))
+
+    def hello(self, barrier):
+        def one(step, carry):
+            pl.semaphore_signal(
+                barrier, inc=1, device_id=self.place(step), device_id_type=MESH_IDS
+            )
+            return carry
+
+        lax.fori_loop(1, self.total, one, 0)
+        return self.total - 1
+
+    def begin(self):
+        def one(step, carry):
+            self.copy(step).start()
+            return carry
+
+        lax.fori_loop(1, self.total, one, 0)
+        self.outs_refs[0][self.me()] = self.ins_refs[0][...]
+
+    def end(self):
+        def one(step, carry):
+            self.copy(step).wait()
+            return carry
+
+        lax.fori_loop(1, self.total, one, 0)
+
+
 class GridTask(Task):
     def __init__(self):
         self.cross = lax.axis_size("dp") // LINE
@@ -423,6 +471,69 @@
             for i in range(self.cross - 1):
                 total = total + buf[i, z].astype(jnp.float32)
             o_ref[z] = total.astype(jnp.bfloat16)
+
+
+class SpreadLine(GridTask):
+    def __init__(self, block):
+        super().__init__()
+        self.ins = (block,)
+        self.outs = (shaped((LINE,) + block.shape, block.dtype),)
+        self.scratch = (dma(LINE - 1), dma(LINE - 1))
+
+    def targets(self):
+        line, cross = self.place()
+        return [lax.rem(line + step, LINE) for step in range(1, LINE)]
+
+    def partners(self):
+        line, cross = self.place()
+        return [{"dp": other * self.cross + cross} for other in self.targets()]
+
+    def begin(self):
+        (x_ref,), (o_ref,), (send, recv) = self.ins_refs, self.outs_refs, self.scratch_refs
+        line, cross = self.place()
+        self.copies = [
+            remote(x_ref, o_ref.at[line], send.at[i], recv.at[i], partner)
+            for i, partner in enumerate(self.partners())
+        ]
+        for copy in self.copies:
+            copy.start()
+        o_ref[line] = x_ref[...]
+
+    def end(self):
+        for copy in self.copies:
+            copy.wait()
+
+
+class SpreadCross(GridTask):
+    def __init__(self, blocks):
+        super().__init__()
+        self.ins = (blocks,)
+        self.outs = (shaped((LINE, self.cross) + blocks.shape[1:], blocks.dtype),)
+        others = max(self.cross - 1, 1)
+        self.scratch = (dma(others, LINE), dma(others, LINE))
+
+    def partners(self):
+        line, cross = self.place()
+        return [
+            {"dp": line * self.cross + lax.rem(cross + step, self.cross)}
+            for step in range(1, self.cross)
+        ]
+
+    def begin(self):
+        (x_ref,), (o_ref,), (send, recv) = self.ins_refs, self.outs_refs, self.scratch_refs
+        line, cross = self.place()
+        self.copies = []
+        for i, partner in enumerate(self.partners()):
+            for z in range(LINE):
+                copy = remote(x_ref.at[z], o_ref.at[z, cross], send.at[i, z], recv.at[i, z], partner)
+                copy.start()
+                self.copies.append(copy)
+        for z in range(LINE):
+            o_ref[z, cross] = x_ref[z]
+
+    def end(self):
+        for copy in self.copies:
+            copy.wait()
 
 
 class ReduceLine(GridTask):
@@ -559,52 +670,6 @@
         self.settle()
 
 
-def gather_all_kernel(groups, width, x_ref, o_ref, send, recv):
-    total = groups * width
-    me = lax.axis_index("dp") * width + lax.axis_index("tensor")
-
-    def place(step):
-        other = lax.rem(me + step, total)
-        return (other // width, lax.rem(other, width))
-
-    barrier = pltpu.get_barrier_semaphore()
-
-    def hello(step, carry):
-        pl.semaphore_signal(barrier, inc=1, device_id=place(step), device_id_type=MESH_IDS)
-        return carry
-
-    lax.fori_loop(1, total, hello, 0)
-    pl.semaphore_wait(barrier, total - 1)
-
-    def copy(step):
-        return remote(x_ref, o_ref.at[me], send.at[step], recv.at[step], place(step))
-
-    def begin(step, carry):
-        copy(step).start()
-        return carry
-
-    def finish(step, carry):
-        copy(step).wait()
-        return carry
-
-    lax.fori_loop(1, total, begin, 0)
-    o_ref[me] = x_ref[...]
-    lax.fori_loop(1, total, finish, 0)
-
-
-def gather_all(block, collective):
-    groups, width = lax.axis_size("dp"), lax.axis_size("tensor")
-    total = groups * width
-    return pl.pallas_call(
-        partial(gather_all_kernel, groups, width),
-        out_shape=jax.ShapeDtypeStruct((total,) + block.shape, block.dtype),
-        in_specs=[in_vmem()],
-        out_specs=in_vmem(),
-        scratch_shapes=[pltpu.SemaphoreType.DMA((total,)), pltpu.SemaphoreType.DMA((total,))],
-        compiler_params=comm_params(collective),
-    )(block)
-
-
 Q_BLOCK = 256
 K_BLOCK = 256
 
@@ -864,35 +929,191 @@
     )
 
 
-def layer_forward(emb_all, seq_ids, bounds, row_params, col_local, layer_mats):
-    qkv_full, out_full, up_full, down_full = layer_mats
-    col_width = qkv_full.shape[2]
-    tok_dev = emb_all.shape[0] // lax.axis_size("tensor")
-    first_moment_all = norm_rows(emb_all, row_params[0], row_params[3]).astype(jnp.bfloat16)
-    emb_rows = lax.dynamic_slice_in_dim(emb_all, lax.axis_index("tensor") * tok_dev, tok_dev, 0)
-    norm_first = norm_rows(emb_rows, row_params[0], row_params[3])
+def gelu_parts(upper):
+    distance = jnp.abs(upper) * 0.7071067811865476
+    step = 1.0 / (1.0 + 0.3275911 * distance)
+    bell = jnp.exp(-distance * distance)
+    series = step * (
+        0.254829592
+        + step * (-0.284496736 + step * (1.421413741 + step * (-1.453152027 + step * 1.061405429)))
+    )
+    tail = 0.5 * series * bell
+    share = jnp.where(upper >= 0.0, 1.0 - tail, tail)
+    return (upper * share, share + upper * (bell * 0.3989422804014327))
+
+
+def expand_kernel(rows_ref, weight_ref, bias_ref, hidden_ref, slope_ref):
+    units = weight_ref.shape[1]
+    rows = rows_ref[...]
+    for first in range(0, units, 256):
+        lanes = pl.ds(first, 256)
+        upper = multiply_arrays(rows, weight_ref[:, lanes]) + bias_ref[:, lanes]
+        hidden, slope = gelu_parts(upper)
+        hidden_ref[:, lanes] = hidden.astype(jnp.bfloat16)
+        slope_ref[:, lanes] = slope
+
+
+def expand(rows, weight, bias):
+    slots, depth = rows.shape
+    units = weight.shape[1]
+    tall = 256
+    return pl.pallas_call(
+        expand_kernel,
+        grid=(slots // tall,),
+        out_shape=[shaped((slots, units), jnp.bfloat16), shaped((slots, units), jnp.float32)],
+        in_specs=[
+            pl.BlockSpec((tall, depth), lambda i: (i, 0)),
+            pl.BlockSpec((depth, units), lambda i: (0, 0)),
+            pl.BlockSpec((1, units), lambda i: (0, 0)),
+        ],
+        out_specs=[
+            pl.BlockSpec((tall, units), lambda i: (i, 0)),
+            pl.BlockSpec((tall, units), lambda i: (i, 0)),
+        ],
+        compiler_params=pltpu.CompilerParams(vmem_limit_bytes=VMEM_BYTES),
+    )(rows, weight, bias)
+
+
+EMBED_ROWS = 128
+MARGIN = 256
+
+
+def embed_kernel(
+    start_ref, span_ref, own_ref, tok_ref, pos_ref, seq_ref, row_ref, low_ref, emb_ref, norm_ref, padded
+):
+    slots = tok_ref.shape[0]
+    blocks, own_blocks = slots // EMBED_ROWS, emb_ref.shape[0] // EMBED_ROWS
+    padded[pl.ds(MARGIN, pos_ref.shape[0])] = pos_ref[...]
+    gain, shift = row_ref[0:1], row_ref[3:4]
+
+    def one_block(b, carry):
+        rows = block_span(b, EMBED_ROWS)
+        seq = seq_ref[rows, 0:1]
+
+        def pick(s, placed):
+            first = MARGIN + 2 + b * EMBED_ROWS - start_ref[s]
+            base = first // 8
+            window = padded[pl.ds(pl.multiple_of(base * 8, 8), EMBED_ROWS + 8)]
+            window = pltpu.roll(window, EMBED_ROWS + 8 - (first - base * 8), 0)
+            return jnp.where(seq == s, window[:EMBED_ROWS], placed)
+
+        placed = lax.fori_loop(
+            span_ref[0, b], span_ref[1, b], pick, jnp.zeros((EMBED_ROWS, tok_ref.shape[1]), jnp.float32)
+        )
+        emb = tok_ref[rows].astype(jnp.float32) + placed
+        norm = norm_rows(emb, gain, shift)
+        low_ref[rows] = norm.astype(jnp.bfloat16)
+        own = b - own_ref[0] * own_blocks
+
+        @pl.when((own >= 0) & (own < own_blocks))
+        def _():
+            own_rows = block_span(own, EMBED_ROWS)
+            emb_ref[own_rows] = emb
+            norm_ref[own_rows] = norm
+
+        return carry
+
+    lax.fori_loop(0, blocks, one_block, 0)
+
+
+def embed(tok_all, pos_full, seq_ids, lengths, row_params):
+    slots, depth = tok_all.shape
+    own = slots // lax.axis_size("tensor")
+    ends = jnp.cumsum(lengths)
+    starts = ends - lengths
+    first = jnp.arange(slots // EMBED_ROWS, dtype=jnp.int32) * EMBED_ROWS
+    spans = jnp.stack(
+        [
+            jnp.sum((ends[None, :] <= first[:, None]).astype(jnp.int32), axis=1),
+            jnp.sum((starts[None, :] < first[:, None] + EMBED_ROWS).astype(jnp.int32), axis=1),
+        ]
+    )
+    return pl.pallas_call(
+        embed_kernel,
+        out_shape=[
+            shaped((slots, depth), jnp.bfloat16),
+            shaped((own, depth), jnp.float32),
+            shaped((own, depth), jnp.float32),
+        ],
+        in_specs=[in_scalars()] * 3 + [in_vmem()] * 4,
+        out_specs=[in_vmem()] * 3,
+        scratch_shapes=[
+            pltpu.VMEM((MARGIN + MAXLEN + EMBED_ROWS + 24, depth), jnp.float32)
+        ],
+        compiler_params=pltpu.CompilerParams(vmem_limit_bytes=VMEM_BYTES),
+    )(
+        starts,
+        spans,
+        lax.axis_index("tensor").astype(jnp.int32)[None],
+        tok_all,
+        pos_full,
+        seq_ids[:, None],
+        row_params,
+    )
+
+
+SCATTER_ROWS = 512
+
+
+def scatter_kernel(index_ref, rows_ref, grad_ref, square_ref):
+    first = pl.program_id(0) * SCATTER_ROWS
+    slots = index_ref.shape[1]
+    here = (
+        lax.broadcasted_iota(jnp.int32, (SCATTER_ROWS, slots), 0) + first == index_ref[...]
+    ).astype(jnp.float32)
+    grad = multiply_arrays(here.astype(jnp.bfloat16), rows_ref[...])
+    grad_ref[...] = grad
+
+    @pl.when(pl.program_id(0) == 0)
+    def _():
+        square_ref[...] = jnp.zeros_like(square_ref)
+
+    square_ref[...] += jnp.sum(
+        (grad * grad).reshape(SCATTER_ROWS // 8, 8, grad.shape[1]), axis=0
+    )
+
+
+def scatter_rows(index, rows, height):
+    slots, width = rows.shape
+    grad, squares = pl.pallas_call(
+        scatter_kernel,
+        grid=(pl.cdiv(height, SCATTER_ROWS),),
+        out_shape=[shaped((height, width), jnp.float32), shaped((8, width), jnp.float32)],
+        in_specs=[
+            pl.BlockSpec((1, slots), lambda i: (0, 0)),
+            pl.BlockSpec((slots, width), lambda i: (0, 0)),
+        ],
+        out_specs=[
+            pl.BlockSpec((SCATTER_ROWS, width), lambda i: (i, 0)),
+            pl.BlockSpec((8, width), lambda i: (0, 0)),
+        ],
+        compiler_params=pltpu.CompilerParams(vmem_limit_bytes=VMEM_BYTES),
+    )(index[None], rows)
+    return (grad, jnp.sum(squares))
+
+
+def layer_forward(embedded, seq_ids, bounds, row_params, col_local, layer_mats):
+    first_moment_all, emb_rows, norm_first = embedded
+    qkv_full, out_full, up_half, down_low = layer_mats
+    col_width = col_local.shape[1]
     qkv_bias = jnp.concatenate([col_local[0], jnp.zeros_like(col_local[0]), col_local[1]])
-    qkv_out = (
-        multiply_arrays(first_moment_all, qkv_full.reshape(D, 3 * col_width)) + qkv_bias
-    ).astype(jnp.bfloat16)
+    qkv_out = (multiply_arrays(first_moment_all, qkv_full) + qkv_bias).astype(jnp.bfloat16)
     attn_low, log_total = attend(qkv_out, seq_ids, bounds)
-    first_sum = (
-        norm_first
-        + exchange(5, Fold(multiply_arrays(attn_low, out_full).astype(jnp.bfloat16)))
-        + row_params[6]
-    )
+    first_back = jnp.einsum("tc,dc->td", attn_low, out_full, preferred_element_type=jnp.float32)
+    first_branch, up_full, down_half = exchange(
+        5, Fold(first_back.astype(jnp.bfloat16)), SpreadCross(up_half), SpreadLine(down_low)
+    )
+    up_full = up_full.reshape(D, -1)
+    first_sum = norm_first + first_branch + row_params[6]
     norm_second = norm_rows(first_sum, row_params[1], row_params[4])
-    second_all = exchange(6, Spread(norm_second.astype(jnp.bfloat16)))
-    expansion_result = multiply_arrays(second_all, up_full.reshape(D, -1)) + col_local[2:].reshape(
-        -1
-    )
-    hidden_low = jax.nn.gelu(expansion_result, approximate=False).astype(jnp.bfloat16)
+    second_all, down_full = exchange(
+        6, Spread(norm_second.astype(jnp.bfloat16)), SpreadCross(down_half)
+    )
+    down_full = down_full.reshape(D, -1)
+    hidden_low, slope = expand(second_all, up_full, col_local[2:].reshape(1, -1))
+    second_back = jnp.einsum("tf,df->td", hidden_low, down_full, preferred_element_type=jnp.float32)
     second_sum = (
-        norm_second
-        + exchange(
-            7, Fold(multiply_arrays(hidden_low, down_full.reshape(-1, D)).astype(jnp.bfloat16))
-        )
-        + row_params[7]
+        norm_second + exchange(7, Fold(second_back.astype(jnp.bfloat16))) + row_params[7]
     )
     norm_third = norm_rows(second_sum, row_params[2], row_params[5])
     saved_vals = (
@@ -903,11 +1124,11 @@
         attn_low,
         first_sum,
         second_all,
-        expansion_result,
+        slope,
         hidden_low,
         second_sum,
     )
-    return (norm_third, saved_vals)
+    return (norm_third, saved_vals, (qkv_full, out_full, up_full, down_full))
 
 
 def turned_grad(left_all, right_all):
@@ -926,23 +1147,19 @@
         attn_low,
         first_sum,
         second_all,
-        expansion_result,
+        slope,
         hidden_low,
         second_sum,
     ) = saved_vals
-    col_width = qkv_full.shape[2]
+    col_width = out_full.shape[1]
     grad_second, gain_c, shift_c = norm_back(second_sum, row_params[2], row_params[5], grad_third)
     mixed_low = grad_second.astype(jnp.bfloat16)
     mixed_all = exchange(10, Spread(mixed_low))
     down_grad = turned_grad(mixed_all, hidden_low)
-    hidden_grad = jnp.einsum(
-        "td,fd->tf", mixed_all, down_full.reshape(-1, D), preferred_element_type=jnp.float32
-    )
-    gelu_pull = jax.vjp(partial(jax.nn.gelu, approximate=False), expansion_result)[1]
-    up_low = gelu_pull(hidden_grad)[0].astype(jnp.bfloat16)
+    up_low = (multiply_arrays(mixed_all, down_full) * slope).astype(jnp.bfloat16)
     up_grad = turned_grad(second_all, up_low)
     second_back = jnp.einsum(
-        "tf,df->td", up_low, up_full.reshape(D, -1), preferred_element_type=jnp.float32
+        "tf,df->td", up_low, up_full, preferred_element_type=jnp.float32
     ).astype(jnp.bfloat16)
     second_back, down_half = exchange(11, Fold(second_back), ReduceCross(down_grad))
     second_total = grad_second + second_back
@@ -952,13 +1169,11 @@
         12, Spread(branch_low), ReduceLine(down_half), ReduceCross(up_grad)
     )
     out_grad = turned_grad(branch_all, attn_low)
-    attn_grad = jnp.einsum(
-        "td,cd->tc", branch_all, out_full, preferred_element_type=jnp.float32
-    ).astype(jnp.bfloat16)
+    attn_grad = multiply_arrays(branch_all, out_full).astype(jnp.bfloat16)
     qkv_low = attend_back(qkv_out, attn_grad, log_total, seq_ids, bounds)
     qkv_grad = turned_grad(first_moment_all, qkv_low)
     first_back = jnp.einsum(
-        "tc,dc->td", qkv_low, qkv_full.reshape(D, -1), preferred_element_type=jnp.float32
+        "tc,dc->td", qkv_low, qkv_full, preferred_element_type=jnp.float32
     ).astype(jnp.bfloat16)
     first_back, up_sum, out_half, qkv_half = exchange(
         13, Fold(first_back), ReduceLine(up_half), ReduceCross(out_grad), ReduceCross(qkv_grad)
@@ -1137,7 +1352,7 @@
     )(pooled, head_weight, pairs[:, None])
 
 
-CAPACITY = 256
+CAPACITY = 192
 
 
 def body(
@@ -1193,7 +1408,11 @@
         ],
         axis=0,
     )
-    gathered = gather_all(block, 1)
+    qkv_low = query_key_value_weight.astype(jnp.bfloat16).reshape(-1, 3 * col_width)
+    out_low = out_weight.T.astype(jnp.bfloat16)
+    up_low = up_weight.astype(jnp.bfloat16).reshape(qkv_low.shape[0], -1)
+    down_low = down_weight.reshape(-1, down_weight.shape[2]).T.astype(jnp.bfloat16)
+    gathered, qkv_half = exchange(1, GatherAll(block), SpreadLine(qkv_low))
     all_ids = gathered[:, :id_rows].reshape(-1)
     pairs = gathered[:: tensor_count, 2 * id_rows, :anchors].reshape(-1)
     own_perm = lax.dynamic_slice_in_dim(
@@ -1201,11 +1420,13 @@
     )[:, id_rows : 2 * id_rows].reshape(-1)
     slot, listed, counts_out = make_plan(own_perm, all_ids, CAPACITY, vocab_local, groups)
     slot = slot[0]
-    list_rows = CAPACITY // 128
+    list_rows = -(-CAPACITY // 128)
     top_count = jnp.max(counts_out)
     request = jnp.concatenate(
         [
-            listed.reshape(groups, list_rows, 128),
+            jnp.pad(
+                listed.reshape(groups, CAPACITY), ((0, 0), (0, list_rows * 128 - CAPACITY))
+            ).reshape(groups, list_rows, 128),
             jnp.broadcast_to(top_count, (groups, 8 - list_rows, 128)),
         ],
         axis=1,
@@ -1213,13 +1434,14 @@
     asked = exchange(2, Swap(request, "dp"))
     overflow = jnp.max(asked[:, list_rows]) > CAPACITY
     offset = group_index * vocab_local
-    asked_rows = asked[:, :list_rows].reshape(-1) - offset
+    asked_rows = asked[:, :list_rows].reshape(groups, -1)[:, :CAPACITY].reshape(-1) - offset
     asked_safe = jnp.clip(asked_rows, 0, vocab_local - 1)
     sent_rows = jnp.take(tok_table, asked_safe, axis=0).astype(jnp.bfloat16)
-    got_rows, pos_full = exchange(
+    got_rows, pos_full, out_half = exchange(
         3,
         Swap(sent_rows.reshape(groups, CAPACITY, col_width), "dp"),
         Spread(pos_table, columns=True, chunks=1),
+        SpreadLine(out_low),
     )
     got_rows = got_rows.reshape(-1, col_width)
     chooser = (slot[:, None] == jnp.arange(groups * CAPACITY, dtype=jnp.int32)[None, :]).astype(
@@ -1251,14 +1473,18 @@
         spread_wide,
         lambda: multiply_arrays(chooser, got_rows).astype(jnp.bfloat16),
     )
-    emb_all = exchange(4, Spread(tok_cols, columns=True)).astype(jnp.float32) + jnp.take(pos_full, positions, axis=0)
-    layer_mats = (
-        lax.all_gather(query_key_value_weight.astype(jnp.bfloat16), "dp", axis=0, tiled=True),
-        lax.all_gather(out_weight.astype(jnp.bfloat16), "dp", axis=1, tiled=True),
-        lax.all_gather(up_weight.astype(jnp.bfloat16), "dp", axis=0, tiled=True),
-        lax.all_gather(down_weight.astype(jnp.bfloat16), "dp", axis=2, tiled=True),
-    )
-    norm_third, saved_vals = layer_forward(emb_all, seq_ids, bounds, row_params, col_bias, layer_mats)
+    tok_all, qkv_full, out_full, up_half = exchange(
+        4,
+        Spread(tok_cols, columns=True),
+        SpreadCross(qkv_half),
+        SpreadCross(out_half),
+        SpreadLine(up_low),
+    )
+    layer_mats = (qkv_full.reshape(D, -1), out_full.reshape(D, -1), up_half, down_low)
+    embedded = embed(tok_all, pos_full, seq_ids, lengths, row_params)
+    norm_third, saved_vals, layer_mats = layer_forward(
+        embedded, seq_ids, bounds, row_params, col_bias, layer_mats
+    )
     row_member = lax.dynamic_slice_in_dim(member, tensor_index * tok_dev, tok_dev, 0).astype(
         jnp.float32
     )
@@ -1291,20 +1517,20 @@
     ).astype(jnp.bfloat16)
     pos_grad = multiply_arrays(pos_pick, cols_grad)
     shared = jnp.concatenate([pos_grad, col_grad], axis=0)
-    shared_rows = -(-shared.shape[0] // (8 * groups)) * 8
+    shared_rows = -(-shared.shape[0] // (16 * groups)) * 16
     shared = jnp.pad(shared, ((0, shared_rows * groups - shared.shape[0]), (0, 0)))
     merged = jnp.einsum("kn,kc->nc", chooser, cols_grad, preferred_element_type=jnp.float32)
     back_rows, shared_parts = exchange(
         15,
         Swap(merged.astype(jnp.bfloat16).reshape(groups, CAPACITY, col_width), "dp"),
-        Swap(shared.reshape(groups, shared_rows, col_width), "dp"),
-    )
-    shared_own = jnp.sum(shared_parts, axis=0)
+        Swap(shared.astype(jnp.bfloat16).reshape(groups, shared_rows, col_width), "dp"),
+    )
+    shared_own = jnp.sum(shared_parts.astype(jnp.float32), axis=0)
 
     def add_wide():
         wanted = every_slot_id() - offset
         inside = (wanted >= 0) & (wanted < vocab_local)
-        return (
+        grad = (
             jnp.zeros(tok_table.shape, jnp.float32)
             .at[jnp.clip(wanted, 0, vocab_local - 1)]
             .add(
@@ -1315,21 +1541,19 @@
                 )
             )
         )
-
-    def add_listed():
-        return (
-            jnp.zeros(tok_table.shape, jnp.float32)
-            .at[jnp.where(asked_rows < 0, vocab_local, asked_rows)]
-            .add(back_rows.reshape(-1, col_width).astype(jnp.float32), mode="drop")
-        )
-
-    tok_grad = lax.cond(overflow, add_wide, add_listed)
+        return (grad, jnp.sum(grad * grad))
+
+    tok_grad, tok_squares = lax.cond(
+        overflow,
+        add_wide,
+        lambda: scatter_rows(asked_rows, back_rows.reshape(-1, col_width), vocab_local),
+    )
     qkv_grad = qkv_sum.reshape(query_key_value_weight.shape)
     out_grad = out_sum.T
     up_grad = up_sum.reshape(up_weight.shape)
     down_grad = down_sum.T.reshape(down_weight.shape)
     local_squares = (
-        jnp.sum(tok_grad * tok_grad)
+        tok_squares
         + jnp.sum(qkv_grad * qkv_grad)
         + jnp.sum(out_grad * out_grad)
         + jnp.sum(up_grad * up_grad)

time: 859 us -> 793 us (0.923)
  Pallas kernels: 479 us -> 547 us
  other arithmetic: 124 us -> 82.1 us
  matrix products: 130 us -> 89.9 us
  blocking collectives: 35.6 us -> 0 us
  local copies, waits for them, and re-layouts: 54.4 us -> 43.8 us
    all_gather x1 -> x0, blocking collectives: 35.6 us -> none  [body(): lax.all_gather(out_weight.astype(jnp.bfloat16), 'dp', axis=1, tiled=True)]
    dot_general x6 -> x5, matrix products: 61.4 us -> 26.5 us  [multiply_arrays(): return jnp.dot(left_mat, right_mat, preferred_element_type=jnp.float32)]
    pallas_call x1 -> x3, Pallas kernels: 13 us -> 46.2 us  [the longest x1 19.6 us: embed(): pl.pallas_call(embed_kernel, out_shape=[shaped((slots, depth), jnp.bfloat...]
    pallas_call x14 -> x15, Pallas kernels: 394 us -> 423 us  [exchange(): pl.pallas_call(kernel, out_shape=[out for task in tasks for out in task.o...]
    scatter-add x1 -> x0, other arithmetic: 15.9 us -> none  [add_listed(): return jnp.zeros(tok_table.shape, jnp.float32).at[jnp.where(asked_rows <...]
    gather x1 -> x0, local copies, waits for them, and re-layouts: 9.82 us -> none  [body(): jnp.take(pos_full, positions, axis=0)]
    convert_element_type x6 -> x5, other arithmetic: 12.2 us -> 3.25 us  [the longest x1 1.39 us: layer_forward(): norm_second.astype(jnp.bfloat16)]
    unnamed x139 -> x129, local copies, waits for them, and re-layouts: 20.8 us -> 20.5 us
  transfers between devices with their start and end apart: 3 -> 0, of which waited for: 0 -> 0; matrix products, arithmetic and copies ran while one was open for 11% -> 0% of each run, Pallas kernels for 13% -> 0%
where the time goes in v3:
time: 793 us; the launch traced here: 786 us
  Pallas kernels  547 us (69%)
  matrix products  89.9 us (11%)
  other arithmetic  82.1 us (10%)
  local copies, waits for them, and re-layouts  43.8 us (6%)
  between operations  23.3 us (3%)
    pallas_call x15, Pallas kernels, exchange(): pl.pallas_call(kernel, out_shape=[out for task in tasks for out in task.o...  423 us
    sub x9, other arithmetic, adam_step(): weight - step_rate * (first_hat / (jnp.sqrt(second_hat) + ADAM_EPS) + dec...  38.7 us
    pallas_call x1, Pallas kernels, attend_back(): pl.pallas_call(attend_back_kernel, out_shape=jax.ShapeDtypeStruct(qkv_out...  33.3 us
    dot_general x5, matrix products, multiply_arrays(): return jnp.dot(left_mat, right_mat, preferred_element_type=jnp.float32)  26.5 us
    pallas_call x1, Pallas kernels, attend(): pl.pallas_call(attend_kernel, out_shape=[jax.ShapeDtypeStruct((slots, col...  22.7 us
    unnamed x129, local copies, waits for them, and re-layouts  20.5 us
    pallas_call x1, Pallas kernels, embed(): pl.pallas_call(embed_kernel, out_shape=[shaped((slots, depth), jnp.bfloat...  19.6 us
    dot_general x4, matrix products, turned_grad(): jnp.einsum('td,tc->dc', left_all, right_all, preferred_element_type=jnp.f...  18.7 us

profile of v3, /device:TPU:0, one launch (start us, length us, event | category | flops | bytes accessed | tf_op | source)
XLA Modules:
  0.0 786.3 jit_solution(2133546080843246577)
XLA Ops:
  16.4 29.5 %shard_map.518 = (s32[32,16,128]{2,1,0:T(8,128)S(1)}, bf16[4,128,768]{2,1,0:T(8,128)(2,1)}) custom-call(s32[16,128]{1,0:T(8,128)} %add_add_fusion.7.refs_0_, bf16[128,768]{1,0:T(8,128)(2,1)} %copy.108.refs_1_), custom_call_target="tpu_custom_call" | custom-call | tf_op jit(solution)/shard_map/pallas_call | solution.py:122
  47.4 10.4 %shard_map.519 = (s32[1,2048]{1,0:T(1,128)}, s32[1,1536]{1,0:T(1,128)}, s32[8,128]{1,0:T(8,128)}) custom-call(s32[1,2048]{1,0:T(1,128)} %bitcast.201, bf16[128,128]{1,0:T(8,128)(2,1)} %get-tuple-element.316.low_ref, bf16[128,128]{1,0:T(8,128)(2,1)} %get-tuple-element.315.high_ref), custom_call_target="tpu_custom_call" | custom-call | tf_op jit(solution)/shard_map/pallas_call | solution.py:1285
  61.2 11.0 %shard_map.520 = s32[8,8,128]{2,1,0:T(8,128)} custom-call(s32[8,8,128]{2,1,0:T(8,128)} %concatenate.17.refs_0_), custom_call_target="tpu_custom_call" | custom-call | tf_op jit(solution)/shard_map/pallas_call | solution.py:122
  75.7 6.5 gather_fusion.3
  84.2 28.5 %shard_map.521 = (bf16[8,192,256]{2,1,0:T(8,128)(2,1)S(1)}, f32[514,1024]{1,0:T(8,128)}, bf16[4,128,256]{2,1,0:T(8,128)(2,1)}) custom-call(bf16[8,192,256]{2,1,0:T(8,128)(2,1)} %select_convert_fusion.refs_0_, f32[514,256]{1,0:T(8,128)} %refs_1_.1, bf16[128,256]{1,0:T(8,128)(2,1)} %convert_bitcast_fusion.refs_2_), custom_call_target="tpu_custom_call" | custom-call | tf_op jit(solution)/shard_map/pallas_call | solution.py:122
  113.8 3.4 conditional.2
  113.8 2.9 convolution_convert_fusion
  119.1 30.6 %shard_map.522 = (bf16[2048,1024]{1,0:T(8,128)(2,1)}, bf16[4,2,128,768]{3,2,1,0:T(8,128)(2,1)}, bf16[4,2,128,256]{3,2,1,0:T(8,128)(2,1)}, bf16[4,128,1024]{2,1,0:T(8,128)(2,1)}) custom-call(bf16[2048,256]{1,0:T(8,128)(2,1)} %get-tuple-element.341.refs_0_, bf16[4,128,768]{2,1,0:T(8,128)(2,1)} %get-tuple-element.129.refs_1_, ...), custom_call_target="tpu_custom_call" | custom-call | tf_op jit(solution)/shard_map/pallas_call | solution.py:122
  151.2 19.6 %shard_map.523 = (bf16[2048,1024]{1,0:T(8,128)(2,1)}, f32[512,1024]{1,0:T(8,128)}, f32[512,1024]{1,0:T(8,128)}) custom-call(s32[8]{0:T(128)} %bitcast_subtract_fusion.1.start_ref, s32[2,16]{1,0:T(2,128)} %pad_add_fusion.span_ref, s32[1]{0:T(128)} %bitcast.11.own_ref, bf16[2048,1024]{1,0:T(8,128)(2,1)} %get-tuple-element.131.tok_ref, ...), custom_call_target="tpu_custom_call" | custom-call | tf_op jit(solution)/shard_map/pallas_call | solution.py:1031
  171.8 7.3 add_convert_fusion.qkv_ref
  179.7 22.7 %shard_map.524 = (bf16[2048,256]{1,0:T(8,128)(2,1)}, f32[8,2048]{1,0:T(8,128)}) custom-call(s32[8]{0:T(128)} %get-tuple-element.336.low_ref, s32[8]{0:T(128)} %get-tuple-element.335.high_ref, bf16[2048,768]{1,0:T(8,128)(2,1)} %add_convert_fusion.qkv_ref, s32[2048,1]{1,0:T(8,128)} %copy.111.seq_ref.seq_col_ref, s32[8,2048]{1,0:T(8,128)} %broadcast_in_dim.178.seq_row_ref), custom_call_target="tpu_custom_call" | custom-call | tf_op jit(solution)/shard_map/pallas_call | solution.py:798
  202.4 4.6 convolution_convert_fusion.1.refs_0_
  207.9 33.8 %shard_map.525 = (f32[512,1024]{1,0:T(8,128)}, bf16[4,2,128,1024]{3,2,1,0:T(8,128)(2,1)}, bf16[4,128,1024]{2,1,0:T(8,128)(2,1)}) custom-call(bf16[2048,1024]{1,0:T(8,128)(2,1)} %convolution_convert_fusion.1.refs_0_, bf16[4,128,1024]{2,1,0:T(8,128)(2,1)} %get-tuple-element.138.refs_1_, bf16[128,1024]{1,0:T(8,128)(2,1)} %bitcast.175), custom_call_target="tpu_custom_call" | custom-call | tf_op jit(solution)/shard_map/pallas_call | solution.py:122
  241.7 2.5 fusion.81
  246.0 32.2 %shard_map.526 = (bf16[2048,1024]{1,0:T(8,128)(2,1)}, bf16[4,2,128,1024]{3,2,1,0:T(8,128)(2,1)}) custom-call(bf16[512,1024]{1,0:T(8,128)(2,1)} %fusion.21.refs_0_, bf16[4,128,1024]{2,1,0:T(8,128)(2,1)} %get-tuple-element.140.refs_1_), custom_call_target="tpu_custom_call" | custom-call | tf_op jit(solution)/shard_map/pallas_call | solution.py:122
  278.9 15.9 %shard_map.527 = (bf16[2048,1024]{1,0:T(8,128)(2,1)}, f32[2048,1024]{1,0:T(8,128)}) custom-call(bf16[2048,1024]{1,0:T(8,128)(2,1)} %get-tuple-element.141.rows_ref, bf16[1024,1024]{1,0:T(8,128)(2,1)} %bitcast.160, f32[1,1024]{1,0:T(1,128)} %bitcast.212), custom_call_target="tpu_custom_call" | custom-call | tf_op jit(solution)/shard_map/pallas_call | solution.py:960
  294.8 9.4 %convolution_convert_fusion.4.refs_0_ = bf16[2048,1024]{1,0:T(8,128)(2,1)} fusion(bf16[2048,1024]{1,0:T(8,128)(2,1)} %get-tuple-element.143, bf16[1024,1024]{1,0:T(8,128)(2,1)} %bitcast.227), kind=kOutput, calls=%fused_computation.47 | convolution fusion | flops 4297064448 | bytes 10485760 | tf_op jit(solution)/shard_map/tf,df->td/dot_general | solution.py:1114
  304.2 30.9 %shard_map.528 = f32[512,1024]{1,0:T(8,128)} custom-call(bf16[2048,1024]{1,0:T(8,128)(2,1)} %convolution_convert_fusion.4.refs_0_), custom_call_target="tpu_custom_call" | custom-call | tf_op jit(solution)/shard_map/pallas_call | solution.py:122
  335.1 2.3 fusion.80
  339.2 3.3 fusion.24.refs_0_
  342.6 14.0 %shard_map.529 = f32[8,8,1024]{2,1,0:T(8,128)} custom-call(f32[8,1024]{1,0:T(8,128)} %fusion.24.refs_0_), custom_call_target="tpu_custom_call" | custom-call | tf_op jit(solution)/shard_map/pallas_call | solution.py:122
  358.0 11.1 %shard_map.530 = (f32[8,128]{1,0:T(8,128)}, bf16[64,1024]{1,0:T(8,128)(2,1)}, f32[64,1024]{1,0:T(8,128)}, f32[64,1024]{1,0:T(8,128)}) custom-call(f32[64,1024]{1,0:T(8,128)} %bitcast.166, f32[1024,1024]{1,0:T(8,128)} %head_ref.1, s32[64,1]{1,0:T(8,128)} %broadcast_in_dim_reshape_squeeze.4.pair_ref), custom_call_target="tpu_custom_call" | custom-call | tf_op jit(solution)/shard_map/pallas_call | solution.py:1341
  374.1 3.4 multiply_reduce_fusion.3
  380.8 30.2 %shard_map.531 = bf16[2048,1024]{1,0:T(8,128)(2,1)} custom-call(bf16[512,1024]{1,0:T(8,128)(2,1)} %get-tuple-element.300.refs_0_), custom_call_target="tpu_custom_call" | custom-call | tf_op jit(solution)/shard_map/pallas_call | solution.py:122
  411.0 9.9 %fusion.85 = (bf16[1024]{0:T(1024)(128)(2,1)S(1)}, bf16[2048,1024]{1,0:T(8,128)(2,1)S(1)}) fusion(f32[2048,1024]{1,0:T(8,128)} %get-tuple-element.148, bf16[2048,1024]{1,0:T(8,128)(2,1)} %shard_map.531, bf16[1024,1024]{1,0:T(8,128)(2,1)} %bitcast.228), kind=kOutput, calls=%fused_computation.226 | convolution fusion | flops 4301257728 | bytes 18876416 | tf_op jit(solution)/shard_map/dot_general | solution.py:30
  421.0 6.1 convolution_convert_fusion.3.refs_0_
  427.1 6.2 convolution_convert_fusion.7
  433.3 32.4 %shard_map.532 = (f32[512,1024]{1,0:T(8,128)}, bf16[4,128,1024]{2,1,0:T(8,128)(2,1)}) custom-call(bf16[2048,1024]{1,0:T(8,128)(2,1)} %convolution_convert_fusion.3.refs_0_, bf16[4,2,128,1024]{3,2,1,0:T(8,128)(2,1)} %bitcast.157), custom_call_target="tpu_custom_call" | custom-call | tf_op jit(solution)/shard_map/pallas_call | solution.py:122
  465.7 3.2 multiply_reduce_fusion.4
  473.5 5.7 convolution_convert_fusion.6
  479.2 31.8 %shard_map.533 = (bf16[2048,1024]{1,0:T(8,128)(2,1)}, f32[128,1024]{1,0:T(8,128)}, bf16[4,128,1024]{2,1,0:T(8,128)(2,1)}) custom-call(bf16[512,1024]{1,0:T(8,128)(2,1)} %get-tuple-element.302.refs_0_, bf16[4,128,1024]{2,1,0:T(8,128)(2,1)} %get-tuple-element.150.refs_1_, bf16[4,2,128,1024]{3,2,1,0:T(8,128)(2,1)} %bitcast.159), custom_call_target="tpu_custom_call" | custom-call | tf_op jit(solution)/shard_map/pallas_call | solution.py:122
  511.1 4.4 convolution_convert_fusion.5.grad_ref
  515.5 33.3 %shard_map.534 = bf16[2048,768]{1,0:T(8,128)(2,1)} custom-call(s32[8]{0:T(128)} %get-tuple-element.336.low_ref, s32[8]{0:T(128)} %get-tuple-element.335.high_ref, bf16[2048,768]{1,0:T(8,128)(2,1)} %add_convert_fusion.qkv_ref, bf16[2048,256]{1,0:T(8,128)(2,1)} %convolution_convert_fusion.5.grad_ref, f32[8,2048]{1,0:T(8,128)} %get-tuple-element.152.log_ref, ...), custom_call_target="tpu_custom_call" | custom-call | tf_op jit(solution)/shard_map/pallas_call | solution.py:908
  548.8 7.2 convolution_convert_fusion.2.refs_0_
  559.4 4.7 convolution_convert_fusion.8
  564.1 34.4 %shard_map.535 = (f32[512,1024]{1,0:T(8,128)}, f32[128,1024]{1,0:T(8,128)}, bf16[4,128,256]{2,1,0:T(8,128)(2,1)}, bf16[4,128,768]{2,1,0:T(8,128)(2,1)}) custom-call(bf16[2048,1024]{1,0:T(8,128)(2,1)} %convolution_convert_fusion.2.refs_0_, bf16[4,128,1024]{2,1,0:T(8,128)(2,1)} %get-tuple-element.153.refs_1_, bf16[4,2,128,256]{3,2,1,0:T(8,128)(2,1)} %bitcast.181, ...), custom_call_target="tpu_custom_call" | custom-call | tf_op jit(solution)/shard_map/pallas_call | solution.py:122
  598.5 3.2 multiply_reduce_fusion.2
  604.6 28.8 %shard_map.536 = (bf16[4,512,256]{2,1,0:T(8,128)(2,1)}, f32[128,768]{1,0:T(8,128)}, f32[128,256]{1,0:T(8,128)}) custom-call(bf16[4,512,256]{2,1,0:T(8,128)(2,1)} %bitcast.154, bf16[4,128,768]{2,1,0:T(8,128)(2,1)} %get-tuple-element.155.refs_1_, bf16[4,128,256]{2,1,0:T(8,128)(2,1)} %get-tuple-element.156.refs_2_), custom_call_target="tpu_custom_call" | custom-call | tf_op jit(solution)/shard_map/pallas_call | solution.py:122
  633.4 6.1 fusion.15
  642.8 28.5 %shard_map.537 = (bf16[8,192,256]{2,1,0:T(8,128)(2,1)S(1)}, bf16[8,80,256]{2,1,0:T(8,128)(2,1)}) custom-call(bf16[8,192,256]{2,1,0:T(8,128)(2,1)} %bitcast.177, bf16[8,80,256]{2,1,0:T(8,128)(2,1)} %bitcast.164), custom_call_target="tpu_custom_call" | custom-call | tf_op jit(solution)/shard_map/pallas_call | solution.py:122
  671.5 12.9 %conditional.3 = (f32[6284,256]{1,0:T(8,128)}, f32[]{:T(128)}) conditional(s32[]{:T(128)} %convert_element_type.133, (s32[]{:T(128)}, s32[8,192]{1,0:T(8,128)S(1)}, bf16[8,192,256]{2,1,0:T(8,128)(2,1)S(1)}) %tuple.93, (s32[32,16,128]{2,1,0:T(8,128)}, s32[16384]{0:T(1024)S(1)}, s32[]{:T(128)}, bf16[2048,256]{1,0:T(8,128)(2,1)}) %tuple.92), branch_computations={%region_34.37_spmd, %region_36.40_spmd} | conditional | flops 16242687 | bytes 50390084 | solution.py:1546
  672.2 10.6 %branch_0_fun.1 = (f32[6284,256]{1,0:T(8,128)}, f32[8,256]{1,0:T(8,128)}) custom-call(s32[1,1536]{1,0:T(1,128)} %sub.106.index_ref, bf16[1536,256]{1,0:T(8,128)(2,1)S(1)} %bitcast.176), custom_call_target="tpu_custom_call" | custom-call | tf_op jit(solution)/shard_map/cond/branch_0_fun/pallas_call | solution.py:1078
  693.1 26.1 %shard_map.538 = (f32[1,16,1024]{2,1,0:T(8,128)}, f32[8,80,256]{2,1,0:T(8,128)}) custom-call(f32[16,1024]{1,0:T(8,128)} %concatenate.20.refs_0_, f32[80,256]{1,0:T(8,128)} %copy-done.22), custom_call_target="tpu_custom_call" | custom-call | tf_op jit(solution)/shard_map/pallas_call | solution.py:122
  723.1 4.5 multiply_reduce_fusion.1
  728.3 17.4 %multiply_subtract_fusion = (f32[6284,256]{1,0:T(8,128)}, f32[6284,256]{1,0:T(8,128)}, f32[6284,256]{1,0:T(8,128)}) fusion(f32[6284,256]{1,0:T(8,128)} %param.41, f32[6284,256]{1,0:T(8,128)} %get-tuple-element.168, f32[]{:T(128)S(6)} %min_shard_map.3, f32[6284,256]{1,0:T(8,128)} %param.42, f32[6284,256]{1,0:T(8,128)} %param.43), kind=kLoop, calls=%fused_computation.33 | loop fusion | flops 25739264 | bytes 45043716 | tf_op jit(solution)/shard_map/sub | solution.py:64
  759.2 3.0 multiply_subtract_fusion.4
  762.5 2.4 multiply_subtract_fusion.3
  765.0 10.9 %multiply_subtract_fusion.1 = (f32[1024,1024]{1,0:T(8,128)}, f32[1024,1024]{1,0:T(8,128)}, f32[1024,1024]{1,0:T(8,128)}) fusion(f32[1024,1024]{1,0:T(8,128)} %head_ref.1, f32[1024,1024]{1,0:T(8,128)} %get-tuple-element.334, f32[]{:T(128)S(6)} %min_shard_map.3, f32[1024,1024]{1,0:T(8,128)} %param.60, f32[1024,1024]{1,0:T(8,128)} %param.61), kind=kLoop, calls=%fused_computation.41 | loop fusion | flops 16777216 | bytes 29360132 | tf_op jit(solution)/shard_map/sub | solution.py:64
  (238 shorter events, 78.5 us)
Async XLA Ops:
  15.5 66.7 %copy-start.9 = (f32[128,3,256]{0,2,1:T(8,128)}, f32[128,3,256]{0,2,1:T(8,128)S(1)}, u32[]{:S(2)}) copy-start(f32[128,3,256]{0,2,1:T(8,128)S(1)} %copy.107) | copy-start | bytes 1179652
  45.9 67.9 %copy-start.34 = (s32[32,16,128]{2,1,0:T(8,128)}, s32[32,16,128]{2,1,0:T(8,128)S(1)}, u32[]{:S(2)}) copy-start(s32[32,16,128]{2,1,0:T(8,128)S(1)} %get-tuple-element.124) | copy-start | bytes 786436
  75.7 7.7 copy-start.36
  82.2 30.5 %copy-start.45 = (s32[1,2048]{1,0:T(1,128)S(1)}, s32[1,2048]{1,0:T(1,128)}, u32[]{:S(2)}) copy-start(s32[1,2048]{1,0:T(1,128)} %get-tuple-element.128) | copy-start | bytes 24580
  83.5 30.3 %copy-start.20 = (f32[256,128]{0,1:T(8,128)}, f32[256,128]{0,1:T(8,128)S(1)}, u32[]{:S(2)}) copy-start(f32[256,128]{0,1:T(8,128)S(1)} %copy.110) | copy-start | bytes 393220
  151.2 20.5 %copy-start.43 = (f32[6,256]{1,0:T(8,128)S(1)}, f32[6,256]{1,0:T(8,128)}, u32[]{:S(2)}) copy-start(f32[6,256]{1,0:T(8,128)} %param.62) | copy-start | bytes 18436
  151.2 20.6 %copy-start.52 = (bf16[4,2,128,768]{3,2,1,0:T(8,128)(2,1)S(1)}, bf16[4,2,128,768]{3,2,1,0:T(8,128)(2,1)}, u32[]{:S(2)}) copy-start(bf16[4,2,128,768]{3,2,1,0:T(8,128)(2,1)} %get-tuple-element.135) | copy-start | bytes 4718596
  179.1 23.4 %copy-start.27 = (bf16[4,2,128,256]{3,2,1,0:T(8,128)(2,1)S(1)}, bf16[4,2,128,256]{3,2,1,0:T(8,128)(2,1)}, u32[]{:S(2)}) copy-start(bf16[4,2,128,256]{3,2,1,0:T(8,128)(2,1)} %get-tuple-element.137) | copy-start | bytes 1572868
  202.4 4.6 copy-start.14
  374.1 3.5 copy-start.2
  411.0 10.0 %copy-start.18 = (bf16[4,2,128,1024]{3,2,1,0:T(8,128)(2,1)S(1)}, bf16[4,2,128,1024]{3,2,1,0:T(8,128)(2,1)}, u32[]{:S(2)}) copy-start(bf16[4,2,128,1024]{3,2,1,0:T(8,128)(2,1)} %get-tuple-element.142) | copy-start | bytes 6291460
  421.0 6.2 copy-start.54
  421.0 6.1 copy-start.7
  421.0 6.1 copy-start.50
  468.9 4.6 copy-start.55
  515.5 33.3 %copy-start.53 = (bf16[4,2,128,768]{3,2,1,0:T(8,128)(2,1)S(1)}, bf16[4,2,128,768]{3,2,1,0:T(8,128)(2,1)}, u32[]{:S(2)}) copy-start(bf16[4,2,128,768]{3,2,1,0:T(8,128)(2,1)} %get-tuple-element.135) | copy-start | bytes 4718596
  548.8 7.2 copy-start.11
  548.8 7.2 copy-start.51
  556.1 3.3 copy-start.49
  564.1 34.4 %copy-start = (f32[512,1024]{1,0:T(8,128)S(1)}, f32[512,1024]{1,0:T(8,128)}, u32[]{:S(2)}) copy-start(f32[512,1024]{1,0:T(8,128)} %get-tuple-element.146) | copy-start | bytes 6291460
  564.1 34.4 %copy-start.40 = (f32[1,1024]{1,0:T(1,128)S(1)}, f32[1,1024]{1,0:T(1,128)}, u32[]{:S(2)}) copy-start(f32[1,1024]{1,0:T(1,128)} %get-tuple-element.317) | copy-start | bytes 12292
  602.5 30.9 %copy-start.46 = (s32[1,2048]{1,0:T(1,128)S(1)}, s32[1,2048]{1,0:T(1,128)}, u32[]{:S(2)}) copy-start(s32[1,2048]{1,0:T(1,128)} %get-tuple-element.128) | copy-start | bytes 24580
  633.4 6.1 copy-start.6
  640.1 31.3 %copy-start.38 = (s32[1,8,2,128]{3,1,2,0:T(8,128)S(1)}, s32[1,8,2,128]{3,1,2,0:T(8,128)}, u32[]{:S(2)}) copy-start(s32[1,8,2,128]{3,1,2,0:T(8,128)} %copy-done.37) | copy-start | bytes 24580
  671.4 13.0 %copy-start.19 = (f32[128,768]{1,0:T(8,128)S(1)}, f32[128,768]{1,0:T(8,128)}, u32[]{:S(2)}) copy-start(f32[128,768]{1,0:T(8,128)} %get-tuple-element.160) | copy-start | bytes 1179652
  671.4 15.0 %copy-start.28 = (f32[128,256]{1,0:T(8,128)S(1)}, f32[128,256]{1,0:T(8,128)}, u32[]{:S(2)}) copy-start(f32[128,256]{1,0:T(8,128)} %get-tuple-element.161) | copy-start | bytes 393220
  671.4 16.2 %copy-start.17 = (f32[128,1024]{1,0:T(8,128)S(1)}, f32[128,1024]{1,0:T(8,128)}, u32[]{:S(2)}) copy-start(f32[128,1024]{1,0:T(8,128)} %get-tuple-element.162) | copy-start | bytes 1572868
  671.4 17.6 %copy-start.16 = (f32[128,1024]{1,0:T(8,128)S(1)}, f32[128,1024]{1,0:T(8,128)}, u32[]{:S(2)}) copy-start(f32[128,1024]{1,0:T(8,128)} %get-tuple-element.163) | copy-start | bytes 1572868
  671.4 19.0 %copy-start.31 = (bf16[8,80,256]{2,1,0:T(8,128)(2,1)S(1)}, bf16[8,80,256]{2,1,0:T(8,128)(2,1)}, u32[]{:S(2)}) copy-start(bf16[8,80,256]{2,1,0:T(8,128)(2,1)} %get-tuple-element.164) | copy-start | bytes 983044
  671.4 51.6 %copy-start.33 = (f32[64,1024]{1,0:T(8,128)S(1)}, f32[64,1024]{1,0:T(8,128)}, u32[]{:S(2)}) copy-start(f32[64,1024]{1,0:T(8,128)} %get-tuple-element.167) | copy-start | bytes 786436
  671.5 51.6 %copy-start.35 = (bf16[64,1024]{1,0:T(8,128)(2,1)S(1)}, bf16[64,1024]{1,0:T(8,128)(2,1)}, u32[]{:S(2)}) copy-start(bf16[64,1024]{1,0:T(8,128)(2,1)} %get-tuple-element.166) | copy-start | bytes 393220
  728.3 17.5 %copy-start.12 = (f32[514,256]{1,0:T(8,128)S(1)}, f32[514,256]{1,0:T(8,128)}, u32[]{:S(2)}) copy-start(f32[514,256]{1,0:T(8,128)} %refs_1_.1) | copy-start | bytes 1579012
  728.3 17.5 %copy-start.23 = (f32[514,256]{1,0:T(8,128)S(1)}, f32[514,256]{1,0:T(8,128)}, u32[]{:S(2)}) copy-start(f32[514,256]{1,0:T(8,128)} %param.45) | copy-start | bytes 1579012
  728.3 17.5 %copy-start.24 = (f32[514,256]{1,0:T(8,128)S(1)}, f32[514,256]{1,0:T(8,128)}, u32[]{:S(2)}) copy-start(f32[514,256]{1,0:T(8,128)} %param.46) | copy-start | bytes 1579012
  728.3 17.5 %copy-start.29 = (f32[8,80,256]{2,1,0:T(8,128)S(1)}, f32[8,80,256]{2,1,0:T(8,128)}, u32[]{:S(2)}) copy-start(f32[8,80,256]{2,1,0:T(8,128)} %get-tuple-element.169) | copy-start | bytes 1966084
  745.8 4.5 copy-start.10
  748.3 8.1 %copy-start.21 = (f32[256,128]{0,1:T(8,128)S(1)}, f32[256,128]{0,1:T(8,128)}, u32[]{:S(2)}) copy-start(f32[256,128]{0,1:T(8,128)} %copy-done.20) | copy-start | bytes 393220
  752.6 6.6 copy-start.13
  752.6 6.6 copy-start.25
  759.2 3.3 copy-start.15
  759.2 3.3 copy-start.26
  764.9 11.0 %copy-start.44 = (f32[6,256]{1,0:T(8,128)S(1)}, f32[6,256]{1,0:T(8,128)}, u32[]{:S(2)}) copy-start(f32[6,256]{1,0:T(8,128)} %param.62) | copy-start | bytes 18436
  764.9 11.0 %copy-start.47 = (f32[6,256]{1,0:T(8,128)S(1)}, f32[6,256]{1,0:T(8,128)}, u32[]{:S(2)}) copy-start(f32[6,256]{1,0:T(8,128)} %param.63) | copy-start | bytes 18436
  764.9 11.0 %copy-start.48 = (f32[6,256]{1,0:T(8,128)S(1)}, f32[6,256]{1,0:T(8,128)}, u32[]{:S(2)}) copy-start(f32[6,256]{1,0:T(8,128)} %param.64) | copy-start | bytes 18436
  764.9 12.3 %copy-start.32 = (f32[8,1024]{1,0:T(8,128)S(1)}, f32[8,1024]{1,0:T(8,128)}, u32[]{:S(2)}) copy-start(f32[8,1024]{1,0:T(8,128)} %row_ref.1) | copy-start | bytes 98308
  765.0 12.3 %copy-start.39 = (f32[1,16,1024]{2,1,0:T(8,128)S(1)}, f32[1,16,1024]{2,1,0:T(8,128)}, u32[]{:S(2)}) copy-start(f32[1,16,1024]{2,1,0:T(8,128)} %get-tuple-element.165) | copy-start | bytes 196612
  765.0 12.3 %copy-start.41 = (f32[8,1024]{1,0:T(8,128)S(1)}, f32[8,1024]{1,0:T(8,128)}, u32[]{:S(2)}) copy-start(f32[8,1024]{1,0:T(8,128)} %param.66) | copy-start | bytes 98308
  765.0 12.3 %copy-start.42 = (f32[8,1024]{1,0:T(8,128)S(1)}, f32[8,1024]{1,0:T(8,128)}, u32[]{:S(2)}) copy-start(f32[8,1024]{1,0:T(8,128)} %param.67) | copy-start | bytes 98308
  (8 other events, 14.2 us)

commit v4 on v3

--- a/solution.py
+++ b/solution.py
@@ -38,11 +38,6 @@
     center = values - jnp.mean(values, axis=1, keepdims=True)
     inverse = lax.rsqrt(jnp.mean(center * center, axis=1, keepdims=True) + LN_EPS)
     return center * inverse * gain_row + bias_row
-
-
-def norm_back(values, gain_row, bias_row, grad_rows):
-    norm_pull = jax.vjp(norm_rows, values, gain_row, bias_row)[1]
-    return norm_pull(grad_rows)
 
 
 def seq_layout(lengths, slot_total):
@@ -244,27 +239,26 @@
         super().__init__()
         height, depth = parts.shape[0] // self.width, parts.shape[1]
         far_rows = max(self.rows - 1, 1)
-        self.chunks = chunks
-        self.ins = (parts,)
-        self.outs = (shaped((height, depth), jnp.float32),)
-        self.scratch = (
+        self.chunks, self.height, self.depth = chunks, height, depth
+        self.parts = parts
+        self.fold_scratch = (
             pltpu.VMEM((self.rows, height, depth), jnp.bfloat16),
             pltpu.VMEM((far_rows, height, depth), jnp.bfloat16),
             pltpu.VMEM((far_rows, height, depth), jnp.bfloat16),
+            pltpu.VMEM((height, depth), jnp.float32),
         ) + tuple(dma(self.rows, chunks) for _ in range(4))
 
     def span(self, owner, part):
-        height = self.outs[0].shape[0]
-        size = height // self.chunks
-        return pl.ds(pl.multiple_of(owner * height + part * size, size), size)
+        size = self.height // self.chunks
+        return pl.ds(pl.multiple_of(owner * self.height + part * size, size), size)
 
     def local(self, part):
-        size = self.outs[0].shape[0] // self.chunks
+        size = self.height // self.chunks
         return pl.ds(part * size, size)
 
     def begin(self):
-        (p_ref,) = self.ins_refs
-        near_buf, near_send, near_recv = self.scratch_refs[0], *self.scratch_refs[3:5]
+        p_ref = self.ins_refs[0]
+        near_buf, near_send, near_recv = self.scratch_refs[0], *self.scratch_refs[4:6]
         me, core, row, mate = tensor_place(self.width)
         self.near = {}
         for step in list(range(1, self.rows)) + [0]:
@@ -281,8 +275,9 @@
                 self.near[step, part] = copy
 
     def middle(self):
-        (p_ref,), (o_ref,) = self.ins_refs, self.outs_refs
-        near_buf, sum_buf, far_buf, near_send, near_recv, far_send, far_recv = self.scratch_refs
+        p_ref = self.ins_refs[0]
+        near_buf, sum_buf, far_buf, total_buf = self.scratch_refs[:4]
+        far_send, far_recv = self.scratch_refs[6:8]
         me, core, row, mate = tensor_place(self.width)
         self.far = {}
         for step in range(1, self.rows):
@@ -306,20 +301,189 @@
         for part in range(self.chunks):
             local = self.local(part)
             self.near[0, part].wait_recv()
-            o_ref[local] = p_ref[self.span(me, part)].astype(jnp.float32) + near_buf[
+            total_buf[local] = p_ref[self.span(me, part)].astype(jnp.float32) + near_buf[
                 0, local
             ].astype(jnp.float32)
 
+    def folded(self, part):
+        far_buf, total_buf = self.scratch_refs[2:4]
+        local = self.local(part)
+        total = total_buf[local]
+        for step in range(1, self.rows):
+            self.far[step, part].wait_recv()
+            total = total + far_buf[step - 1, local].astype(jnp.float32)
+        return total
+
+    def settle_fold(self):
+        for copy in list(self.near.values()) + list(self.far.values()):
+            copy.wait_send()
+
+
+class Relay:
+    def relay_scratch(self):
+        return (pltpu.VMEM((self.height, self.depth), jnp.bfloat16),) + tuple(
+            dma(self.rows, self.chunks) for _ in range(4)
+        )
+
+    def relay_open(self, part, low):
+        buf, far_send, far_recv, near_send, near_recv = self.scratch_refs[-5:]
+        all_ref = self.outs_refs[0]
+        me, core, row, mate = tensor_place(self.width)
+        local = self.local(part)
+        buf[local] = low
+        if part == 0:
+            self.sent, self.relay_near = {}, []
+        for step in range(1, self.rows):
+            copy = remote(
+                buf.at[local],
+                all_ref.at[self.span(me, part)],
+                far_send.at[step, part],
+                far_recv.at[step, part],
+                {"tensor": lax.rem(row + step, self.rows) * 2 + core},
+            )
+            copy.start()
+            self.sent[step, part] = copy
+        copy = remote(
+            buf.at[local],
+            all_ref.at[self.span(me, part)],
+            near_send.at[0, part],
+            near_recv.at[0, part],
+            {"tensor": mate},
+        )
+        copy.start()
+        self.relay_near.append(copy)
+        all_ref[self.span(me, part)] = low
+
+    def relay_close(self):
+        buf, far_send, far_recv, near_send, near_recv = self.scratch_refs[-5:]
+        all_ref = self.outs_refs[0]
+        me, core, row, mate = tensor_place(self.width)
+        for part in range(self.chunks):
+            for step in range(1, self.rows):
+                self.sent[step, part].wait_recv()
+                source = lax.rem(row + self.rows - step, self.rows) * 2 + core
+                window = all_ref.at[self.span(source, part)]
+                copy = remote(
+                    window, window, near_send.at[step, part], near_recv.at[step, part], {"tensor": mate}
+                )
+                copy.start()
+                self.relay_near.append(copy)
+        for copy in self.relay_near:
+            copy.wait()
+        for copy in self.sent.values():
+            copy.wait_send()
+
+
+def split_three(values):
+    pieces, rest = [], values
+    for _ in range(3):
+        pieces.append(rest.astype(jnp.bfloat16))
+        rest = rest - pieces[-1].astype(jnp.float32)
+    return pieces
+
+
+def norm_pull(values, gain, grads):
+    center = values - jnp.mean(values, axis=1, keepdims=True)
+    inverse = lax.rsqrt(jnp.mean(center * center, axis=1, keepdims=True) + LN_EPS)
+    unit = center * inverse
+    scaled = grads * gain
+    pull = inverse * (
+        scaled
+        - jnp.mean(scaled, axis=1, keepdims=True)
+        - unit * jnp.mean(scaled * unit, axis=1, keepdims=True)
+    )
+    return (
+        pull,
+        jnp.sum(grads * unit, axis=0, keepdims=True),
+        jnp.sum(grads, axis=0, keepdims=True),
+    )
+
+
+class FoldNormSpread(Relay, Fold):
+    def __init__(self, parts, residual, row_params):
+        super().__init__(parts)
+        own = shaped((self.height, self.depth), jnp.float32)
+        self.ins = (parts, residual, row_params)
+        self.outs = (shaped(parts.shape, jnp.bfloat16), own, own)
+        self.scratch = self.fold_scratch + self.relay_scratch()
+
     def end(self):
-        (o_ref,) = self.outs_refs
-        far_buf = self.scratch_refs[2]
+        p_ref, residual_ref, row_ref = self.ins_refs
+        all_ref, sum_ref, norm_ref = self.outs_refs
         for part in range(self.chunks):
             local = self.local(part)
-            for step in range(1, self.rows):
-                self.far[step, part].wait_recv()
-                o_ref[local] += far_buf[step - 1, local].astype(jnp.float32)
-        for copy in list(self.near.values()) + list(self.far.values()):
-            copy.wait_send()
+            total = residual_ref[local] + self.folded(part) + row_ref[6:7]
+            sum_ref[local] = total
+            norm = norm_rows(total, row_ref[1:2], row_ref[4:5])
+            norm_ref[local] = norm
+            self.relay_open(part, norm.astype(jnp.bfloat16))
+        self.relay_close()
+        self.settle_fold()
+
+
+class FoldPullSpread(Relay, Fold):
+    def __init__(self, parts, residual, values, row_params):
+        super().__init__(parts)
+        own = shaped((self.height, self.depth), jnp.float32)
+        self.ins = (parts, residual, values, row_params)
+        self.outs = (shaped(parts.shape, jnp.bfloat16), own, shaped((8, self.depth), jnp.float32))
+        self.scratch = self.fold_scratch + self.relay_scratch()
+
+    def end(self):
+        p_ref, residual_ref, value_ref, row_ref = self.ins_refs
+        all_ref, grad_ref, side_ref = self.outs_refs
+        side_ref[...] = jnp.zeros_like(side_ref)
+        for part in range(self.chunks):
+            local = self.local(part)
+            pull, gain, shift = norm_pull(
+                value_ref[local], row_ref[1:2], residual_ref[local] + self.folded(part)
+            )
+            grad_ref[local] = pull
+            low = pull.astype(jnp.bfloat16)
+            self.relay_open(part, low)
+            side_ref[0:1] += gain
+            side_ref[1:2] += shift
+            side_ref[2:3] += jnp.sum(low.astype(jnp.float32), axis=0, keepdims=True)
+        self.relay_close()
+        self.settle_fold()
+
+
+class PullSpread(Relay, Pair):
+    def __init__(self, pooled_grad, counts, members, values, row_params):
+        super().__init__()
+        self.height, self.depth = values.shape
+        self.chunks = CHUNKS
+        own = shaped(values.shape, jnp.float32)
+        self.ins = (pooled_grad, counts, members, values, row_params)
+        self.outs = (
+            shaped((self.width * self.height, self.depth), jnp.bfloat16),
+            own,
+            shaped((8, self.depth), jnp.float32),
+        )
+        self.scratch = self.relay_scratch()
+
+    span, local = Fold.span, Fold.local
+
+    def begin(self):
+        pooled_ref, count_ref, member_ref, value_ref, row_ref = self.ins_refs
+        all_ref, grad_ref, side_ref = self.outs_refs
+        side_ref[...] = jnp.zeros_like(side_ref)
+        anchors = count_ref.shape[0]
+        rows = block_span(lax.axis_index("dp"), anchors)
+        pieces = jnp.concatenate(split_three(pooled_ref[rows] / count_ref[...]), axis=0)
+        for part in range(self.chunks):
+            local = self.local(part)
+            grads = multiply_arrays(member_ref[local], pieces)
+            pull, gain, shift = norm_pull(value_ref[local], row_ref[2:3], grads)
+            grad_ref[local] = pull
+            low = pull.astype(jnp.bfloat16)
+            self.relay_open(part, low)
+            side_ref[0:1] += gain
+            side_ref[1:2] += shift
+            side_ref[2:3] += jnp.sum(low.astype(jnp.float32), axis=0, keepdims=True)
+
+    def end(self):
+        self.relay_close()
 
 
 class Swap(Task):
@@ -412,6 +576,106 @@
             return carry
 
         lax.fori_loop(1, self.total, one, 0)
+
+
+class FoldPool(Fold):
+    def __init__(self, parts, residual, members, counts, row_params):
+        super().__init__(parts)
+        anchors = members.shape[0]
+        self.total = SumAll(shaped((anchors, self.depth), jnp.float32), True)
+        self.ins = (parts, residual, members, counts, row_params)
+        self.outs = (shaped((self.height, self.depth), jnp.float32),) + self.total.outs
+        self.scratch = (
+            self.fold_scratch
+            + (pltpu.VMEM((anchors, self.depth), jnp.float32),)
+            + self.total.scratch
+        )
+
+    def hello(self, barrier):
+        return super().hello(barrier) + self.total.hello(barrier)
+
+    def end(self):
+        p_ref, residual_ref, member_ref, count_ref, row_ref = self.ins_refs
+        sum_ref = self.outs_refs[0]
+        at = len(self.fold_scratch)
+        pooled = self.scratch_refs[at]
+        size = self.height // self.chunks
+        parts = []
+        for part in range(self.chunks):
+            local = self.local(part)
+            total = residual_ref[local] + self.folded(part) + row_ref[7:8]
+            sum_ref[local] = total
+            norm = norm_rows(total, row_ref[2:3], row_ref[5:6])
+            member = member_ref[:, part * size : (part + 1) * size]
+            for piece in split_three(norm):
+                parts.append(multiply_arrays(member, piece))
+        pooled[...] = sum(parts[1:], parts[0]) / count_ref[...]
+        total = self.total
+        total.ins_refs, total.outs_refs = (pooled,), self.outs_refs[1:]
+        total.scratch_refs = self.scratch_refs[at + 1 :]
+        total.begin()
+        total.middle()
+        total.end()
+        self.settle_fold()
+
+
+class FoldPullSwap(Fold):
+    def __init__(self, parts, residual, values, row_params):
+        super().__init__(parts)
+        self.narrow = self.depth // self.width
+        self.ins = (parts, residual, values, row_params)
+        self.outs = (
+            shaped((self.width, self.height, self.narrow), jnp.bfloat16),
+            shaped((8, self.depth), jnp.float32),
+        )
+        self.scratch = self.fold_scratch + (
+            pltpu.VMEM((self.height, self.depth), jnp.bfloat16),
+            dma(self.width, self.chunks),
+            dma(self.width, self.chunks),
+        )
+
+    def partners(self):
+        me = lax.axis_index("tensor")
+        return [{"tensor": lax.rem(me + step, self.width)} for step in range(1, self.width)]
+
+    def end(self):
+        p_ref, residual_ref, value_ref, row_ref = self.ins_refs
+        cols_ref, side_ref = self.outs_refs
+        buf, send, recv = self.scratch_refs[-3:]
+        side_ref[...] = jnp.zeros_like(side_ref)
+        me = lax.axis_index("tensor")
+
+        def lanes(owner):
+            return pl.ds(pl.multiple_of(owner * self.narrow, self.narrow), self.narrow)
+
+        copies = []
+        for part in range(self.chunks):
+            local = self.local(part)
+            pull, gain, shift = norm_pull(
+                value_ref[local], row_ref[0:1], residual_ref[local] + self.folded(part)
+            )
+            buf[local] = pull.astype(jnp.bfloat16)
+            for step in range(1, self.width):
+                other = lax.rem(me + step, self.width)
+                copy = remote(
+                    buf.at[local, lanes(other)],
+                    cols_ref.at[me, local],
+                    send.at[step, part],
+                    recv.at[step, part],
+                    {"tensor": other},
+                )
+                copy.start()
+                copies.append(copy)
+            cols_ref[me, local] = buf[local, lanes(me)]
+            side_ref[0:1] += gain
+            side_ref[1:2] += shift
+        for copy in copies:
+            copy.wait()
+        self.settle_fold()
+
+
+def eight_rows(values):
+    return jnp.sum(values.reshape(values.shape[0] // 8, 8, values.shape[1]), axis=0)
 
 
 class GridTask(Task):
@@ -504,6 +768,60 @@
             copy.wait()
 
 
+class Chain(Task):
+    def __init__(self, first, second):
+        self.first, self.second = first, second
+        self.ins = first.ins
+        self.outs = first.outs + second.outs
+        self.scratch = first.scratch + second.scratch
+
+    def hello(self, barrier):
+        return self.first.hello(barrier) + self.second.hello(barrier)
+
+    def begin(self):
+        outs, scratch = len(self.first.outs), len(self.first.scratch)
+        self.first.ins_refs, self.first.outs_refs = self.ins_refs, self.outs_refs[:outs]
+        self.first.scratch_refs = self.scratch_refs[:scratch]
+        self.second.ins_refs, self.second.outs_refs = self.outs_refs[:outs], self.outs_refs[outs:]
+        self.second.scratch_refs = self.scratch_refs[scratch:]
+        self.first.begin()
+
+    def middle(self):
+        self.first.end()
+        self.second.begin()
+
+    def end(self):
+        self.second.end()
+
+
+class Later(Task):
+    def __init__(self, task):
+        self.task = task
+        self.ins, self.outs, self.scratch = task.ins, task.outs, task.scratch
+
+    def hello(self, barrier):
+        return self.task.hello(barrier)
+
+    def middle(self):
+        task = self.task
+        task.ins_refs, task.outs_refs = self.ins_refs, self.outs_refs
+        task.scratch_refs = self.scratch_refs
+        task.begin()
+
+    def end(self):
+        self.task.end()
+
+
+def reduce_grid(blocks):
+    first = ReduceCross(blocks)
+    return Chain(first, ReduceLine(first.outs[0]))
+
+
+def spread_grid(block):
+    first = SpreadLine(block)
+    return Chain(first, SpreadCross(first.outs[0]))
+
+
 class SpreadCross(GridTask):
     def __init__(self, blocks):
         super().__init__()
@@ -536,12 +854,65 @@
             copy.wait()
 
 
+class GatherGrid(GridTask):
+    def __init__(self, block):
+        super().__init__()
+        self.ins = (block,)
+        self.outs = (shaped((LINE, self.cross) + block.shape, block.dtype),)
+        others = max(self.cross - 1, 1)
+        self.scratch = (dma(LINE - 1), dma(LINE - 1), dma(others, LINE), dma(others, LINE))
+
+    def lines(self):
+        line, cross = self.place()
+        return [
+            {"dp": lax.rem(line + step, LINE) * self.cross + cross} for step in range(1, LINE)
+        ]
+
+    def crosses(self):
+        line, cross = self.place()
+        return [
+            {"dp": line * self.cross + lax.rem(cross + step, self.cross)}
+            for step in range(1, self.cross)
+        ]
+
+    def partners(self):
+        return self.lines() + self.crosses()
+
+    def begin(self):
+        (x_ref,), (o_ref,), sems = self.ins_refs, self.outs_refs, self.scratch_refs
+        line, cross = self.place()
+        self.copies = [
+            remote(x_ref, o_ref.at[line, cross], sems[0].at[i], sems[1].at[i], partner)
+            for i, partner in enumerate(self.lines())
+        ]
+        for copy in self.copies:
+            copy.start()
+        o_ref[line, cross] = x_ref[...]
+
+    def middle(self):
+        (o_ref,), sems = self.outs_refs, self.scratch_refs
+        line, cross = self.place()
+        for copy in self.copies:
+            copy.wait()
+        self.copies = []
+        for i, partner in enumerate(self.crosses()):
+            for z in range(LINE):
+                window = o_ref.at[z, cross]
+                copy = remote(window, window, sems[2].at[i, z], sems[3].at[i, z], partner)
+                copy.start()
+                self.copies.append(copy)
+
+    def end(self):
+        for copy in self.copies:
+            copy.wait()
+
+
 class ReduceLine(GridTask):
     def __init__(self, blocks):
         super().__init__()
         shape = blocks.shape[1:]
         self.ins = (blocks,)
-        self.outs = (shaped(shape, jnp.float32),)
+        self.outs = (shaped(shape, jnp.float32), shaped((8, shape[1]), jnp.float32))
         self.scratch = (pltpu.VMEM((LINE - 1,) + shape, jnp.bfloat16), dma(LINE - 1), dma(LINE - 1))
 
     def targets(self):
@@ -565,7 +936,8 @@
             copy.start()
 
     def end(self):
-        (x_ref,), (o_ref,), (buf, send, recv) = self.ins_refs, self.outs_refs, self.scratch_refs
+        (x_ref,), (o_ref, square_ref) = self.ins_refs, self.outs_refs
+        buf = self.scratch_refs[0]
         line, cross = self.place()
         for copy in self.copies:
             copy.wait()
@@ -573,6 +945,7 @@
         for i in range(LINE - 1):
             total = total + buf[i].astype(jnp.float32)
         o_ref[...] = total
+        square_ref[...] = eight_rows(total * total)
 
 
 class SumAll(Task):
@@ -975,11 +1348,13 @@
 
 
 EMBED_ROWS = 128
+EMBED_PART = 16
 MARGIN = 256
 
 
 def embed_kernel(
-    start_ref, span_ref, own_ref, tok_ref, pos_ref, seq_ref, row_ref, low_ref, emb_ref, norm_ref, padded
+    start_ref, span_ref, own_ref, tok_ref, pos_ref, seq_ref, row_ref, low_ref, emb_ref, norm_ref,
+    padded, placed, normed,
 ):
     slots = tok_ref.shape[0]
     blocks, own_blocks = slots // EMBED_ROWS, emb_ref.shape[0] // EMBED_ROWS
@@ -990,26 +1365,34 @@
         rows = block_span(b, EMBED_ROWS)
         seq = seq_ref[rows, 0:1]
 
-        def pick(s, placed):
+        def pick(s, state):
             first = MARGIN + 2 + b * EMBED_ROWS - start_ref[s]
             base = first // 8
-            window = padded[pl.ds(pl.multiple_of(base * 8, 8), EMBED_ROWS + 8)]
-            window = pltpu.roll(window, EMBED_ROWS + 8 - (first - base * 8), 0)
-            return jnp.where(seq == s, window[:EMBED_ROWS], placed)
-
-        placed = lax.fori_loop(
-            span_ref[0, b], span_ref[1, b], pick, jnp.zeros((EMBED_ROWS, tok_ref.shape[1]), jnp.float32)
-        )
-        emb = tok_ref[rows].astype(jnp.float32) + placed
-        norm = norm_rows(emb, gain, shift)
-        low_ref[rows] = norm.astype(jnp.bfloat16)
+            shift = EMBED_PART + 8 - (first - base * 8)
+            for at in range(0, EMBED_ROWS, EMBED_PART):
+                window = padded[pl.ds(pl.multiple_of(base * 8 + at, 8), EMBED_PART + 8)]
+                window = pltpu.roll(window, shift, 0)[:EMBED_PART]
+                local = pl.ds(at, EMBED_PART)
+                placed[local] = jnp.where(seq[at : at + EMBED_PART] == s, window, placed[local])
+            return state
+
+        lax.fori_loop(span_ref[0, b], span_ref[1, b], pick, 0)
         own = b - own_ref[0] * own_blocks
-
-        @pl.when((own >= 0) & (own < own_blocks))
+        kept = (own >= 0) & (own < own_blocks)
+        own_first = jnp.where(kept, own, 0) * EMBED_ROWS
+        for at in range(0, EMBED_ROWS, EMBED_PART):
+            local = pl.ds(pl.multiple_of(b * EMBED_ROWS + at, EMBED_PART), EMBED_PART)
+            emb = tok_ref[local].astype(jnp.float32) + placed[pl.ds(at, EMBED_PART)]
+            norm = norm_rows(emb, gain, shift)
+            low_ref[local] = norm.astype(jnp.bfloat16)
+            placed[pl.ds(at, EMBED_PART)] = emb
+            normed[pl.ds(at, EMBED_PART)] = norm
+
+        @pl.when(kept)
         def _():
-            own_rows = block_span(own, EMBED_ROWS)
-            emb_ref[own_rows] = emb
-            norm_ref[own_rows] = norm
+            own_rows = pl.ds(pl.multiple_of(own_first, EMBED_ROWS), EMBED_ROWS)
+            emb_ref[own_rows] = placed[...]
+            norm_ref[own_rows] = normed[...]
 
         return carry
 
@@ -1038,7 +1421,9 @@
         in_specs=[in_scalars()] * 3 + [in_vmem()] * 4,
         out_specs=[in_vmem()] * 3,
         scratch_shapes=[
-            pltpu.VMEM((MARGIN + MAXLEN + EMBED_ROWS + 24, depth), jnp.float32)
+            pltpu.VMEM((MARGIN + MAXLEN + EMBED_ROWS + 24, depth), jnp.float32),
+            pltpu.VMEM((EMBED_ROWS, depth), jnp.float32),
+            pltpu.VMEM((EMBED_ROWS, depth), jnp.float32),
         ],
         compiler_params=pltpu.CompilerParams(vmem_limit_bytes=VMEM_BYTES),
     )(
@@ -1068,14 +1453,12 @@
     def _():
         square_ref[...] = jnp.zeros_like(square_ref)
 
-    square_ref[...] += jnp.sum(
-        (grad * grad).reshape(SCATTER_ROWS // 8, 8, grad.shape[1]), axis=0
-    )
+    square_ref[...] += eight_rows(grad * grad)
 
 
 def scatter_rows(index, rows, height):
     slots, width = rows.shape
-    grad, squares = pl.pallas_call(
+    return pl.pallas_call(
         scatter_kernel,
         grid=(pl.cdiv(height, SCATTER_ROWS),),
         out_shape=[shaped((height, width), jnp.float32), shaped((8, width), jnp.float32)],
@@ -1089,10 +1472,9 @@
         ],
         compiler_params=pltpu.CompilerParams(vmem_limit_bytes=VMEM_BYTES),
     )(index[None], rows)
-    return (grad, jnp.sum(squares))
-
-
-def layer_forward(embedded, seq_ids, bounds, row_params, col_local, layer_mats):
+
+
+def layer_forward(embedded, seq_ids, bounds, members, counts, row_params, col_local, layer_mats):
     first_moment_all, emb_rows, norm_first = embedded
     qkv_full, out_full, up_half, down_low = layer_mats
     col_width = col_local.shape[1]
@@ -1100,22 +1482,19 @@
     qkv_out = (multiply_arrays(first_moment_all, qkv_full) + qkv_bias).astype(jnp.bfloat16)
     attn_low, log_total = attend(qkv_out, seq_ids, bounds)
     first_back = jnp.einsum("tc,dc->td", attn_low, out_full, preferred_element_type=jnp.float32)
-    first_branch, up_full, down_half = exchange(
-        5, Fold(first_back.astype(jnp.bfloat16)), SpreadCross(up_half), SpreadLine(down_low)
+    second_all, first_sum, norm_second, up_full, _, down_full = exchange(
+        5,
+        FoldNormSpread(first_back.astype(jnp.bfloat16), norm_first, row_params),
+        SpreadCross(up_half),
+        spread_grid(down_low),
     )
     up_full = up_full.reshape(D, -1)
-    first_sum = norm_first + first_branch + row_params[6]
-    norm_second = norm_rows(first_sum, row_params[1], row_params[4])
-    second_all, down_full = exchange(
-        6, Spread(norm_second.astype(jnp.bfloat16)), SpreadCross(down_half)
-    )
     down_full = down_full.reshape(D, -1)
     hidden_low, slope = expand(second_all, up_full, col_local[2:].reshape(1, -1))
     second_back = jnp.einsum("tf,df->td", hidden_low, down_full, preferred_element_type=jnp.float32)
-    second_sum = (
-        norm_second + exchange(7, Fold(second_back.astype(jnp.bfloat16))) + row_params[7]
-    )
-    norm_third = norm_rows(second_sum, row_params[2], row_params[5])
+    second_sum, pooled = exchange(
+        7, FoldPool(second_back.astype(jnp.bfloat16), norm_second, members, counts, row_params)
+    )
     saved_vals = (
         emb_rows,
         first_moment_all,
@@ -1128,7 +1507,7 @@
         hidden_low,
         second_sum,
     )
-    return (norm_third, saved_vals, (qkv_full, out_full, up_full, down_full))
+    return (pooled, saved_vals, (qkv_full, out_full, up_full, down_full))
 
 
 def turned_grad(left_all, right_all):
@@ -1137,7 +1516,7 @@
     return grad.astype(jnp.bfloat16).reshape(groups, grad.shape[0] // groups, grad.shape[1])
 
 
-def layer_backward(grad_third, seq_ids, bounds, row_params, layer_mats, saved_vals):
+def layer_backward(pooled_grad, counts, members, seq_ids, bounds, row_params, layer_mats, saved_vals):
     qkv_full, out_full, up_full, down_full = layer_mats
     (
         emb_rows,
@@ -1152,21 +1531,20 @@
         second_sum,
     ) = saved_vals
     col_width = out_full.shape[1]
-    grad_second, gain_c, shift_c = norm_back(second_sum, row_params[2], row_params[5], grad_third)
-    mixed_low = grad_second.astype(jnp.bfloat16)
-    mixed_all = exchange(10, Spread(mixed_low))
+    mixed_all, grad_second, side_c = exchange(
+        10, PullSpread(pooled_grad, counts, jnp.tile(members.T, (1, 3)), second_sum, row_params)
+    )
     down_grad = turned_grad(mixed_all, hidden_low)
     up_low = (multiply_arrays(mixed_all, down_full) * slope).astype(jnp.bfloat16)
     up_grad = turned_grad(second_all, up_low)
     second_back = jnp.einsum(
         "tf,df->td", up_low, up_full, preferred_element_type=jnp.float32
     ).astype(jnp.bfloat16)
-    second_back, down_half = exchange(11, Fold(second_back), ReduceCross(down_grad))
-    second_total = grad_second + second_back
-    grad_first, gain_b, shift_b = norm_back(first_sum, row_params[1], row_params[4], second_total)
-    branch_low = grad_first.astype(jnp.bfloat16)
-    branch_all, down_sum, up_half = exchange(
-        12, Spread(branch_low), ReduceLine(down_half), ReduceCross(up_grad)
+    branch_all, grad_first, side_b, _, down_sum, down_squares, up_half = exchange(
+        11,
+        FoldPullSpread(second_back, grad_second, first_sum, row_params),
+        reduce_grid(down_grad),
+        Later(ReduceCross(up_grad)),
     )
     out_grad = turned_grad(branch_all, attn_low)
     attn_grad = multiply_arrays(branch_all, out_full).astype(jnp.bfloat16)
@@ -1175,30 +1553,38 @@
     first_back = jnp.einsum(
         "tc,dc->td", qkv_low, qkv_full, preferred_element_type=jnp.float32
     ).astype(jnp.bfloat16)
-    first_back, up_sum, out_half, qkv_half = exchange(
-        13, Fold(first_back), ReduceLine(up_half), ReduceCross(out_grad), ReduceCross(qkv_grad)
-    )
-    first_total = grad_first + first_back
-    emb_grad, gain_a, shift_a = norm_back(emb_rows, row_params[0], row_params[3], first_total)
+    cols_grad, side_a, up_sum, up_squares, _, out_sum, out_squares, _, qkv_sum, qkv_squares = exchange(
+        13,
+        FoldPullSwap(first_back, grad_first, emb_rows, row_params),
+        ReduceLine(up_half),
+        reduce_grid(out_grad),
+        reduce_grid(qkv_grad),
+    )
     qkv_cols = jnp.sum(qkv_low.astype(jnp.float32), axis=0).reshape(3, col_width)
     up_cols = jnp.sum(up_low.astype(jnp.float32), axis=0).reshape(-1, col_width)
     col_grad = jnp.concatenate([qkv_cols[0:1], qkv_cols[2:3], up_cols], axis=0)
-    row_grad = jnp.stack(
+    row_grad = jnp.concatenate(
         [
-            gain_a,
-            gain_b,
-            gain_c,
-            shift_a,
-            shift_b,
-            shift_c,
-            jnp.sum(branch_low.astype(jnp.float32), axis=0),
-            jnp.sum(mixed_low.astype(jnp.float32), axis=0),
+            side_a[0:1],
+            side_b[0:1],
+            side_c[0:1],
+            side_a[1:2],
+            side_b[1:2],
+            side_c[1:2],
+            side_b[2:3],
+            side_c[2:3],
         ]
     )
-    return (emb_grad, (qkv_half, out_half, up_sum, down_sum), col_grad, row_grad)
-
-
-def plan_kernel(capacity, vocab_local, groups, perm_ref, low_ref, high_ref, slot_ref, list_ref, count_ref, id_buf, own_buf):
+    return (
+        cols_grad,
+        (qkv_sum, out_sum, up_sum, down_sum),
+        (qkv_squares, out_squares, up_squares + down_squares),
+        col_grad,
+        row_grad,
+    )
+
+
+def plan_kernel(capacity, vocab_local, groups, perm_ref, low_ref, high_ref, slot_ref, ask_ref, id_buf, own_buf):
     slots = perm_ref.shape[1]
     table_rows = low_ref.shape[1]
     block = 128
@@ -1251,8 +1637,12 @@
         own_buf[pl.ds(b * block, block), :] = jnp.broadcast_to(
             own_slot[:, b * block : (b + 1) * block], (block, block)
         ).T
-    width = list_ref.shape[1]
-    target = lax.broadcasted_iota(jnp.int32, (1, width), 1).astype(jnp.float32)
+    list_rows = -(-capacity // 128)
+    stride = list_rows * 128
+    width = groups * stride
+    index = lax.broadcasted_iota(jnp.int32, (1, width), 1)
+    target = (index // stride * capacity + lax.rem(index, stride)).astype(jnp.float32)
+    target = jnp.where(lax.rem(index, stride) < capacity, target, -2.0)
 
     def settle(b, carry):
         slot, listed = carry
@@ -1273,8 +1663,13 @@
         (jnp.full((1, slots), -1.0, jnp.float32), jnp.full((1, width), -1.0, jnp.float32)),
     )
     slot_ref[...] = slot.astype(jnp.int32)
-    list_ref[...] = listed.astype(jnp.int32)
-    count_ref[...] = jnp.broadcast_to(running, count_ref.shape).astype(jnp.int32)
+    listed = listed.astype(jnp.int32)
+    most = jnp.max(running, axis=0, keepdims=True).astype(jnp.int32)
+    for group in range(groups):
+        for row in range(list_rows):
+            first_lane = group * stride + row * 128
+            ask_ref[group, row : row + 1] = listed[:, first_lane : first_lane + 128]
+        ask_ref[group, list_rows:] = jnp.broadcast_to(most, (8 - list_rows, 128))
 
 
 def make_plan(perm, all_ids, capacity, vocab_local, groups):
@@ -1286,11 +1681,10 @@
         partial(plan_kernel, capacity, vocab_local, groups),
         out_shape=[
             jax.ShapeDtypeStruct((1, slots), jnp.int32),
-            jax.ShapeDtypeStruct((1, groups * capacity), jnp.int32),
-            jax.ShapeDtypeStruct((groups, 128), jnp.int32),
+            jax.ShapeDtypeStruct((groups, 8, 128), jnp.int32),
         ],
         in_specs=[in_vmem()] * 3,
-        out_specs=[in_vmem()] * 3,
+        out_specs=[in_vmem()] * 2,
         scratch_shapes=[pltpu.VMEM((slots, 128), jnp.float32), pltpu.VMEM((slots, 128), jnp.float32)],
         compiler_params=pltpu.CompilerParams(vmem_limit_bytes=VMEM_BYTES),
     )(perm[None], low.astype(jnp.bfloat16), high.astype(jnp.bfloat16))
@@ -1331,9 +1725,24 @@
         unit_grad = jnp.where(lane < depth // fraction, unit_grad, 0.0)
         inner = jnp.sum(unit_grad * prefix, axis=1, keepdims=True)
         grads = grads + inverse * unit_grad - prefix * (inverse * inverse * inverse * inner)
-    loss_ref[...] = jnp.broadcast_to(loss, loss_ref.shape)
+    low_wide = low.astype(jnp.float32)
+    head_squares = jnp.sum(
+        exact(low_wide, low_wide, ((1,), (1,))) * exact(grads, grads, ((1,), (1,))), keepdims=True
+    )
+    line = lax.broadcasted_iota(jnp.int32, loss_ref.shape, 0)
+    loss_ref[...] = jnp.where(line == 0, loss, head_squares)
     grad_ref[...] = grads
-    back_ref[...] = exact(grads, head_low.astype(jnp.float32), ((1,), (1,)))
+    pieces, rest = [], grads
+    for _ in range(3):
+        pieces.append(rest.astype(jnp.bfloat16))
+        rest = rest - pieces[-1].astype(jnp.float32)
+    product = lax.dot_general(
+        jnp.concatenate(pieces, axis=0),
+        head_low,
+        (((1,), (1,)), ((), ())),
+        preferred_element_type=jnp.float32,
+    )
+    back_ref[...] = product[:total] + product[total : 2 * total] + product[2 * total :]
 
 
 def contrast_step(pooled, head_weight, pairs):
@@ -1402,57 +1811,50 @@
     block = jnp.concatenate(
         [
             token_ids.reshape(id_rows, 128),
-            slot_perm.reshape(id_rows, 128),
             jnp.pad(pair_index, (0, 128 - anchors))[None],
-            jnp.zeros((16 - 2 * id_rows - 1, 128), jnp.int32),
+            jnp.zeros((7 - id_rows, 128), jnp.int32),
         ],
         axis=0,
     )
+    perm_block = jnp.pad(slot_perm.reshape(id_rows, 128), ((0, 8 - id_rows), (0, 0)))
     qkv_low = query_key_value_weight.astype(jnp.bfloat16).reshape(-1, 3 * col_width)
     out_low = out_weight.T.astype(jnp.bfloat16)
     up_low = up_weight.astype(jnp.bfloat16).reshape(qkv_low.shape[0], -1)
     down_low = down_weight.reshape(-1, down_weight.shape[2]).T.astype(jnp.bfloat16)
-    gathered, qkv_half = exchange(1, GatherAll(block), SpreadLine(qkv_low))
+    gathered, perms, out_half = exchange(
+        1, GatherAll(block), Gather(perm_block, "tensor"), SpreadLine(out_low)
+    )
     all_ids = gathered[:, :id_rows].reshape(-1)
-    pairs = gathered[:: tensor_count, 2 * id_rows, :anchors].reshape(-1)
-    own_perm = lax.dynamic_slice_in_dim(
-        gathered, group_index * tensor_count, tensor_count, 0
-    )[:, id_rows : 2 * id_rows].reshape(-1)
-    slot, listed, counts_out = make_plan(own_perm, all_ids, CAPACITY, vocab_local, groups)
+    pairs = gathered[::tensor_count, id_rows, :anchors].reshape(-1)
+    own_perm = perms[:, :id_rows].reshape(-1)
+    slot, request = make_plan(own_perm, all_ids, CAPACITY, vocab_local, groups)
     slot = slot[0]
     list_rows = -(-CAPACITY // 128)
-    top_count = jnp.max(counts_out)
-    request = jnp.concatenate(
-        [
-            jnp.pad(
-                listed.reshape(groups, CAPACITY), ((0, 0), (0, list_rows * 128 - CAPACITY))
-            ).reshape(groups, list_rows, 128),
-            jnp.broadcast_to(top_count, (groups, 8 - list_rows, 128)),
-        ],
-        axis=1,
-    )
     asked = exchange(2, Swap(request, "dp"))
     overflow = jnp.max(asked[:, list_rows]) > CAPACITY
     offset = group_index * vocab_local
     asked_rows = asked[:, :list_rows].reshape(groups, -1)[:, :CAPACITY].reshape(-1) - offset
     asked_safe = jnp.clip(asked_rows, 0, vocab_local - 1)
     sent_rows = jnp.take(tok_table, asked_safe, axis=0).astype(jnp.bfloat16)
-    got_rows, pos_full, out_half = exchange(
+    got_rows, pos_full, qkv_half, out_full = exchange(
         3,
         Swap(sent_rows.reshape(groups, CAPACITY, col_width), "dp"),
         Spread(pos_table, columns=True, chunks=1),
-        SpreadLine(out_low),
+        SpreadLine(qkv_low),
+        SpreadCross(out_half),
     )
     got_rows = got_rows.reshape(-1, col_width)
-    chooser = (slot[:, None] == jnp.arange(groups * CAPACITY, dtype=jnp.int32)[None, :]).astype(
-        jnp.bfloat16
-    )
+
+    def chooser(slots):
+        places = jnp.arange(groups * CAPACITY, dtype=jnp.int32)
+        return (slots[:, None] == places[None, :]).astype(jnp.bfloat16)
+
     lengths = seq_lengths[0]
     seq_ids, positions, member = seq_layout(lengths, tok_grp)
     bounds = block_bounds(lengths, tok_grp)
 
     def every_slot_id():
-        every_perm = gathered[:, id_rows : 2 * id_rows].reshape(-1)
+        every_perm = lax.all_gather(slot_perm, ("dp", "tensor"), axis=0, tiled=True)
         return jnp.take(all_ids, every_perm, axis=0)
 
     def spread_wide():
@@ -1471,46 +1873,32 @@
     tok_cols = lax.cond(
         overflow,
         spread_wide,
-        lambda: multiply_arrays(chooser, got_rows).astype(jnp.bfloat16),
-    )
-    tok_all, qkv_full, out_full, up_half = exchange(
+        lambda: multiply_arrays(chooser(slot), got_rows).astype(jnp.bfloat16),
+    )
+    tok_all, qkv_full, up_half = exchange(
         4,
         Spread(tok_cols, columns=True),
         SpreadCross(qkv_half),
-        SpreadCross(out_half),
         SpreadLine(up_low),
     )
     layer_mats = (qkv_full.reshape(D, -1), out_full.reshape(D, -1), up_half, down_low)
     embedded = embed(tok_all, pos_full, seq_ids, lengths, row_params)
-    norm_third, saved_vals, layer_mats = layer_forward(
-        embedded, seq_ids, bounds, row_params, col_bias, layer_mats
-    )
-    row_member = lax.dynamic_slice_in_dim(member, tensor_index * tok_dev, tok_dev, 0).astype(
-        jnp.float32
+    members = lax.dynamic_slice_in_dim(member, tensor_index * tok_dev, tok_dev, 0).T.astype(
+        jnp.bfloat16
     )
     counts = lengths.astype(jnp.float32)[:, None]
-    pooled = exchange(9, SumAll(exact_multiply(row_member.T, norm_third) / counts, True))
+    pooled, saved_vals, layer_mats = layer_forward(
+        embedded, seq_ids, bounds, members, counts, row_params, col_bias, layer_mats
+    )
     loss_out, pooled_low, vec_grad, pooled_grad = contrast_step(
         pooled.reshape(-1, D), head_weight, pairs
     )
     head_sum = exact_multiply(pooled_low.astype(jnp.float32).T, vec_grad)
-    own_grad = lax.dynamic_slice_in_dim(pooled_grad, group_index * anchors, anchors, 0)
-    grad_third = exact_multiply(row_member, own_grad / counts)
-    emb_grad, halves, col_grad, row_grad = layer_backward(
-        grad_third, seq_ids, bounds, row_params, layer_mats, saved_vals
-    )
-    qkv_half, out_half, up_sum, down_sum = halves
-    cols_grad, qkv_sum, out_sum = exchange(
-        14,
-        Swap(
-            emb_grad.astype(jnp.bfloat16)
-            .reshape(tok_dev, tensor_count, col_width)
-            .swapaxes(0, 1),
-            "tensor",
-        ),
-        ReduceLine(qkv_half),
-        ReduceLine(out_half),
-    )
+    cols_grad, sums, grid_squares, col_grad, row_grad = layer_backward(
+        pooled_grad, counts, members, seq_ids, bounds, row_params, layer_mats, saved_vals
+    )
+    qkv_sum, out_sum, up_sum, down_sum = sums
+    qkv_squares, out_squares, wide_squares = grid_squares
     cols_grad = cols_grad.reshape(tok_grp, col_width)
     pos_pick = (
         jnp.arange(pos_table.shape[0], dtype=jnp.int32)[:, None] == positions[None, :]
@@ -1519,7 +1907,12 @@
     shared = jnp.concatenate([pos_grad, col_grad], axis=0)
     shared_rows = -(-shared.shape[0] // (16 * groups)) * 16
     shared = jnp.pad(shared, ((0, shared_rows * groups - shared.shape[0]), (0, 0)))
-    merged = jnp.einsum("kn,kc->nc", chooser, cols_grad, preferred_element_type=jnp.float32)
+    merged = jnp.einsum(
+        "kn,kc->nc",
+        chooser(lax.optimization_barrier(slot)),
+        cols_grad,
+        preferred_element_type=jnp.float32,
+    )
     back_rows, shared_parts = exchange(
         15,
         Swap(merged.astype(jnp.bfloat16).reshape(groups, CAPACITY, col_width), "dp"),
@@ -1541,35 +1934,35 @@
                 )
             )
         )
-        return (grad, jnp.sum(grad * grad))
+        squares = jnp.sum(grad * grad, axis=0, keepdims=True)
+        return (grad, jnp.pad(squares, ((0, 7), (0, 0))))
 
     tok_grad, tok_squares = lax.cond(
         overflow,
         add_wide,
-        lambda: scatter_rows(asked_rows, back_rows.reshape(-1, col_width), vocab_local),
+        lambda: tuple(scatter_rows(asked_rows, back_rows.reshape(-1, col_width), vocab_local)),
     )
     qkv_grad = qkv_sum.reshape(query_key_value_weight.shape)
-    out_grad = out_sum.T
+    out_grad = lax.optimization_barrier(out_sum.T)
     up_grad = up_sum.reshape(up_weight.shape)
-    down_grad = down_sum.T.reshape(down_weight.shape)
-    local_squares = (
-        tok_squares
-        + jnp.sum(qkv_grad * qkv_grad)
-        + jnp.sum(out_grad * out_grad)
-        + jnp.sum(up_grad * up_grad)
-        + jnp.sum(down_grad * down_grad)
-        + jnp.sum(shared_own * shared_own)
-    )
-    row_block = jnp.concatenate(
-        [row_grad, jnp.pad(local_squares.reshape(1, 1), ((0, 7), (0, D - 1)))], axis=0
-    )
-    row_total, shared_sum = exchange(16, SumAll(row_block, False), Gather(shared_own, "dp"))
+    down_grad = lax.optimization_barrier(down_sum.T.reshape(down_weight.shape))
+    def widen(*parts):
+        joined = jnp.concatenate(parts, axis=1)
+        return jnp.pad(joined, ((0, 0), (0, D - joined.shape[1])))
+
+    square_rows = (
+        widen(wide_squares)
+        + widen(qkv_squares, out_squares)
+        + widen(tok_squares, eight_rows(shared_own * shared_own))
+    )
+    row_block = jnp.concatenate([row_grad, square_rows], axis=0)
+    row_total, shared_sum = exchange(16, SumAll(row_block, False), GatherGrid(shared_own.astype(jnp.bfloat16)))
     row_total = row_total[0]
-    shared_sum = shared_sum.reshape(-1, col_width)
+    shared_sum = shared_sum.reshape(-1, col_width).astype(jnp.float32)
     pos_own = shared_sum[: pos_table.shape[0]]
     col_own = shared_sum[pos_table.shape[0] : pos_table.shape[0] + col_bias.shape[0]]
     row_sum = row_total[:8]
-    squares = row_total[8, 0] + jnp.sum(row_sum * row_sum) + jnp.sum(head_sum * head_sum)
+    squares = jnp.sum(row_total[8:]) + jnp.sum(row_sum * row_sum) + loss_out[1, 0]
     grad_norm = jnp.sqrt(squares)
     clip_scale = jnp.minimum(1.0, CLIP_NORM / (grad_norm + 1e-06))
     tok_new = adam_step(

time: 793 us -> 710 us (0.90)
  other arithmetic: 82.1 us -> 45.2 us
  Pallas kernels: 547 us -> 512 us
    pallas_call x15 -> x11, Pallas kernels: 423 us -> 396 us  [exchange(): pl.pallas_call(kernel, out_shape=[out for task in tasks for out in task.o...]
    reduce_sum x19 -> x1, other arithmetic: 24.8 us -> 0.01 us  [eight_rows(): jnp.sum(values.reshape(values.shape[0] // 8, 8, values.shape[1]), axis=0)]
    sub x9 -> x8, other arithmetic: 38.7 us -> 27.5 us  [adam_step(): weight - step_rate * (first_hat / (jnp.sqrt(second_hat) + ADAM_EPS) + dec...]
    unnamed x129 -> x107, local copies, waits for them, and re-layouts: 20.5 us -> 14.1 us
where the time goes in v4:
time: 710 us; the launch traced here: 702 us
  Pallas kernels  512 us (72%)
  matrix products  87.4 us (12%)
  other arithmetic  45.2 us (6%)
  local copies, waits for them, and re-layouts  38.8 us (5%)
  between operations  18.9 us (3%)
    pallas_call x11, Pallas kernels, exchange(): pl.pallas_call(kernel, out_shape=[out for task in tasks for out in task.o...  396 us
    pallas_call x1, Pallas kernels, attend_back(): pl.pallas_call(attend_back_kernel, out_shape=jax.ShapeDtypeStruct(qkv_out...  33.3 us
    sub x8, other arithmetic, adam_step(): weight - step_rate * (first_hat / (jnp.sqrt(second_hat) + ADAM_EPS) + dec...  27.5 us
    dot_general x5, matrix products, multiply_arrays(): return jnp.dot(left_mat, right_mat, preferred_element_type=jnp.float32)  25.7 us
    pallas_call x1, Pallas kernels, attend(): pl.pallas_call(attend_kernel, out_shape=[jax.ShapeDtypeStruct((slots, col...  22.7 us
    dot_general x4, matrix products, turned_grad(): jnp.einsum('td,tc->dc', left_all, right_all, preferred_element_type=jnp.f...  18.8 us
    pallas_call x1, Pallas kernels, expand(): pl.pallas_call(expand_kernel, grid=(slots // tall,), out_shape=[shaped((s...  15.8 us
    pallas_call x1, Pallas kernels, embed(): pl.pallas_call(embed_kernel, out_shape=[shaped((slots, depth), jnp.bfloat...  14.7 us

profile of v4, /device:TPU:0, one launch (start us, length us, event | category | flops | bytes accessed | tf_op | source)
XLA Modules:
  0.0 702.3 jit_solution(6397132254694788081)
XLA Ops:
  12.3 1.3 add_add_fusion.refs_0_
  16.6 18.2 %shard_map.518 = (s32[32,8,128]{2,1,0:T(8,128)}, s32[4,8,128]{2,1,0:T(8,128)}, bf16[4,128,256]{2,1,0:T(8,128)(2,1)}) custom-call(s32[8,128]{1,0:T(8,128)} %add_add_fusion.refs_0_, s32[8,128]{1,0:T(8,128)} %pad.22.refs_1_, bf16[128,256]{1,0:T(8,128)(2,1)} %convert_bitcast_fusion.refs_2_), custom_call_target="tpu_custom_call" | custom-call | tf_op jit(solution)/shard_map/pallas_call | solution.py:117
  34.7 1.3 slice.85
  37.8 10.9 %shard_map.519 = (s32[1,2048]{1,0:T(1,128)S(1)}, s32[8,8,128]{2,1,0:T(8,128)}) custom-call(s32[1,2048]{1,0:T(1,128)} %bitcast.171, bf16[128,128]{1,0:T(8,128)(2,1)} %get-tuple-element.334.low_ref, bf16[128,128]{1,0:T(8,128)(2,1)} %get-tuple-element.333.high_ref), custom_call_target="tpu_custom_call" | custom-call | tf_op jit(solution)/shard_map/pallas_call | solution.py:1680
  48.7 8.2 %shard_map.520 = s32[8,8,128]{2,1,0:T(8,128)} custom-call(s32[8,8,128]{2,1,0:T(8,128)} %get-tuple-element.131.refs_0_), custom_call_target="tpu_custom_call" | custom-call | tf_op jit(solution)/shard_map/pallas_call | solution.py:117
  56.9 1.4 slice_reduce_fusion.2
  60.5 6.5 gather_fusion.3
  69.2 37.9 %shard_map.521 = (bf16[8,192,256]{2,1,0:T(8,128)(2,1)S(1)}, f32[514,1024]{1,0:T(8,128)}, bf16[4,128,768]{2,1,0:T(8,128)(2,1)}, bf16[4,2,128,256]{3,2,1,0:T(8,128)(2,1)}) custom-call(bf16[8,192,256]{2,1,0:T(8,128)(2,1)} %select_convert_fusion.refs_0_, f32[514,256]{1,0:T(8,128)} %refs_1_.1, bf16[128,768]{1,0:T(8,128)(2,1)} %copy.135.refs_2_, ...), custom_call_target="tpu_custom_call" | custom-call | tf_op jit(solution)/shard_map/pallas_call | solution.py:117
  107.1 3.3 conditional.2
  107.1 3.1 fusion.2
  112.3 32.1 %shard_map.522 = (bf16[2048,1024]{1,0:T(8,128)(2,1)}, bf16[4,2,128,768]{3,2,1,0:T(8,128)(2,1)}, bf16[4,128,1024]{2,1,0:T(8,128)(2,1)}) custom-call(bf16[2048,256]{1,0:T(8,128)(2,1)} %get-tuple-element.359.refs_0_, bf16[4,128,768]{2,1,0:T(8,128)(2,1)} %get-tuple-element.135.refs_1_, bf16[128,1024]{1,0:T(8,128)(2,1)} %bitcast.155), custom_call_target="tpu_custom_call" | custom-call | tf_op jit(solution)/shard_map/pallas_call | solution.py:117
  144.5 1.4 copy.136.seq_ref.seq_col_ref
  145.9 14.7 %shard_map.523 = (bf16[2048,1024]{1,0:T(8,128)(2,1)}, f32[512,1024]{1,0:T(8,128)}, f32[512,1024]{1,0:T(8,128)}) custom-call(s32[8]{0:T(128)} %bitcast_subtract_fusion.1.start_ref, s32[2,16]{1,0:T(2,128)} %pad_add_fusion.span_ref, s32[1]{0:T(128)} %bitcast.15.own_ref, bf16[2048,1024]{1,0:T(8,128)(2,1)} %get-tuple-element.136.tok_ref, ...), custom_call_target="tpu_custom_call" | custom-call | tf_op jit(solution)/shard_map/pallas_call | solution.py:1414
  160.6 7.3 %add_convert_fusion.qkv_ref = bf16[2048,768]{1,0:T(8,128)(2,1)} fusion(bf16[2048,1024]{1,0:T(8,128)(2,1)} %get-tuple-element.138, bf16[1024,768]{1,0:T(8,128)(2,1)S(1)} %bitcast.190, f32[768]{0:T(1024)S(1)} %pad_maximum_fusion), kind=kOutput, calls=%fused_computation.39 | convolution fusion | flops 3224371200 | bytes 8915968 | tf_op jit(solution)/shard_map/dot_general | solution.py:30
  168.6 22.7 %shard_map.524 = (bf16[2048,256]{1,0:T(8,128)(2,1)}, f32[8,2048]{1,0:T(8,128)}) custom-call(s32[8]{0:T(128)} %get-tuple-element.354.low_ref, s32[8]{0:T(128)} %get-tuple-element.353.high_ref, bf16[2048,768]{1,0:T(8,128)(2,1)} %add_convert_fusion.qkv_ref, s32[2048,1]{1,0:T(8,128)} %copy.136.seq_ref.seq_col_ref, s32[8,2048]{1,0:T(8,128)} %broadcast_in_dim.154.seq_row_ref), custom_call_target="tpu_custom_call" | custom-call | tf_op jit(solution)/shard_map/pallas_call | solution.py:1171
  191.3 4.6 convolution_convert_fusion.refs_0_
  196.8 60.7 %shard_map.525 = (bf16[2048,1024]{1,0:T(8,128)(2,1)}, f32[512,1024]{1,0:T(8,128)}, f32[512,1024]{1,0:T(8,128)}, bf16[4,2,128,1024]{3,2,1,0:T(8,128)(2,1)}, bf16[...) custom-call(bf16[2048,1024]{1,0:T(8,128)(2,1)} %convolution_convert_fusion.refs_0_, ...), custom_call_target="tpu_custom_call" | custom-call | tf_op jit(solution)/shard_map/pallas_call | solution.py:117
  258.1 15.8 %shard_map.526 = (bf16[2048,1024]{1,0:T(8,128)(2,1)}, f32[2048,1024]{1,0:T(8,128)}) custom-call(bf16[2048,1024]{1,0:T(8,128)(2,1)} %get-tuple-element.144.rows_ref, bf16[1024,1024]{1,0:T(8,128)(2,1)} %bitcast.140, f32[1,1024]{1,0:T(1,128)} %bitcast.175), custom_call_target="tpu_custom_call" | custom-call | tf_op jit(solution)/shard_map/pallas_call | solution.py:1333
  273.9 8.5 %convolution_convert_fusion.3.refs_0_ = bf16[2048,1024]{1,0:T(8,128)(2,1)} fusion(bf16[2048,1024]{1,0:T(8,128)(2,1)} %get-tuple-element.146, bf16[1024,1024]{1,0:T(8,128)(2,1)S(1)} %bitcast.188), kind=kOutput, calls=%fused_computation.48 | convolution fusion | flops 4297064448 | bytes 10485760 | tf_op jit(solution)/shard_map/tf,df->td/dot_general | solution.py:1494
  283.8 43.7 %shard_map.527 = (f32[512,1024]{1,0:T(8,128)}, f32[8,8,1024]{2,1,0:T(8,128)}) custom-call(bf16[2048,1024]{1,0:T(8,128)(2,1)} %convolution_convert_fusion.3.refs_0_, f32[512,1024]{1,0:T(8,128)} %get-tuple-element.148.refs_1_, bf16[8,512]{1,0:T(8,128)(2,1)} %get-tuple-element.344.refs_2_, f32[8,1]{1,0:T(8,128)} %convert_element_type.147.refs_3_.refs_1_, ...), custom_call_target="tpu_custom_call" | custom-call | tf_op jit(solution)/shard_map/pallas_call | solution.py:117
  329.0 7.8 %shard_map.528 = (f32[8,128]{1,0:T(8,128)}, bf16[64,1024]{1,0:T(8,128)(2,1)}, f32[64,1024]{1,0:T(8,128)}, f32[64,1024]{1,0:T(8,128)}) custom-call(f32[64,1024]{1,0:T(8,128)} %bitcast.166, f32[1024,1024]{1,0:T(8,128)} %head_ref.1, s32[64,1]{1,0:T(8,128)} %broadcast_in_dim_reshape_squeeze.4.pair_ref), custom_call_target="tpu_custom_call" | custom-call | tf_op jit(solution)/shard_map/pallas_call | solution.py:1750
  336.8 1.3 fusion.59
  338.9 31.8 %shard_map.529 = (bf16[2048,1024]{1,0:T(8,128)(2,1)}, f32[512,1024]{1,0:T(8,128)}, f32[8,1024]{1,0:T(8,128)}) custom-call(f32[64,1024]{1,0:T(8,128)} %get-tuple-element.151.refs_0_, f32[8,1]{1,0:T(8,128)} %convert_element_type.147.refs_3_.refs_1_, bf16[512,24]{1,0:T(8,128)(2,1)} %copy.141.refs_2_, f32[512,1024]{1,0:T(8,128)} %get-tuple-element.152.refs_3_, ...), custom_call_target="tpu_custom_call" | custom-call | tf_op jit(solution)/shard_map/pallas_call | solution.py:117
  370.7 8.8 %fusion.61 = (bf16[1024]{0:T(1024)(128)(2,1)S(1)}, bf16[2048,1024]{1,0:T(8,128)(2,1)S(1)}) fusion(f32[2048,1024]{1,0:T(8,128)} %get-tuple-element.154, bf16[2048,1024]{1,0:T(8,128)(2,1)} %get-tuple-element.153, bf16[1024,1024]{1,0:T(8,128)(2,1)S(1)} %bitcast.189), kind=kOutput, calls=%fused_computation.170 | convolution fusion | flops 4301257728 | bytes 18876416 | tf_op jit(solution)/shard_map/dot_general | solution.py:30
  379.6 6.1 convolution_convert_fusion.2.refs_0_
  385.7 5.7 convolution_convert_fusion.6
  391.4 5.9 convolution_convert_fusion.5
  397.3 62.7 %shard_map.530 = (bf16[2048,1024]{1,0:T(8,128)(2,1)}, f32[512,1024]{1,0:T(8,128)}, f32[8,1024]{1,0:T(8,128)}, bf16[4,128,1024]{2,1,0:T(8,128)(2,1)}, f32[128,102...) custom-call(bf16[2048,1024]{1,0:T(8,128)(2,1)} %convolution_convert_fusion.2.refs_0_, ...), custom_call_target="tpu_custom_call" | custom-call | tf_op jit(solution)/shard_map/pallas_call | solution.py:117
  460.0 4.4 convolution_convert_fusion.4.grad_ref
  464.4 33.3 %shard_map.531 = bf16[2048,768]{1,0:T(8,128)(2,1)} custom-call(s32[8]{0:T(128)} %get-tuple-element.354.low_ref, s32[8]{0:T(128)} %get-tuple-element.353.high_ref, bf16[2048,768]{1,0:T(8,128)(2,1)} %add_convert_fusion.qkv_ref, bf16[2048,256]{1,0:T(8,128)(2,1)} %convolution_convert_fusion.4.grad_ref, f32[8,2048]{1,0:T(8,128)} %get-tuple-element.158.log_ref, ...), custom_call_target="tpu_custom_call" | custom-call | tf_op jit(solution)/shard_map/pallas_call | solution.py:1281
  497.7 7.1 %convolution_convert_fusion.1.refs_0_ = bf16[2048,1024]{1,0:T(8,128)(2,1)} fusion(bf16[2048,768]{1,0:T(8,128)(2,1)} %shard_map.531, bf16[1024,768]{1,0:T(8,128)(2,1)S(1)} %bitcast.191), kind=kOutput, calls=%fused_computation.46 | convolution fusion | flops 3223322624 | bytes 8912896 | tf_op jit(solution)/shard_map/tc,dc->td/dot_general | solution.py:1553
  504.8 2.1 convolution_convert_fusion.8
  508.1 5.1 convolution_convert_fusion.7
  513.2 52.3 %shard_map.532 = (bf16[4,512,256]{2,1,0:T(8,128)(2,1)}, f32[8,1024]{1,0:T(8,128)}, f32[128,1024]{1,0:T(8,128)}, f32[8,1024]{1,0:T(8,128)}, bf16[4,128,256]{2,1,0...) custom-call(bf16[2048,1024]{1,0:T(8,128)(2,1)} %convolution_convert_, ...), custom_call_target="tpu_custom_call" | custom-call | tf_op jit(solution)/shard_map/pallas_call | solution.py:117
  568.1 5.9 fusion.17
  574.6 2.0 fusion.19
  577.4 31.3 %shard_map.533 = (bf16[8,192,256]{2,1,0:T(8,128)(2,1)S(1)}, bf16[8,80,256]{2,1,0:T(8,128)(2,1)}) custom-call(bf16[8,192,256]{2,1,0:T(8,128)(2,1)} %bitcast.158, bf16[8,80,256]{2,1,0:T(8,128)(2,1)} %bitcast.146), custom_call_target="tpu_custom_call" | custom-call | tf_op jit(solution)/shard_map/pallas_call | solution.py:117
  609.8 11.5 %conditional.3 = ((f32[6284,256]{1,0:T(8,128)}, f32[8,256]{1,0:T(8,128)S(1)})) conditional(s32[]{:T(128)} %convert_element_type.135, (s32[]{:T(128)}, s32[8,192]{1,0:T(8,128)S(1)}, bf16[8,192,256]{2,1,0:T(8,128)(2,1)S(1)}) %tuple.78, (s32[512]{0:T(512)S(1)}, s32[16384]{0:T(1024)S(1)}, s32[]{:T(128)}, bf16[2048,256]{1,0:T(8,128)(2,1)}) %tuple.80), branch_computations={%region_13.15_spmd, %region_14.18_spmd} | conditional | flops 16242432 | bytes 50336844 | solution.py:1940
  610.5 10.6 %branch_0_fun.1 = (f32[6284,256]{1,0:T(8,128)}, f32[8,256]{1,0:T(8,128)S(1)}) custom-call(s32[1,1536]{1,0:T(1,128)} %sub.80.index_ref, bf16[1536,256]{1,0:T(8,128)(2,1)S(1)} %bitcast.157), custom_call_target="tpu_custom_call" | custom-call | tf_op jit(solution)/shard_map/cond/branch_0_fun/pallas_call | solution.py:1461
  621.3 1.3 concatenate.24.refs_0_
  623.3 17.0 %shard_map.534 = (f32[1,16,1024]{2,1,0:T(8,128)}, bf16[4,2,80,256]{3,2,1,0:T(8,128)(2,1)}) custom-call(f32[16,1024]{1,0:T(8,128)} %concatenate.24.refs_0_, bf16[80,256]{1,0:T(8,128)(2,1)} %convert_element_type.161.refs_1_), custom_call_target="tpu_custom_call" | custom-call | tf_op jit(solution)/shard_map/pallas_call | solution.py:117
  640.3 1.4 multiply_reduce_fusion.1
  643.8 17.4 %multiply_subtract_fusion = (f32[6284,256]{1,0:T(8,128)}, f32[6284,256]{1,0:T(8,128)}, f32[6284,256]{1,0:T(8,128)}) fusion(f32[6284,256]{1,0:T(8,128)} %param.41, f32[6284,256]{1,0:T(8,128)} %get-tuple-element.174, f32[]{:T(128)S(6)} %min_shard_map.3, f32[6284,256]{1,0:T(8,128)} %param.42, f32[6284,256]{1,0:T(8,128)} %param.43), kind=kLoop, calls=%fused_computation.35 | loop fusion | flops 25739264 | bytes 45043716 | tf_op jit(solution)/shard_map/sub | solution.py:59
  661.3 1.4 multiply_subtract_fusion.2
  664.8 1.5 multiply_subtract_fusion.5
  674.8 3.1 multiply_subtract_fusion.4
  679.5 2.6 multiply_subtract_fusion.3
  682.2 10.7 %multiply_subtract_fusion.1 = (f32[1024,1024]{1,0:T(8,128)}, f32[1024,1024]{1,0:T(8,128)}, f32[1024,1024]{1,0:T(8,128)}) fusion(f32[1024,1024]{1,0:T(8,128)} %head_ref.1, f32[]{:T(128)S(6)} %min_shard_map.3, f32[1024,1024]{1,0:T(8,128)} %param.60, f32[1024,1024]{1,0:T(8,128)} %param.61, bf16[64,1024]{1,0:T(8,128)(2,1)S(1)} %copy-done.44, ...), kind=kOutput, calls=%fused_computation.43 | convolution fusion | flops 822083584 | bytes 25559044 | tf_op jit(solution)/shard_map/dot_general | solution.py:34
  (177 shorter events, 42.1 us)
Async XLA Ops:
  15.9 44.6 %copy-start.11 = (f32[256,128]{0,1:T(8,128)}, f32[256,128]{0,1:T(8,128)S(1)}, u32[]{:S(2)}) copy-start(f32[256,128]{0,1:T(8,128)S(1)} %copy.132) | copy-start | bytes 393220
  59.7 0.6 copy-start.23
  60.5 7.7 %copy-start.16 = (f32[128,3,256]{2,0,1:T(8,128)S(1)}, f32[128,3,256]{2,0,1:T(8,128)}, u32[]{:S(2)}) copy-start(f32[128,3,256]{2,0,1:T(8,128)} %param.47) | copy-start | bytes 1179652
  67.0 40.1 %copy-start.31 = (s32[512]{0:T(512)S(1)}, s32[512]{0:T(512)}, u32[]{:S(2)}) copy-start(s32[512]{0:T(512)} %param.38) | copy-start | bytes 6148
  68.3 38.8 %copy-start.2 = (f32[128,3,256]{0,2,1:T(8,128)}, f32[128,3,256]{0,2,1:T(8,128)S(1)}, u32[]{:S(2)}) copy-start(f32[128,3,256]{0,2,1:T(8,128)S(1)} %copy.134) | copy-start | bytes 1179652
  144.5 16.1 %copy-start.29 = (f32[6,256]{1,0:T(8,128)S(1)}, f32[6,256]{1,0:T(8,128)}, u32[]{:S(2)}) copy-start(f32[6,256]{1,0:T(8,128)} %param.62) | copy-start | bytes 18436
  144.5 16.1 %copy-start.41 = (bf16[4,2,128,768]{3,2,1,0:T(8,128)(2,1)S(1)}, bf16[4,2,128,768]{3,2,1,0:T(8,128)(2,1)}, u32[]{:S(2)}) copy-start(bf16[4,2,128,768]{3,2,1,0:T(8,128)(2,1)} %get-tuple-element.139) | copy-start | bytes 4718596
  167.9 23.3 %copy-start.15 = (bf16[4,2,128,256]{3,2,1,0:T(8,128)(2,1)S(1)}, bf16[4,2,128,256]{3,2,1,0:T(8,128)(2,1)}, u32[]{:S(2)}) copy-start(bf16[4,2,128,256]{3,2,1,0:T(8,128)(2,1)} %get-tuple-element.141) | copy-start | bytes 1572868
  191.3 4.6 copy-start.7
  257.5 16.4 %copy-start.40 = (bf16[4,2,128,1024]{3,2,1,0:T(8,128)(2,1)S(1)}, bf16[4,2,128,1024]{3,2,1,0:T(8,128)(2,1)}, u32[]{:S(2)}) copy-start(bf16[4,2,128,1024]{3,2,1,0:T(8,128)(2,1)} %get-tuple-element.147) | copy-start | bytes 6291460
  273.9 9.2 %copy-start.35 = (s32[1,8]{1,0:T(1,128)S(1)}, s32[1,8]{1,0:T(1,128)}, u32[]{:S(2)}) copy-start(s32[1,8]{1,0:T(1,128)} %param.39) | copy-start | bytes 100
  370.7 8.8 %copy-start.9 = (bf16[4,2,128,1024]{3,2,1,0:T(8,128)(2,1)S(1)}, bf16[4,2,128,1024]{3,2,1,0:T(8,128)(2,1)}, u32[]{:S(2)}) copy-start(bf16[4,2,128,1024]{3,2,1,0:T(8,128)(2,1)} %get-tuple-element.145) | copy-start | bytes 6291460
  379.5 6.1 copy-start.37
  379.5 6.1 copy-start.39
  385.7 5.8 copy-start.1
  464.4 33.3 %copy-start.42 = (bf16[4,2,128,768]{3,2,1,0:T(8,128)(2,1)S(1)}, bf16[4,2,128,768]{3,2,1,0:T(8,128)(2,1)}, u32[]{:S(2)}) copy-start(bf16[4,2,128,768]{3,2,1,0:T(8,128)(2,1)} %get-tuple-element.139) | copy-start | bytes 4718596
  497.7 7.1 %copy-start.4 = (bf16[2048,256]{1,0:T(8,128)(2,1)S(1)}, bf16[2048,256]{1,0:T(8,128)(2,1)}, u32[]{:S(2)}) copy-start(bf16[2048,256]{1,0:T(8,128)(2,1)} %get-tuple-element.140) | copy-start | bytes 3145732
  497.7 7.1 %copy-start.38 = (bf16[2048,1024]{1,0:T(8,128)(2,1)S(1)}, bf16[2048,1024]{1,0:T(8,128)(2,1)}, u32[]{:S(2)}) copy-start(bf16[2048,1024]{1,0:T(8,128)(2,1)} %get-tuple-element.157) | copy-start | bytes 12582916
  504.8 2.1 copy-start
  504.8 3.3 copy-start.36
  574.6 35.2 %copy-start.24 = (s32[1,8,2,128]{3,1,2,0:T(8,128)S(1)}, s32[1,8,2,128]{3,1,2,0:T(8,128)}, u32[]{:S(2)}) copy-start(s32[1,8,2,128]{3,1,2,0:T(8,128)} %copy-done.23) | copy-start | bytes 24580
  609.8 11.5 %copy-start.27 = (f32[8,1024]{1,0:T(8,128)S(1)}, f32[8,1024]{1,0:T(8,128)}, u32[]{:S(2)}) copy-start(f32[8,1024]{1,0:T(8,128)} %get-tuple-element.166) | copy-start | bytes 98308
  609.8 11.5 %copy-start.28 = (f32[8,1024]{1,0:T(8,128)S(1)}, f32[8,1024]{1,0:T(8,128)}, u32[]{:S(2)}) copy-start(f32[8,1024]{1,0:T(8,128)} %get-tuple-element.165) | copy-start | bytes 98308
  609.8 11.5 %copy-start.30 = (f32[8,768]{1,0:T(8,128)S(1)}, f32[8,768]{1,0:T(8,128)}, u32[]{:S(2)}) copy-start(f32[8,768]{1,0:T(8,128)} %get-tuple-element.167) | copy-start | bytes 73732
  609.8 11.5 %copy-start.34 = (f32[8,256]{1,0:T(8,128)S(1)}, f32[8,256]{1,0:T(8,128)}, u32[]{:S(2)}) copy-start(f32[8,256]{1,0:T(8,128)} %get-tuple-element.168) | copy-start | bytes 24580
  643.7 17.5 %copy-start.20 = (bf16[4,2,80,256]{3,2,1,0:T(8,128)(2,1)S(1)}, bf16[4,2,80,256]{3,2,1,0:T(8,128)(2,1)}, u32[]{:S(2)}) copy-start(bf16[4,2,80,256]{3,2,1,0:T(8,128)(2,1)} %get-tuple-element.175) | copy-start | bytes 983044
  643.7 17.6 %copy-start.5 = (f32[514,256]{1,0:T(8,128)S(1)}, f32[514,256]{1,0:T(8,128)}, u32[]{:S(2)}) copy-start(f32[514,256]{1,0:T(8,128)} %refs_1_.1) | copy-start | bytes 1579012
  643.7 17.5 %copy-start.13 = (f32[514,256]{1,0:T(8,128)S(1)}, f32[514,256]{1,0:T(8,128)}, u32[]{:S(2)}) copy-start(f32[514,256]{1,0:T(8,128)} %param.45) | copy-start | bytes 1579012
  643.7 17.5 %copy-start.14 = (f32[514,256]{1,0:T(8,128)S(1)}, f32[514,256]{1,0:T(8,128)}, u32[]{:S(2)}) copy-start(f32[514,256]{1,0:T(8,128)} %param.46) | copy-start | bytes 1579012
  661.2 1.6 copy-start.19
  661.2 1.8 copy-start.17
  661.2 2.7 copy-start.18
  661.2 3.6 copy-start.3
  662.8 8.3 %copy-start.12 = (f32[256,128]{0,1:T(8,128)S(1)}, f32[256,128]{0,1:T(8,128)}, u32[]{:S(2)}) copy-start(f32[256,128]{0,1:T(8,128)} %copy-done.11) | copy-start | bytes 393220
  662.8 8.3 %copy-start.22 = (f32[128,256]{1,0:T(8,128)S(1)}, f32[128,256]{1,0:T(8,128)}, u32[]{:S(2)}) copy-start(f32[128,256]{1,0:T(8,128)} %get-tuple-element.177) | copy-start | bytes 393220
  664.8 10.0 %copy-start.6 = (f32[128,4,256]{2,1,0:T(4,128)S(1)}, f32[128,4,256]{2,1,0:T(4,128)}, u32[]{:S(2)}) copy-start(f32[128,4,256]{2,1,0:T(4,128)} %param.53) | copy-start | bytes 1572868
  671.9 7.5 %copy-start.8 = (f32[4,256,128]{2,1,0:T(8,128)S(1)}, f32[4,256,128]{2,1,0:T(8,128)}, u32[]{:S(2)}) copy-start(f32[4,256,128]{2,1,0:T(8,128)} %param.56) | copy-start | bytes 1572868
  674.8 7.3 %copy-start.43 = (f32[64,1024]{1,0:T(8,128)S(1)}, f32[64,1024]{1,0:T(8,128)}, u32[]{:S(2)}) copy-start(f32[64,1024]{1,0:T(8,128)} %get-tuple-element.181) | copy-start | bytes 786436
  674.8 7.3 %copy-start.44 = (bf16[64,1024]{1,0:T(8,128)(2,1)S(1)}, bf16[64,1024]{1,0:T(8,128)(2,1)}, u32[]{:S(2)}) copy-start(bf16[64,1024]{1,0:T(8,128)(2,1)} %get-tuple-element.180) | copy-start | bytes 393220
  682.1 10.7 %copy-start.32 = (f32[6,256]{1,0:T(8,128)S(1)}, f32[6,256]{1,0:T(8,128)}, u32[]{:S(2)}) copy-start(f32[6,256]{1,0:T(8,128)} %param.63) | copy-start | bytes 18436
  682.1 10.7 %copy-start.33 = (f32[6,256]{1,0:T(8,128)S(1)}, f32[6,256]{1,0:T(8,128)}, u32[]{:S(2)}) copy-start(f32[6,256]{1,0:T(8,128)} %param.64) | copy-start | bytes 18436
  682.1 11.4 %copy-start.10 = (f32[8,1024]{1,0:T(8,128)S(1)}, f32[8,1024]{1,0:T(8,128)}, u32[]{:S(2)}) copy-start(f32[8,1024]{1,0:T(8,128)} %refs_3_.3) | copy-start | bytes 98308
  682.1 11.4 %copy-start.21 = (f32[1,16,1024]{2,1,0:T(8,128)S(1)}, f32[1,16,1024]{2,1,0:T(8,128)}, u32[]{:S(2)}) copy-start(f32[1,16,1024]{2,1,0:T(8,128)} %get-tuple-element.173) | copy-start | bytes 196612
  682.1 11.4 %copy-start.25 = (f32[8,1024]{1,0:T(8,128)S(1)}, f32[8,1024]{1,0:T(8,128)}, u32[]{:S(2)}) copy-start(f32[8,1024]{1,0:T(8,128)} %param.66) | copy-start | bytes 98308
  682.1 11.3 %copy-start.26 = (f32[8,1024]{1,0:T(8,128)S(1)}, f32[8,1024]{1,0:T(8,128)}, u32[]{:S(2)}) copy-start(f32[8,1024]{1,0:T(8,128)} %param.67) | copy-start | bytes 98308

commit v5 on v4

--- a/solution.py
+++ b/solution.py
@@ -63,7 +63,7 @@
 
 
 MESH_IDS = pl.DeviceIdType.MESH
-VMEM_BYTES = 60 * 1024 * 1024
+SPARE_BYTES = 6 * 1024 * 1024
 CHUNKS = 4
 LINE = 4
 
@@ -91,9 +91,23 @@
     )
 
 
-def comm_params(collective):
+def room(*items):
+    total = 0
+    for item in items:
+        size = 0
+        if item.dtype == jnp.bfloat16:
+            size = 2
+        elif item.dtype == jnp.float32 or item.dtype == jnp.int32:
+            size = 4
+        for extent in item.shape[:-1]:
+            size = size * extent
+        total = total + size * (-(-item.shape[-1] // 128) * 128)
+    return total + SPARE_BYTES
+
+
+def comm_params(collective, limit):
     return pltpu.CompilerParams(
-        collective_id=collective, has_side_effects=True, vmem_limit_bytes=VMEM_BYTES
+        collective_id=collective, has_side_effects=True, vmem_limit_bytes=limit
     )
 
 
@@ -112,7 +126,10 @@
         for task in tasks:
             task.middle()
         for task in tasks:
+            task.late()
+        for task in tasks[1:]:
             task.end()
+        tasks[0].end()
 
     results = pl.pallas_call(
         kernel,
@@ -120,7 +137,10 @@
         in_specs=[in_vmem() for task in tasks for _ in task.ins],
         out_specs=[in_vmem() for task in tasks for _ in task.outs],
         scratch_shapes=[item for task in tasks for item in task.scratch],
-        compiler_params=comm_params(collective),
+        compiler_params=comm_params(
+            collective,
+            room(*[item for task in tasks for item in task.ins + task.outs + task.scratch]),
+        ),
     )(*[array for task in tasks for array in task.ins])
     return results[0] if len(results) == 1 else results
 
@@ -144,6 +164,9 @@
         pass
 
     def middle(self):
+        pass
+
+    def late(self):
         pass
 
     def end(self):
@@ -407,7 +430,7 @@
         self.outs = (shaped(parts.shape, jnp.bfloat16), own, own)
         self.scratch = self.fold_scratch + self.relay_scratch()
 
-    def end(self):
+    def late(self):
         p_ref, residual_ref, row_ref = self.ins_refs
         all_ref, sum_ref, norm_ref = self.outs_refs
         for part in range(self.chunks):
@@ -417,6 +440,8 @@
             norm = norm_rows(total, row_ref[1:2], row_ref[4:5])
             norm_ref[local] = norm
             self.relay_open(part, norm.astype(jnp.bfloat16))
+
+    def end(self):
         self.relay_close()
         self.settle_fold()
 
@@ -429,7 +454,7 @@
         self.outs = (shaped(parts.shape, jnp.bfloat16), own, shaped((8, self.depth), jnp.float32))
         self.scratch = self.fold_scratch + self.relay_scratch()
 
-    def end(self):
+    def late(self):
         p_ref, residual_ref, value_ref, row_ref = self.ins_refs
         all_ref, grad_ref, side_ref = self.outs_refs
         side_ref[...] = jnp.zeros_like(side_ref)
@@ -444,6 +469,8 @@
             side_ref[0:1] += gain
             side_ref[1:2] += shift
             side_ref[2:3] += jnp.sum(low.astype(jnp.float32), axis=0, keepdims=True)
+
+    def end(self):
         self.relay_close()
         self.settle_fold()
 
@@ -638,7 +665,7 @@
         me = lax.axis_index("tensor")
         return [{"tensor": lax.rem(me + step, self.width)} for step in range(1, self.width)]
 
-    def end(self):
+    def late(self):
         p_ref, residual_ref, value_ref, row_ref = self.ins_refs
         cols_ref, side_ref = self.outs_refs
         buf, send, recv = self.scratch_refs[-3:]
@@ -669,7 +696,10 @@
             cols_ref[me, local] = buf[local, lanes(me)]
             side_ref[0:1] += gain
             side_ref[1:2] += shift
-        for copy in copies:
+        self.copies = copies
+
+    def end(self):
+        for copy in self.copies:
             copy.wait()
         self.settle_fold()
 
@@ -812,9 +842,9 @@
         self.task.end()
 
 
-def reduce_grid(blocks):
+def reduce_grid(blocks, **form):
     first = ReduceCross(blocks)
-    return Chain(first, ReduceLine(first.outs[0]))
+    return Chain(first, ReduceLine(first.outs[0], **form))
 
 
 def spread_grid(block):
@@ -823,12 +853,14 @@
 
 
 class SpreadCross(GridTask):
-    def __init__(self, blocks):
+    def __init__(self, *pieces):
         super().__init__()
-        self.ins = (blocks,)
-        self.outs = (shaped((LINE, self.cross) + blocks.shape[1:], blocks.dtype),)
+        self.ins = pieces
+        self.tall, depth = pieces[0].shape[1:]
+        count = len(pieces)
+        self.outs = (shaped((LINE, self.cross, self.tall * count, depth), pieces[0].dtype),)
         others = max(self.cross - 1, 1)
-        self.scratch = (dma(others, LINE), dma(others, LINE))
+        self.scratch = (dma(others, LINE, count), dma(others, LINE, count))
 
     def partners(self):
         line, cross = self.place()
@@ -838,16 +870,24 @@
         ]
 
     def begin(self):
-        (x_ref,), (o_ref,), (send, recv) = self.ins_refs, self.outs_refs, self.scratch_refs
+        (o_ref,), (send, recv) = self.outs_refs, self.scratch_refs
         line, cross = self.place()
         self.copies = []
-        for i, partner in enumerate(self.partners()):
+        for p, x_ref in enumerate(self.ins_refs):
+            rows = pl.ds(p * self.tall, self.tall)
+            for i, partner in enumerate(self.partners()):
+                for z in range(LINE):
+                    copy = remote(
+                        x_ref.at[z],
+                        o_ref.at[z, cross, rows],
+                        send.at[i, z, p],
+                        recv.at[i, z, p],
+                        partner,
+                    )
+                    copy.start()
+                    self.copies.append(copy)
             for z in range(LINE):
-                copy = remote(x_ref.at[z], o_ref.at[z, cross], send.at[i, z], recv.at[i, z], partner)
-                copy.start()
-                self.copies.append(copy)
-        for z in range(LINE):
-            o_ref[z, cross] = x_ref[z]
+                o_ref[z, cross, rows] = x_ref[z]
 
     def end(self):
         for copy in self.copies:
@@ -908,11 +948,15 @@
 
 
 class ReduceLine(GridTask):
-    def __init__(self, blocks):
+    def __init__(self, blocks, slabs=1, turned=False):
         super().__init__()
         shape = blocks.shape[1:]
+        self.slabs, self.turned = slabs, turned
         self.ins = (blocks,)
-        self.outs = (shaped(shape, jnp.float32), shaped((8, shape[1]), jnp.float32))
+        result = shape[::-1] if turned else shape
+        if slabs > 1:
+            result = (slabs, shape[0], shape[1] // slabs)
+        self.outs = (shaped(result, jnp.float32), shaped((8, shape[1]), jnp.float32))
         self.scratch = (pltpu.VMEM((LINE - 1,) + shape, jnp.bfloat16), dma(LINE - 1), dma(LINE - 1))
 
     def targets(self):
@@ -944,8 +988,15 @@
         total = x_ref[line].astype(jnp.float32)
         for i in range(LINE - 1):
             total = total + buf[i].astype(jnp.float32)
-        o_ref[...] = total
         square_ref[...] = eight_rows(total * total)
+        if self.turned:
+            o_ref[...] = total.T
+        elif self.slabs > 1:
+            narrow = total.shape[1] // self.slabs
+            for slab in range(self.slabs):
+                o_ref[slab] = total[:, slab * narrow : (slab + 1) * narrow]
+        else:
+            o_ref[...] = total
 
 
 class SumAll(Task):
@@ -1180,7 +1231,7 @@
             pltpu.VMEM((columns, slots), jnp.bfloat16),
             pltpu.VMEM((pairs, REACH, K_BLOCK, 2 * Q_BLOCK), jnp.float32),
         ],
-        compiler_params=pltpu.CompilerParams(vmem_limit_bytes=VMEM_BYTES),
+        compiler_params=pltpu.CompilerParams(vmem_limit_bytes=20 * 1024 * 1024),
     )(bounds[0], bounds[1], qkv_out, seq_ids[:, None], jnp.broadcast_to(seq_ids[None], (8, slots)))
 
 
@@ -1290,7 +1341,7 @@
             pltpu.VMEM((slots, columns), jnp.float32),
             pltpu.VMEM((slots, columns), jnp.float32),
         ],
-        compiler_params=pltpu.CompilerParams(vmem_limit_bytes=VMEM_BYTES),
+        compiler_params=pltpu.CompilerParams(vmem_limit_bytes=36 * 1024 * 1024),
     )(
         bounds[0],
         bounds[1],
@@ -1343,7 +1394,7 @@
             pl.BlockSpec((tall, units), lambda i: (i, 0)),
             pl.BlockSpec((tall, units), lambda i: (i, 0)),
         ],
-        compiler_params=pltpu.CompilerParams(vmem_limit_bytes=VMEM_BYTES),
+        compiler_params=pltpu.CompilerParams(vmem_limit_bytes=16 * 1024 * 1024),
     )(rows, weight, bias)
 
 
@@ -1425,7 +1476,7 @@
             pltpu.VMEM((EMBED_ROWS, depth), jnp.float32),
             pltpu.VMEM((EMBED_ROWS, depth), jnp.float32),
         ],
-        compiler_params=pltpu.CompilerParams(vmem_limit_bytes=VMEM_BYTES),
+        compiler_params=pltpu.CompilerParams(vmem_limit_bytes=28 * 1024 * 1024),
     )(
         starts,
         spans,
@@ -1470,7 +1521,7 @@
             pl.BlockSpec((SCATTER_ROWS, width), lambda i: (i, 0)),
             pl.BlockSpec((8, width), lambda i: (0, 0)),
         ],
-        compiler_params=pltpu.CompilerParams(vmem_limit_bytes=VMEM_BYTES),
+        compiler_params=pltpu.CompilerParams(vmem_limit_bytes=20 * 1024 * 1024),
     )(index[None], rows)
 
 
@@ -1543,7 +1594,7 @@
     branch_all, grad_first, side_b, _, down_sum, down_squares, up_half = exchange(
         11,
         FoldPullSpread(second_back, grad_second, first_sum, row_params),
-        reduce_grid(down_grad),
+        reduce_grid(down_grad, turned=True),
         Later(ReduceCross(up_grad)),
     )
     out_grad = turned_grad(branch_all, attn_low)
@@ -1557,8 +1608,8 @@
         13,
         FoldPullSwap(first_back, grad_first, emb_rows, row_params),
         ReduceLine(up_half),
-        reduce_grid(out_grad),
-        reduce_grid(qkv_grad),
+        reduce_grid(out_grad, turned=True),
+        reduce_grid(qkv_grad, slabs=3),
     )
     qkv_cols = jnp.sum(qkv_low.astype(jnp.float32), axis=0).reshape(3, col_width)
     up_cols = jnp.sum(up_low.astype(jnp.float32), axis=0).reshape(-1, col_width)
@@ -1584,7 +1635,7 @@
     )
 
 
-def plan_kernel(capacity, vocab_local, groups, perm_ref, low_ref, high_ref, slot_ref, ask_ref, id_buf, own_buf):
+def plan_kernel(capacity, vocab_local, groups, perm_ref, low_ref, high_ref, pair_ref, slot_ref, ask_ref, id_buf, own_buf):
     slots = perm_ref.shape[1]
     table_rows = low_ref.shape[1]
     block = 128
@@ -1669,10 +1720,11 @@
         for row in range(list_rows):
             first_lane = group * stride + row * 128
             ask_ref[group, row : row + 1] = listed[:, first_lane : first_lane + 128]
-        ask_ref[group, list_rows:] = jnp.broadcast_to(most, (8 - list_rows, 128))
-
-
-def make_plan(perm, all_ids, capacity, vocab_local, groups):
+        ask_ref[group, list_rows : list_rows + 1] = pair_ref[...]
+        ask_ref[group, list_rows + 1 :] = jnp.broadcast_to(most, (7 - list_rows, 128))
+
+
+def make_plan(perm, all_ids, pair_row, capacity, vocab_local, groups):
     slots = perm.shape[0]
     table = all_ids.reshape(-1, 128).T
     high = table // 256
@@ -1683,11 +1735,11 @@
             jax.ShapeDtypeStruct((1, slots), jnp.int32),
             jax.ShapeDtypeStruct((groups, 8, 128), jnp.int32),
         ],
-        in_specs=[in_vmem()] * 3,
+        in_specs=[in_vmem()] * 4,
         out_specs=[in_vmem()] * 2,
         scratch_shapes=[pltpu.VMEM((slots, 128), jnp.float32), pltpu.VMEM((slots, 128), jnp.float32)],
-        compiler_params=pltpu.CompilerParams(vmem_limit_bytes=VMEM_BYTES),
-    )(perm[None], low.astype(jnp.bfloat16), high.astype(jnp.bfloat16))
+        compiler_params=pltpu.CompilerParams(vmem_limit_bytes=16 * 1024 * 1024),
+    )(perm[None], low.astype(jnp.bfloat16), high.astype(jnp.bfloat16), pair_row)
 
 
 def loss_kernel(pooled_ref, head_ref, pair_ref, loss_ref, low_ref, grad_ref, back_ref):
@@ -1757,7 +1809,7 @@
         ],
         in_specs=[in_vmem()] * 3,
         out_specs=[in_vmem()] * 4,
-        compiler_params=pltpu.CompilerParams(vmem_limit_bytes=VMEM_BYTES),
+        compiler_params=pltpu.CompilerParams(vmem_limit_bytes=20 * 1024 * 1024),
     )(pooled, head_weight, pairs[:, None])
 
 
@@ -1808,40 +1860,37 @@
     column_start = tensor_index * col_width
     anchors = pair_index.shape[0]
     id_rows = tok_dev // 128
-    block = jnp.concatenate(
-        [
-            token_ids.reshape(id_rows, 128),
-            jnp.pad(pair_index, (0, 128 - anchors))[None],
-            jnp.zeros((7 - id_rows, 128), jnp.int32),
-        ],
-        axis=0,
-    )
-    perm_block = jnp.pad(slot_perm.reshape(id_rows, 128), ((0, 8 - id_rows), (0, 0)))
-    qkv_low = query_key_value_weight.astype(jnp.bfloat16).reshape(-1, 3 * col_width)
+    pair_row = jnp.pad(pair_index, (0, 128 - anchors))[None]
+    qkv_low = jnp.concatenate(
+        [query_key_value_weight[:, third] for third in range(3)], axis=1
+    ).astype(jnp.bfloat16)
     out_low = out_weight.T.astype(jnp.bfloat16)
     up_low = up_weight.astype(jnp.bfloat16).reshape(qkv_low.shape[0], -1)
     down_low = down_weight.reshape(-1, down_weight.shape[2]).T.astype(jnp.bfloat16)
-    gathered, perms, out_half = exchange(
-        1, GatherAll(block), Gather(perm_block, "tensor"), SpreadLine(out_low)
-    )
-    all_ids = gathered[:, :id_rows].reshape(-1)
-    pairs = gathered[::tensor_count, id_rows, :anchors].reshape(-1)
-    own_perm = perms[:, :id_rows].reshape(-1)
-    slot, request = make_plan(own_perm, all_ids, CAPACITY, vocab_local, groups)
+    half = qkv_low.shape[0] // 2
+    gathered, perms, qkv_first_half = exchange(
+        1,
+        GatherAll(token_ids.reshape(id_rows, 128)),
+        Gather(slot_perm.reshape(id_rows, 128), "tensor"),
+        SpreadLine(qkv_low[:half]),
+    )
+    all_ids = gathered.reshape(-1)
+    own_perm = perms.reshape(-1)
+    slot, request = make_plan(own_perm, all_ids, pair_row, CAPACITY, vocab_local, groups)
     slot = slot[0]
     list_rows = -(-CAPACITY // 128)
     asked = exchange(2, Swap(request, "dp"))
-    overflow = jnp.max(asked[:, list_rows]) > CAPACITY
+    pairs = asked[:, list_rows, :anchors].reshape(-1)
+    overflow = jnp.max(asked[:, list_rows + 1]) > CAPACITY
     offset = group_index * vocab_local
     asked_rows = asked[:, :list_rows].reshape(groups, -1)[:, :CAPACITY].reshape(-1) - offset
     asked_safe = jnp.clip(asked_rows, 0, vocab_local - 1)
     sent_rows = jnp.take(tok_table, asked_safe, axis=0).astype(jnp.bfloat16)
-    got_rows, pos_full, qkv_half, out_full = exchange(
+    got_rows, pos_full, qkv_second_half = exchange(
         3,
         Swap(sent_rows.reshape(groups, CAPACITY, col_width), "dp"),
         Spread(pos_table, columns=True, chunks=1),
-        SpreadLine(qkv_low),
-        SpreadCross(out_half),
+        SpreadLine(qkv_low[half:]),
     )
     got_rows = got_rows.reshape(-1, col_width)
 
@@ -1875,10 +1924,11 @@
         spread_wide,
         lambda: multiply_arrays(chooser(slot), got_rows).astype(jnp.bfloat16),
     )
-    tok_all, qkv_full, up_half = exchange(
+    tok_all, _, out_full, qkv_full, up_half = exchange(
         4,
         Spread(tok_cols, columns=True),
-        SpreadCross(qkv_half),
+        spread_grid(out_low),
+        SpreadCross(qkv_first_half, qkv_second_half),
         SpreadLine(up_low),
     )
     layer_mats = (qkv_full.reshape(D, -1), out_full.reshape(D, -1), up_half, down_low)
@@ -1913,12 +1963,11 @@
         cols_grad,
         preferred_element_type=jnp.float32,
     )
-    back_rows, shared_parts = exchange(
+    back_rows, _, shared_own, shared_squares = exchange(
         15,
         Swap(merged.astype(jnp.bfloat16).reshape(groups, CAPACITY, col_width), "dp"),
-        Swap(shared.astype(jnp.bfloat16).reshape(groups, shared_rows, col_width), "dp"),
-    )
-    shared_own = jnp.sum(shared_parts.astype(jnp.float32), axis=0)
+        reduce_grid(shared.astype(jnp.bfloat16).reshape(groups, shared_rows, col_width)),
+    )
 
     def add_wide():
         wanted = every_slot_id() - offset
@@ -1942,10 +1991,9 @@
         add_wide,
         lambda: tuple(scatter_rows(asked_rows, back_rows.reshape(-1, col_width), vocab_local)),
     )
-    qkv_grad = qkv_sum.reshape(query_key_value_weight.shape)
-    out_grad = lax.optimization_barrier(out_sum.T)
     up_grad = up_sum.reshape(up_weight.shape)
-    down_grad = lax.optimization_barrier(down_sum.T.reshape(down_weight.shape))
+    down_grad = down_sum.reshape(down_weight.shape)
+
     def widen(*parts):
         joined = jnp.concatenate(parts, axis=1)
         return jnp.pad(joined, ((0, 0), (0, D - joined.shape[1])))
@@ -1953,7 +2001,7 @@
     square_rows = (
         widen(wide_squares)
         + widen(qkv_squares, out_squares)
-        + widen(tok_squares, eight_rows(shared_own * shared_own))
+        + widen(tok_squares, shared_squares)
     )
     row_block = jnp.concatenate([row_grad, square_rows], axis=0)
     row_total, shared_sum = exchange(16, SumAll(row_block, False), GatherGrid(shared_own.astype(jnp.bfloat16)))
@@ -1972,15 +2020,16 @@
         pos_table, pos_first, pos_second, pos_own * clip_scale, RATE_MATRIX, DECAY_RATE
     )
     qkv_new = adam_step(
-        query_key_value_weight,
-        qkv_first,
-        qkv_second,
-        qkv_grad * clip_scale,
+        query_key_value_weight.swapaxes(0, 1),
+        qkv_first.swapaxes(0, 1),
+        qkv_second.swapaxes(0, 1),
+        qkv_sum * clip_scale,
         RATE_MATRIX,
         DECAY_RATE,
     )
+    qkv_new = tuple(item.swapaxes(0, 1) for item in qkv_new)
     out_new = adam_step(
-        out_weight, out_first, out_second, out_grad * clip_scale, RATE_MATRIX, DECAY_RATE
+        out_weight, out_first, out_second, out_sum * clip_scale, RATE_MATRIX, DECAY_RATE
     )
     up_new = adam_step(
         up_weight, up_first, up_second, up_grad * clip_scale, RATE_MATRIX, DECAY_RATE

time: 710 us -> 621 us (0.87)
  Pallas kernels: 512 us -> 454 us
  matrix products: 87.4 us -> 73.4 us
  local copies, waits for them, and re-layouts: 38.8 us -> 27 us
    pallas_call x11, Pallas kernels: 396 us -> 357 us  [exchange(): pl.pallas_call(kernel, out_shape=[out for task in tasks for out in task.o...]
    dot_general x5, matrix products: 25.7 us -> 17.2 us  [multiply_arrays(): return jnp.dot(left_mat, right_mat, preferred_element_type=jnp.float32)]
    sub x8 -> x7, other arithmetic: 27.5 us -> 22.6 us  [adam_step(): weight - step_rate * (first_hat / (jnp.sqrt(second_hat) + ADAM_EPS) + dec...]
where the time goes in v5:
time: 621 us; the launch traced here: 614 us
  Pallas kernels  454 us (73%)
  matrix products  73.4 us (12%)
  other arithmetic  39.1 us (6%)
  local copies, waits for them, and re-layouts  27 us (4%)
  between operations  19.4 us (3%)
    pallas_call x11, Pallas kernels, exchange(): pl.pallas_call(kernel, out_shape=[out for task in tasks for out in task.o...  357 us
    pallas_call x1, Pallas kernels, attend_back(): pl.pallas_call(attend_back_kernel, out_shape=jax.ShapeDtypeStruct(qkv_out...  29.8 us
    sub x7, other arithmetic, adam_step(): weight - step_rate * (first_hat / (jnp.sqrt(second_hat) + ADAM_EPS) + dec...  22.6 us
    pallas_call x1, Pallas kernels, attend(): pl.pallas_call(attend_kernel, out_shape=[jax.ShapeDtypeStruct((slots, col...  20 us
    dot_general x4, matrix products, turned_grad(): jnp.einsum('td,tc->dc', left_all, right_all, preferred_element_type=jnp.f...  17.5 us
    dot_general x5, matrix products, multiply_arrays(): return jnp.dot(left_mat, right_mat, preferred_element_type=jnp.float32)  17.2 us
    unnamed x176, local copies, waits for them, and re-layouts  13.1 us
    pallas_call x1, Pallas kernels, expand(): pl.pallas_call(expand_kernel, grid=(slots // tall,), out_shape=[shaped((s...  12.7 us

profile of v5, /device:TPU:0, one launch (start us, length us, event | category | flops | bytes accessed | tf_op | source)
XLA Modules:
  0.0 613.6 jit_solution(12173713393020116949)
XLA Ops:
  8.7 1.2 bitcast_subtract_fusion.2.start_ref
  15.9 1.6 copy.85
  22.5 17.8 %shard_map.518 = (s32[32,4,128]{2,1,0:T(4,128)S(1)}, s32[4,4,128]{2,1,0:T(4,128)S(1)}, bf16[4,64,768]{2,1,0:T(8,128)(2,1)S(1)}) custom-call(s32[4,128]{1,0:T(4,128)S(1)} %bitcast.181, s32[4,128]{1,0:T(4,128)S(1)} %bitcast.204, bf16[64,768]{1,0:T(8,128)(2,1)S(1)} %get-tuple-element.220.refs_2_), custom_call_target="tpu_custom_call" | custom-call | tf_op jit(solution)/shard_map/pallas_call | solution.py:134
  41.3 10.1 %shard_map.519 = (s32[1,2048]{1,0:T(1,128)}, s32[8,8,128]{2,1,0:T(8,128)S(1)}) custom-call(s32[1,2048]{1,0:T(1,128)S(1)} %bitcast.180, bf16[128,128]{1,0:T(8,128)(2,1)S(1)} %get-tuple-element.225.low_ref, bf16[128,128]{1,0:T(8,128)(2,1)S(1)} %get-tuple-element.224.high_ref, s32[1,128]{1,0:T(1,128)S(1)} %pad_bitcast_fusion.pair_ref), custom_call_target="tpu_custom_call" | custom-call | tf_op jit(solution)/shard_map/pallas_call | solution.py:1732
  51.4 7.4 %shard_map.520 = s32[8,8,128]{2,1,0:T(8,128)S(1)} custom-call(s32[8,8,128]{2,1,0:T(8,128)S(1)} %get-tuple-element.132.refs_0_), custom_call_target="tpu_custom_call" | custom-call | tf_op jit(solution)/shard_map/pallas_call | solution.py:134
  61.0 6.5 %gather_fusion.3 = bf16[1536,256]{1,0:T(8,128)(2,1)S(1)} fusion(f32[6284,256]{1,0:T(8,128)} %param.41, s32[2048]{0:T(1024)S(1)} %pad_clamp_fusion), kind=kCustom, calls=%fused_computation.3 | custom fusion | bytes 1579008 | tf_op jit(solution)/shard_map/jit(_take)/gather | solution.py:1888
  68.2 28.3 %shard_map.521 = (bf16[8,192,256]{2,1,0:T(8,128)(2,1)S(1)}, f32[514,1024]{1,0:T(8,128)S(1)}, bf16[4,64,768]{2,1,0:T(8,128)(2,1)S(1)}) custom-call(bf16[8,192,256]{2,1,0:T(8,128)(2,1)S(1)} %select_convert_fusion.refs_0_, f32[514,256]{1,0:T(8,128)S(1)} %copy-done.7, bf16[64,768]{1,0:T(8,128)(2,1)S(1)} %get-tuple-element.219.refs_2_), custom_call_target="tpu_custom_call" | custom-call | tf_op jit(solution)/shard_map/pallas_call | solution.py:134
  96.4 1.3 copy-done.5
  98.5 4.2 conditional.2
  98.5 4.0 fusion.2
  105.6 32.3 %shard_map.522 = (bf16[2048,1024]{1,0:T(8,128)(2,1)S(1)}, bf16[4,128,256]{2,1,0:T(8,128)(2,1)}, bf16[4,2,128,256]{3,2,1,0:T(8,128)(2,1)S(1)}, bf16[4,2,128,768]{...) custom-call(bf16[2048,256]{1,0:T(8,128)(2,1)} %get-tuple-element.250.refs_0_, bf16[128,256]{1,0:T(8,128)(2,1)S(1)} %bitcast.178, ...), custom_call_target="tpu_custom_call" | custom-call | tf_op jit(solution)/shard_map/pallas_call | solution.py:134
  139.4 8.8 %shard_map.523 = (bf16[2048,1024]{1,0:T(8,128)(2,1)S(1)}, f32[512,1024]{1,0:T(8,128)S(1)}, f32[512,1024]{1,0:T(8,128)S(1)}) custom-call(s32[8]{0:T(128)S(1)} %copy-done.46, s32[2,16]{1,0:T(2,128)S(1)} %copy-done.44, s32[1]{0:T(128)} %bitcast.15.own_ref, bf16[2048,1024]{1,0:T(8,128)(2,1)S(1)} %get-tuple-element.137.tok_ref, f32[514,1024]{1,0:T(8,128)S(1)} %copy-done.6, ...), custom_call_target="tpu_custom_call" | custom-call | tf_op jit(solution)/shard_map/pallas_call | solution.py:1465
  148.2 3.6 add_convert_fusion.qkv_ref
  151.9 20.0 %shard_map.524 = (bf16[2048,256]{1,0:T(8,128)(2,1)S(1)}, f32[8,2048]{1,0:T(8,128)S(1)}) custom-call(s32[8]{0:T(128)S(1)} %copy-done.42, s32[8]{0:T(128)S(1)} %copy-done.40, bf16[2048,768]{1,0:T(8,128)(2,1)S(1)} %add_convert_fusion.qkv_ref, s32[2048,1]{1,0:T(8,128)S(1)} %copy.86.seq_ref.seq_col_ref, s32[8,2048]{1,0:T(8,128)S(1)} %broadcast_in_dim.150.seq_row_ref), custom_call_target="tpu_custom_call" | custom-call | tf_op jit(solution)/shard_map/pallas_call | solution.py:1222
  172.6 1.3 convolution_convert_fusion.refs_0_
  173.9 54.9 %shard_map.525 = (bf16[2048,1024]{1,0:T(8,128)(2,1)S(1)}, f32[512,1024]{1,0:T(8,128)S(1)}, f32[512,1024]{1,0:T(8,128)S(1)}, bf16[4,2,128,1024]{3,2,1,0:T(8,128)(...) custom-call(bf16[2048,1024]{1,0:T(8,128)(2,1)S(1)} %convolution_convert_fusion.refs_0_, ...), custom_call_target="tpu_custom_call" | custom-call | tf_op jit(solution)/shard_map/pallas_call | solution.py:134
  228.9 1.3 copy-done.49
  230.2 12.7 %shard_map.526 = (bf16[2048,1024]{1,0:T(8,128)(2,1)S(1)}, f32[2048,1024]{1,0:T(8,128)S(1)}) custom-call(bf16[2048,1024]{1,0:T(8,128)(2,1)S(1)} %get-tuple-element.145.rows_ref, bf16[1024,1024]{1,0:T(8,128)(2,1)S(1)} %bitcast.165, f32[1,1024]{1,0:T(1,128)S(1)} %bitcast.179), custom_call_target="tpu_custom_call" | custom-call | tf_op jit(solution)/shard_map/pallas_call | solution.py:1384
  242.9 6.8 %convolution_convert_fusion.3.refs_0_ = bf16[2048,1024]{1,0:T(8,128)(2,1)S(1)} fusion(bf16[2048,1024]{1,0:T(8,128)(2,1)S(1)} %get-tuple-element.147, bf16[1024,1024]{1,0:T(8,128)(2,1)} %bitcast.182), kind=kOutput, calls=%fused_computation.48 | convolution fusion | flops 4297064448 | bytes 10485760 | tf_op jit(solution)/shard_map/tf,df->td/dot_general | solution.py:1545
  249.8 38.7 %shard_map.527 = (f32[512,1024]{1,0:T(8,128)S(1)}, f32[8,8,1024]{2,1,0:T(8,128)S(1)}) custom-call(bf16[2048,1024]{1,0:T(8,128)(2,1)S(1)} %convolution_convert_fusion.3.refs_0_, f32[512,1024]{1,0:T(8,128)S(1)} %get-tuple-element.149.refs_1_, bf16[8,512]{1,0:T(8,128)(2,1)S(1)} %get-tuple-element.235.refs_2_, f32[8,1]{1,0:T(8,128)S(1)} %convert_element_type.141.refs_3_.refs_1_, ...), custom_call_target="tpu_custom_call" | custom-call | tf_op jit(solution)/shard_map/pallas_call | solution.py:134
  288.6 4.9 shard_map.528
  294.1 27.6 %shard_map.529 = (bf16[2048,1024]{1,0:T(8,128)(2,1)S(1)}, f32[512,1024]{1,0:T(8,128)S(1)}, f32[8,1024]{1,0:T(8,128)S(1)}) custom-call(f32[64,1024]{1,0:T(8,128)S(1)} %get-tuple-element.152.refs_0_, f32[8,1]{1,0:T(8,128)S(1)} %convert_element_type.141.refs_3_.refs_1_, bf16[512,24]{1,0:T(8,128)(2,1)S(1)} %copy-done.25, ...), custom_call_target="tpu_custom_call" | custom-call | tf_op jit(solution)/shard_map/pallas_call | solution.py:134
  321.8 1.3 copy-done.16
  323.1 6.0 fusion.66
  329.1 5.8 convolution_convert_fusion.6
  334.9 6.0 convolution_convert_fusion.5
  340.9 9.6 %convolution_convert_fusion.2.refs_0_ = bf16[2048,1024]{1,0:T(8,128)(2,1)} fusion(bf16[2048,1024]{1,0:T(8,128)(2,1)} %get-tuple-element.243, bf16[1024,1024]{1,0:T(8,128)(2,1)} %bitcast.166), kind=kOutput, calls=%fused_computation.47 | convolution fusion | flops 4297064448 | bytes 10485760 | tf_op jit(solution)/shard_map/tf,df->td/dot_general | solution.py:1591
  350.5 57.4 %shard_map.530 = (bf16[2048,1024]{1,0:T(8,128)(2,1)S(1)}, f32[512,1024]{1,0:T(8,128)S(1)}, f32[8,1024]{1,0:T(8,128)S(1)}, bf16[4,128,1024]{2,1,0:T(8,128)(2,1)},...) custom-call(bf16[2048,1024]{1,0:T(8,128)(2,1)} %convolution_convert_fusion.2.refs_0_, ...), custom_call_target="tpu_custom_call" | custom-call | tf_op jit(solution)/shard_map/pallas_call | solution.py:134
  408.0 2.1 convolution_convert_fusion.8
  410.8 1.3 convolution_convert_fusion.4.grad_ref
  412.1 29.8 %shard_map.531 = bf16[2048,768]{1,0:T(8,128)(2,1)S(1)} custom-call(s32[8]{0:T(128)S(1)} %copy-done.43, s32[8]{0:T(128)S(1)} %copy-done.41, bf16[2048,768]{1,0:T(8,128)(2,1)S(1)} %copy-done.1, bf16[2048,256]{1,0:T(8,128)(2,1)S(1)} %convolution_convert_fusion.4.grad_ref, f32[8,2048]{1,0:T(8,128)S(1)} %copy-done.39, s32[2048,1]{1,0:T(8,128)S(1)} %copy.86.seq_ref.seq_col_ref, ...), custom_call_target="tpu_custom_call" | custom-call | tf_op jit(solution)/shard_map/pallas_call | solution.py:1332
  441.9 3.6 convolution_convert_fusion.7
  445.6 2.4 reduce.3
  448.0 6.0 convolution_convert_fusion.1.refs_0_
  454.0 47.8 %shard_map.532 = (bf16[4,512,256]{2,1,0:T(8,128)(2,1)}, f32[8,1024]{1,0:T(8,128)S(1)}, f32[128,1024]{1,0:T(8,128)S(1)}, f32[8,1024]{1,0:T(8,128)S(1)}, bf16[4,12...) custom-call(bf16[2048,1024]{1,0:T(8,128)(2,1)S(1)} %convolution_conv, ...), custom_call_target="tpu_custom_call" | custom-call | tf_op jit(solution)/shard_map/pallas_call | solution.py:134
  501.9 2.3 fusion.19
  504.3 5.5 fusion.17
  509.8 28.0 %shard_map.533 = (bf16[8,192,256]{2,1,0:T(8,128)(2,1)}, bf16[4,80,256]{2,1,0:T(8,128)(2,1)}, f32[80,256]{1,0:T(8,128)S(1)}, f32[8,256]{1,0:T(8,128)S(1)}) custom-call(bf16[8,192,256]{2,1,0:T(8,128)(2,1)S(1)} %bitcast.173, bf16[4,2,80,256]{3,2,1,0:T(8,128)(2,1)S(1)} %bitcast.170), custom_call_target="tpu_custom_call" | custom-call | tf_op jit(solution)/shard_map/pallas_call | solution.py:134
  537.9 11.4 %conditional.3 = ((f32[6284,256]{1,0:T(8,128)}, f32[8,256]{1,0:T(8,128)S(1)})) conditional(s32[]{:T(128)} %convert_element_type.128, (s32[]{:T(128)}, s32[8,192]{1,0:T(8,128)S(1)}, bf16[8,192,256]{2,1,0:T(8,128)(2,1)}) %tuple.76, (s32[512]{0:T(512)S(1)}, s32[16384]{0:T(1024)S(1)}, s32[]{:T(128)}, bf16[2048,256]{1,0:T(8,128)(2,1)}) %tuple.77), branch_computations={%region_13.15_spmd, %region_14.18_spmd} | conditional | flops 16242432 | bytes 50336844 | solution.py:1989
  538.0 11.2 %branch_0_fun.1 = (f32[6284,256]{1,0:T(8,128)}, f32[8,256]{1,0:T(8,128)S(1)}) custom-call(s32[1,1536]{1,0:T(1,128)S(1)} %sub.80.index_ref, bf16[1536,256]{1,0:T(8,128)(2,1)} %bitcast.198), custom_call_target="tpu_custom_call" | custom-call | tf_op jit(solution)/shard_map/cond/branch_0_fun/pallas_call | solution.py:1512
  549.5 16.3 %shard_map.534 = (f32[1,16,1024]{2,1,0:T(8,128)S(1)}, bf16[4,2,80,256]{3,2,1,0:T(8,128)(2,1)S(1)}) custom-call(f32[16,1024]{1,0:T(8,128)S(1)} %concatenate.25.refs_0_, bf16[80,256]{1,0:T(8,128)(2,1)S(1)} %convert_element_type.154.refs_1_), custom_call_target="tpu_custom_call" | custom-call | tf_op jit(solution)/shard_map/pallas_call | solution.py:134
  572.0 1.3 multiply_subtract_fusion.7
  573.3 2.5 fusion.36
  575.9 2.8 multiply_subtract_fusion.2
  578.8 1.9 multiply_subtract_fusion.4
  580.7 1.4 multiply_subtract_fusion.3
  582.2 9.6 %multiply_subtract_fusion.1 = (f32[1024,1024]{1,0:T(8,128)}, f32[1024,1024]{1,0:T(8,128)}, f32[1024,1024]{1,0:T(8,128)}) fusion(f32[1024,1024]{1,0:T(8,128)S(1)} %copy-done.4, f32[]{:T(128)S(6)} %min_shard_map.3, f32[1024,1024]{1,0:T(8,128)S(1)} %copy-done.81, f32[1024,1024]{1,0:T(8,128)} %param.61, bf16[64,1024]{1,0:T(8,128)(2,1)S(1)} %copy-done.55, ...), kind=kOutput, calls=%fused_computation.43 | convolution fusion | flops 822083584 | bytes 25559044 | tf_op jit(solution)/shard_map/dot_general | solution.py:34
  591.8 13.6 %multiply_subtract_fusion = (f32[6284,256]{1,0:T(8,128)}, f32[6284,256]{1,0:T(8,128)}, f32[6284,256]{1,0:T(8,128)}) fusion(f32[6284,256]{1,0:T(8,128)S(1)} %bitcast.190, f32[6284,256]{1,0:T(8,128)} %get-tuple-element.176, f32[]{:T(128)S(6)} %min_shard_map.3, f32[6284,256]{1,0:T(8,128)} %param.42, f32[6284,256]{1,0:T(8,128)} %param.43), kind=kLoop, calls=%fused_computation.35 | loop fusion | flops 25739264 | bytes 45043716 | tf_op jit(solution)/shard_map/sub | solution.py:59
  (237 shorter events, 26.8 us)
Async XLA Ops:
  7.2 15.3 %copy-start.75 = (s32[512]{0:T(512)S(1)}, s32[512]{0:T(512)}, u32[]{:S(2)}) copy-start(s32[512]{0:T(512)} %param.38) | copy-start | bytes 6148
  7.2 15.3 %copy-start.45 = (s32[512]{0:T(512)S(1)}, s32[512]{0:T(512)}, u32[]{:S(2)}) copy-start(s32[512]{0:T(512)} %param.37) | copy-start | bytes 6148
  41.1 10.3 %copy-start.56 = (s32[32,4,128]{2,1,0:T(4,128)}, s32[32,4,128]{2,1,0:T(4,128)S(1)}, u32[]{:S(2)}) copy-start(s32[32,4,128]{2,1,0:T(4,128)S(1)} %get-tuple-element.131) | copy-start | bytes 196612
  60.1 7.7 %copy-start.70 = (s32[1,8,2,128]{3,1,2,0:T(8,128)}, s32[1,8,2,128]{3,1,2,0:T(8,128)S(1)}, u32[]{:S(2)}) copy-start(s32[1,8,2,128]{3,1,2,0:T(8,128)S(1)} %copy.98) | copy-start | bytes 24580
  61.0 7.2 %copy-start.7 = (f32[514,256]{1,0:T(8,128)S(1)}, f32[514,256]{1,0:T(8,128)}, u32[]{:S(2)}) copy-start(f32[514,256]{1,0:T(8,128)} %refs_1_.1) | copy-start | bytes 1579012
  98.5 39.4 %copy-start.6 = (f32[514,1024]{1,0:T(8,128)S(1)}, f32[514,1024]{1,0:T(8,128)}, u32[]{:S(2)}) copy-start(f32[514,1024]{1,0:T(8,128)} %copy-done.5) | copy-start | bytes 6316036
  98.5 39.4 %copy-start.20 = (f32[8,1024]{1,0:T(8,128)S(1)}, f32[8,1024]{1,0:T(8,128)}, u32[]{:S(2)}) copy-start(f32[8,1024]{1,0:T(8,128)} %refs_3_.3) | copy-start | bytes 98308
  137.9 14.0 %copy-start.51 = (bf16[4,2,128,768]{3,2,1,0:T(8,128)(2,1)}, bf16[4,2,128,768]{3,2,1,0:T(8,128)(2,1)S(1)}, u32[]{:S(2)}) copy-start(bf16[4,2,128,768]{3,2,1,0:T(8,128)(2,1)S(1)} %get-tuple-element.140) | copy-start | bytes 4718596
  137.9 34.7 %copy-start.22 = (bf16[4,2,128,256]{3,2,1,0:T(8,128)(2,1)}, bf16[4,2,128,256]{3,2,1,0:T(8,128)(2,1)S(1)}, u32[]{:S(2)}) copy-start(bf16[4,2,128,256]{3,2,1,0:T(8,128)(2,1)S(1)} %get-tuple-element.142) | copy-start | bytes 1572868
  137.9 10.3 %copy-start.80 = (f32[768]{0:T(1024)S(1)}, f32[768]{0:T(1024)}, u32[]{:S(2)}) copy-start(f32[768]{0:T(1024)} %pad_maximum_fusion.1) | copy-start | bytes 9220
  151.9 20.7 %copy-start = (bf16[2048,768]{1,0:T(8,128)(2,1)}, bf16[2048,768]{1,0:T(8,128)(2,1)S(1)}, u32[]{:S(2)}) copy-start(bf16[2048,768]{1,0:T(8,128)(2,1)S(1)} %add_convert_fusion.qkv_ref) | copy-start | bytes 9437188
  228.9 20.9 %copy-start.11 = (f32[512,1024]{1,0:T(8,128)}, f32[512,1024]{1,0:T(8,128)S(1)}, u32[]{:S(2)}) copy-start(f32[512,1024]{1,0:T(8,128)S(1)} %get-tuple-element.157.refs_2_) | copy-start | bytes 6291460
  228.9 20.9 %copy-start.13 = (bf16[4,2,128,1024]{3,2,1,0:T(8,128)(2,1)}, bf16[4,2,128,1024]{3,2,1,0:T(8,128)(2,1)S(1)}, u32[]{:S(2)}) copy-start(bf16[4,2,128,1024]{3,2,1,0:T(8,128)(2,1)S(1)} %get-tuple-element.146) | copy-start | bytes 6291460
  249.8 38.8 %copy-start.3 = (f32[1024,1024]{1,0:T(8,128)S(1)}, f32[1024,1024]{1,0:T(8,128)}, u32[]{:S(2)}) copy-start(f32[1024,1024]{1,0:T(8,128)} %head_ref.1) | copy-start | bytes 12582916
  249.8 38.8 %copy-start.37 = (s32[64,1]{1,0:T(8,128)S(1)}, s32[64,1]{1,0:T(8,128)}, u32[]{:S(2)}) copy-start(s32[64,1]{1,0:T(8,128)} %broadcast_in_dim_reshape_squeeze.4.pair_ref) | copy-start | bytes 772
  249.8 44.3 %copy-start.25 = (bf16[512,24]{1,0:T(8,128)(2,1)S(1)}, bf16[512,24]{1,0:T(8,128)(2,1)}, u32[]{:S(2)}) copy-start(bf16[512,24]{1,0:T(8,128)(2,1)} %copy.91.refs_2_) | copy-start | bytes 73732
  288.6 34.5 %copy-start.50 = (bf16[4,2,128,1024]{3,2,1,0:T(8,128)(2,1)S(1)}, bf16[4,2,128,1024]{3,2,1,0:T(8,128)(2,1)}, u32[]{:S(2)}) copy-start(bf16[4,2,128,1024]{3,2,1,0:T(8,128)(2,1)} %copy-done.49) | copy-start | bytes 6291460
  293.5 28.2 %copy-start.52 = (f32[64,1024]{1,0:T(8,128)}, f32[64,1024]{1,0:T(8,128)S(1)}, u32[]{:S(2)}) copy-start(f32[64,1024]{1,0:T(8,128)S(1)} %get-tuple-element.183) | copy-start | bytes 786436
  293.5 28.2 %copy-start.54 = (bf16[64,1024]{1,0:T(8,128)(2,1)}, bf16[64,1024]{1,0:T(8,128)(2,1)S(1)}, u32[]{:S(2)}) copy-start(bf16[64,1024]{1,0:T(8,128)(2,1)S(1)} %get-tuple-element.182) | copy-start | bytes 393220
  340.9 9.6 %copy-start.12 = (f32[512,1024]{1,0:T(8,128)S(1)}, f32[512,1024]{1,0:T(8,128)}, u32[]{:S(2)}) copy-start(f32[512,1024]{1,0:T(8,128)} %copy-done.11) | copy-start | bytes 6291460
  340.9 9.6 %copy-start.17 = (f32[512,1024]{1,0:T(8,128)S(1)}, f32[512,1024]{1,0:T(8,128)}, u32[]{:S(2)}) copy-start(f32[512,1024]{1,0:T(8,128)} %copy-done.16) | copy-start | bytes 6291460
  340.9 9.6 %copy-start.18 = (bf16[1024,1024]{1,0:T(8,128)(2,1)S(1)}, bf16[1024,1024]{1,0:T(8,128)(2,1)}, u32[]{:S(2)}) copy-start(bf16[1024,1024]{1,0:T(8,128)(2,1)} %convolution_convert_fusion.6) | copy-start | bytes 6291460
  340.9 9.6 %copy-start.19 = (bf16[1024,1024]{1,0:T(8,128)(2,1)S(1)}, bf16[1024,1024]{1,0:T(8,128)(2,1)}, u32[]{:S(2)}) copy-start(bf16[1024,1024]{1,0:T(8,128)(2,1)} %convolution_convert_fusion.5) | copy-start | bytes 6291460
  412.1 29.8 %copy-start.48 = (bf16[2048,1024]{1,0:T(8,128)(2,1)S(1)}, bf16[2048,1024]{1,0:T(8,128)(2,1)}, u32[]{:S(2)}) copy-start(bf16[2048,1024]{1,0:T(8,128)(2,1)} %copy-done.47) | copy-start | bytes 12582916
  454.0 47.9 %copy-start.79 = (s32[2048]{0:T(1024)S(1)}, s32[2048]{0:T(1024)}, u32[]{:S(2)}) copy-start(s32[2048]{0:T(1024)} %subtract_add_fusion) | copy-start | bytes 24580
  501.8 7.9 %copy-start.28 = (f32[128,1024]{1,0:T(8,128)}, f32[128,1024]{1,0:T(8,128)S(1)}, u32[]{:S(2)}) copy-start(f32[128,1024]{1,0:T(8,128)S(1)} %get-tuple-element.180) | copy-start | bytes 1572868
  501.8 7.9 %copy-start.30 = (f32[3,128,256]{2,1,0:T(8,128)}, f32[3,128,256]{2,1,0:T(8,128)S(1)}, u32[]{:S(2)}) copy-start(f32[3,128,256]{2,1,0:T(8,128)S(1)} %get-tuple-element.178) | copy-start | bytes 1179652
  504.2 33.5 %copy-start.57 = (s32[32,4,128]{2,1,0:T(4,128)S(1)}, s32[32,4,128]{2,1,0:T(4,128)}, u32[]{:S(2)}) copy-start(s32[32,4,128]{2,1,0:T(4,128)} %copy-done.56) | copy-start | bytes 196612
  504.3 33.5 %copy-start.71 = (s32[1,8,2,128]{3,1,2,0:T(8,128)S(1)}, s32[1,8,2,128]{3,1,2,0:T(8,128)}, u32[]{:S(2)}) copy-start(s32[1,8,2,128]{3,1,2,0:T(8,128)} %copy-done.70) | copy-start | bytes 24580
  504.3 33.5 %copy-start.76 = (s32[512]{0:T(512)S(1)}, s32[512]{0:T(512)}, u32[]{:S(2)}) copy-start(s32[512]{0:T(512)} %param.38) | copy-start | bytes 6148
  537.8 11.6 %copy-start.77 = (f32[1,1024]{1,0:T(1,128)S(1)}, f32[1,1024]{1,0:T(1,128)}, u32[]{:S(2)}) copy-start(f32[1,1024]{1,0:T(1,128)} %get-tuple-element.230) | copy-start | bytes 12292
  537.8 11.6 %copy-start.78 = (f32[1,1024]{1,0:T(1,128)S(1)}, f32[1,1024]{1,0:T(1,128)}, u32[]{:S(2)}) copy-start(f32[1,1024]{1,0:T(1,128)} %get-tuple-element.231) | copy-start | bytes 12292
  537.8 30.6 %copy-start.27 = (f32[1024,128]{1,0:T(8,128)S(1)}, f32[1024,128]{1,0:T(8,128)}, u32[]{:S(2)}) copy-start(f32[1024,128]{1,0:T(8,128)} %copy-done.26) | copy-start | bytes 1572868
  537.9 31.5 %copy-start.29 = (f32[128,1024]{1,0:T(8,128)S(1)}, f32[128,1024]{1,0:T(8,128)}, u32[]{:S(2)}) copy-start(f32[128,1024]{1,0:T(8,128)} %copy-done.28) | copy-start | bytes 1572868
  537.9 32.5 %copy-start.72 = (f32[8,1024]{1,0:T(8,128)S(1)}, f32[8,1024]{1,0:T(8,128)}, u32[]{:S(2)}) copy-start(f32[8,1024]{1,0:T(8,128)} %param.66) | copy-start | bytes 98308
  537.9 32.5 %copy-start.73 = (f32[8,1024]{1,0:T(8,128)S(1)}, f32[8,1024]{1,0:T(8,128)}, u32[]{:S(2)}) copy-start(f32[8,1024]{1,0:T(8,128)} %param.67) | copy-start | bytes 98308
  537.9 33.2 %copy-start.67 = (f32[256,128]{1,0:T(8,128)S(1)}, f32[256,128]{1,0:T(8,128)}, u32[]{:S(2)}) copy-start(f32[256,128]{1,0:T(8,128)} %param.50) | copy-start | bytes 393220
  537.9 33.1 %copy-start.68 = (f32[256,128]{1,0:T(8,128)S(1)}, f32[256,128]{1,0:T(8,128)}, u32[]{:S(2)}) copy-start(f32[256,128]{1,0:T(8,128)} %param.51) | copy-start | bytes 393220
  537.9 33.1 %copy-start.69 = (f32[256,128]{1,0:T(8,128)S(1)}, f32[256,128]{1,0:T(8,128)}, u32[]{:S(2)}) copy-start(f32[256,128]{1,0:T(8,128)} %param.52) | copy-start | bytes 393220
  549.4 22.6 %copy-start.74 = (f32[6,256]{1,0:T(8,128)S(1)}, f32[6,256]{1,0:T(8,128)}, u32[]{:S(2)}) copy-start(f32[6,256]{1,0:T(8,128)} %param.62) | copy-start | bytes 18436
  549.4 24.0 %copy-start.31 = (f32[3,128,256]{2,1,0:T(8,128)S(1)}, f32[3,128,256]{2,1,0:T(8,128)}, u32[]{:S(2)}) copy-start(f32[3,128,256]{2,1,0:T(8,128)} %copy-done.30) | copy-start | bytes 1179652
  549.4 26.5 %copy-start.8 = (f32[514,256]{1,0:T(8,128)S(1)}, f32[514,256]{1,0:T(8,128)}, u32[]{:S(2)}) copy-start(f32[514,256]{1,0:T(8,128)} %refs_1_.1) | copy-start | bytes 1579012
  571.1 7.7 %copy-start.58 = (f32[128,4,256]{2,1,0:T(4,128)S(1)}, f32[128,4,256]{2,1,0:T(4,128)}, u32[]{:S(2)}) copy-start(f32[128,4,256]{2,1,0:T(4,128)} %param.53) | copy-start | bytes 1572868
  571.1 7.7 %copy-start.60 = (f32[128,4,256]{2,1,0:T(4,128)S(1)}, f32[128,4,256]{2,1,0:T(4,128)}, u32[]{:S(2)}) copy-start(f32[128,4,256]{2,1,0:T(4,128)} %mul.537) | copy-start | bytes 1572868
  571.1 7.7 %copy-start.63 = (f32[128,4,256]{2,1,0:T(4,128)S(1)}, f32[128,4,256]{2,1,0:T(4,128)}, u32[]{:S(2)}) copy-start(f32[128,4,256]{2,1,0:T(4,128)} %param.54) | copy-start | bytes 1572868
  571.1 7.7 %copy-start.64 = (f32[128,4,256]{2,1,0:T(4,128)S(1)}, f32[128,4,256]{2,1,0:T(4,128)}, u32[]{:S(2)}) copy-start(f32[128,4,256]{2,1,0:T(4,128)} %param.55) | copy-start | bytes 1572868
  582.1 9.7 %slice-start = ((s8[6438912]{0:T(1024)(128)(4,1)}), s8[4194304]{0:T(1024)(128)(4,1)S(1)}, s32[]{:S(2)}) async-start(s8[6438912]{0:T(1024)(128)(4,1)} %bitcast.189), calls=%async_computation.3 | async-start | bytes 8388608
  582.2 9.6 %slice-start.1 = ((s8[6438912]{0:T(1024)(128)(4,1)}), s8[2244608]{0:T(1024)(128)(4,1)S(1)}, s32[]{:S(2)}) async-start(s8[6438912]{0:T(1024)(128)(4,1)} %bitcast.189), calls=%async_computation.4 | async-start | bytes 4489216
  (37 other events, 106.9 us)

commit v6 on v5

--- a/solution.py
+++ b/solution.py
@@ -1095,7 +1095,7 @@
 
 
 Q_BLOCK = 256
-K_BLOCK = 256
+K_BLOCK = 128
 
 
 def split_pair(wide):
@@ -1380,7 +1380,7 @@
 def expand(rows, weight, bias):
     slots, depth = rows.shape
     units = weight.shape[1]
-    tall = 256
+    tall = 512
     return pl.pallas_call(
         expand_kernel,
         grid=(slots // tall,),
@@ -1394,7 +1394,7 @@
             pl.BlockSpec((tall, units), lambda i: (i, 0)),
             pl.BlockSpec((tall, units), lambda i: (i, 0)),
         ],
-        compiler_params=pltpu.CompilerParams(vmem_limit_bytes=16 * 1024 * 1024),
+        compiler_params=pltpu.CompilerParams(vmem_limit_bytes=20 * 1024 * 1024),
     )(rows, weight, bias)
 
 
@@ -1738,7 +1738,7 @@
         in_specs=[in_vmem()] * 4,
         out_specs=[in_vmem()] * 2,
         scratch_shapes=[pltpu.VMEM((slots, 128), jnp.float32), pltpu.VMEM((slots, 128), jnp.float32)],
-        compiler_params=pltpu.CompilerParams(vmem_limit_bytes=16 * 1024 * 1024),
+        compiler_params=pltpu.CompilerParams(vmem_limit_bytes=20 * 1024 * 1024),
     )(perm[None], low.astype(jnp.bfloat16), high.astype(jnp.bfloat16), pair_row)
 
 

time: 621 us -> 640 us (1.031)
  Pallas kernels: 454 us -> 474 us
    pallas_call x11, Pallas kernels: 357 us -> 369 us  [exchange(): pl.pallas_call(kernel, out_shape=[out for task in tasks for out in task.o...]
where the time goes in v6:
time: 640 us; the launch traced here: 633 us
  Pallas kernels  474 us (74%)
  matrix products  73.4 us (11%)
  other arithmetic  39.1 us (6%)
  local copies, waits for them, and re-layouts  27 us (4%)
  between operations  19.4 us (3%)
    pallas_call x11, Pallas kernels, exchange(): pl.pallas_call(kernel, out_shape=[out for task in tasks for out in task.o...  369 us
    pallas_call x1, Pallas kernels, attend_back(): pl.pallas_call(attend_back_kernel, out_shape=jax.ShapeDtypeStruct(qkv_out...  35.2 us
    sub x7, other arithmetic, adam_step(): weight - step_rate * (first_hat / (jnp.sqrt(second_hat) + ADAM_EPS) + dec...  22.6 us
    pallas_call x1, Pallas kernels, attend(): pl.pallas_call(attend_kernel, out_shape=[jax.ShapeDtypeStruct((slots, col...  22.4 us
    dot_general x4, matrix products, turned_grad(): jnp.einsum('td,tc->dc', left_all, right_all, preferred_element_type=jnp.f...  17.5 us
    dot_general x5, matrix products, multiply_arrays(): return jnp.dot(left_mat, right_mat, preferred_element_type=jnp.float32)  17.2 us
    unnamed x176, local copies, waits for them, and re-layouts  13.1 us

profile of v6, /device:TPU:0, one launch (start us, length us, event | category | flops | bytes accessed | tf_op | source)
XLA Modules:
  0.0 633.0 jit_solution(5672130847798626060)
XLA Ops:
  8.7 1.2 bitcast_subtract_fusion.2.start_ref
  15.9 1.6 copy.85
  22.5 17.8 %shard_map.518 = (s32[32,4,128]{2,1,0:T(4,128)S(1)}, s32[4,4,128]{2,1,0:T(4,128)S(1)}, bf16[4,64,768]{2,1,0:T(8,128)(2,1)S(1)}) custom-call(s32[4,128]{1,0:T(4,128)S(1)} %bitcast.181, s32[4,128]{1,0:T(4,128)S(1)} %bitcast.204, bf16[64,768]{1,0:T(8,128)(2,1)S(1)} %get-tuple-element.220.refs_2_), custom_call_target="tpu_custom_call" | custom-call | tf_op jit(solution)/shard_map/pallas_call | solution.py:134
  41.3 10.1 %shard_map.519 = (s32[1,2048]{1,0:T(1,128)}, s32[8,8,128]{2,1,0:T(8,128)S(1)}) custom-call(s32[1,2048]{1,0:T(1,128)S(1)} %bitcast.180, bf16[128,128]{1,0:T(8,128)(2,1)S(1)} %get-tuple-element.225.low_ref, bf16[128,128]{1,0:T(8,128)(2,1)S(1)} %get-tuple-element.224.high_ref, s32[1,128]{1,0:T(1,128)S(1)} %pad_bitcast_fusion.pair_ref), custom_call_target="tpu_custom_call" | custom-call | tf_op jit(solution)/shard_map/pallas_call | solution.py:1732
  51.4 7.4 %shard_map.520 = s32[8,8,128]{2,1,0:T(8,128)S(1)} custom-call(s32[8,8,128]{2,1,0:T(8,128)S(1)} %get-tuple-element.132.refs_0_), custom_call_target="tpu_custom_call" | custom-call | tf_op jit(solution)/shard_map/pallas_call | solution.py:134
  61.0 6.5 %gather_fusion.3 = bf16[1536,256]{1,0:T(8,128)(2,1)S(1)} fusion(f32[6284,256]{1,0:T(8,128)} %param.41, s32[2048]{0:T(1024)S(1)} %pad_clamp_fusion), kind=kCustom, calls=%fused_computation.3 | custom fusion | bytes 1579008 | tf_op jit(solution)/shard_map/jit(_take)/gather | solution.py:1888
  68.2 28.3 %shard_map.521 = (bf16[8,192,256]{2,1,0:T(8,128)(2,1)S(1)}, f32[514,1024]{1,0:T(8,128)S(1)}, bf16[4,64,768]{2,1,0:T(8,128)(2,1)S(1)}) custom-call(bf16[8,192,256]{2,1,0:T(8,128)(2,1)S(1)} %select_convert_fusion.refs_0_, f32[514,256]{1,0:T(8,128)S(1)} %copy-done.7, bf16[64,768]{1,0:T(8,128)(2,1)S(1)} %get-tuple-element.219.refs_2_), custom_call_target="tpu_custom_call" | custom-call | tf_op jit(solution)/shard_map/pallas_call | solution.py:134
  96.4 1.3 copy-done.5
  98.5 4.2 conditional.2
  98.5 4.0 fusion.2
  105.6 32.3 %shard_map.522 = (bf16[2048,1024]{1,0:T(8,128)(2,1)S(1)}, bf16[4,128,256]{2,1,0:T(8,128)(2,1)}, bf16[4,2,128,256]{3,2,1,0:T(8,128)(2,1)S(1)}, bf16[4,2,128,768]{...) custom-call(bf16[2048,256]{1,0:T(8,128)(2,1)} %get-tuple-element.250.refs_0_, bf16[128,256]{1,0:T(8,128)(2,1)S(1)} %bitcast.178, ...), custom_call_target="tpu_custom_call" | custom-call | tf_op jit(solution)/shard_map/pallas_call | solution.py:134
  139.4 8.6 %shard_map.523 = (bf16[2048,1024]{1,0:T(8,128)(2,1)S(1)}, f32[512,1024]{1,0:T(8,128)S(1)}, f32[512,1024]{1,0:T(8,128)S(1)}) custom-call(s32[8]{0:T(128)S(1)} %copy-done.46, s32[2,16]{1,0:T(2,128)S(1)} %copy-done.44, s32[1]{0:T(128)} %bitcast.15.own_ref, bf16[2048,1024]{1,0:T(8,128)(2,1)S(1)} %get-tuple-element.137.tok_ref, f32[514,1024]{1,0:T(8,128)S(1)} %copy-done.6, ...), custom_call_target="tpu_custom_call" | custom-call | tf_op jit(solution)/shard_map/pallas_call | solution.py:1465
  148.1 3.6 add_convert_fusion.qkv_ref
  151.8 22.4 %shard_map.524 = (bf16[2048,256]{1,0:T(8,128)(2,1)S(1)}, f32[8,2048]{1,0:T(8,128)S(1)}) custom-call(s32[8]{0:T(128)S(1)} %copy-done.42, s32[8]{0:T(128)S(1)} %copy-done.40, bf16[2048,768]{1,0:T(8,128)(2,1)S(1)} %add_convert_fusion.qkv_ref, s32[2048,1]{1,0:T(8,128)S(1)} %copy.86.seq_ref.seq_col_ref, s32[8,2048]{1,0:T(8,128)S(1)} %broadcast_in_dim.150.seq_row_ref), custom_call_target="tpu_custom_call" | custom-call | tf_op jit(solution)/shard_map/pallas_call | solution.py:1222
  174.9 1.3 convolution_convert_fusion.refs_0_
  176.2 58.6 %shard_map.525 = (bf16[2048,1024]{1,0:T(8,128)(2,1)S(1)}, f32[512,1024]{1,0:T(8,128)S(1)}, f32[512,1024]{1,0:T(8,128)S(1)}, bf16[4,2,128,1024]{3,2,1,0:T(8,128)(...) custom-call(bf16[2048,1024]{1,0:T(8,128)(2,1)S(1)} %convolution_convert_fusion.refs_0_, ...), custom_call_target="tpu_custom_call" | custom-call | tf_op jit(solution)/shard_map/pallas_call | solution.py:134
  234.8 1.3 copy-done.49
  236.1 11.8 %shard_map.526 = (bf16[2048,1024]{1,0:T(8,128)(2,1)S(1)}, f32[2048,1024]{1,0:T(8,128)S(1)}) custom-call(bf16[2048,1024]{1,0:T(8,128)(2,1)S(1)} %get-tuple-element.145.rows_ref, bf16[1024,1024]{1,0:T(8,128)(2,1)S(1)} %bitcast.165, f32[1,1024]{1,0:T(1,128)S(1)} %bitcast.179), custom_call_target="tpu_custom_call" | custom-call | tf_op jit(solution)/shard_map/pallas_call | solution.py:1384
  248.0 6.8 %convolution_convert_fusion.3.refs_0_ = bf16[2048,1024]{1,0:T(8,128)(2,1)S(1)} fusion(bf16[2048,1024]{1,0:T(8,128)(2,1)S(1)} %get-tuple-element.147, bf16[1024,1024]{1,0:T(8,128)(2,1)} %bitcast.182), kind=kOutput, calls=%fused_computation.48 | convolution fusion | flops 4297064448 | bytes 10485760 | tf_op jit(solution)/shard_map/tf,df->td/dot_general | solution.py:1545
  254.9 39.6 %shard_map.527 = (f32[512,1024]{1,0:T(8,128)S(1)}, f32[8,8,1024]{2,1,0:T(8,128)S(1)}) custom-call(bf16[2048,1024]{1,0:T(8,128)(2,1)S(1)} %convolution_convert_fusion.3.refs_0_, f32[512,1024]{1,0:T(8,128)S(1)} %get-tuple-element.149.refs_1_, bf16[8,512]{1,0:T(8,128)(2,1)S(1)} %get-tuple-element.235.refs_2_, f32[8,1]{1,0:T(8,128)S(1)} %convert_element_type.141.refs_3_.refs_1_, ...), custom_call_target="tpu_custom_call" | custom-call | tf_op jit(solution)/shard_map/pallas_call | solution.py:134
  294.5 4.9 shard_map.528
  300.0 27.6 %shard_map.529 = (bf16[2048,1024]{1,0:T(8,128)(2,1)S(1)}, f32[512,1024]{1,0:T(8,128)S(1)}, f32[8,1024]{1,0:T(8,128)S(1)}) custom-call(f32[64,1024]{1,0:T(8,128)S(1)} %get-tuple-element.152.refs_0_, f32[8,1]{1,0:T(8,128)S(1)} %convert_element_type.141.refs_3_.refs_1_, bf16[512,24]{1,0:T(8,128)(2,1)S(1)} %copy-done.25, ...), custom_call_target="tpu_custom_call" | custom-call | tf_op jit(solution)/shard_map/pallas_call | solution.py:134
  327.7 1.3 copy-done.16
  329.0 6.0 fusion.66
  335.0 5.8 convolution_convert_fusion.6
  340.8 6.0 convolution_convert_fusion.5
  346.8 9.6 %convolution_convert_fusion.2.refs_0_ = bf16[2048,1024]{1,0:T(8,128)(2,1)} fusion(bf16[2048,1024]{1,0:T(8,128)(2,1)} %get-tuple-element.243, bf16[1024,1024]{1,0:T(8,128)(2,1)} %bitcast.166), kind=kOutput, calls=%fused_computation.47 | convolution fusion | flops 4297064448 | bytes 10485760 | tf_op jit(solution)/shard_map/tf,df->td/dot_general | solution.py:1591
  356.5 57.2 %shard_map.530 = (bf16[2048,1024]{1,0:T(8,128)(2,1)S(1)}, f32[512,1024]{1,0:T(8,128)S(1)}, f32[8,1024]{1,0:T(8,128)S(1)}, bf16[4,128,1024]{2,1,0:T(8,128)(2,1)},...) custom-call(bf16[2048,1024]{1,0:T(8,128)(2,1)} %convolution_convert_fusion.2.refs_0_, ...), custom_call_target="tpu_custom_call" | custom-call | tf_op jit(solution)/shard_map/pallas_call | solution.py:134
  413.7 2.1 convolution_convert_fusion.8
  416.4 1.3 convolution_convert_fusion.4.grad_ref
  417.7 35.2 %shard_map.531 = bf16[2048,768]{1,0:T(8,128)(2,1)S(1)} custom-call(s32[8]{0:T(128)S(1)} %copy-done.43, s32[8]{0:T(128)S(1)} %copy-done.41, bf16[2048,768]{1,0:T(8,128)(2,1)S(1)} %copy-done.1, bf16[2048,256]{1,0:T(8,128)(2,1)S(1)} %convolution_convert_fusion.4.grad_ref, f32[8,2048]{1,0:T(8,128)S(1)} %copy-done.39, s32[2048,1]{1,0:T(8,128)S(1)} %copy.86.seq_ref.seq_col_ref, ...), custom_call_target="tpu_custom_call" | custom-call | tf_op jit(solution)/shard_map/pallas_call | solution.py:1332
  452.9 3.6 convolution_convert_fusion.7
  456.6 2.4 reduce.3
  459.0 6.0 convolution_convert_fusion.1.refs_0_
  465.1 54.7 %shard_map.532 = (bf16[4,512,256]{2,1,0:T(8,128)(2,1)}, f32[8,1024]{1,0:T(8,128)S(1)}, f32[128,1024]{1,0:T(8,128)S(1)}, f32[8,1024]{1,0:T(8,128)S(1)}, bf16[4,12...) custom-call(bf16[2048,1024]{1,0:T(8,128)(2,1)S(1)} %convolution_conv, ...), custom_call_target="tpu_custom_call" | custom-call | tf_op jit(solution)/shard_map/pallas_call | solution.py:134
  519.9 2.3 fusion.19
  522.2 5.5 fusion.17
  527.7 29.9 %shard_map.533 = (bf16[8,192,256]{2,1,0:T(8,128)(2,1)}, bf16[4,80,256]{2,1,0:T(8,128)(2,1)}, f32[80,256]{1,0:T(8,128)S(1)}, f32[8,256]{1,0:T(8,128)S(1)}) custom-call(bf16[8,192,256]{2,1,0:T(8,128)(2,1)S(1)} %bitcast.173, bf16[4,2,80,256]{3,2,1,0:T(8,128)(2,1)S(1)} %bitcast.170), custom_call_target="tpu_custom_call" | custom-call | tf_op jit(solution)/shard_map/pallas_call | solution.py:134
  557.8 11.4 %conditional.3 = ((f32[6284,256]{1,0:T(8,128)}, f32[8,256]{1,0:T(8,128)S(1)})) conditional(s32[]{:T(128)} %convert_element_type.128, (s32[]{:T(128)}, s32[8,192]{1,0:T(8,128)S(1)}, bf16[8,192,256]{2,1,0:T(8,128)(2,1)}) %tuple.76, (s32[512]{0:T(512)S(1)}, s32[16384]{0:T(1024)S(1)}, s32[]{:T(128)}, bf16[2048,256]{1,0:T(8,128)(2,1)}) %tuple.77), branch_computations={%region_13.15_spmd, %region_14.18_spmd} | conditional | flops 16242432 | bytes 50336844 | solution.py:1989
  557.9 11.2 %branch_0_fun.1 = (f32[6284,256]{1,0:T(8,128)}, f32[8,256]{1,0:T(8,128)S(1)}) custom-call(s32[1,1536]{1,0:T(1,128)S(1)} %sub.81.index_ref, bf16[1536,256]{1,0:T(8,128)(2,1)} %bitcast.198), custom_call_target="tpu_custom_call" | custom-call | tf_op jit(solution)/shard_map/cond/branch_0_fun/pallas_call | solution.py:1512
  569.3 15.9 %shard_map.534 = (f32[1,16,1024]{2,1,0:T(8,128)S(1)}, bf16[4,2,80,256]{3,2,1,0:T(8,128)(2,1)S(1)}) custom-call(f32[16,1024]{1,0:T(8,128)S(1)} %concatenate.25.refs_0_, bf16[80,256]{1,0:T(8,128)(2,1)S(1)} %convert_element_type.154.refs_1_), custom_call_target="tpu_custom_call" | custom-call | tf_op jit(solution)/shard_map/pallas_call | solution.py:134
  591.4 1.3 multiply_subtract_fusion.7
  592.7 2.5 fusion.36
  595.3 2.8 multiply_subtract_fusion.2
  598.1 1.9 multiply_subtract_fusion.4
  600.1 1.4 multiply_subtract_fusion.3
  601.6 9.6 %multiply_subtract_fusion.1 = (f32[1024,1024]{1,0:T(8,128)}, f32[1024,1024]{1,0:T(8,128)}, f32[1024,1024]{1,0:T(8,128)}) fusion(f32[1024,1024]{1,0:T(8,128)S(1)} %copy-done.4, f32[]{:T(128)S(6)} %min_shard_map.3, f32[1024,1024]{1,0:T(8,128)S(1)} %copy-done.81, f32[1024,1024]{1,0:T(8,128)} %param.61, bf16[64,1024]{1,0:T(8,128)(2,1)S(1)} %copy-done.55, ...), kind=kOutput, calls=%fused_computation.43 | convolution fusion | flops 822083584 | bytes 25559044 | tf_op jit(solution)/shard_map/dot_general | solution.py:34
  611.2 13.6 %multiply_subtract_fusion = (f32[6284,256]{1,0:T(8,128)}, f32[6284,256]{1,0:T(8,128)}, f32[6284,256]{1,0:T(8,128)}) fusion(f32[6284,256]{1,0:T(8,128)S(1)} %bitcast.190, f32[6284,256]{1,0:T(8,128)} %get-tuple-element.176, f32[]{:T(128)S(6)} %min_shard_map.3, f32[6284,256]{1,0:T(8,128)} %param.42, f32[6284,256]{1,0:T(8,128)} %param.43), kind=kLoop, calls=%fused_computation.35 | loop fusion | flops 25739264 | bytes 45043716 | tf_op jit(solution)/shard_map/sub | solution.py:59
  (237 shorter events, 26.8 us)
Async XLA Ops:
  7.2 15.3 %copy-start.75 = (s32[512]{0:T(512)S(1)}, s32[512]{0:T(512)}, u32[]{:S(2)}) copy-start(s32[512]{0:T(512)} %param.38) | copy-start | bytes 6148
  7.2 15.3 %copy-start.45 = (s32[512]{0:T(512)S(1)}, s32[512]{0:T(512)}, u32[]{:S(2)}) copy-start(s32[512]{0:T(512)} %param.37) | copy-start | bytes 6148
  41.1 10.3 %copy-start.56 = (s32[32,4,128]{2,1,0:T(4,128)}, s32[32,4,128]{2,1,0:T(4,128)S(1)}, u32[]{:S(2)}) copy-start(s32[32,4,128]{2,1,0:T(4,128)S(1)} %get-tuple-element.131) | copy-start | bytes 196612
  60.1 7.7 %copy-start.70 = (s32[1,8,2,128]{3,1,2,0:T(8,128)}, s32[1,8,2,128]{3,1,2,0:T(8,128)S(1)}, u32[]{:S(2)}) copy-start(s32[1,8,2,128]{3,1,2,0:T(8,128)S(1)} %copy.98) | copy-start | bytes 24580
  61.0 7.2 %copy-start.7 = (f32[514,256]{1,0:T(8,128)S(1)}, f32[514,256]{1,0:T(8,128)}, u32[]{:S(2)}) copy-start(f32[514,256]{1,0:T(8,128)} %refs_1_.1) | copy-start | bytes 1579012
  98.5 39.4 %copy-start.6 = (f32[514,1024]{1,0:T(8,128)S(1)}, f32[514,1024]{1,0:T(8,128)}, u32[]{:S(2)}) copy-start(f32[514,1024]{1,0:T(8,128)} %copy-done.5) | copy-start | bytes 6316036
  98.5 39.4 %copy-start.20 = (f32[8,1024]{1,0:T(8,128)S(1)}, f32[8,1024]{1,0:T(8,128)}, u32[]{:S(2)}) copy-start(f32[8,1024]{1,0:T(8,128)} %refs_3_.3) | copy-start | bytes 98308
  137.9 13.8 %copy-start.51 = (bf16[4,2,128,768]{3,2,1,0:T(8,128)(2,1)}, bf16[4,2,128,768]{3,2,1,0:T(8,128)(2,1)S(1)}, u32[]{:S(2)}) copy-start(bf16[4,2,128,768]{3,2,1,0:T(8,128)(2,1)S(1)} %get-tuple-element.140) | copy-start | bytes 4718596
  137.9 37.0 %copy-start.22 = (bf16[4,2,128,256]{3,2,1,0:T(8,128)(2,1)}, bf16[4,2,128,256]{3,2,1,0:T(8,128)(2,1)S(1)}, u32[]{:S(2)}) copy-start(bf16[4,2,128,256]{3,2,1,0:T(8,128)(2,1)S(1)} %get-tuple-element.142) | copy-start | bytes 1572868
  137.9 10.1 %copy-start.80 = (f32[768]{0:T(1024)S(1)}, f32[768]{0:T(1024)}, u32[]{:S(2)}) copy-start(f32[768]{0:T(1024)} %pad_maximum_fusion.1) | copy-start | bytes 9220
  151.8 23.1 %copy-start = (bf16[2048,768]{1,0:T(8,128)(2,1)}, bf16[2048,768]{1,0:T(8,128)(2,1)S(1)}, u32[]{:S(2)}) copy-start(bf16[2048,768]{1,0:T(8,128)(2,1)S(1)} %add_convert_fusion.qkv_ref) | copy-start | bytes 9437188
  234.8 20.0 %copy-start.11 = (f32[512,1024]{1,0:T(8,128)}, f32[512,1024]{1,0:T(8,128)S(1)}, u32[]{:S(2)}) copy-start(f32[512,1024]{1,0:T(8,128)S(1)} %get-tuple-element.157.refs_2_) | copy-start | bytes 6291460
  234.8 20.0 %copy-start.13 = (bf16[4,2,128,1024]{3,2,1,0:T(8,128)(2,1)}, bf16[4,2,128,1024]{3,2,1,0:T(8,128)(2,1)S(1)}, u32[]{:S(2)}) copy-start(bf16[4,2,128,1024]{3,2,1,0:T(8,128)(2,1)S(1)} %get-tuple-element.146) | copy-start | bytes 6291460
  254.8 39.7 %copy-start.3 = (f32[1024,1024]{1,0:T(8,128)S(1)}, f32[1024,1024]{1,0:T(8,128)}, u32[]{:S(2)}) copy-start(f32[1024,1024]{1,0:T(8,128)} %head_ref.1) | copy-start | bytes 12582916
  254.8 39.7 %copy-start.37 = (s32[64,1]{1,0:T(8,128)S(1)}, s32[64,1]{1,0:T(8,128)}, u32[]{:S(2)}) copy-start(s32[64,1]{1,0:T(8,128)} %broadcast_in_dim_reshape_squeeze.4.pair_ref) | copy-start | bytes 772
  254.9 45.2 %copy-start.25 = (bf16[512,24]{1,0:T(8,128)(2,1)S(1)}, bf16[512,24]{1,0:T(8,128)(2,1)}, u32[]{:S(2)}) copy-start(bf16[512,24]{1,0:T(8,128)(2,1)} %copy.91.refs_2_) | copy-start | bytes 73732
  294.5 34.5 %copy-start.50 = (bf16[4,2,128,1024]{3,2,1,0:T(8,128)(2,1)S(1)}, bf16[4,2,128,1024]{3,2,1,0:T(8,128)(2,1)}, u32[]{:S(2)}) copy-start(bf16[4,2,128,1024]{3,2,1,0:T(8,128)(2,1)} %copy-done.49) | copy-start | bytes 6291460
  299.4 28.2 %copy-start.52 = (f32[64,1024]{1,0:T(8,128)}, f32[64,1024]{1,0:T(8,128)S(1)}, u32[]{:S(2)}) copy-start(f32[64,1024]{1,0:T(8,128)S(1)} %get-tuple-element.183) | copy-start | bytes 786436
  299.5 28.2 %copy-start.54 = (bf16[64,1024]{1,0:T(8,128)(2,1)}, bf16[64,1024]{1,0:T(8,128)(2,1)S(1)}, u32[]{:S(2)}) copy-start(bf16[64,1024]{1,0:T(8,128)(2,1)S(1)} %get-tuple-element.182) | copy-start | bytes 393220
  346.8 9.6 %copy-start.12 = (f32[512,1024]{1,0:T(8,128)S(1)}, f32[512,1024]{1,0:T(8,128)}, u32[]{:S(2)}) copy-start(f32[512,1024]{1,0:T(8,128)} %copy-done.11) | copy-start | bytes 6291460
  346.8 9.6 %copy-start.17 = (f32[512,1024]{1,0:T(8,128)S(1)}, f32[512,1024]{1,0:T(8,128)}, u32[]{:S(2)}) copy-start(f32[512,1024]{1,0:T(8,128)} %copy-done.16) | copy-start | bytes 6291460
  346.8 9.6 %copy-start.18 = (bf16[1024,1024]{1,0:T(8,128)(2,1)S(1)}, bf16[1024,1024]{1,0:T(8,128)(2,1)}, u32[]{:S(2)}) copy-start(bf16[1024,1024]{1,0:T(8,128)(2,1)} %convolution_convert_fusion.6) | copy-start | bytes 6291460
  346.8 9.6 %copy-start.19 = (bf16[1024,1024]{1,0:T(8,128)(2,1)S(1)}, bf16[1024,1024]{1,0:T(8,128)(2,1)}, u32[]{:S(2)}) copy-start(bf16[1024,1024]{1,0:T(8,128)(2,1)} %convolution_convert_fusion.5) | copy-start | bytes 6291460
  417.7 35.2 %copy-start.48 = (bf16[2048,1024]{1,0:T(8,128)(2,1)S(1)}, bf16[2048,1024]{1,0:T(8,128)(2,1)}, u32[]{:S(2)}) copy-start(bf16[2048,1024]{1,0:T(8,128)(2,1)} %copy-done.47) | copy-start | bytes 12582916
  465.0 54.8 %copy-start.79 = (s32[2048]{0:T(1024)S(1)}, s32[2048]{0:T(1024)}, u32[]{:S(2)}) copy-start(s32[2048]{0:T(1024)} %subtract_add_fusion) | copy-start | bytes 24580
  519.8 7.9 %copy-start.28 = (f32[128,1024]{1,0:T(8,128)}, f32[128,1024]{1,0:T(8,128)S(1)}, u32[]{:S(2)}) copy-start(f32[128,1024]{1,0:T(8,128)S(1)} %get-tuple-element.180) | copy-start | bytes 1572868
  519.8 7.9 %copy-start.30 = (f32[3,128,256]{2,1,0:T(8,128)}, f32[3,128,256]{2,1,0:T(8,128)S(1)}, u32[]{:S(2)}) copy-start(f32[3,128,256]{2,1,0:T(8,128)S(1)} %get-tuple-element.178) | copy-start | bytes 1179652
  522.2 35.4 %copy-start.57 = (s32[32,4,128]{2,1,0:T(4,128)S(1)}, s32[32,4,128]{2,1,0:T(4,128)}, u32[]{:S(2)}) copy-start(s32[32,4,128]{2,1,0:T(4,128)} %copy-done.56) | copy-start | bytes 196612
  522.2 35.4 %copy-start.71 = (s32[1,8,2,128]{3,1,2,0:T(8,128)S(1)}, s32[1,8,2,128]{3,1,2,0:T(8,128)}, u32[]{:S(2)}) copy-start(s32[1,8,2,128]{3,1,2,0:T(8,128)} %copy-done.70) | copy-start | bytes 24580
  522.2 35.4 %copy-start.76 = (s32[512]{0:T(512)S(1)}, s32[512]{0:T(512)}, u32[]{:S(2)}) copy-start(s32[512]{0:T(512)} %param.38) | copy-start | bytes 6148
  557.6 11.6 %copy-start.77 = (f32[1,1024]{1,0:T(1,128)S(1)}, f32[1,1024]{1,0:T(1,128)}, u32[]{:S(2)}) copy-start(f32[1,1024]{1,0:T(1,128)} %get-tuple-element.230) | copy-start | bytes 12292
  557.7 11.6 %copy-start.78 = (f32[1,1024]{1,0:T(1,128)S(1)}, f32[1,1024]{1,0:T(1,128)}, u32[]{:S(2)}) copy-start(f32[1,1024]{1,0:T(1,128)} %get-tuple-element.231) | copy-start | bytes 12292
  557.7 30.2 %copy-start.27 = (f32[1024,128]{1,0:T(8,128)S(1)}, f32[1024,128]{1,0:T(8,128)}, u32[]{:S(2)}) copy-start(f32[1024,128]{1,0:T(8,128)} %copy-done.26) | copy-start | bytes 1572868
  557.7 31.0 %copy-start.29 = (f32[128,1024]{1,0:T(8,128)S(1)}, f32[128,1024]{1,0:T(8,128)}, u32[]{:S(2)}) copy-start(f32[128,1024]{1,0:T(8,128)} %copy-done.28) | copy-start | bytes 1572868
  557.7 32.1 %copy-start.72 = (f32[8,1024]{1,0:T(8,128)S(1)}, f32[8,1024]{1,0:T(8,128)}, u32[]{:S(2)}) copy-start(f32[8,1024]{1,0:T(8,128)} %param.66) | copy-start | bytes 98308
  557.7 32.1 %copy-start.73 = (f32[8,1024]{1,0:T(8,128)S(1)}, f32[8,1024]{1,0:T(8,128)}, u32[]{:S(2)}) copy-start(f32[8,1024]{1,0:T(8,128)} %param.67) | copy-start | bytes 98308
  557.7 32.7 %copy-start.67 = (f32[256,128]{1,0:T(8,128)S(1)}, f32[256,128]{1,0:T(8,128)}, u32[]{:S(2)}) copy-start(f32[256,128]{1,0:T(8,128)} %param.50) | copy-start | bytes 393220
  557.7 32.7 %copy-start.68 = (f32[256,128]{1,0:T(8,128)S(1)}, f32[256,128]{1,0:T(8,128)}, u32[]{:S(2)}) copy-start(f32[256,128]{1,0:T(8,128)} %param.51) | copy-start | bytes 393220
  557.7 32.7 %copy-start.69 = (f32[256,128]{1,0:T(8,128)S(1)}, f32[256,128]{1,0:T(8,128)}, u32[]{:S(2)}) copy-start(f32[256,128]{1,0:T(8,128)} %param.52) | copy-start | bytes 393220
  569.2 22.2 %copy-start.74 = (f32[6,256]{1,0:T(8,128)S(1)}, f32[6,256]{1,0:T(8,128)}, u32[]{:S(2)}) copy-start(f32[6,256]{1,0:T(8,128)} %param.62) | copy-start | bytes 18436
  569.2 23.5 %copy-start.31 = (f32[3,128,256]{2,1,0:T(8,128)S(1)}, f32[3,128,256]{2,1,0:T(8,128)}, u32[]{:S(2)}) copy-start(f32[3,128,256]{2,1,0:T(8,128)} %copy-done.30) | copy-start | bytes 1179652
  569.3 26.0 %copy-start.8 = (f32[514,256]{1,0:T(8,128)S(1)}, f32[514,256]{1,0:T(8,128)}, u32[]{:S(2)}) copy-start(f32[514,256]{1,0:T(8,128)} %refs_1_.1) | copy-start | bytes 1579012
  590.4 7.7 %copy-start.58 = (f32[128,4,256]{2,1,0:T(4,128)S(1)}, f32[128,4,256]{2,1,0:T(4,128)}, u32[]{:S(2)}) copy-start(f32[128,4,256]{2,1,0:T(4,128)} %param.53) | copy-start | bytes 1572868
  590.4 7.7 %copy-start.60 = (f32[128,4,256]{2,1,0:T(4,128)S(1)}, f32[128,4,256]{2,1,0:T(4,128)}, u32[]{:S(2)}) copy-start(f32[128,4,256]{2,1,0:T(4,128)} %mul.537) | copy-start | bytes 1572868
  590.5 7.7 %copy-start.63 = (f32[128,4,256]{2,1,0:T(4,128)S(1)}, f32[128,4,256]{2,1,0:T(4,128)}, u32[]{:S(2)}) copy-start(f32[128,4,256]{2,1,0:T(4,128)} %param.54) | copy-start | bytes 1572868
  590.5 7.7 %copy-start.64 = (f32[128,4,256]{2,1,0:T(4,128)S(1)}, f32[128,4,256]{2,1,0:T(4,128)}, u32[]{:S(2)}) copy-start(f32[128,4,256]{2,1,0:T(4,128)} %param.55) | copy-start | bytes 1572868
  601.5 9.7 %slice-start = ((s8[6438912]{0:T(1024)(128)(4,1)}), s8[4194304]{0:T(1024)(128)(4,1)S(1)}, s32[]{:S(2)}) async-start(s8[6438912]{0:T(1024)(128)(4,1)} %bitcast.189), calls=%async_computation.3 | async-start | bytes 8388608
  601.5 9.6 %slice-start.1 = ((s8[6438912]{0:T(1024)(128)(4,1)}), s8[2244608]{0:T(1024)(128)(4,1)S(1)}, s32[]{:S(2)}) async-start(s8[6438912]{0:T(1024)(128)(4,1)} %bitcast.189), calls=%async_computation.4 | async-start | bytes 4489216
  (37 other events, 106.9 us)

commit v7 on v6

--- a/solution.py
+++ b/solution.py
@@ -1095,7 +1095,7 @@
 
 
 Q_BLOCK = 256
-K_BLOCK = 128
+K_BLOCK = 512
 
 
 def split_pair(wide):
@@ -1209,7 +1209,7 @@
     return (lowest // K_BLOCK, (highest + K_BLOCK - 1) // K_BLOCK)
 
 
-REACH = (2 * MAXLEN - 2) // K_BLOCK + Q_BLOCK // K_BLOCK + 1
+REACH = (2 * MAXLEN - 2 + Q_BLOCK) // K_BLOCK + 1
 
 
 def in_scalars():

time: 640 us -> 618 us (0.966)
  Pallas kernels: 474 us -> 450 us
    pallas_call x11, Pallas kernels: 369 us -> 358 us  [exchange(): pl.pallas_call(kernel, out_shape=[out for task in tasks for out in task.o...]
    pallas_call x1, Pallas kernels: 35.2 us -> 28.3 us  [attend_back(): pl.pallas_call(attend_back_kernel, out_shape=jax.ShapeDtypeStruct(qkv_out...]
where the time goes in v7:
time: 618 us; the launch traced here: 610 us
  Pallas kernels  450 us (73%)
  matrix products  73.4 us (12%)
  other arithmetic  39.1 us (6%)
  local copies, waits for them, and re-layouts  27 us (4%)
  between operations  19.4 us (3%)
    pallas_call x11, Pallas kernels, exchange(): pl.pallas_call(kernel, out_shape=[out for task in tasks for out in task.o...  358 us
    pallas_call x1, Pallas kernels, attend_back(): pl.pallas_call(attend_back_kernel, out_shape=jax.ShapeDtypeStruct(qkv_out...  28.3 us
    sub x7, other arithmetic, adam_step(): weight - step_rate * (first_hat / (jnp.sqrt(second_hat) + ADAM_EPS) + dec...  22.6 us
    dot_general x4, matrix products, turned_grad(): jnp.einsum('td,tc->dc', left_all, right_all, preferred_element_type=jnp.f...  17.5 us
    pallas_call x1, Pallas kernels, attend(): pl.pallas_call(attend_kernel, out_shape=[jax.ShapeDtypeStruct((slots, col...  17.4 us
    dot_general x5, matrix products, multiply_arrays(): return jnp.dot(left_mat, right_mat, preferred_element_type=jnp.float32)  17.2 us
    unnamed x176, local copies, waits for them, and re-layouts  13.1 us

profile of v7, /device:TPU:0, one launch (start us, length us, event | category | flops | bytes accessed | tf_op | source)
XLA Modules:
  0.0 609.6 jit_solution(916007567497154410)
XLA Ops:
  8.7 1.2 bitcast_subtract_fusion.2.start_ref
  15.9 1.6 copy.85
  22.5 17.8 %shard_map.518 = (s32[32,4,128]{2,1,0:T(4,128)S(1)}, s32[4,4,128]{2,1,0:T(4,128)S(1)}, bf16[4,64,768]{2,1,0:T(8,128)(2,1)S(1)}) custom-call(s32[4,128]{1,0:T(4,128)S(1)} %bitcast.181, s32[4,128]{1,0:T(4,128)S(1)} %bitcast.204, bf16[64,768]{1,0:T(8,128)(2,1)S(1)} %get-tuple-element.220.refs_2_), custom_call_target="tpu_custom_call" | custom-call | tf_op jit(solution)/shard_map/pallas_call | solution.py:134
  41.3 10.1 %shard_map.519 = (s32[1,2048]{1,0:T(1,128)}, s32[8,8,128]{2,1,0:T(8,128)S(1)}) custom-call(s32[1,2048]{1,0:T(1,128)S(1)} %bitcast.180, bf16[128,128]{1,0:T(8,128)(2,1)S(1)} %get-tuple-element.225.low_ref, bf16[128,128]{1,0:T(8,128)(2,1)S(1)} %get-tuple-element.224.high_ref, s32[1,128]{1,0:T(1,128)S(1)} %pad_bitcast_fusion.pair_ref), custom_call_target="tpu_custom_call" | custom-call | tf_op jit(solution)/shard_map/pallas_call | solution.py:1732
  51.4 7.4 %shard_map.520 = s32[8,8,128]{2,1,0:T(8,128)S(1)} custom-call(s32[8,8,128]{2,1,0:T(8,128)S(1)} %get-tuple-element.132.refs_0_), custom_call_target="tpu_custom_call" | custom-call | tf_op jit(solution)/shard_map/pallas_call | solution.py:134
  61.0 6.5 %gather_fusion.3 = bf16[1536,256]{1,0:T(8,128)(2,1)S(1)} fusion(f32[6284,256]{1,0:T(8,128)} %param.41, s32[2048]{0:T(1024)S(1)} %pad_clamp_fusion), kind=kCustom, calls=%fused_computation.3 | custom fusion | bytes 1579008 | tf_op jit(solution)/shard_map/jit(_take)/gather | solution.py:1888
  68.2 28.3 %shard_map.521 = (bf16[8,192,256]{2,1,0:T(8,128)(2,1)S(1)}, f32[514,1024]{1,0:T(8,128)S(1)}, bf16[4,64,768]{2,1,0:T(8,128)(2,1)S(1)}) custom-call(bf16[8,192,256]{2,1,0:T(8,128)(2,1)S(1)} %select_convert_fusion.refs_0_, f32[514,256]{1,0:T(8,128)S(1)} %copy-done.7, bf16[64,768]{1,0:T(8,128)(2,1)S(1)} %get-tuple-element.219.refs_2_), custom_call_target="tpu_custom_call" | custom-call | tf_op jit(solution)/shard_map/pallas_call | solution.py:134
  96.4 1.3 copy-done.5
  98.5 4.0 conditional.2
  98.5 4.0 fusion.2
  105.3 32.3 %shard_map.522 = (bf16[2048,1024]{1,0:T(8,128)(2,1)S(1)}, bf16[4,128,256]{2,1,0:T(8,128)(2,1)}, bf16[4,2,128,256]{3,2,1,0:T(8,128)(2,1)S(1)}, bf16[4,2,128,768]{...) custom-call(bf16[2048,256]{1,0:T(8,128)(2,1)} %get-tuple-element.250.refs_0_, bf16[128,256]{1,0:T(8,128)(2,1)S(1)} %bitcast.178, ...), custom_call_target="tpu_custom_call" | custom-call | tf_op jit(solution)/shard_map/pallas_call | solution.py:134
  139.2 9.0 %shard_map.523 = (bf16[2048,1024]{1,0:T(8,128)(2,1)S(1)}, f32[512,1024]{1,0:T(8,128)S(1)}, f32[512,1024]{1,0:T(8,128)S(1)}) custom-call(s32[8]{0:T(128)S(1)} %copy-done.46, s32[2,16]{1,0:T(2,128)S(1)} %copy-done.44, s32[1]{0:T(128)} %bitcast.15.own_ref, bf16[2048,1024]{1,0:T(8,128)(2,1)S(1)} %get-tuple-element.137.tok_ref, f32[514,1024]{1,0:T(8,128)S(1)} %copy-done.6, ...), custom_call_target="tpu_custom_call" | custom-call | tf_op jit(solution)/shard_map/pallas_call | solution.py:1465
  148.2 3.6 add_convert_fusion.qkv_ref
  151.9 17.4 %shard_map.524 = (bf16[2048,256]{1,0:T(8,128)(2,1)S(1)}, f32[8,2048]{1,0:T(8,128)S(1)}) custom-call(s32[8]{0:T(128)S(1)} %copy-done.42, s32[8]{0:T(128)S(1)} %copy-done.40, bf16[2048,768]{1,0:T(8,128)(2,1)S(1)} %add_convert_fusion.qkv_ref, s32[2048,1]{1,0:T(8,128)S(1)} %copy.86.seq_ref.seq_col_ref, s32[8,2048]{1,0:T(8,128)S(1)} %broadcast_in_dim.150.seq_row_ref), custom_call_target="tpu_custom_call" | custom-call | tf_op jit(solution)/shard_map/pallas_call | solution.py:1222
  170.0 1.3 convolution_convert_fusion.refs_0_
  171.3 55.1 %shard_map.525 = (bf16[2048,1024]{1,0:T(8,128)(2,1)S(1)}, f32[512,1024]{1,0:T(8,128)S(1)}, f32[512,1024]{1,0:T(8,128)S(1)}, bf16[4,2,128,1024]{3,2,1,0:T(8,128)(...) custom-call(bf16[2048,1024]{1,0:T(8,128)(2,1)S(1)} %convolution_convert_fusion.refs_0_, ...), custom_call_target="tpu_custom_call" | custom-call | tf_op jit(solution)/shard_map/pallas_call | solution.py:134
  226.4 1.3 copy-done.49
  227.7 11.8 %shard_map.526 = (bf16[2048,1024]{1,0:T(8,128)(2,1)S(1)}, f32[2048,1024]{1,0:T(8,128)S(1)}) custom-call(bf16[2048,1024]{1,0:T(8,128)(2,1)S(1)} %get-tuple-element.145.rows_ref, bf16[1024,1024]{1,0:T(8,128)(2,1)S(1)} %bitcast.165, f32[1,1024]{1,0:T(1,128)S(1)} %bitcast.179), custom_call_target="tpu_custom_call" | custom-call | tf_op jit(solution)/shard_map/pallas_call | solution.py:1384
  239.5 6.8 %convolution_convert_fusion.3.refs_0_ = bf16[2048,1024]{1,0:T(8,128)(2,1)S(1)} fusion(bf16[2048,1024]{1,0:T(8,128)(2,1)S(1)} %get-tuple-element.147, bf16[1024,1024]{1,0:T(8,128)(2,1)} %bitcast.182), kind=kOutput, calls=%fused_computation.48 | convolution fusion | flops 4297064448 | bytes 10485760 | tf_op jit(solution)/shard_map/tf,df->td/dot_general | solution.py:1545
  246.4 38.7 %shard_map.527 = (f32[512,1024]{1,0:T(8,128)S(1)}, f32[8,8,1024]{2,1,0:T(8,128)S(1)}) custom-call(bf16[2048,1024]{1,0:T(8,128)(2,1)S(1)} %convolution_convert_fusion.3.refs_0_, f32[512,1024]{1,0:T(8,128)S(1)} %get-tuple-element.149.refs_1_, bf16[8,512]{1,0:T(8,128)(2,1)S(1)} %get-tuple-element.235.refs_2_, f32[8,1]{1,0:T(8,128)S(1)} %convert_element_type.141.refs_3_.refs_1_, ...), custom_call_target="tpu_custom_call" | custom-call | tf_op jit(solution)/shard_map/pallas_call | solution.py:134
  285.2 4.9 shard_map.528
  290.7 27.6 %shard_map.529 = (bf16[2048,1024]{1,0:T(8,128)(2,1)S(1)}, f32[512,1024]{1,0:T(8,128)S(1)}, f32[8,1024]{1,0:T(8,128)S(1)}) custom-call(f32[64,1024]{1,0:T(8,128)S(1)} %get-tuple-element.152.refs_0_, f32[8,1]{1,0:T(8,128)S(1)} %convert_element_type.141.refs_3_.refs_1_, bf16[512,24]{1,0:T(8,128)(2,1)S(1)} %copy-done.25, ...), custom_call_target="tpu_custom_call" | custom-call | tf_op jit(solution)/shard_map/pallas_call | solution.py:134
  318.3 1.3 copy-done.16
  319.7 6.0 fusion.66
  325.7 5.8 convolution_convert_fusion.6
  331.5 6.0 convolution_convert_fusion.5
  337.5 9.6 %convolution_convert_fusion.2.refs_0_ = bf16[2048,1024]{1,0:T(8,128)(2,1)} fusion(bf16[2048,1024]{1,0:T(8,128)(2,1)} %get-tuple-element.243, bf16[1024,1024]{1,0:T(8,128)(2,1)} %bitcast.166), kind=kOutput, calls=%fused_computation.47 | convolution fusion | flops 4297064448 | bytes 10485760 | tf_op jit(solution)/shard_map/tf,df->td/dot_general | solution.py:1591
  347.1 57.5 %shard_map.530 = (bf16[2048,1024]{1,0:T(8,128)(2,1)S(1)}, f32[512,1024]{1,0:T(8,128)S(1)}, f32[8,1024]{1,0:T(8,128)S(1)}, bf16[4,128,1024]{2,1,0:T(8,128)(2,1)},...) custom-call(bf16[2048,1024]{1,0:T(8,128)(2,1)} %convolution_convert_fusion.2.refs_0_, ...), custom_call_target="tpu_custom_call" | custom-call | tf_op jit(solution)/shard_map/pallas_call | solution.py:134
  404.7 2.1 convolution_convert_fusion.8
  407.4 1.3 convolution_convert_fusion.4.grad_ref
  408.7 28.3 %shard_map.531 = bf16[2048,768]{1,0:T(8,128)(2,1)S(1)} custom-call(s32[8]{0:T(128)S(1)} %copy-done.43, s32[8]{0:T(128)S(1)} %copy-done.41, bf16[2048,768]{1,0:T(8,128)(2,1)S(1)} %copy-done.1, bf16[2048,256]{1,0:T(8,128)(2,1)S(1)} %convolution_convert_fusion.4.grad_ref, f32[8,2048]{1,0:T(8,128)S(1)} %copy-done.39, s32[2048,1]{1,0:T(8,128)S(1)} %copy.86.seq_ref.seq_col_ref, ...), custom_call_target="tpu_custom_call" | custom-call | tf_op jit(solution)/shard_map/pallas_call | solution.py:1332
  437.1 3.6 convolution_convert_fusion.7
  440.7 2.4 reduce.3
  443.2 6.0 convolution_convert_fusion.1.refs_0_
  449.2 47.8 %shard_map.532 = (bf16[4,512,256]{2,1,0:T(8,128)(2,1)}, f32[8,1024]{1,0:T(8,128)S(1)}, f32[128,1024]{1,0:T(8,128)S(1)}, f32[8,1024]{1,0:T(8,128)S(1)}, bf16[4,12...) custom-call(bf16[2048,1024]{1,0:T(8,128)(2,1)S(1)} %convolution_conv, ...), custom_call_target="tpu_custom_call" | custom-call | tf_op jit(solution)/shard_map/pallas_call | solution.py:134
  497.1 2.3 fusion.19
  499.4 5.5 fusion.17
  504.9 29.3 %shard_map.533 = (bf16[8,192,256]{2,1,0:T(8,128)(2,1)}, bf16[4,80,256]{2,1,0:T(8,128)(2,1)}, f32[80,256]{1,0:T(8,128)S(1)}, f32[8,256]{1,0:T(8,128)S(1)}) custom-call(bf16[8,192,256]{2,1,0:T(8,128)(2,1)S(1)} %bitcast.173, bf16[4,2,80,256]{3,2,1,0:T(8,128)(2,1)S(1)} %bitcast.170), custom_call_target="tpu_custom_call" | custom-call | tf_op jit(solution)/shard_map/pallas_call | solution.py:134
  534.4 11.4 %conditional.3 = ((f32[6284,256]{1,0:T(8,128)}, f32[8,256]{1,0:T(8,128)S(1)})) conditional(s32[]{:T(128)} %convert_element_type.128, (s32[]{:T(128)}, s32[8,192]{1,0:T(8,128)S(1)}, bf16[8,192,256]{2,1,0:T(8,128)(2,1)}) %tuple.76, (s32[512]{0:T(512)S(1)}, s32[16384]{0:T(1024)S(1)}, s32[]{:T(128)}, bf16[2048,256]{1,0:T(8,128)(2,1)}) %tuple.77), branch_computations={%region_13.15_spmd, %region_14.18_spmd} | conditional | flops 16242432 | bytes 50336844 | solution.py:1989
  534.5 11.2 %branch_0_fun.1 = (f32[6284,256]{1,0:T(8,128)}, f32[8,256]{1,0:T(8,128)S(1)}) custom-call(s32[1,1536]{1,0:T(1,128)S(1)} %sub.81.index_ref, bf16[1536,256]{1,0:T(8,128)(2,1)} %bitcast.198), custom_call_target="tpu_custom_call" | custom-call | tf_op jit(solution)/shard_map/cond/branch_0_fun/pallas_call | solution.py:1512
  545.9 15.9 %shard_map.534 = (f32[1,16,1024]{2,1,0:T(8,128)S(1)}, bf16[4,2,80,256]{3,2,1,0:T(8,128)(2,1)S(1)}) custom-call(f32[16,1024]{1,0:T(8,128)S(1)} %concatenate.25.refs_0_, bf16[80,256]{1,0:T(8,128)(2,1)S(1)} %convert_element_type.154.refs_1_), custom_call_target="tpu_custom_call" | custom-call | tf_op jit(solution)/shard_map/pallas_call | solution.py:134
  568.0 1.3 multiply_subtract_fusion.7
  569.4 2.5 fusion.36
  571.9 2.8 multiply_subtract_fusion.2
  574.8 1.9 multiply_subtract_fusion.4
  576.7 1.4 multiply_subtract_fusion.3
  578.2 9.6 %multiply_subtract_fusion.1 = (f32[1024,1024]{1,0:T(8,128)}, f32[1024,1024]{1,0:T(8,128)}, f32[1024,1024]{1,0:T(8,128)}) fusion(f32[1024,1024]{1,0:T(8,128)S(1)} %copy-done.4, f32[]{:T(128)S(6)} %min_shard_map.3, f32[1024,1024]{1,0:T(8,128)S(1)} %copy-done.81, f32[1024,1024]{1,0:T(8,128)} %param.61, bf16[64,1024]{1,0:T(8,128)(2,1)S(1)} %copy-done.55, ...), kind=kOutput, calls=%fused_computation.43 | convolution fusion | flops 822083584 | bytes 25559044 | tf_op jit(solution)/shard_map/dot_general | solution.py:34
  587.8 13.6 %multiply_subtract_fusion = (f32[6284,256]{1,0:T(8,128)}, f32[6284,256]{1,0:T(8,128)}, f32[6284,256]{1,0:T(8,128)}) fusion(f32[6284,256]{1,0:T(8,128)S(1)} %bitcast.190, f32[6284,256]{1,0:T(8,128)} %get-tuple-element.176, f32[]{:T(128)S(6)} %min_shard_map.3, f32[6284,256]{1,0:T(8,128)} %param.42, f32[6284,256]{1,0:T(8,128)} %param.43), kind=kLoop, calls=%fused_computation.35 | loop fusion | flops 25739264 | bytes 45043716 | tf_op jit(solution)/shard_map/sub | solution.py:59
  (237 shorter events, 26.8 us)
Async XLA Ops:
  7.2 15.3 %copy-start.75 = (s32[512]{0:T(512)S(1)}, s32[512]{0:T(512)}, u32[]{:S(2)}) copy-start(s32[512]{0:T(512)} %param.38) | copy-start | bytes 6148
  7.2 15.3 %copy-start.45 = (s32[512]{0:T(512)S(1)}, s32[512]{0:T(512)}, u32[]{:S(2)}) copy-start(s32[512]{0:T(512)} %param.37) | copy-start | bytes 6148
  41.1 10.3 %copy-start.56 = (s32[32,4,128]{2,1,0:T(4,128)}, s32[32,4,128]{2,1,0:T(4,128)S(1)}, u32[]{:S(2)}) copy-start(s32[32,4,128]{2,1,0:T(4,128)S(1)} %get-tuple-element.131) | copy-start | bytes 196612
  60.1 7.7 %copy-start.70 = (s32[1,8,2,128]{3,1,2,0:T(8,128)}, s32[1,8,2,128]{3,1,2,0:T(8,128)S(1)}, u32[]{:S(2)}) copy-start(s32[1,8,2,128]{3,1,2,0:T(8,128)S(1)} %copy.98) | copy-start | bytes 24580
  61.0 7.2 %copy-start.7 = (f32[514,256]{1,0:T(8,128)S(1)}, f32[514,256]{1,0:T(8,128)}, u32[]{:S(2)}) copy-start(f32[514,256]{1,0:T(8,128)} %refs_1_.1) | copy-start | bytes 1579012
  98.5 39.2 %copy-start.6 = (f32[514,1024]{1,0:T(8,128)S(1)}, f32[514,1024]{1,0:T(8,128)}, u32[]{:S(2)}) copy-start(f32[514,1024]{1,0:T(8,128)} %copy-done.5) | copy-start | bytes 6316036
  98.5 39.2 %copy-start.20 = (f32[8,1024]{1,0:T(8,128)S(1)}, f32[8,1024]{1,0:T(8,128)}, u32[]{:S(2)}) copy-start(f32[8,1024]{1,0:T(8,128)} %refs_3_.3) | copy-start | bytes 98308
  137.7 14.2 %copy-start.51 = (bf16[4,2,128,768]{3,2,1,0:T(8,128)(2,1)}, bf16[4,2,128,768]{3,2,1,0:T(8,128)(2,1)S(1)}, u32[]{:S(2)}) copy-start(bf16[4,2,128,768]{3,2,1,0:T(8,128)(2,1)S(1)} %get-tuple-element.140) | copy-start | bytes 4718596
  137.7 32.2 %copy-start.22 = (bf16[4,2,128,256]{3,2,1,0:T(8,128)(2,1)}, bf16[4,2,128,256]{3,2,1,0:T(8,128)(2,1)S(1)}, u32[]{:S(2)}) copy-start(bf16[4,2,128,256]{3,2,1,0:T(8,128)(2,1)S(1)} %get-tuple-element.142) | copy-start | bytes 1572868
  137.7 10.5 %copy-start.80 = (f32[768]{0:T(1024)S(1)}, f32[768]{0:T(1024)}, u32[]{:S(2)}) copy-start(f32[768]{0:T(1024)} %pad_maximum_fusion.1) | copy-start | bytes 9220
  151.9 18.0 %copy-start = (bf16[2048,768]{1,0:T(8,128)(2,1)}, bf16[2048,768]{1,0:T(8,128)(2,1)S(1)}, u32[]{:S(2)}) copy-start(bf16[2048,768]{1,0:T(8,128)(2,1)S(1)} %add_convert_fusion.qkv_ref) | copy-start | bytes 9437188
  226.4 20.0 %copy-start.11 = (f32[512,1024]{1,0:T(8,128)}, f32[512,1024]{1,0:T(8,128)S(1)}, u32[]{:S(2)}) copy-start(f32[512,1024]{1,0:T(8,128)S(1)} %get-tuple-element.157.refs_2_) | copy-start | bytes 6291460
  226.4 20.0 %copy-start.13 = (bf16[4,2,128,1024]{3,2,1,0:T(8,128)(2,1)}, bf16[4,2,128,1024]{3,2,1,0:T(8,128)(2,1)S(1)}, u32[]{:S(2)}) copy-start(bf16[4,2,128,1024]{3,2,1,0:T(8,128)(2,1)S(1)} %get-tuple-element.146) | copy-start | bytes 6291460
  246.4 38.8 %copy-start.3 = (f32[1024,1024]{1,0:T(8,128)S(1)}, f32[1024,1024]{1,0:T(8,128)}, u32[]{:S(2)}) copy-start(f32[1024,1024]{1,0:T(8,128)} %head_ref.1) | copy-start | bytes 12582916
  246.4 38.8 %copy-start.37 = (s32[64,1]{1,0:T(8,128)S(1)}, s32[64,1]{1,0:T(8,128)}, u32[]{:S(2)}) copy-start(s32[64,1]{1,0:T(8,128)} %broadcast_in_dim_reshape_squeeze.4.pair_ref) | copy-start | bytes 772
  246.4 44.3 %copy-start.25 = (bf16[512,24]{1,0:T(8,128)(2,1)S(1)}, bf16[512,24]{1,0:T(8,128)(2,1)}, u32[]{:S(2)}) copy-start(bf16[512,24]{1,0:T(8,128)(2,1)} %copy.91.refs_2_) | copy-start | bytes 73732
  285.2 34.5 %copy-start.50 = (bf16[4,2,128,1024]{3,2,1,0:T(8,128)(2,1)S(1)}, bf16[4,2,128,1024]{3,2,1,0:T(8,128)(2,1)}, u32[]{:S(2)}) copy-start(bf16[4,2,128,1024]{3,2,1,0:T(8,128)(2,1)} %copy-done.49) | copy-start | bytes 6291460
  290.1 28.2 %copy-start.52 = (f32[64,1024]{1,0:T(8,128)}, f32[64,1024]{1,0:T(8,128)S(1)}, u32[]{:S(2)}) copy-start(f32[64,1024]{1,0:T(8,128)S(1)} %get-tuple-element.183) | copy-start | bytes 786436
  290.1 28.2 %copy-start.54 = (bf16[64,1024]{1,0:T(8,128)(2,1)}, bf16[64,1024]{1,0:T(8,128)(2,1)S(1)}, u32[]{:S(2)}) copy-start(bf16[64,1024]{1,0:T(8,128)(2,1)S(1)} %get-tuple-element.182) | copy-start | bytes 393220
  337.5 9.6 %copy-start.12 = (f32[512,1024]{1,0:T(8,128)S(1)}, f32[512,1024]{1,0:T(8,128)}, u32[]{:S(2)}) copy-start(f32[512,1024]{1,0:T(8,128)} %copy-done.11) | copy-start | bytes 6291460
  337.5 9.6 %copy-start.17 = (f32[512,1024]{1,0:T(8,128)S(1)}, f32[512,1024]{1,0:T(8,128)}, u32[]{:S(2)}) copy-start(f32[512,1024]{1,0:T(8,128)} %copy-done.16) | copy-start | bytes 6291460
  337.5 9.6 %copy-start.18 = (bf16[1024,1024]{1,0:T(8,128)(2,1)S(1)}, bf16[1024,1024]{1,0:T(8,128)(2,1)}, u32[]{:S(2)}) copy-start(bf16[1024,1024]{1,0:T(8,128)(2,1)} %convolution_convert_fusion.6) | copy-start | bytes 6291460
  337.5 9.6 %copy-start.19 = (bf16[1024,1024]{1,0:T(8,128)(2,1)S(1)}, bf16[1024,1024]{1,0:T(8,128)(2,1)}, u32[]{:S(2)}) copy-start(bf16[1024,1024]{1,0:T(8,128)(2,1)} %convolution_convert_fusion.5) | copy-start | bytes 6291460
  408.7 28.3 %copy-start.48 = (bf16[2048,1024]{1,0:T(8,128)(2,1)S(1)}, bf16[2048,1024]{1,0:T(8,128)(2,1)}, u32[]{:S(2)}) copy-start(bf16[2048,1024]{1,0:T(8,128)(2,1)} %copy-done.47) | copy-start | bytes 12582916
  449.2 47.9 %copy-start.79 = (s32[2048]{0:T(1024)S(1)}, s32[2048]{0:T(1024)}, u32[]{:S(2)}) copy-start(s32[2048]{0:T(1024)} %subtract_add_fusion) | copy-start | bytes 24580
  497.0 7.9 %copy-start.28 = (f32[128,1024]{1,0:T(8,128)}, f32[128,1024]{1,0:T(8,128)S(1)}, u32[]{:S(2)}) copy-start(f32[128,1024]{1,0:T(8,128)S(1)} %get-tuple-element.180) | copy-start | bytes 1572868
  497.0 7.9 %copy-start.30 = (f32[3,128,256]{2,1,0:T(8,128)}, f32[3,128,256]{2,1,0:T(8,128)S(1)}, u32[]{:S(2)}) copy-start(f32[3,128,256]{2,1,0:T(8,128)S(1)} %get-tuple-element.178) | copy-start | bytes 1179652
  499.4 34.8 %copy-start.57 = (s32[32,4,128]{2,1,0:T(4,128)S(1)}, s32[32,4,128]{2,1,0:T(4,128)}, u32[]{:S(2)}) copy-start(s32[32,4,128]{2,1,0:T(4,128)} %copy-done.56) | copy-start | bytes 196612
  499.4 34.8 %copy-start.71 = (s32[1,8,2,128]{3,1,2,0:T(8,128)S(1)}, s32[1,8,2,128]{3,1,2,0:T(8,128)}, u32[]{:S(2)}) copy-start(s32[1,8,2,128]{3,1,2,0:T(8,128)} %copy-done.70) | copy-start | bytes 24580
  499.4 34.8 %copy-start.76 = (s32[512]{0:T(512)S(1)}, s32[512]{0:T(512)}, u32[]{:S(2)}) copy-start(s32[512]{0:T(512)} %param.38) | copy-start | bytes 6148
  534.3 11.6 %copy-start.77 = (f32[1,1024]{1,0:T(1,128)S(1)}, f32[1,1024]{1,0:T(1,128)}, u32[]{:S(2)}) copy-start(f32[1,1024]{1,0:T(1,128)} %get-tuple-element.230) | copy-start | bytes 12292
  534.3 11.6 %copy-start.78 = (f32[1,1024]{1,0:T(1,128)S(1)}, f32[1,1024]{1,0:T(1,128)}, u32[]{:S(2)}) copy-start(f32[1,1024]{1,0:T(1,128)} %get-tuple-element.231) | copy-start | bytes 12292
  534.3 30.2 %copy-start.27 = (f32[1024,128]{1,0:T(8,128)S(1)}, f32[1024,128]{1,0:T(8,128)}, u32[]{:S(2)}) copy-start(f32[1024,128]{1,0:T(8,128)} %copy-done.26) | copy-start | bytes 1572868
  534.3 31.0 %copy-start.29 = (f32[128,1024]{1,0:T(8,128)S(1)}, f32[128,1024]{1,0:T(8,128)}, u32[]{:S(2)}) copy-start(f32[128,1024]{1,0:T(8,128)} %copy-done.28) | copy-start | bytes 1572868
  534.3 32.1 %copy-start.72 = (f32[8,1024]{1,0:T(8,128)S(1)}, f32[8,1024]{1,0:T(8,128)}, u32[]{:S(2)}) copy-start(f32[8,1024]{1,0:T(8,128)} %param.66) | copy-start | bytes 98308
  534.3 32.1 %copy-start.73 = (f32[8,1024]{1,0:T(8,128)S(1)}, f32[8,1024]{1,0:T(8,128)}, u32[]{:S(2)}) copy-start(f32[8,1024]{1,0:T(8,128)} %param.67) | copy-start | bytes 98308
  534.3 32.7 %copy-start.67 = (f32[256,128]{1,0:T(8,128)S(1)}, f32[256,128]{1,0:T(8,128)}, u32[]{:S(2)}) copy-start(f32[256,128]{1,0:T(8,128)} %param.50) | copy-start | bytes 393220
  534.3 32.7 %copy-start.68 = (f32[256,128]{1,0:T(8,128)S(1)}, f32[256,128]{1,0:T(8,128)}, u32[]{:S(2)}) copy-start(f32[256,128]{1,0:T(8,128)} %param.51) | copy-start | bytes 393220
  534.4 32.7 %copy-start.69 = (f32[256,128]{1,0:T(8,128)S(1)}, f32[256,128]{1,0:T(8,128)}, u32[]{:S(2)}) copy-start(f32[256,128]{1,0:T(8,128)} %param.52) | copy-start | bytes 393220
  545.8 22.2 %copy-start.74 = (f32[6,256]{1,0:T(8,128)S(1)}, f32[6,256]{1,0:T(8,128)}, u32[]{:S(2)}) copy-start(f32[6,256]{1,0:T(8,128)} %param.62) | copy-start | bytes 18436
  545.8 23.5 %copy-start.31 = (f32[3,128,256]{2,1,0:T(8,128)S(1)}, f32[3,128,256]{2,1,0:T(8,128)}, u32[]{:S(2)}) copy-start(f32[3,128,256]{2,1,0:T(8,128)} %copy-done.30) | copy-start | bytes 1179652
  545.9 26.0 %copy-start.8 = (f32[514,256]{1,0:T(8,128)S(1)}, f32[514,256]{1,0:T(8,128)}, u32[]{:S(2)}) copy-start(f32[514,256]{1,0:T(8,128)} %refs_1_.1) | copy-start | bytes 1579012
  567.1 7.7 %copy-start.58 = (f32[128,4,256]{2,1,0:T(4,128)S(1)}, f32[128,4,256]{2,1,0:T(4,128)}, u32[]{:S(2)}) copy-start(f32[128,4,256]{2,1,0:T(4,128)} %param.53) | copy-start | bytes 1572868
  567.1 7.7 %copy-start.60 = (f32[128,4,256]{2,1,0:T(4,128)S(1)}, f32[128,4,256]{2,1,0:T(4,128)}, u32[]{:S(2)}) copy-start(f32[128,4,256]{2,1,0:T(4,128)} %mul.537) | copy-start | bytes 1572868
  567.1 7.7 %copy-start.63 = (f32[128,4,256]{2,1,0:T(4,128)S(1)}, f32[128,4,256]{2,1,0:T(4,128)}, u32[]{:S(2)}) copy-start(f32[128,4,256]{2,1,0:T(4,128)} %param.54) | copy-start | bytes 1572868
  567.1 7.7 %copy-start.64 = (f32[128,4,256]{2,1,0:T(4,128)S(1)}, f32[128,4,256]{2,1,0:T(4,128)}, u32[]{:S(2)}) copy-start(f32[128,4,256]{2,1,0:T(4,128)} %param.55) | copy-start | bytes 1572868
  578.2 9.7 %slice-start = ((s8[6438912]{0:T(1024)(128)(4,1)}), s8[4194304]{0:T(1024)(128)(4,1)S(1)}, s32[]{:S(2)}) async-start(s8[6438912]{0:T(1024)(128)(4,1)} %bitcast.189), calls=%async_computation.3 | async-start | bytes 8388608
  578.2 9.6 %slice-start.1 = ((s8[6438912]{0:T(1024)(128)(4,1)}), s8[2244608]{0:T(1024)(128)(4,1)S(1)}, s32[]{:S(2)}) async-start(s8[6438912]{0:T(1024)(128)(4,1)} %bitcast.189), calls=%async_computation.4 | async-start | bytes 4489216
  (37 other events, 106.9 us)
